TPU v7x, 32 devices: a whole 2x2x4 slice. The times are simulated.
32 devices in a mesh: role: 4 (over x, core), contr: 2 (over y), horiz: 4 (over z).
Axes of the slice: x: 2, y: 2, z: 4, core: 2. Of those that a mesh axis runs over, the one named last changes fastest.
Arguments:
- tops: bfloat16 [3, 320, 320, 320], P(None, 'contr', 'horiz', 'role'), may hold values from -6 to 6
- bottoms: bfloat16 [3, 320, 320, 2, 320], P(None, 'contr', 'horiz'), may hold values from -0.01953125 to 0.01953125
- left_iso: bfloat16 [320, 8, 320], P(None, None, 'horiz'), may hold values from -0.3125 to 0.3125
- right_iso: bfloat16 [320, 320, 320], P(('contr', 'horiz')), may hold values from -0.01953125 to 0.01953125
Outputs:
- coarse: float32 [2, 2, 8, 320], replicated
All inputs are finite; a program needn't handle non-finite values.
Results may differ from a plain program's by a relative error of at most 0.0081.
Values may be sent and summed in bfloat16 or wider, within the bound.
No kernel may reach another device: no remote copies, remote signals or barrier semaphores. Data moves between devices by JAX's collectives and lax.ppermute only.
A program may use at most 320 MiB of HBM per device.

v0:
```python
import jax
import jax.numpy as jnp
from jax import lax
from jax.sharding import PartitionSpec as P


def on_device(tops, bottoms, left_iso, right_iso):
    top_stack = jnp.stack([tops[0], tops[2], tops[1], tops[0]])[:, :, :, None, :]
    upper = lax.all_to_all(top_stack, "role", split_axis=0, concat_axis=4, tiled=True)
    upper = upper.reshape(upper.shape[1], upper.shape[2], upper.shape[4])
    which = lax.axis_index("role")
    slots = jnp.arange(4, dtype=jnp.int32)
    kind_table = jnp.array([0, 0, 1, 2], jnp.int32)
    lower_kind = jnp.sum(jnp.where(slots == which, kind_table, 0))
    lower = lax.dynamic_index_in_dim(bottoms, lower_kind, 0, keepdims=False)
    depth, slab, downs, full = lower.shape
    lower_mat = lower.reshape(depth * slab, downs * full)
    outs = left_iso.shape[1]
    piece = lax.all_gather(upper, "horiz", axis=1, tiled=True)
    count = piece.shape[1]
    expanded = jnp.einsum(
        "krl,lam->rakm", piece, left_iso, preferred_element_type=jnp.float32
    ).astype(jnp.bfloat16)
    summed = jnp.dot(
        expanded.reshape(count * outs, depth * slab), lower_mat, preferred_element_type=jnp.float32
    )
    partial_rows = summed.reshape(count, outs, downs, full)
    share = lax.psum_scatter(partial_rows, ("contr", "horiz"), scatter_dimension=0, tiled=True)
    piece_out = jnp.einsum(
        "xadr,xrb->dab", share.astype(jnp.bfloat16), right_iso, preferred_element_type=jnp.float32
    )
    bulk_table = jnp.array([1.0, 0.0, 0.0, 0.0], jnp.float32)
    moment_table = jnp.array([0.0, 0.25, 0.5, 0.25], jnp.float32)
    bulk_weight = jnp.sum(jnp.where(slots == which, bulk_table, 0.0))
    moment_weight = jnp.sum(jnp.where(slots == which, moment_table, 0.0))
    weighted = jnp.stack([piece_out * bulk_weight, piece_out * moment_weight])
    coarse = lax.psum(weighted, ("role", "contr", "horiz"))
    return coarse


def solution(mesh):
    placed = (
        P(None, "contr", "horiz", "role"),
        P(None, "contr", "horiz", None, None),
        P(None, None, "horiz"),
        P(("contr", "horiz"), None, None),
    )
    return jax.shard_map(on_device, mesh=mesh, in_specs=placed, out_specs=P(), check_vma=False)
```

profile of v0, /device:TPU:0, one launch (start us, length us, event | category | flops | bytes accessed | tf_op | source)
XLA Modules:
  0.0 1243.3 jit_solution(5354633536726865326)
XLA Ops:
  6.5 0.0 copy-start
  6.5 0.0 all-gather.2.cloned.1.call-start
  6.5 4.8 fusion.8
  11.3 3.6 maximum_bitcast_fusion
  14.9 147.7 %all_to_all.15 = bf16[4,160,80,1,80]{4,2,1,3,0:T(8,128)(2,1)S(1)} all-to-all(bf16[4,160,80,1,80]{4,2,1,3,0:T(8,128)(2,1)S(1)} %maximum_bitcast_fusion), channel_id=1, replica_groups=mesh['role'=4,'contr'=2,'horiz'=4] {'role'}, dimensions={0} | all-to-all | bytes 16384000 | tf_op jit(solution)/shard_map/all_to_all | solution.py:9
  162.6 31.9 %copy.17 = bf16[1,160,80,1,4,80]{5,4,2,1,3,0:T(4,128)(2,1)} copy(bf16[1,160,80,1,4,80]{5,2,1,4,3,0:T(8,128)(2,1)S(1)} %bitcast.49) | data formatting | bytes 16384000 | tf_op jit(solution)/shard_map/all_to_all | solution.py:9
  194.4 20.8 %reshape.13 = bf16[160,80,320]{2,1,0:T(8,128)(2,1)} reshape(bf16[1,160,80,1,4,80]{5,4,2,1,3,0:T(4,128)(2,1)} %copy.17) | data formatting | bytes 16384000 | tf_op jit(solution)/shard_map/reshape | solution.py:10
  215.2 0.0 all-gather.2.cloned.1.call-update
  215.2 0.2 reduce-scatter.2.cloned.1.call-start
  215.5 0.6 select_reduce_fusion.2
  218.0 18.0 %constant_dynamic-slice_fusion = bf16[1,160,80,2,320]{4,3,2,1,0:T(2,128)(2,1)} fusion(bf16[3,160,80,2,320]{4,3,2,1,0:T(2,128)(2,1)} %param.8, s32[]{:T(128)S(6)} %select_n.16), kind=kLoop, calls=%fused_computation.15 | loop fusion | bytes 32768004 | tf_op jit(solution)/shard_map/jit(dynamic_index_in_dim)/dynamic_slice | solution.py:15
  236.0 38.0 %reshape.14 = bf16[12800,640]{1,0:T(8,128)(2,1)} reshape(bf16[1,160,80,2,320]{4,3,2,1,0:T(2,128)(2,1)} %constant_dynamic-slice_fusion) | data formatting | bytes 32768000 | tf_op jit(solution)/shard_map/reshape | solution.py:17
  274.0 21.8 %copy.19 = bf16[640,12800]{1,0:T(8,128)(2,1)} copy(bf16[640,12800]{0,1:T(8,128)(2,1)} %bitcast.48) | data formatting | bytes 32768000 | tf_op jit(solution)/shard_map/dot_general | solution.py:24
  295.9 577.4 %all-gather.2.cloned.1.call-done = bf16[160,320,320]{2,1,0:T(8,128)(2,1)} async-done(((bf16[160,80,320]{2,1,0:T(8,128)(2,1)}), bf16[160,320,320]{2,1,0:T(8,128)(2,1)}) %all-gather.2.cloned.1.call-update) | async-done | bytes 32768016 | tf_op jit(solution)/shard_map/all_gather | solution.py:19
  873.2 50.8 %convert_bitcast_fusion = bf16[320,8,160,80]{0,3,1,2:T(8,128)(2,1)} fusion(bf16[160,320,320]{2,1,0:T(8,128)(2,1)} %all-gather.2.cloned.1.call-done, bf16[320,8,80]{0,2,1:T(8,128)(2,1)S(1)} %copy-done), kind=kOutput, calls=%fused_computation | convolution fusion | flops 21004288000 | bytes 98713600 | tf_op jit(solution)/shard_map/krl,lam->rakm/dot_general | solution.py:21
  924.0 51.6 %copy.18 = bf16[320,8,160,80]{0,3,2,1:T(8,128)(2,1)} copy(bf16[320,8,160,80]{0,3,1,2:T(8,128)(2,1)} %convert_bitcast_fusion) | data formatting | bytes 131072000 | tf_op jit(solution)/shard_map/convert_element_type | solution.py:23
  975.6 0.0 copy-start.1
  975.6 74.2 %fusion.13 = f32[320,8,2,320]{3,0,2,1:T(8,128)} fusion(bf16[320,8,12800,1]{0,2,3,1:T(8,128)(2,1)} %bitcast.22, bf16[2,320,12800,1]{2,1,0,3:T(8,128)(2,1)} %bitcast.50), kind=kOutput, calls=%fused_computation.17 | convolution fusion | flops 41943040000 | bytes 88473600 | tf_op jit(solution)/shard_map/dot_general | solution.py:24
  1049.8 0.0 reduce-scatter.2.cloned.1.call-update
  1049.8 0.7 select_reduce_fusion
  1050.5 137.8 %reduce-scatter.2.cloned.1.call-done = f32[40,8,2,320]{3,0,2,1:T(8,128)} async-done(((f32[320,8,2,320]{3,0,2,1:T(8,128)}), f32[40,8,2,320]{3,0,2,1:T(8,128)}) %reduce-scatter.2.cloned.1.call-update) | async-done | bytes 819216 | tf_op jit(solution)/shard_map/reduce_scatter | solution.py:28
  1188.3 1.3 convert_element_type.11
  1189.6 6.6 multiply_bitcast_fusion.1
  1196.2 40.2 %psum.7 = f32[2,2,8,320]{3,2,1,0:T(8,128)} all-reduce(f32[2,2,8,320]{3,2,1,0:T(8,128)S(1)} %pad_maximum_fusion), channel_id=1, replica_groups=mesh['role'=4,'contr'=2,'horiz'=4] {'role','contr','horiz'}, use_global_device_ids=true, to_apply=%region_4.5 | all-reduce | flops 10240 | bytes 81920 | tf_op jit(solution)/shard_map/psum | solution.py:37
  (9 shorter events, 0.0 us)
Async XLA Ops:
  6.5 866.7 %copy-start = (bf16[320,8,80]{0,2,1:T(8,128)(2,1)S(1)}, bf16[320,8,80]{0,2,1:T(8,128)(2,1)}, u32[]{:S(2)}) copy-start(bf16[320,8,80]{0,2,1:T(8,128)(2,1)} %param.9) | copy-start | bytes 1228804
  6.5 866.7 %all-gather.2.cloned.1.call-start = ((), (), s32[]{:S(2)}) async-start(), calls=%async_computation.2 | async-start | bytes 49152000 | tf_op jit(solution)/shard_map/all_gather | solution.py:19
  194.4 21.1 %copy-start.4 = (s32[4]{0:T(128)S(1)}, s32[4]{0:T(128)}, u32[]{:S(2)}) copy-start(s32[4]{0:T(128)} %constant.20.clone) | copy-start | bytes 52
  215.2 973.1 %reduce-scatter.2.cloned.1.call-start = ((), (), s32[]{:S(2)}) async-start(), calls=%async_computation.3 | async-start | bytes 8847360 | tf_op jit(solution)/shard_map/reduce_scatter | solution.py:28
  975.6 74.2 %copy-start.2 = (f32[4]{0:T(128)S(1)}, f32[4]{0:T(128)}, u32[]{:S(2)}) copy-start(f32[4]{0:T(128)} %constant.22.clone) | copy-start | bytes 52
  975.6 74.2 %copy-start.3 = (f32[4]{0:T(128)S(1)}, f32[4]{0:T(128)}, u32[]{:S(2)}) copy-start(f32[4]{0:T(128)} %constant.21.clone) | copy-start | bytes 52
  975.6 260.8 %copy-start.1 = (bf16[320,8,80]{0,2,1:T(8,128)(2,1)S(1)}, bf16[320,8,80]{0,2,1:T(8,128)(2,1)}, u32[]{:S(2)}) copy-start(bf16[320,8,80]{0,2,1:T(8,128)(2,1)} %param.9) | copy-start | bytes 1228804
Sparse Core Ops, SparseCore 0:
  215.3 657.8 all-gather.1
  1049.9 138.3 reduce-scatter.1
where the time goes:
time: 1250 us; the launch traced here: 1240 us
  waiting for transfers between devices  715 us (57%)
  blocking collectives  188 us (15%)
  local copies, waits for them, and re-layouts  187 us (15%)
  matrix products  132 us (11%)
  between operations  15.4 us (1%)
    all_gather x1, waiting for transfers between devices, on_device(): piece = lax.all_gather(upper, 'horiz', axis=1, tiled=True)  577 us
    all_to_all x1, blocking collectives, on_device(): lax.all_to_all(top_stack, 'role', split_axis=0, concat_axis=4, tiled=True)  148 us
    reduce_scatter x1, waiting for transfers between devices, on_device(): lax.psum_scatter(partial_rows, ('contr', 'horiz'), scatter_dimension=0, t...  138 us
    dot_general x1, matrix products, on_device(): jnp.dot(expanded.reshape(count * outs, depth * slab), lower_mat, preferre...  74.2 us
    convert_element_type x1, local copies, waits for them, and re-layouts, on_device(): expanded = jnp.einsum('krl,lam->rakm', piece, left_iso, preferred_element...  51.6 us
    dot_general x1, matrix products, on_device(): jnp.einsum('krl,lam->rakm', piece, left_iso, preferred_element_type=jnp.f...  50.8 us
    psum x1, blocking collectives, on_device(): coarse = lax.psum(weighted, ('role', 'contr', 'horiz'))  40.2 us
    reshape x1, local copies, waits for them, and re-layouts, on_device(): lower_mat = lower.reshape(depth * slab, downs * full)  38 us
  transfers between devices with their start and end apart: 2, of which 2 were waited for; matrix products, arithmetic and copies ran while one was open for 6% of the time, Pallas kernels for 0%

commit v1 on v0

v1 whole, which is shorter than its diff:
```python
import functools

import jax
import jax.numpy as jnp
from jax import lax
from jax.experimental import pallas as pl
from jax.experimental.pallas import tpu as pltpu
from jax.sharding import PartitionSpec as P

LANES = 128
ROWS = 16


def split_sizes(total, count):
    best = 1
    for n in range(1, count + 1):
        if count % n == 0 and total % n == 0 and (total // n) % ROWS == 0:
            best = n
    return best


def group_size(depth):
    best = depth
    for size in range(2, 11, 2):
        if depth % size == 0:
            best = size
    return best


def pack_kernel(group, *refs):
    pieces, (even_ref, odd_ref) = refs[:-2], refs[-2:]
    kinds, depth, rows, width = pieces[0].shape
    total = width * len(pieces)
    mains = total // LANES
    rest = total - mains * LANES
    groups = depth // group
    half = (group + 1) // 2

    def place(slot, shift):
        shape = (width, (mains + 1) * LANES)
        target = slot * width + lax.broadcasted_iota(jnp.int32, shape, 0)
        target = jnp.where(target >= mains * LANES, target + shift, target)
        hit = lax.broadcasted_iota(jnp.int32, shape, 1) == target
        return jnp.where(hit, 1.0, 0.0).astype(jnp.bfloat16)

    tables = [[place(s, shift) for s in range(len(pieces))] for shift in (0, rest)]
    for kind in range(kinds):
        out_ref, at = (odd_ref, 0) if kind == 1 else (even_ref, kind // 2)
        tails = []
        for part, (lo, hi) in enumerate(((0, half), (half, group))):
            if lo == hi:
                continue
            got = 0.0
            for slot, ref in enumerate(pieces):
                block = ref[kind].reshape(groups, group, rows, width)[:, lo:hi]
                got = got + jnp.dot(
                    block.reshape(groups * (hi - lo) * rows, width),
                    tables[part][slot],
                    preferred_element_type=jnp.float32,
                )
            got = got.reshape(groups, hi - lo, rows, (mains + 1) * LANES)
            for main in range(mains):
                out_ref[at, :, main * group + lo:main * group + hi] = got[
                    ..., main * LANES:(main + 1) * LANES
                ].astype(jnp.bfloat16)
            tails.append(got[..., mains * LANES:])
        base = mains * group
        first = tails[0]
        if len(tails) == 1:
            out_ref[at, :, base:base + half] = first.astype(jnp.bfloat16)
        else:
            both = tails[1].shape[1]
            out_ref[at, :, base:base + both] = (first[:, :both] + tails[1]).astype(jnp.bfloat16)
            if both < half:
                out_ref[at, :, base + both:base + half] = first[:, both:].astype(jnp.bfloat16)


def pack(pieces, group):
    kinds, depth, rows, width = pieces[0].shape
    mains = width * len(pieces) // LANES
    planes = mains * group + (group + 1) // 2
    shape = (depth // group, planes, rows, LANES)
    out = [
        jax.ShapeDtypeStruct((2,) + shape, jnp.bfloat16),
        jax.ShapeDtypeStruct((1,) + shape, jnp.bfloat16),
    ]
    return pl.pallas_call(
        functools.partial(pack_kernel, group),
        out_shape=out,
        in_specs=[pl.BlockSpec(memory_space=pltpu.VMEM)] * len(pieces),
        out_specs=[pl.BlockSpec(memory_space=pltpu.VMEM)] * 2,
        compiler_params=pltpu.CompilerParams(vmem_limit_bytes=32 * 2 ** 20),
        cost_estimate=pl.CostEstimate(flops=2 * 10 ** 9, bytes_accessed=4 * 2 ** 20, transcendentals=0),
        name="pack",
    )(*pieces)


def chunk_kernel(sides, group, outs, spot_ref, *refs):
    steps = sides - 1
    even_own, odd_own = refs[0], refs[1]
    even_right, even_left = refs[2:2 + steps], refs[2 + steps:2 + 2 * steps]
    at = 2 + 2 * steps
    odd_right, odd_left = refs[at:at + steps - 1], refs[at + steps - 1:at + 2 * (steps - 1)]
    at += 2 * (steps - 1)
    left_ref, next_left_ref, low_ref, next_low_ref = refs[at:at + 4]
    out_refs = refs[at + 4:at + 4 + outs]
    even, odd, spread, total, sems = refs[at + 4 + outs:]
    here, role = spot_ref[0], spot_ref[1]
    step, last = pl.program_id(0), pl.num_programs(0) - 1
    inner = jnp.logical_and(here > 0, here < sides - 1)
    rows = even.shape[-2]
    half = (group + 1) // 2
    mains = (even.shape[3] - half) // group
    windows = left_ref.shape[2] // LANES

    @pl.when(step == 0)
    def _():
        total[...] = jnp.zeros_like(total)

        def fetch(src, dst, sem, act):
            copy = pltpu.make_async_copy(src, dst, sem)
            if act:
                copy.start()
            else:
                copy.wait()

        fetch(even_own, even.at[here], sems.at[0], True)
        for gap in range(1, sides):
            slot = lax.rem(here + sides - gap, sides)

            @pl.when(here >= gap)
            def _():
                fetch(even_right[gap - 1], even.at[slot], sems.at[gap], True)

            @pl.when(here < gap)
            def _():
                fetch(even_left[sides - gap - 1], even.at[slot], sems.at[gap], True)

        @pl.when(inner)
        def _():
            fetch(odd_own, odd.at[here], sems.at[sides], True)
            for gap in range(1, sides):
                slot = lax.rem(here + sides - gap, sides)
                if gap <= steps - 1:
                    @pl.when(here >= gap)
                    def _():
                        fetch(odd_right[gap - 1], odd.at[slot], sems.at[sides + gap], True)
                if sides - gap <= steps - 1:
                    @pl.when(here < gap)
                    def _():
                        fetch(odd_left[sides - gap - 1], odd.at[slot], sems.at[sides + gap], True)

        for gap in range(sides):
            fetch(even_own, even.at[lax.rem(here + sides - gap, sides)], sems.at[gap], False)

        @pl.when(inner)
        def _():
            for gap in range(sides):
                fetch(odd_own, odd.at[lax.rem(here + sides - gap, sides)], sems.at[sides + gap], False)

    def expand(source, kind, table, slot):
        for part, (lo, hi) in enumerate(((0, half), (half, group))):
            if lo == hi:
                continue
            count = hi - lo
            planes = [
                source[:, kind, step, main * group + lo:main * group + hi] for main in range(mains)
            ] + [source[:, kind, step, mains * group:mains * group + count]]
            wide = jnp.concatenate([p.reshape(sides * count * rows, LANES) for p in planes], axis=1)
            got = jnp.dot(wide, table[part], preferred_element_type=jnp.float32).astype(jnp.bfloat16)
            got = got.reshape(sides, count, rows, windows * LANES)
            for k in range(count):
                for a in range(windows):
                    spread[slot, a, :, (lo + k) * LANES:(lo + k + 1) * LANES] = got[
                        :, k, :, a * LANES:(a + 1) * LANES
                    ].reshape(sides * rows, LANES)

    def product(slot, low):
        full = spread[slot].reshape(windows * sides * rows, group * LANES)
        return jnp.dot(
            full, low.reshape(group * LANES, low.shape[-1]), preferred_element_type=jnp.float32
        )

    expand(even, 0, left_ref, 0)
    expand(even, 1, left_ref, 1)
    total[0] += product(0, low_ref[0])
    total[1] += product(1, low_ref[0])
    total[1] += product(0, low_ref[2])

    @pl.when(inner)
    def _():
        expand(odd, 0, left_ref, 0)
        expand(odd, 0, next_left_ref, 1)
        total[1] += product(0, low_ref[1])
        total[1] += product(1, next_low_ref[...])

    @pl.when(step == last)
    def _():
        for offset in range(outs):
            which = offset ^ role
            value = total[which // 2]
            width = value.shape[1] // 2
            value = jnp.where(which % 2 == 1, value[:, width:], value[:, :width])
            out_refs[offset][...] = value.reshape(out_refs[offset].shape).astype(jnp.bfloat16)


def chunk_product(spot, blocks, tables, lows, sides, group, outs):
    even_own = blocks[0]
    _, groups, planes, rows, _ = even_own.shape
    left_table, next_table = tables
    low, next_low = lows
    windows = left_table.shape[2] // LANES
    full = low.shape[-1]
    count = windows * sides * rows
    whole = lambda arr: pl.BlockSpec(arr.shape, lambda g, s: (0,) * arr.ndim)
    out = [jax.ShapeDtypeStruct((windows, sides * rows, full // 2), jnp.bfloat16)] * outs
    depth = groups * group
    flops = 2 * count * depth * LANES * (5 * full) + 2 * 4 * sides * rows * depth * 3 * LANES * windows * LANES
    return pl.pallas_call(
        functools.partial(chunk_kernel, sides, group, outs),
        out_shape=out,
        grid_spec=pltpu.PrefetchScalarGridSpec(
            num_scalar_prefetch=1,
            grid=(groups,),
            in_specs=[pl.BlockSpec(memory_space=pl.ANY)] * len(blocks)
            + [
                whole(left_table),
                whole(next_table),
                pl.BlockSpec((3, group) + low.shape[2:], lambda g, s: (0, g, 0, 0)),
                pl.BlockSpec((group,) + next_low.shape[1:], lambda g, s: (g, 0, 0)),
            ],
            out_specs=[pl.BlockSpec(o.shape, lambda g, s: (0, 0, 0)) for o in out],
            scratch_shapes=[
                pltpu.VMEM((sides, 2, groups, planes, rows, LANES), jnp.bfloat16),
                pltpu.VMEM((sides, 1, groups, planes, rows, LANES), jnp.bfloat16),
                pltpu.VMEM((2, windows, sides * rows, group * LANES), jnp.bfloat16),
                pltpu.VMEM((2, count, full), jnp.float32),
                pltpu.SemaphoreType.DMA((2 * sides,)),
            ],
        ),
        compiler_params=pltpu.CompilerParams(vmem_limit_bytes=56 * 2 ** 20),
        cost_estimate=pl.CostEstimate(flops=flops, bytes_accessed=30 * 2 ** 20, transcendentals=0),
        name="chunk_product",
    )(spot, *blocks, left_table, next_table, low, next_low)


def tied(value, *after):
    return lax.optimization_barrier((value,) + after)[0]


def on_device(sizes, tops, bottoms, left_iso, right_iso):
    roles, contrs, sides = sizes
    role = lax.axis_index("role")
    here = lax.axis_index("horiz")
    kinds, depth_all, rows_all, width = tops.shape
    depth = depth_all // roles
    group = group_size(depth)
    share = right_iso.shape[0]
    chunks = split_sizes(rows_all, share)
    unit = share // chunks
    windows = left_iso.shape[1]
    slab = left_iso.shape[2]
    spot = jnp.stack([here, role]).astype(jnp.int32)

    cut = tops.reshape(kinds, depth_all, contrs, chunks, unit, width)

    def exchange(t):
        part = cut[:, :, :, t].reshape(kinds, depth_all, contrs * unit, width)
        pieces = []
        for s in range(roles):
            piece = lax.dynamic_slice_in_dim(part, (role ^ s) * depth, depth, 1)
            if s:
                piece = lax.ppermute(piece, "role", [(j, j ^ s) for j in range(roles)])
            pieces.append(piece)
        return pieces

    def flows(block, reach, low_end, high_end):
        right, left = [], []
        now = block
        for d in range(1, reach + 1):
            now = lax.ppermute(
                now, "horiz", [(z, z + 1) for z in range(d - 1, sides - 1) if low_end <= z + 1 <= high_end]
            )
            right.append(now)
        now = block
        for d in range(1, reach + 1):
            now = lax.ppermute(
                now, "horiz", [(z, z - 1) for z in range(sides - d, 0, -1) if low_end <= z - 1 <= high_end]
            )
            left.append(now)
        return right, left

    hand = [(0, 1), (sides - 1, sides - 2)]
    left_all = jnp.concatenate(
        [lax.dynamic_slice_in_dim(left_iso, (role ^ s) * width, width, 0) for s in range(roles)], axis=0
    )
    total = left_all.shape[0]
    mains = total // LANES * LANES
    rest = total - mains

    def table(flat):
        wide = jnp.pad(flat.reshape(total, windows, slab), ((0, 0), (0, 0), (0, LANES - slab)))
        wide = wide.reshape(total, windows * LANES)
        first = jnp.pad(wide, ((0, LANES - rest), (0, 0)))
        blank = jnp.zeros((rest, windows * LANES), wide.dtype)
        second = jnp.concatenate([wide[:mains], blank, wide[mains:]], axis=0)
        second = jnp.pad(second, ((0, LANES - 2 * rest), (0, 0)))
        return jnp.stack([first, second])

    flat_left = left_all.reshape(total, windows * slab)
    low = lax.dynamic_slice_in_dim(bottoms, role * depth, depth, 1)
    downs, full = low.shape[3], low.shape[4]
    low = low.reshape(kinds, depth, slab, downs * full)
    low = low * jnp.array([1, 2, 1], low.dtype).reshape(kinds, 1, 1, 1)

    packed = []
    for t in range(chunks):
        packed.append(pack(exchange(t), group))
    next_flat = lax.ppermute(flat_left, "horiz", hand)
    next_low = lax.ppermute(low[1], "horiz", hand)
    pad_low = lambda arr: jnp.pad(arr, [(0, 0)] * (arr.ndim - 2) + [(0, LANES - slab), (0, 0)])
    tables = (table(flat_left), table(next_flat))
    lows = (pad_low(low), pad_low(next_low))

    projected = 0.0
    for t in range(chunks):
        even, odd = packed[t]
        even_right, even_left = flows(even, sides - 1, 0, sides - 1)
        odd_right, odd_left = flows(odd, sides - 2, 1, sides - 2)
        blocks = [even, odd] + even_right + even_left + odd_right + odd_left
        parts = chunk_product(spot, blocks, tables, lows, sides, group, roles)
        summed = parts[0].astype(jnp.float32)
        for s in range(1, roles):
            got = lax.ppermute(parts[s], "role", [(j, j ^ s) for j in range(roles)])
            summed = summed + got.astype(jnp.float32)
        summed = summed.reshape(windows, sides * contrs, unit, full)
        count = sides * contrs
        step = contrs // 2
        place = lax.axis_index("contr")
        while step:
            count //= 2
            bit = (place // step) % 2
            keep = lax.dynamic_slice_in_dim(summed, bit * count, count, 1)
            give = lax.dynamic_slice_in_dim(summed, (1 - bit) * count, count, 1).astype(jnp.bfloat16)
            got = lax.ppermute(give, "contr", [(j, j ^ step) for j in range(contrs)])
            summed = keep + got.astype(jnp.float32)
            step //= 2
        mine = lax.dynamic_slice_in_dim(summed, here, 1, 1)
        for s in range(1, sides):
            give = lax.dynamic_slice_in_dim(summed, lax.rem(here + s, sides), 1, 1).astype(jnp.bfloat16)
            got = lax.ppermute(give, "horiz", [(z, (z + s) % sides) for z in range(sides)])
            mine = mine + got.astype(jnp.float32)
        mine = mine.reshape(windows, unit, full).astype(jnp.bfloat16)
        projected = projected + jnp.einsum(
            "aur,urb->ab", mine, right_iso[t * unit:(t + 1) * unit], preferred_element_type=jnp.float32
        )

    projected = projected * jnp.where(role >= downs, 0.25, 1.0)
    for axis, size in (("contr", contrs), ("horiz", sides)):
        s = 1
        while s < size:
            projected = projected + lax.ppermute(projected, axis, [(j, j ^ s) for j in range(size)])
            s *= 2
    pieces = [projected] + [
        lax.ppermute(projected, "role", [(j, j ^ s) for j in range(roles)]) for s in range(1, roles)
    ]
    pieces = jnp.stack(pieces)
    order = [lax.dynamic_index_in_dim(pieces, q ^ role, 0, keepdims=False) for q in range(roles)]
    return jnp.stack(order).reshape(roles // downs, downs, windows, -1)


def solution(mesh):
    placed = (
        P(None, "contr", "horiz", "role"),
        P(None, "contr", "horiz", None, None),
        P(None, None, "horiz"),
        P(("contr", "horiz"), None, None),
    )
    sizes = tuple(mesh.shape[axis] for axis in ("role", "contr", "horiz"))
    body = functools.partial(on_device, sizes)
    return jax.shard_map(body, mesh=mesh, in_specs=placed, out_specs=P(), check_vma=False)
```

time: 1250 us -> 803 us (0.64)
  waiting for transfers between devices: 715 us -> 276 us
  starting transfers between devices: 0.22 us -> 258 us
  blocking collectives: 188 us -> 0 us
  Pallas kernels: 0 us -> 153 us
  matrix products: 132 us -> 2.09 us
  local copies, waits for them, and re-layouts: 187 us -> 88.4 us
  between operations: 15.4 us -> 2.01 us
    all_gather x1 -> x0, waiting for transfers between devices: 577 us -> none  [on_device(): piece = lax.all_gather(upper, 'horiz', axis=1, tiled=True)]
    ppermute x0 -> x108, waiting for transfers between devices: none -> 276 us  [the longest x25 110 us: flows(): lax.ppermute(now, 'horiz', [(z, z + 1) for z in range(d - 1, sides - 1) i...]
    ppermute x0 -> x108, starting transfers between devices: none -> 258 us  [the longest x25 98.1 us: flows(): lax.ppermute(now, 'horiz', [(z, z + 1) for z in range(d - 1, sides - 1) i...]
    pallas_call x0 -> x10, Pallas kernels: none -> 153 us  [the longest x5 142 us: chunk_product(): pl.pallas_call(functools.partial(chunk_kernel, sides, group, outs), out_s...]
    all_to_all x1 -> x0, blocking collectives: 148 us -> none  [on_device(): lax.all_to_all(top_stack, 'role', split_axis=0, concat_axis=4, tiled=True)]
    reduce_scatter x1 -> x0, waiting for transfers between devices: 138 us -> none  [on_device(): lax.psum_scatter(partial_rows, ('contr', 'horiz'), scatter_dimension=0, t...]
    dot_general x3 -> x5, matrix products: 132 us -> 2.09 us  [on_device(): jnp.einsum('aur,urb->ab', mine, right_iso[t * unit:(t + 1) * unit], prefe...]
    convert_element_type x1 -> x5, local copies, waits for them, and re-layouts: 51.6 us -> 0.14 us  [on_device(): lax.dynamic_slice_in_dim(summed, lax.rem(here + s, sides), 1, 1)]
  transfers between devices with their start and end apart: 2 -> 108, of which waited for: 2 -> 41; matrix products, arithmetic and copies ran while one was open for 6% -> 11% of each run, Pallas kernels for 0% -> 19%
where the time goes in v1:
time: 803 us; the launch traced here: 793 us
  waiting for transfers between devices  276 us (34%)
  starting transfers between devices  258 us (32%)
  Pallas kernels  153 us (19%)
  local copies, waits for them, and re-layouts  88.4 us (11%)
  other arithmetic  13.5 us (2%)
    pallas_call x5, Pallas kernels, chunk_product(): pl.pallas_call(functools.partial(chunk_kernel, sides, group, outs), out_s...  142 us
    ppermute x25, waiting for transfers between devices, flows(): lax.ppermute(now, 'horiz', [(z, z + 1) for z in range(d - 1, sides - 1) i...  110 us
    ppermute x25, starting transfers between devices, flows(): lax.ppermute(now, 'horiz', [(z, z + 1) for z in range(d - 1, sides - 1) i...  98.1 us
    ppermute x25, waiting for transfers between devices, flows(): lax.ppermute(now, 'horiz', [(z, z - 1) for z in range(sides - d, 0, -1) i...  63.8 us
    ppermute x5, starting transfers between devices, on_device(): got = lax.ppermute(give, 'contr', [(j, j ^ step) for j in range(contrs)])  59.7 us
    ppermute x15, waiting for transfers between devices, exchange(): piece = lax.ppermute(piece, 'role', [(j, j ^ s) for j in range(roles)])  47.9 us
    ppermute x15, starting transfers between devices, on_device(): lax.ppermute(give, 'horiz', [(z, (z + s) % sides) for z in range(sides)])  38.4 us
    ppermute x25, starting transfers between devices, flows(): lax.ppermute(now, 'horiz', [(z, z - 1) for z in range(sides - d, 0, -1) i...  31.4 us
  transfers between devices with their start and end apart: 108, of which 41 were waited for; matrix products, arithmetic and copies ran while one was open for 11% of the time, Pallas kernels for 19%

profile of v1, /device:TPU:0, one launch (start us, length us, event | category | flops | bytes accessed | tf_op | source)
XLA Modules:
  0.0 792.6 jit_solution(17506682161813470277)
XLA Ops:
  14.7 12.8 %constant_dynamic-slice_fusion.30 = bf16[3,40,80,2,320]{4,3,2,1,0:T(2,128)(2,1)} fusion(bf16[3,160,80,2,320]{4,3,2,1,0:T(2,128)(2,1)} %param.6, s32[]{:T(128)S(6)} %select_n.121), kind=kLoop, calls=%fused_computation.115 | loop fusion | bytes 24576004 | tf_op jit(solution)/shard_map/dynamic_slice | solution.py:311
  27.5 28.6 %reshape.57 = bf16[3,40,80,640]{3,2,1,0:T(8,128)(2,1)} reshape(bf16[3,40,80,2,320]{4,3,2,1,0:T(2,128)(2,1)} %constant_dynamic-slice_fusion.30) | data formatting | bytes 24576000 | tf_op jit(solution)/shard_map/reshape | solution.py:313
  89.8 9.8 %collective-permute-done.44.refs_3_ = bf16[3,40,16,80]{3,2,1,0:T(8,128)(2,1)S(1)} collective-permute-done((bf16[3,40,16,80]{3,2,1,0:T(8,128)(2,1)}, bf16[3,40,16,80]{3,2,1,0:T(8,128)(2,1)S(1)}, u32[]{:S(2)}, u32[]{:S(2)}) %collective-permute-start.44) | collective-permute-done | bytes 307232 | tf_op jit(solution)/shard_map/ppermute | solution.py:273
  100.0 10.3 %collective-permute-done.1.refs_2_ = bf16[3,40,16,80]{3,2,1,0:T(8,128)(2,1)S(1)} collective-permute-done((bf16[3,40,16,80]{3,2,1,0:T(8,128)(2,1)}, bf16[3,40,16,80]{3,2,1,0:T(8,128)(2,1)S(1)}, u32[]{:S(2)}, u32[]{:S(2)}) %collective-permute-start.1) | collective-permute-done | bytes 307232 | tf_op jit(solution)/shard_map/ppermute | solution.py:273
  113.0 7.7 collective-permute-done.2.refs_3_
  132.1 9.6 %collective-permute-done.24.refs_3_ = bf16[3,40,16,80]{3,2,1,0:T(8,128)(2,1)S(1)} collective-permute-done((bf16[3,40,16,80]{3,2,1,0:T(8,128)(2,1)S(1)}, bf16[3,40,16,80]{3,2,1,0:T(8,128)(2,1)S(1)}, u32[]{:S(2)}, u32[]{:S(2)}) %collective-permute-start.24) | collective-permute-done | bytes 307232 | tf_op jit(solution)/shard_map/ppermute | solution.py:273
  150.6 71.3 %collective-permute-done.91.refs_8_ = bf16[1,4,25,16,128]{4,3,2,1,0:T(8,128)(2,1)S(1)} collective-permute-done((bf16[1,4,25,16,128]{4,3,2,1,0:T(8,128)(2,1)S(1)}, bf16[1,4,25,16,128]{4,3,2,1,0:T(8,128)(2,1)S(1)}, u32[]{:S(2)}, u32[]{:S(2)}) %collective-permute-start.91) | collective-permute-done | bytes 409632 | tf_op jit(solution)/shard_map/ppermute | solution.py:281
  254.1 19.7 %collective-permute-done.31.refs_8_ = bf16[1,4,25,16,128]{4,3,2,1,0:T(8,128)(2,1)S(1)} collective-permute-done((bf16[1,4,25,16,128]{4,3,2,1,0:T(8,128)(2,1)S(1)}, bf16[1,4,25,16,128]{4,3,2,1,0:T(8,128)(2,1)S(1)}, u32[]{:S(2)}, u32[]{:S(2)}) %collective-permute-start.31) | collective-permute-done | bytes 409632 | tf_op jit(solution)/shard_map/ppermute | solution.py:281
  283.2 23.6 %collective-permute-start.45 = (bf16[2,4,25,16,128]{4,3,2,1,0:T(8,128)(2,1)S(1)}, bf16[2,4,25,16,128]{4,3,2,1,0:T(8,128)(2,1)S(1)}, u32[]{:S(2)}, u32[]{:S(2)}) collective-permute-start(bf16[2,4,25,16,128]{4,3,2,1,0:T(8,128)(2,1)S(1)} %get-tuple-element.47.refs_0_), channel_id=1, source_target_pairs={{0,1},{1,2},{2,3},{4,5},{5,6},{6,7},{8,9},{9,10},{10,11},{12,13},{... | collective-permute-start | bytes 2457608 | tf_op jit(solution)/shard_map/ppermute | solution.py:281
  311.7 11.4 %collective-permute-done.45.refs_2_ = bf16[2,4,25,16,128]{4,3,2,1,0:T(8,128)(2,1)S(1)} collective-permute-done((bf16[2,4,25,16,128]{4,3,2,1,0:T(8,128)(2,1)S(1)}, bf16[2,4,25,16,128]{4,3,2,1,0:T(8,128)(2,1)S(1)}, u32[]{:S(2)}, u32[]{:S(2)}) %collective-permute-start.45) | collective-permute-done | bytes 819232 | tf_op jit(solution)/shard_map/ppermute | solution.py:281
  323.1 19.8 %collective-permute-start.3 = (bf16[2,4,25,16,128]{4,3,2,1,0:T(8,128)(2,1)S(1)}, bf16[2,4,25,16,128]{4,3,2,1,0:T(8,128)(2,1)}, u32[]{:S(2)}, u32[]{:S(2)}) collective-permute-start(bf16[2,4,25,16,128]{4,3,2,1,0:T(8,128)(2,1)S(1)} %get-tuple-element.35.refs_0_), channel_id=1, source_target_pairs={{0,1},{1,2},{2,3},{4,5},{5,6},{6,7},{8,9},{9,10},{10,11},{12,13},{... | collective-permute-start | bytes 2457608 | tf_op jit(solution)/shard_map/ppermute | solution.py:281
  369.1 14.5 %collective-permute-done.89.refs_6_ = bf16[2,4,25,16,128]{4,3,2,1,0:T(8,128)(2,1)} collective-permute-done((bf16[2,4,25,16,128]{4,3,2,1,0:T(8,128)(2,1)}, bf16[2,4,25,16,128]{4,3,2,1,0:T(8,128)(2,1)}, u32[]{:S(2)}, u32[]{:S(2)}) %collective-permute-start.89) | collective-permute-done | bytes 819232 | tf_op jit(solution)/shard_map/ppermute | solution.py:287
  398.4 10.4 %collective-permute-start.25 = (bf16[2,4,25,16,128]{4,3,2,1,0:T(8,128)(2,1)S(1)}, bf16[2,4,25,16,128]{4,3,2,1,0:T(8,128)(2,1)S(1)}, u32[]{:S(2)}, u32[]{:S(2)}) collective-permute-start(bf16[2,4,25,16,128]{4,3,2,1,0:T(8,128)(2,1)S(1)} %get-tuple-element.41.refs_0_), channel_id=1, source_target_pairs={{0,1},{1,2},{2,3},{4,5},{5,6},{6,7},{8,9},{9,10},{10,11},{12,13},{... | collective-permute-start | bytes 2457608 | tf_op jit(solution)/shard_map/ppermute | solution.py:281
  418.9 28.3 %chunk_product.9 = (bf16[8,64,320]{2,1,0:T(8,128)(2,1)}, bf16[8,64,320]{2,1,0:T(8,128)(2,1)}, bf16[8,64,320]{2,1,0:T(8,128)(2,1)}, bf16[8,64,320]{2,1,0:T(8,128)(2,1)}) custom-call(s32[2]{0:T(128)} %pad_add_fusion.spot_ref, bf16[2,4,25,16,128]{4,3,2,1,0:T(8,128)(2,1)} %copy-done.4, bf16[1,4,25,16,128]{4,3,2,1,0:T(8,128)(2,1)} %copy-done.11, ...), custom_call_target="tpu_custom_call" | custom-call | flops 24830279680 | bytes 31457280 | tf_op jit(solution)/shard_map/chunk_product/pallas_call | solution.py:219
  453.7 28.3 %chunk_product.8 = (bf16[8,64,320]{2,1,0:T(8,128)(2,1)}, bf16[8,64,320]{2,1,0:T(8,128)(2,1)}, bf16[8,64,320]{2,1,0:T(8,128)(2,1)}, bf16[8,64,320]{2,1,0:T(8,128)(2,1)}) custom-call(s32[2]{0:T(128)} %pad_add_fusion.spot_ref, bf16[2,4,25,16,128]{4,3,2,1,0:T(8,128)(2,1)} %copy-done.3, bf16[1,4,25,16,128]{4,3,2,1,0:T(8,128)(2,1)} %copy-done.10, ...), custom_call_target="tpu_custom_call" | custom-call | flops 24830279680 | bytes 31457280 | tf_op jit(solution)/shard_map/chunk_product/pallas_call | solution.py:219
  488.0 16.1 %collective-permute-done.7.refs_6_ = bf16[2,4,25,16,128]{4,3,2,1,0:T(8,128)(2,1)S(1)} collective-permute-done((bf16[2,4,25,16,128]{4,3,2,1,0:T(8,128)(2,1)}, bf16[2,4,25,16,128]{4,3,2,1,0:T(8,128)(2,1)S(1)}, u32[]{:S(2)}, u32[]{:S(2)}) %collective-permute-start.7) | collective-permute-done | bytes 819232 | tf_op jit(solution)/shard_map/ppermute | solution.py:287
  506.9 7.8 collective-permute-done.50.refs_7_
  516.2 28.2 %chunk_product.7 = (bf16[8,64,320]{2,1,0:T(8,128)(2,1)}, bf16[8,64,320]{2,1,0:T(8,128)(2,1)}, bf16[8,64,320]{2,1,0:T(8,128)(2,1)}, bf16[8,64,320]{2,1,0:T(8,128)(2,1)}) custom-call(s32[2]{0:T(128)} %pad_add_fusion.spot_ref, bf16[2,4,25,16,128]{4,3,2,1,0:T(8,128)(2,1)} %copy-done.2, bf16[1,4,25,16,128]{4,3,2,1,0:T(8,128)(2,1)} %copy-done.9, ...), custom_call_target="tpu_custom_call" | custom-call | flops 24830279680 | bytes 31457280 | tf_op jit(solution)/shard_map/chunk_product/pallas_call | solution.py:219
  557.8 28.3 %chunk_product.5 = (bf16[8,64,320]{2,1,0:T(8,128)(2,1)}, bf16[8,64,320]{2,1,0:T(8,128)(2,1)}, bf16[8,64,320]{2,1,0:T(8,128)(2,1)}, bf16[8,64,320]{2,1,0:T(8,128)(2,1)}) custom-call(s32[2]{0:T(128)} %pad_add_fusion.spot_ref, bf16[2,4,25,16,128]{4,3,2,1,0:T(8,128)(2,1)} %copy-done.1, bf16[1,4,25,16,128]{4,3,2,1,0:T(8,128)(2,1)} %copy-done.8, ...), custom_call_target="tpu_custom_call" | custom-call | flops 24830279680 | bytes 31457280 | tf_op jit(solution)/shard_map/chunk_product/pallas_call | solution.py:219
  594.3 28.7 %chunk_product.6 = (bf16[8,64,320]{2,1,0:T(8,128)(2,1)}, bf16[8,64,320]{2,1,0:T(8,128)(2,1)}, bf16[8,64,320]{2,1,0:T(8,128)(2,1)}, bf16[8,64,320]{2,1,0:T(8,128)(2,1)}) custom-call(s32[2]{0:T(128)} %pad_add_fusion.spot_ref, bf16[2,4,25,16,128]{4,3,2,1,0:T(8,128)(2,1)} %copy-done, bf16[1,4,25,16,128]{4,3,2,1,0:T(8,128)(2,1)} %copy-done.7, ...), custom_call_target="tpu_custom_call" | custom-call | flops 24830279680 | bytes 31457280 | tf_op jit(solution)/shard_map/chunk_product/pallas_call | solution.py:219
  627.2 7.4 collective-permute-done.77
  642.8 8.6 %collective-permute-done.57 = bf16[8,64,320]{2,1,0:T(8,128)(2,1)S(1)} collective-permute-done((bf16[8,64,320]{2,1,0:T(8,128)(2,1)S(1)}, bf16[8,64,320]{2,1,0:T(8,128)(2,1)S(1)}, u32[]{:S(2)}, u32[]{:S(2)}) %collective-permute-start.57) | collective-permute-done | bytes 327712 | tf_op jit(solution)/shard_map/ppermute | solution.py:334
  659.5 55.4 %collective-permute-start.98 = (bf16[8,4,8,320]{3,0,2,1:T(8,128)(2,1)S(1)}, bf16[8,4,8,320]{3,0,2,1:T(8,128)(2,1)S(1)}, u32[]{:S(2)}, u32[]{:S(2)}) collective-permute-start(bf16[8,4,8,320]{3,0,2,1:T(8,128)(2,1)S(1)} %copy.77), channel_id=1, source_target_pairs={{0,4},{4,0},{1,5},{5,1},{2,6},{6,2},{3,7},{7,3},{8,12},{12,8},{9,1... | collective-permute-start | bytes 491528 | tf_op jit(solution)/shard_map/ppermute | solution.py:345
  722.7 17.8 %collective-permute-start.100 = (bf16[8,1,8,320]{3,0,2,1:T(8,128)(2,1)S(1)}, bf16[8,1,8,320]{3,0,2,1:T(8,128)(2,1)S(1)}, u32[]{:S(2)}, u32[]{:S(2)}) collective-permute-start(bf16[8,1,8,320]{3,0,2,1:T(8,128)(2,1)S(1)} %get-tuple-element.96), channel_id=1, source_target_pairs={{0,2},{1,3},{2,0},{3,1},{4,6},{5,7},{6,4},{7,5},{8,10},{9,11},{10,... | collective-permute-start | bytes 122888 | tf_op jit(solution)/shard_map/ppermute | solution.py:351
  (436 shorter events, 286.2 us)
Async XLA Ops:
  8.3 56.6 %collective-permute-start.82 = (bf16[3,40,16,80]{3,2,1,0:T(8,128)(2,1)}, bf16[3,40,16,80]{3,2,1,0:T(8,128)(2,1)S(1)}, u32[]{:S(2)}, u32[]{:S(2)}) collective-permute-start(bf16[3,40,16,80]{3,2,1,0:T(8,128)(2,1)} %get-tuple-element.72), channel_id=1, source_target_pairs={{0,8},{8,0},{16,24},{24,16},{1,9},{9,1},{17,25},{25,17},{2,10},{10... | collective-permute-start | bytes 921608 | tf_op jit(solution)/shard_map/ppermute | solution.py:273
  8.8 60.9 %collective-permute-start.83 = (bf16[3,40,16,80]{3,2,1,0:T(8,128)(2,1)}, bf16[3,40,16,80]{3,2,1,0:T(8,128)(2,1)S(1)}, u32[]{:S(2)}, u32[]{:S(2)}) collective-permute-start(bf16[3,40,16,80]{3,2,1,0:T(8,128)(2,1)} %get-tuple-element.71), channel_id=1, source_target_pairs={{0,16},{8,24},{16,0},{24,8},{1,17},{9,25},{17,1},{25,9},{2,18},{10... | collective-permute-start | bytes 921608 | tf_op jit(solution)/shard_map/ppermute | solution.py:273
  11.3 59.2 %collective-permute-start.84 = (bf16[3,40,16,80]{3,2,1,0:T(8,128)(2,1)S(1)}, bf16[3,40,16,80]{3,2,1,0:T(8,128)(2,1)}, u32[]{:S(2)}, u32[]{:S(2)}) collective-permute-start(bf16[3,40,16,80]{3,2,1,0:T(8,128)(2,1)S(1)} %get-tuple-element.70), channel_id=1, source_target_pairs={{0,24},{8,16},{16,8},{24,0},{1,25},{9,17},{17,9},{25,1},{2,26},{10... | collective-permute-start | bytes 921608 | tf_op jit(solution)/shard_map/ppermute | solution.py:273
  12.7 59.4 %collective-permute-start.62 = (bf16[3,40,16,80]{3,2,1,0:T(8,128)(2,1)}, bf16[3,40,16,80]{3,2,1,0:T(8,128)(2,1)S(1)}, u32[]{:S(2)}, u32[]{:S(2)}) collective-permute-start(bf16[3,40,16,80]{3,2,1,0:T(8,128)(2,1)} %get-tuple-element.76), channel_id=1, source_target_pairs={{0,8},{8,0},{16,24},{24,16},{1,9},{9,1},{17,25},{25,17},{2,10},{10... | collective-permute-start | bytes 921608 | tf_op jit(solution)/shard_map/ppermute | solution.py:273
  12.8 60.9 %collective-permute-start.63 = (bf16[3,40,16,80]{3,2,1,0:T(8,128)(2,1)}, bf16[3,40,16,80]{3,2,1,0:T(8,128)(2,1)}, u32[]{:S(2)}, u32[]{:S(2)}) collective-permute-start(bf16[3,40,16,80]{3,2,1,0:T(8,128)(2,1)} %get-tuple-element.75), channel_id=1, source_target_pairs={{0,16},{8,24},{16,0},{24,8},{1,17},{9,25},{17,1},{25,9},{2,18},{10... | collective-permute-start | bytes 921608 | tf_op jit(solution)/shard_map/ppermute | solution.py:273
  80.8 64.4 %collective-permute-start.13 = (bf16[320,640]{0,1:T(8,128)(2,1)S(1)}, bf16[320,640]{0,1:T(8,128)(2,1)S(1)}, u32[]{:S(2)}, u32[]{:S(2)}) collective-permute-start(bf16[320,640]{0,1:T(8,128)(2,1)S(1)} %bitcast.96), channel_id=1, source_target_pairs={{0,1},{3,2},{4,5},{7,6},{8,9},{11,10},{12,13},{15,14},{16,17},{19,... | collective-permute-start | bytes 1228808 | tf_op jit(solution)/shard_map/ppermute | solution.py:319
  120.6 267.7 %collective-permute-start.14 = (bf16[40,80,640]{2,1,0:T(8,128)(2,1)}, bf16[40,80,640]{2,1,0:T(8,128)(2,1)}, u32[]{:S(2)}, u32[]{:S(2)}) collective-permute-start(bf16[40,80,640]{2,1,0:T(8,128)(2,1)} %slice_bitcast_fusion), channel_id=1, source_target_pairs={{0,1},{3,2},{4,5},{7,6},{8,9},{11,10},{12,13},{15,14},{16,17},{19,... | collective-permute-start | bytes 12288008 | tf_op jit(solution)/shard_map/ppermute | solution.py:320
  128.8 93.1 %collective-permute-start.91 = (bf16[1,4,25,16,128]{4,3,2,1,0:T(8,128)(2,1)S(1)}, bf16[1,4,25,16,128]{4,3,2,1,0:T(8,128)(2,1)S(1)}, u32[]{:S(2)}, u32[]{:S(2)}) collective-permute-start(bf16[1,4,25,16,128]{4,3,2,1,0:T(8,128)(2,1)S(1)} %get-tuple-element.60.refs_1_), channel_id=1, source_target_pairs={{0,1},{1,2},{4,5},{5,6},{8,9},{9,10},{12,13},{13,14},{16,17},{17,1... | collective-permute-start | bytes 1228808 | tf_op jit(solution)/shard_map/ppermute | solution.py:281
  131.4 94.9 %collective-permute-start.93 = (bf16[1,4,25,16,128]{4,3,2,1,0:T(8,128)(2,1)S(1)}, bf16[1,4,25,16,128]{4,3,2,1,0:T(8,128)(2,1)S(1)}, u32[]{:S(2)}, u32[]{:S(2)}) collective-permute-start(bf16[1,4,25,16,128]{4,3,2,1,0:T(8,128)(2,1)S(1)} %get-tuple-element.60.refs_1_), channel_id=1, source_target_pairs={{3,2},{2,1},{7,6},{6,5},{11,10},{10,9},{15,14},{14,13},{19,18},{18... | collective-permute-start | bytes 1228808 | tf_op jit(solution)/shard_map/ppermute | solution.py:287
  141.7 89.0 %collective-permute-start.71 = (bf16[1,4,25,16,128]{4,3,2,1,0:T(8,128)(2,1)S(1)}, bf16[1,4,25,16,128]{4,3,2,1,0:T(8,128)(2,1)S(1)}, u32[]{:S(2)}, u32[]{:S(2)}) collective-permute-start(bf16[1,4,25,16,128]{4,3,2,1,0:T(8,128)(2,1)S(1)} %get-tuple-element.54.refs_1_), channel_id=1, source_target_pairs={{0,1},{1,2},{4,5},{5,6},{8,9},{9,10},{12,13},{13,14},{16,17},{17,1... | collective-permute-start | bytes 1228808 | tf_op jit(solution)/shard_map/ppermute | solution.py:281
  145.2 89.9 %collective-permute-start.73 = (bf16[1,4,25,16,128]{4,3,2,1,0:T(8,128)(2,1)S(1)}, bf16[1,4,25,16,128]{4,3,2,1,0:T(8,128)(2,1)S(1)}, u32[]{:S(2)}, u32[]{:S(2)}) collective-permute-start(bf16[1,4,25,16,128]{4,3,2,1,0:T(8,128)(2,1)S(1)} %get-tuple-element.54.refs_1_), channel_id=1, source_target_pairs={{3,2},{2,1},{7,6},{6,5},{11,10},{10,9},{15,14},{14,13},{19,18},{18... | collective-permute-start | bytes 1228808 | tf_op jit(solution)/shard_map/ppermute | solution.py:287
  398.4 48.8 %collective-permute-start.25 = (bf16[2,4,25,16,128]{4,3,2,1,0:T(8,128)(2,1)S(1)}, bf16[2,4,25,16,128]{4,3,2,1,0:T(8,128)(2,1)S(1)}, u32[]{:S(2)}, u32[]{:S(2)}) collective-permute-start(bf16[2,4,25,16,128]{4,3,2,1,0:T(8,128)(2,1)S(1)} %get-tuple-element.41.refs_0_), channel_id=1, source_target_pairs={{0,1},{1,2},{2,3},{4,5},{5,6},{6,7},{8,9},{9,10},{10,11},{12,13},{... | collective-permute-start | bytes 2457608 | tf_op jit(solution)/shard_map/ppermute | solution.py:281
  449.3 54.8 %collective-permute-start.7 = (bf16[2,4,25,16,128]{4,3,2,1,0:T(8,128)(2,1)}, bf16[2,4,25,16,128]{4,3,2,1,0:T(8,128)(2,1)S(1)}, u32[]{:S(2)}, u32[]{:S(2)}) collective-permute-start(bf16[2,4,25,16,128]{4,3,2,1,0:T(8,128)(2,1)} %collective-permute-done.6.refs_5_), channel_id=1, source_target_pairs={{2,1},{1,0},{6,5},{5,4},{10,9},{9,8},{14,13},{13,12},{18,17},{17,1... | collective-permute-start | bytes 2457608 | tf_op jit(solution)/shard_map/ppermute | solution.py:287
  450.6 54.8 %collective-permute-start.47 = (bf16[2,4,25,16,128]{4,3,2,1,0:T(8,128)(2,1)S(1)}, bf16[2,4,25,16,128]{4,3,2,1,0:T(8,128)(2,1)}, u32[]{:S(2)}, u32[]{:S(2)}) collective-permute-start(bf16[2,4,25,16,128]{4,3,2,1,0:T(8,128)(2,1)S(1)} %collective-permute-done.46.refs_3_), channel_id=1, source_target_pairs={{2,3},{6,7},{10,11},{14,15},{18,19},{22,23},{26,27},{30,31}} | collective-permute-start | bytes 2457608 | tf_op jit(solution)/shard_map/ppermute | solution.py:281
  452.2 62.5 %collective-permute-start.50 = (bf16[2,4,25,16,128]{4,3,2,1,0:T(8,128)(2,1)S(1)}, bf16[2,4,25,16,128]{4,3,2,1,0:T(8,128)(2,1)}, u32[]{:S(2)}, u32[]{:S(2)}) collective-permute-start(bf16[2,4,25,16,128]{4,3,2,1,0:T(8,128)(2,1)S(1)} %collective-permute-done.49.refs_6_), channel_id=1, source_target_pairs={{1,0},{5,4},{9,8},{13,12},{17,16},{21,20},{25,24},{29,28}} | collective-permute-start | bytes 2457608 | tf_op jit(solution)/shard_map/ppermute | solution.py:287
  486.5 58.0 %collective-permute-start.12 = (bf16[1,4,25,16,128]{4,3,2,1,0:T(8,128)(2,1)}, bf16[1,4,25,16,128]{4,3,2,1,0:T(8,128)(2,1)S(1)}, u32[]{:S(2)}, u32[]{:S(2)}) collective-permute-start(bf16[1,4,25,16,128]{4,3,2,1,0:T(8,128)(2,1)} %collective-permute-done.11.refs_10_), channel_id=1, source_target_pairs={{2,1},{6,5},{10,9},{14,13},{18,17},{22,21},{26,25},{30,29}} | collective-permute-start | bytes 1228808 | tf_op jit(solution)/shard_map/ppermute | solution.py:287
  487.2 58.0 %collective-permute-start.26 = (bf16[2,4,25,16,128]{4,3,2,1,0:T(8,128)(2,1)S(1)}, bf16[2,4,25,16,128]{4,3,2,1,0:T(8,128)(2,1)S(1)}, u32[]{:S(2)}, u32[]{:S(2)}) collective-permute-start(bf16[2,4,25,16,128]{4,3,2,1,0:T(8,128)(2,1)S(1)} %collective-permute-done.25.refs_2_), channel_id=1, source_target_pairs={{1,2},{2,3},{5,6},{6,7},{9,10},{10,11},{13,14},{14,15},{17,18},{18... | collective-permute-start | bytes 2457608 | tf_op jit(solution)/shard_map/ppermute | solution.py:281
  556.9 66.1 %collective-permute-start.95 = (bf16[8,64,320]{2,1,0:T(8,128)(2,1)}, bf16[8,64,320]{2,1,0:T(8,128)(2,1)S(1)}, u32[]{:S(2)}, u32[]{:S(2)}) collective-permute-start(bf16[8,64,320]{2,1,0:T(8,128)(2,1)} %get-tuple-element.62), channel_id=1, source_target_pairs={{0,8},{8,0},{16,24},{24,16},{1,9},{9,1},{17,25},{25,17},{2,10},{10... | collective-permute-start | bytes 983048 | tf_op jit(solution)/shard_map/ppermute | solution.py:334
  636.0 78.9 %collective-permute-start.17 = (bf16[8,64,320]{2,1,0:T(8,128)(2,1)S(1)}, bf16[8,64,320]{2,1,0:T(8,128)(2,1)S(1)}, u32[]{:S(2)}, u32[]{:S(2)}) collective-permute-start(bf16[8,64,320]{2,1,0:T(8,128)(2,1)S(1)} %copy-done.67), channel_id=1, source_target_pairs={{0,24},{8,16},{16,8},{24,0},{1,25},{9,17},{17,9},{25,1},{2,26},{10... | collective-permute-start | bytes 983048 | tf_op jit(solution)/shard_map/ppermute | solution.py:334
  642.6 74.6 %collective-permute-start.35 = (bf16[8,64,320]{2,1,0:T(8,128)(2,1)S(1)}, bf16[8,64,320]{2,1,0:T(8,128)(2,1)S(1)}, u32[]{:S(2)}, u32[]{:S(2)}) collective-permute-start(bf16[8,64,320]{2,1,0:T(8,128)(2,1)S(1)} %copy-done.72), channel_id=1, source_target_pairs={{0,8},{8,0},{16,24},{24,16},{1,9},{9,1},{17,25},{25,17},{2,10},{10... | collective-permute-start | bytes 983048 | tf_op jit(solution)/shard_map/ppermute | solution.py:334
  651.4 66.1 %collective-permute-start.36 = (bf16[8,64,320]{2,1,0:T(8,128)(2,1)S(1)}, bf16[8,64,320]{2,1,0:T(8,128)(2,1)S(1)}, u32[]{:S(2)}, u32[]{:S(2)}) collective-permute-start(bf16[8,64,320]{2,1,0:T(8,128)(2,1)S(1)} %copy-done.70), channel_id=1, source_target_pairs={{0,16},{8,24},{16,0},{24,8},{1,17},{9,25},{17,1},{25,9},{2,18},{10... | collective-permute-start | bytes 983048 | tf_op jit(solution)/shard_map/ppermute | solution.py:334
  653.6 65.7 %collective-permute-start.37 = (bf16[8,64,320]{2,1,0:T(8,128)(2,1)S(1)}, bf16[8,64,320]{2,1,0:T(8,128)(2,1)S(1)}, u32[]{:S(2)}, u32[]{:S(2)}) collective-permute-start(bf16[8,64,320]{2,1,0:T(8,128)(2,1)S(1)} %copy-done.68), channel_id=1, source_target_pairs={{0,24},{8,16},{16,8},{24,0},{1,25},{9,17},{17,9},{25,1},{2,26},{10... | collective-permute-start | bytes 983048 | tf_op jit(solution)/shard_map/ppermute | solution.py:334
  659.5 63.0 %collective-permute-start.98 = (bf16[8,4,8,320]{3,0,2,1:T(8,128)(2,1)S(1)}, bf16[8,4,8,320]{3,0,2,1:T(8,128)(2,1)S(1)}, u32[]{:S(2)}, u32[]{:S(2)}) collective-permute-start(bf16[8,4,8,320]{3,0,2,1:T(8,128)(2,1)S(1)} %copy.77), channel_id=1, source_target_pairs={{0,4},{4,0},{1,5},{5,1},{2,6},{6,2},{3,7},{7,3},{8,12},{12,8},{9,1... | collective-permute-start | bytes 491528 | tf_op jit(solution)/shard_map/ppermute | solution.py:345
  722.7 47.7 %collective-permute-start.100 = (bf16[8,1,8,320]{3,0,2,1:T(8,128)(2,1)S(1)}, bf16[8,1,8,320]{3,0,2,1:T(8,128)(2,1)S(1)}, u32[]{:S(2)}, u32[]{:S(2)}) collective-permute-start(bf16[8,1,8,320]{3,0,2,1:T(8,128)(2,1)S(1)} %get-tuple-element.96), channel_id=1, source_target_pairs={{0,2},{1,3},{2,0},{3,1},{4,6},{5,7},{6,4},{7,5},{8,10},{9,11},{10,... | collective-permute-start | bytes 122888 | tf_op jit(solution)/shard_map/ppermute | solution.py:351
  (163 other events, 5806.2 us)

commit v2 on v1

v2 whole, which is shorter than its diff:
```python
import functools

import jax
import jax.numpy as jnp
from jax import lax
from jax.experimental import pallas as pl
from jax.experimental.pallas import tpu as pltpu
from jax.sharding import PartitionSpec as P

LANES = 128
ROWS = 16


def split_sizes(total, count):
    best = 1
    for n in range(1, count + 1):
        if count % n == 0 and total % n == 0 and (total // n) % ROWS == 0:
            best = n
    return best


def group_size(depth):
    best = depth
    for size in range(2, 11, 2):
        if depth % size == 0:
            best = size
    return best


def pack_kernel(group, *refs):
    pieces, (even_ref, odd_ref) = refs[:-2], refs[-2:]
    kinds, depth, rows, width = pieces[0].shape
    total = width * len(pieces)
    mains = total // LANES
    rest = total - mains * LANES
    groups = depth // group
    half = (group + 1) // 2

    def place(slot, shift):
        shape = (width, (mains + 1) * LANES)
        target = slot * width + lax.broadcasted_iota(jnp.int32, shape, 0)
        target = jnp.where(target >= mains * LANES, target + shift, target)
        hit = lax.broadcasted_iota(jnp.int32, shape, 1) == target
        return jnp.where(hit, 1.0, 0.0).astype(jnp.bfloat16)

    tables = [[place(s, shift) for s in range(len(pieces))] for shift in (0, rest)]
    for kind in range(kinds):
        out_ref, at = (odd_ref, 0) if kind == 1 else (even_ref, kind // 2)
        tails = []
        for part, (lo, hi) in enumerate(((0, half), (half, group))):
            if lo == hi:
                continue
            got = 0.0
            for slot, ref in enumerate(pieces):
                block = ref[kind].reshape(groups, group, rows, width)[:, lo:hi]
                got = got + jnp.dot(
                    block.reshape(groups * (hi - lo) * rows, width),
                    tables[part][slot],
                    preferred_element_type=jnp.float32,
                )
            got = got.reshape(groups, hi - lo, rows, (mains + 1) * LANES)
            for main in range(mains):
                out_ref[at, :, main * group + lo:main * group + hi] = got[
                    ..., main * LANES:(main + 1) * LANES
                ].astype(jnp.bfloat16)
            tails.append(got[..., mains * LANES:])
        base = mains * group
        first = tails[0]
        if len(tails) == 1:
            out_ref[at, :, base:base + half] = first.astype(jnp.bfloat16)
        else:
            both = tails[1].shape[1]
            out_ref[at, :, base:base + both] = (first[:, :both] + tails[1]).astype(jnp.bfloat16)
            if both < half:
                out_ref[at, :, base + both:base + half] = first[:, both:].astype(jnp.bfloat16)


def pack(pieces, group):
    kinds, depth, rows, width = pieces[0].shape
    mains = width * len(pieces) // LANES
    planes = mains * group + (group + 1) // 2
    shape = (depth // group, planes, rows, LANES)
    out = [
        jax.ShapeDtypeStruct((2,) + shape, jnp.bfloat16),
        jax.ShapeDtypeStruct((1,) + shape, jnp.bfloat16),
    ]
    return pl.pallas_call(
        functools.partial(pack_kernel, group),
        out_shape=out,
        in_specs=[pl.BlockSpec(memory_space=pltpu.VMEM)] * len(pieces),
        out_specs=[pl.BlockSpec(memory_space=pltpu.VMEM)] * 2,
        compiler_params=pltpu.CompilerParams(vmem_limit_bytes=32 * 2 ** 20),
        cost_estimate=pl.CostEstimate(flops=2 * 10 ** 9, bytes_accessed=4 * 2 ** 20, transcendentals=0),
        name="pack",
    )(*pieces)


def fetch(src, dst, sem):
    pltpu.make_async_copy(src, dst, sem).start()


def expand(source, step, group, tables, spread):
    sides, kinds, _, _, rows, _ = source.shape
    half = (group + 1) // 2
    mains = (source.shape[3] - half) // group
    windows = spread[0].shape[0]
    for part, (lo, hi) in enumerate(((0, half), (half, group))):
        if lo == hi:
            continue
        count = hi - lo
        planes = [
            source[:, :, step, main * group + lo:main * group + hi] for main in range(mains)
        ] + [source[:, :, step, mains * group:mains * group + count]]
        wide = jnp.concatenate([p.reshape(sides * kinds * count * rows, LANES) for p in planes], axis=1)
        for slot, table in enumerate(tables):
            got = jnp.dot(wide, table[part], preferred_element_type=jnp.float32).astype(jnp.bfloat16)
            got = got.reshape(sides, kinds, count, rows, windows * LANES)
            for kind in range(kinds):
                for k in range(count):
                    for a in range(windows):
                        spread[slot + kind][a, :, (lo + k) * LANES:(lo + k + 1) * LANES] = got[
                            :, kind, k, :, a * LANES:(a + 1) * LANES
                        ].reshape(sides * rows, LANES)


def flat(ref):
    windows, rows, lanes = ref.shape
    return ref[...].reshape(windows * rows, lanes)


def even_kernel(sides, group, use_ends, use_inner, spot_ref, *refs):
    inner_blocks, end_blocks = refs[:sides], refs[sides:2 * sides]
    left_ref, first_ref, last_ref, total = refs[2 * sides:2 * sides + 4]
    even, spread_a, spread_b, sems = refs[2 * sides + 4:]
    here = spot_ref[0]
    step = pl.program_id(0)
    inner = jnp.logical_and(here > 0, here < sides - 1)
    work = jnp.logical_or(jnp.logical_and(inner, use_inner), jnp.logical_and(jnp.logical_not(inner), use_ends))

    @pl.when(work)
    def _():
        @pl.when(step == 0)
        def _():
            total[...] = jnp.zeros_like(total)

            @pl.when(inner)
            def _():
                for at, turn in enumerate((0, 1, 3, 2)):
                    fetch(inner_blocks[at], even.at[here ^ turn], sems.at[at])

            @pl.when(jnp.logical_not(inner))
            def _():
                for at, turn in enumerate((0, 1, 2, 3)):
                    fetch(end_blocks[at], even.at[here ^ turn], sems.at[at])

            for at in range(sides):
                pltpu.make_async_copy(inner_blocks[at], even.at[at], sems.at[at]).wait()

        expand(even, step, group, (left_ref,), (spread_a, spread_b))
        first = first_ref[...].reshape(group * LANES, first_ref.shape[-1])
        last = last_ref[...].reshape(group * LANES, last_ref.shape[-1])
        total[0] += jnp.dot(flat(spread_a), first, preferred_element_type=jnp.float32)
        total[1] += jnp.dot(flat(spread_b), first, preferred_element_type=jnp.float32)
        total[1] += jnp.dot(flat(spread_a), last, preferred_element_type=jnp.float32)

    @pl.when(jnp.logical_and(step == 0, jnp.logical_not(work)))
    def _():
        total[...] = jnp.zeros_like(total)


def even_product(spot, inner_blocks, end_blocks, table, first, last, sides, group):
    some = inner_blocks or end_blocks
    use_inner, use_ends = inner_blocks is not None, end_blocks is not None
    _, groups, planes, rows, _ = some[0].shape
    windows = table.shape[2] // LANES
    full = first.shape[-1]
    count = windows * sides * rows
    whole = lambda arr: pl.BlockSpec(arr.shape, lambda g, s: (0,) * len(arr.shape))
    low = pl.BlockSpec((group,) + first.shape[1:], lambda g, s: (g, 0, 0))
    out = jax.ShapeDtypeStruct((2, count, full), jnp.float32)
    depth = groups * group
    flops = 2 * count * depth * LANES * 3 * full + 4 * sides * rows * depth * 3 * LANES * windows * LANES
    return pl.pallas_call(
        functools.partial(even_kernel, sides, group, use_ends, use_inner),
        out_shape=out,
        grid_spec=pltpu.PrefetchScalarGridSpec(
            num_scalar_prefetch=1,
            grid=(groups,),
            in_specs=[pl.BlockSpec(memory_space=pl.ANY)] * (2 * sides) + [whole(table), low, low],
            out_specs=whole(out),
            scratch_shapes=[
                pltpu.VMEM((sides, 2, groups, planes, rows, LANES), jnp.bfloat16),
                pltpu.VMEM((windows, sides * rows, group * LANES), jnp.bfloat16),
                pltpu.VMEM((windows, sides * rows, group * LANES), jnp.bfloat16),
                pltpu.SemaphoreType.DMA((sides,)),
            ],
        ),
        compiler_params=pltpu.CompilerParams(vmem_limit_bytes=40 * 2 ** 20),
        cost_estimate=pl.CostEstimate(flops=flops, bytes_accessed=20 * 2 ** 20, transcendentals=0),
        name="even_product",
    )(spot, *(inner_blocks or some), *(end_blocks or some), table, first, last)


def odd_kernel(sides, group, outs, spot_ref, *refs):
    blocks = refs[:sides]
    inner_part, end_part = refs[sides:sides + 2]
    left_ref, next_left_ref, low_ref, next_low_ref = refs[sides + 2:sides + 6]
    out_refs = refs[sides + 6:sides + 6 + outs]
    odd, spread_a, spread_b, total, sems = refs[sides + 6 + outs:]
    here, role = spot_ref[0], spot_ref[1]
    step, last = pl.program_id(0), pl.num_programs(0) - 1
    inner = jnp.logical_and(here > 0, here < sides - 1)

    @pl.when(step == 0)
    def _():
        @pl.when(inner)
        def _():
            fetch(inner_part, total, sems.at[sides])
            for at, turn in enumerate((0, 1, 3, 2)):
                fetch(blocks[at], odd.at[here ^ turn], sems.at[at])
            for at in range(sides):
                pltpu.make_async_copy(blocks[at], odd.at[at], sems.at[at]).wait()

        @pl.when(jnp.logical_not(inner))
        def _():
            fetch(end_part, total, sems.at[sides])

        pltpu.make_async_copy(inner_part, total, sems.at[sides]).wait()

    @pl.when(inner)
    def _():
        expand(odd, step, group, (left_ref, next_left_ref), (spread_a, spread_b))
        low = low_ref[...].reshape(group * LANES, low_ref.shape[-1])
        next_low = next_low_ref[...].reshape(group * LANES, low_ref.shape[-1])
        total[1] += jnp.dot(flat(spread_a), low, preferred_element_type=jnp.float32)
        total[1] += jnp.dot(flat(spread_b), next_low, preferred_element_type=jnp.float32)

    @pl.when(step == last)
    def _():
        for offset in range(outs):
            which = offset ^ role
            value = total[which // 2]
            width = value.shape[1] // 2
            value = jnp.where(which % 2 == 1, value[:, width:], value[:, :width])
            out_refs[offset][...] = value.reshape(out_refs[offset].shape).astype(jnp.bfloat16)


def odd_product(spot, blocks, inner_part, end_part, tables, lows, sides, group, outs):
    _, groups, planes, rows, _ = blocks[0].shape
    table, next_table = tables
    low, next_low = lows
    windows = table.shape[2] // LANES
    full = low.shape[-1]
    count = windows * sides * rows
    whole = lambda arr: pl.BlockSpec(arr.shape, lambda g, s: (0,) * len(arr.shape))
    part = pl.BlockSpec((group,) + low.shape[1:], lambda g, s: (g, 0, 0))
    out = [jax.ShapeDtypeStruct((windows, sides * rows, full // 2), jnp.bfloat16)] * outs
    depth = groups * group
    flops = 2 * count * depth * LANES * 2 * full + 4 * sides * rows * depth * 3 * LANES * windows * LANES
    return pl.pallas_call(
        functools.partial(odd_kernel, sides, group, outs),
        out_shape=out,
        grid_spec=pltpu.PrefetchScalarGridSpec(
            num_scalar_prefetch=1,
            grid=(groups,),
            in_specs=[pl.BlockSpec(memory_space=pl.ANY)] * (sides + 2)
            + [whole(table), whole(next_table), part, part],
            out_specs=[whole(o) for o in out],
            scratch_shapes=[
                pltpu.VMEM((sides, 1, groups, planes, rows, LANES), jnp.bfloat16),
                pltpu.VMEM((windows, sides * rows, group * LANES), jnp.bfloat16),
                pltpu.VMEM((windows, sides * rows, group * LANES), jnp.bfloat16),
                pltpu.VMEM((2, count, full), jnp.float32),
                pltpu.SemaphoreType.DMA((sides + 1,)),
            ],
        ),
        compiler_params=pltpu.CompilerParams(vmem_limit_bytes=40 * 2 ** 20),
        cost_estimate=pl.CostEstimate(flops=flops, bytes_accessed=20 * 2 ** 20, transcendentals=0),
        name="odd_product",
    )(spot, *blocks, inner_part, end_part, table, next_table, low, next_low)


def tie(*values):
    return lax.optimization_barrier(values)


def on_device(sizes, tops, bottoms, left_iso, right_iso):
    roles, contrs, sides = sizes
    role = lax.axis_index("role")
    here = lax.axis_index("horiz")
    kinds, depth_all, rows_all, width = tops.shape
    depth = depth_all // roles
    group = group_size(depth)
    share = right_iso.shape[0]
    chunks = split_sizes(rows_all, share)
    unit = share // chunks
    windows = left_iso.shape[1]
    slab = left_iso.shape[2]
    downs, full = bottoms.shape[3], bottoms.shape[4]
    spot = jnp.stack([here, role]).astype(jnp.int32)

    cut = tops.reshape(kinds, depth_all, contrs, chunks, unit, width)

    def exchange(t, place):
        part = cut[:, :, :, t].reshape(kinds, depth_all, contrs * unit, width)
        pieces = []
        for s in range(roles):
            piece = lax.dynamic_slice_in_dim(part, (place ^ s) * depth, depth, 1)
            if s:
                piece = lax.ppermute(piece, "role", [(j, j ^ s) for j in range(roles)])
            pieces.append(piece)
        return pieces

    def lower(kind, place):
        low = lax.dynamic_slice_in_dim(bottoms[kind], place * depth, depth, 0)
        return low.reshape(depth, slab, downs * full)

    def padded(low):
        return jnp.pad(low, ((0, 0), (0, LANES - slab), (0, 0)))

    pairs = [(z, z ^ 1) for z in range(sides)]
    hand = [(z, z ^ 1) for z in (0, sides - 1)]
    cross = [(z, z ^ 3) for z in range(1, sides - 1)]
    back = [(z, z ^ 1) for z in range(1, sides - 1)]
    move = lambda value, perm: lax.ppermute(value, "horiz", perm)

    pieces = exchange(0, role)
    left_all = jnp.concatenate(
        [lax.dynamic_slice_in_dim(left_iso, (role ^ s) * width, width, 0) for s in range(roles)], axis=0
    )
    total = left_all.shape[0]
    mains = total // LANES * LANES
    rest = total - mains

    def table(flat_left):
        wide = jnp.pad(
            flat_left.reshape(total, windows, slab), ((0, 0), (0, 0), (0, LANES - slab))
        ).reshape(total, windows * LANES)
        first = jnp.pad(wide, ((0, LANES - rest), (0, 0)))
        blank = jnp.zeros((rest, windows * LANES), wide.dtype)
        second = jnp.concatenate([wide[:mains], blank, wide[mains:]], axis=0)
        second = jnp.pad(second, ((0, LANES - 2 * rest), (0, 0)))
        return jnp.stack([first, second])

    flat_left = left_all.reshape(total, windows * slab)
    middle = lower(1, role) * jnp.asarray(2, bottoms.dtype)
    next_middle = move(middle, hand)
    own = {0: pack(pieces, group)}
    next_left = move(flat_left, hand)
    late, _ = tie(role, own[0][0])
    pieces = exchange(1, late) if chunks > 1 else None

    near = {}
    far = {}
    sums, shares = {}, {}
    lows = tables = None
    mark = own[0][0]
    for r in range(chunks + 3):
        if r < chunks:
            a, b, mark = tie(*own[r], mark)
            if r:
                held = tie(a, b, mark, *near[r - 1])
                a, b, mark, near[r - 1] = held[0], held[1], held[2], held[3:]
            own[r] = (a, b)
            near[r] = (move(a, pairs), move(b, hand), move(a, cross), move(b, cross))
        elif r == chunks:
            held = tie(mark, *near[r - 1])
            mark, near[r - 1] = held[0], held[1:]
        if r + 1 < chunks:
            own[r + 1] = pack(pieces, group)
            late, _ = tie(role, own[r + 1][0])
            pieces = exchange(r + 2, late) if r + 2 < chunks else None
        if r == 0:
            late, _ = tie(role, own[0][0])
            lows = (padded(lower(0, late)), padded(lower(2, late)), padded(middle))
            tables = (table(flat_left), table(next_left))
            mark = lows[1]
        t = r - 4
        if 0 <= t < chunks:
            shares[t] = odd_product(
                spot, (own[t][1], near[t][1], near[t][3], far[t][1]), sums[t + 2], sums[t + 3],
                tables, (lows[2], padded(next_middle)), sides, group, roles,
            )
            mark = shares[t][0]
        ready = [mark]
        for t in (r - 1, r - 2):
            if 0 <= t < chunks:
                ready += list(near[t])
        for t in (r - 2, r - 3):
            if t in far:
                ready += list(far[t])
        ready = list(tie(*ready))
        mark = ready.pop(0)
        for t in (r - 1, r - 2):
            if 0 <= t < chunks:
                near[t], ready = tuple(ready[:4]), ready[4:]
        for t in (r - 2, r - 3):
            if t in far:
                count = len(far[t])
                far[t], ready = tuple(ready[:count]), ready[count:]
        t = r - 1
        if 0 <= t < chunks:
            far[t] = (move(near[t][0], cross), move(near[t][1], cross), move(near[t][2], back))
        t = r - 2
        if 0 <= t < chunks:
            far[t] = far[t] + (move(far[t][0], back),)
        if r >= 2:
            t = r - 2
            inner_blocks = (own[t][0], near[t][0], near[t][2], far[t][0]) if t < chunks else None
            t = r - 3
            end_blocks = (own[t][0], near[t][0], far[t][2], far[t][3]) if 0 <= t else None
            sums[r] = even_product(spot, inner_blocks, end_blocks, tables[0], lows[0], lows[1], sides, group)
            mark = sums[r]
    t = chunks - 1
    shares[t] = odd_product(
        spot, (own[t][1], near[t][1], near[t][3], far[t][1]), sums[t + 2], sums[t + 3],
        tables, (lows[2], padded(next_middle)), sides, group, roles,
    )

    projected = 0.0
    for t in range(chunks):
        parts = shares[t]
        summed = parts[0].astype(jnp.float32)
        for s in range(1, roles):
            got = lax.ppermute(parts[s], "role", [(j, j ^ s) for j in range(roles)])
            summed = summed + got.astype(jnp.float32)
        summed = summed.reshape(windows, sides * contrs, unit, full)
        count = sides * contrs
        step = contrs // 2
        place = lax.axis_index("contr")
        while step:
            count //= 2
            bit = (place // step) % 2
            keep = lax.dynamic_slice_in_dim(summed, bit * count, count, 1)
            give = lax.dynamic_slice_in_dim(summed, (1 - bit) * count, count, 1).astype(jnp.bfloat16)
            got = lax.ppermute(give, "contr", [(j, j ^ step) for j in range(contrs)])
            summed = keep + got.astype(jnp.float32)
            step //= 2
        mine = lax.dynamic_slice_in_dim(summed, here, 1, 1)
        for s in range(1, sides):
            give = lax.dynamic_slice_in_dim(summed, here ^ s, 1, 1).astype(jnp.bfloat16)
            got = lax.ppermute(give, "horiz", [(z, z ^ s) for z in range(sides)])
            mine = mine + got.astype(jnp.float32)
        mine = mine.reshape(windows, unit, full).astype(jnp.bfloat16)
        projected = projected + jnp.einsum(
            "aur,urb->ab", mine, right_iso[t * unit:(t + 1) * unit], preferred_element_type=jnp.float32
        )

    projected = projected * jnp.where(role >= downs, 0.25, 1.0)
    for axis, size in (("contr", contrs), ("horiz", sides)):
        s = 1
        while s < size:
            projected = projected + lax.ppermute(projected, axis, [(j, j ^ s) for j in range(size)])
            s *= 2
    pieces = [projected] + [
        lax.ppermute(projected, "role", [(j, j ^ s) for j in range(roles)]) for s in range(1, roles)
    ]
    pieces = jnp.stack(pieces)
    order = [lax.dynamic_index_in_dim(pieces, q ^ role, 0, keepdims=False) for q in range(roles)]
    return jnp.stack(order).reshape(roles // downs, downs, windows, -1)


def solution(mesh):
    placed = (
        P(None, "contr", "horiz", "role"),
        P(None, "contr", "horiz", None, None),
        P(None, None, "horiz"),
        P(("contr", "horiz"), None, None),
    )
    sizes = tuple(mesh.shape[axis] for axis in ("role", "contr", "horiz"))
    body = functools.partial(on_device, sizes)
    return jax.shard_map(body, mesh=mesh, in_specs=placed, out_specs=P(), check_vma=False)
```

time: 803 us -> 839 us (1.045)
  local copies, waits for them, and re-layouts: 88.4 us -> 178 us
  waiting for transfers between devices: 276 us -> 221 us
  starting transfers between devices: 258 us -> 214 us
  Pallas kernels: 153 us -> 185 us
    ppermute x67 -> x57, waiting for transfers between devices: 184 us -> 120 us  [the longest x42 118 us: on_device(): move = lambda value, perm: lax.ppermute(value, 'horiz', perm)]
    ppermute x5, starting transfers between devices: 59.7 us -> 4.75 us  [on_device(): got = lax.ppermute(give, 'contr', [(j, j ^ step) for j in range(contrs)])]
    slice x0 -> x1, local copies, waits for them, and re-layouts: none -> 44 us  [lower(): low = lax.dynamic_slice_in_dim(bottoms[kind], place * depth, depth, 0)]
    ppermute x15, waiting for transfers between devices: 28.4 us -> 70.7 us  [on_device(): got = lax.ppermute(parts[s], 'role', [(j, j ^ s) for j in range(roles)])]
    ppermute x15, waiting for transfers between devices: 47.9 us -> 6.31 us  [exchange(): piece = lax.ppermute(piece, 'role', [(j, j ^ s) for j in range(roles)])]
    pallas_call x5 -> x11, Pallas kernels: 142 us -> 170 us  [the longest x6 135 us: even_product(): pl.pallas_call(functools.partial(even_kernel, sides, group, use_ends, use...]
    unnamed x163 -> x183, local copies, waits for them, and re-layouts: 7.34 us -> 30.8 us
    pad x4 -> x6, local copies, waits for them, and re-layouts: 14.1 us -> 26.6 us  [the longest x4 23.4 us: padded(): return jnp.pad(low, ((0, 0), (0, LANES - slab), (0, 0)))]
  transfers between devices with their start and end apart: 108 -> 98, of which waited for: 41 -> 23; matrix products, arithmetic and copies ran while one was open for 11% -> 20% of each run, Pallas kernels for 19% -> 22%
where the time goes in v2:
time: 839 us; the launch traced here: 828 us
  waiting for transfers between devices  221 us (26%)
  starting transfers between devices  214 us (26%)
  Pallas kernels  185 us (22%)
  local copies, waits for them, and re-layouts  178 us (21%)
  other arithmetic  17.4 us (2%)
  matrix products  10.2 us (1%)
    pallas_call x6, Pallas kernels, even_product(): pl.pallas_call(functools.partial(even_kernel, sides, group, use_ends, use...  135 us
    ppermute x42, starting transfers between devices, on_device(): move = lambda value, perm: lax.ppermute(value, 'horiz', perm)  119 us
    ppermute x42, waiting for transfers between devices, on_device(): move = lambda value, perm: lax.ppermute(value, 'horiz', perm)  118 us
    ppermute x15, waiting for transfers between devices, on_device(): got = lax.ppermute(parts[s], 'role', [(j, j ^ s) for j in range(roles)])  70.7 us
    ppermute x15, starting transfers between devices, on_device(): got = lax.ppermute(give, 'horiz', [(z, z ^ s) for z in range(sides)])  68.1 us
    slice x1, local copies, waits for them, and re-layouts, lower(): low = lax.dynamic_slice_in_dim(bottoms[kind], place * depth, depth, 0)  44 us
    pallas_call x5, Pallas kernels, odd_product(): pl.pallas_call(functools.partial(odd_kernel, sides, group, outs), out_sha...  35.3 us
    unnamed x183, local copies, waits for them, and re-layouts  30.8 us
  transfers between devices with their start and end apart: 98, of which 23 were waited for; matrix products, arithmetic and copies ran while one was open for 20% of the time, Pallas kernels for 22%

profile of v2, /device:TPU:0, one launch (start us, length us, event | category | flops | bytes accessed | tf_op | source)
XLA Modules:
  0.0 827.5 jit_solution(11061763300422543976)
XLA Ops:
  16.0 44.0 %fusion.55 = (bf16[1,160,80,2,320]{4,3,2,1,0:T(2,128)(2,1)}, bf16[1,160,80,2,320]{4,3,2,1,0:T(2,128)(2,1)}, bf16[1,160,80,2,320]{4,3,2,1,0:T(2,128)(2,1)}) fusion(bf16[3,160,80,2,320]{4,3,2,1,0:T(2,128)(2,1)} %param.5), kind=kLoop, calls=%fused_computation.125 | loop fusion | bytes 98304000 | tf_op jit(solution)/shard_map/slice | solution.py:315
  59.9 8.5 %dynamic-slice_multiply_fusion = bf16[1,40,80,2,320]{4,3,2,1,0:T(2,128)(2,1)} fusion(bf16[1,160,80,2,320]{4,3,2,1,0:T(2,128)(2,1)} %get-tuple-element.279, s32[]{:T(128)S(6)} %select_n.149), kind=kLoop, calls=%fused_computation | loop fusion | flops 2048000 | bytes 8192004 | tf_op jit(solution)/shard_map/mul | solution.py:346
  124.9 10.5 %mul.117 = bf16[40,80,640]{2,1,0:T(8,128)(2,1)} reshape(bf16[1,40,80,2,320]{4,3,2,1,0:T(2,128)(2,1)} %dynamic-slice_multiply_fusion) | data formatting | bytes 8192000 | tf_op jit(solution)/shard_map/mul | solution.py:346
  156.2 9.7 %constant_dynamic-slice_fusion.18 = (bf16[1,40,80,2,320]{4,3,2,1,0:T(2,128)(2,1)}, bf16[1,40,80,2,320]{4,3,2,1,0:T(2,128)(2,1)}) fusion(bf16[1,160,80,2,320]{4,3,2,1,0:T(2,128)(2,1)} %get-tuple-element.281, s32[]{:T(128)S(6)} %select_n.165, bf16[1,160,80,2,320]{4,3,2,1,0:T(2,128)(2,1)} %get-tuple-element.280), kind=kLoop, calls=%fused_computation.102 | loop fusion | bytes 16384004 | tf_op jit(solution)/shard_map/dynamic_slice | solution.py:315
  165.9 94.8 %collective-permute-done.14.refs_1_ = bf16[1,4,25,16,128]{4,3,2,1,0:T(8,128)(2,1)S(1)} collective-permute-done((bf16[1,4,25,16,128]{4,3,2,1,0:T(8,128)(2,1)S(1)}, bf16[1,4,25,16,128]{4,3,2,1,0:T(8,128)(2,1)S(1)}, u32[]{:S(2)}, u32[]{:S(2)}) %collective-permute-start.14) | collective-permute-done | bytes 409632 | tf_op jit(solution)/shard_map/ppermute | solution.py:325
  270.7 10.5 %reshape.64 = bf16[40,80,640]{2,1,0:T(8,128)(2,1)} reshape(bf16[1,40,80,2,320]{4,3,2,1,0:T(2,128)(2,1)} %get-tuple-element.333) | data formatting | bytes 8192000 | tf_op jit(solution)/shard_map/reshape | solution.py:316
  287.1 10.5 %reshape.65 = bf16[40,80,640]{2,1,0:T(8,128)(2,1)} reshape(bf16[1,40,80,2,320]{4,3,2,1,0:T(2,128)(2,1)} %get-tuple-element.332) | data formatting | bytes 8192000 | tf_op jit(solution)/shard_map/reshape | solution.py:316
  327.8 13.9 %collective-permute-done.24.refs_1_ = bf16[1,4,25,16,128]{4,3,2,1,0:T(8,128)(2,1)S(1)} collective-permute-done((bf16[1,4,25,16,128]{4,3,2,1,0:T(8,128)(2,1)S(1)}, bf16[1,4,25,16,128]{4,3,2,1,0:T(8,128)(2,1)S(1)}, u32[]{:S(2)}, u32[]{:S(2)}) %collective-permute-start.24) | collective-permute-done | bytes 409632 | tf_op jit(solution)/shard_map/ppermute | solution.py:325
  353.3 28.4 %collective-permute-start.43 = (bf16[2,4,25,16,128]{4,3,2,1,0:T(8,128)(2,1)S(1)}, bf16[2,4,25,16,128]{4,3,2,1,0:T(8,128)(2,1)S(1)}, u32[]{:S(2)}, u32[]{:S(2)}) collective-permute-start(bf16[2,4,25,16,128]{4,3,2,1,0:T(8,128)(2,1)S(1)} %copy-done.3), channel_id=1, source_target_pairs={{0,1},{1,0},{2,3},{3,2},{4,5},{5,4},{6,7},{7,6},{8,9},{9,8},{10,11... | collective-permute-start | bytes 2457608 | tf_op jit(solution)/shard_map/ppermute | solution.py:325
  388.0 26.6 %even_product.7.refs_5_.refs_4_ = f32[2,512,640]{2,1,0:T(8,128)S(1)} custom-call(s32[2]{0:T(128)S(1)} %copy-done.67, bf16[2,4,25,16,128]{4,3,2,1,0:T(8,128)(2,1)S(1)} %copy-done.16, bf16[2,4,25,16,128]{4,3,2,1,0:T(8,128)(2,1)S(1)} %copy-done.21, bf16[2,4,25,16,128]{4,3,2,1,0:T(8,128)(2,1)S(1)} %copy-done.23, ...), custom_call_target="tpu_custom_call" | custom-call | flops 14092861440 | bytes 20971520 | tf_op jit(solution)/shard_map/even_product/pallas_call | solution.py:183
  446.2 15.8 %collective-permute-start.59 = (bf16[1,4,25,16,128]{4,3,2,1,0:T(8,128)(2,1)S(1)}, bf16[1,4,25,16,128]{4,3,2,1,0:T(8,128)(2,1)S(1)}, u32[]{:S(2)}, u32[]{:S(2)}) collective-permute-start(bf16[1,4,25,16,128]{4,3,2,1,0:T(8,128)(2,1)S(1)} %get-tuple-element.229.refs_0_), channel_id=1, source_target_pairs={{0,1},{3,2},{4,5},{7,6},{8,9},{11,10},{12,13},{15,14},{16,17},{19,... | collective-permute-start | bytes 1228808 | tf_op jit(solution)/shard_map/ppermute | solution.py:325
  462.7 25.6 %even_product.8.refs_5_.refs_4_ = f32[2,512,640]{2,1,0:T(8,128)S(1)} custom-call(s32[2]{0:T(128)S(1)} %copy-done.67, bf16[2,4,25,16,128]{4,3,2,1,0:T(8,128)(2,1)} %get-tuple-element.175.refs_0_.refs_4_, bf16[2,4,25,16,128]{4,3,2,1,0:T(8,128)(2,1)S(1)} %collective-permute-done.23.refs_1_.refs_5_, ...), custom_call_target="tpu_custom_call" | custom-call | flops 14092861440 | bytes 20971520 | tf_op jit(solution)/shard_map/even_product/pallas_call | solution.py:183
  493.4 7.8 odd_product.6
  547.7 16.0 %collective-permute-start.55 = (bf16[8,1,8,320]{3,0,2,1:T(8,128)(2,1)S(1)}, bf16[8,1,8,320]{3,0,2,1:T(8,128)(2,1)S(1)}, u32[]{:S(2)}, u32[]{:S(2)}) collective-permute-start(bf16[8,1,8,320]{3,0,2,1:T(8,128)(2,1)S(1)} %get-tuple-element.323), channel_id=1, source_target_pairs={{0,1},{1,0},{2,3},{3,2},{4,5},{5,4},{6,7},{7,6},{8,9},{9,8},{10,11... | collective-permute-start | bytes 122888 | tf_op jit(solution)/shard_map/ppermute | solution.py:442
  563.9 26.8 %even_product.9.refs_5_.refs_4_ = f32[2,512,640]{2,1,0:T(8,128)S(1)} custom-call(s32[2]{0:T(128)S(1)} %copy-done.68, bf16[2,4,25,16,128]{4,3,2,1,0:T(8,128)(2,1)S(1)} %copy-done.4, bf16[2,4,25,16,128]{4,3,2,1,0:T(8,128)(2,1)S(1)} %copy-done.6, bf16[2,4,25,16,128]{4,3,2,1,0:T(8,128)(2,1)S(1)} %copy-done.14, ...), custom_call_target="tpu_custom_call" | custom-call | flops 14092861440 | bytes 20971520 | tf_op jit(solution)/shard_map/even_product/pallas_call | solution.py:183
  602.1 7.8 collective-permute-done.67
  627.0 15.2 %collective-permute-start.37 = (bf16[8,1,8,320]{3,0,2,1:T(8,128)(2,1)S(1)}, bf16[8,1,8,320]{3,0,2,1:T(8,128)(2,1)S(1)}, u32[]{:S(2)}, u32[]{:S(2)}) collective-permute-start(bf16[8,1,8,320]{3,0,2,1:T(8,128)(2,1)S(1)} %get-tuple-element.320), channel_id=1, source_target_pairs={{0,1},{1,0},{2,3},{3,2},{4,5},{5,4},{6,7},{7,6},{8,9},{9,8},{10,11... | collective-permute-start | bytes 122888 | tf_op jit(solution)/shard_map/ppermute | solution.py:442
  642.5 20.0 %collective-permute-start.38 = (bf16[8,1,8,320]{3,0,2,1:T(8,128)(2,1)S(1)}, bf16[8,1,8,320]{3,0,2,1:T(8,128)(2,1)S(1)}, u32[]{:S(2)}, u32[]{:S(2)}) collective-permute-start(bf16[8,1,8,320]{3,0,2,1:T(8,128)(2,1)S(1)} %get-tuple-element.322), channel_id=1, source_target_pairs={{0,2},{1,3},{2,0},{3,1},{4,6},{5,7},{6,4},{7,5},{8,10},{9,11},{10,... | collective-permute-start | bytes 122888 | tf_op jit(solution)/shard_map/ppermute | solution.py:442
  666.9 25.4 %even_product.10.refs_5_.refs_4_ = f32[2,512,640]{2,1,0:T(8,128)S(1)} custom-call(s32[2]{0:T(128)S(1)} %copy-done.68, bf16[2,4,25,16,128]{4,3,2,1,0:T(8,128)(2,1)} %get-tuple-element.228.refs_0_.refs_4_, bf16[2,4,25,16,128]{4,3,2,1,0:T(8,128)(2,1)} %collective-permute-done.58.refs_1_.refs_5_, bf16[2,4,25,16,128]{4,3,2,1,0:T(8,128)(2,1)} %collective-permute-done.60.refs_2_, ...), custom_call_target="tpu_custom_call" | custom-call | flops 14092861440 | bytes 20971520 | tf_op jit(solution)/shard_map/even_product/pallas_call | solution.py:183
  719.3 7.5 collective-permute-done.79
  727.8 8.8 %collective-permute-done.84.refs_3_.refs_7_ = bf16[2,4,25,16,128]{4,3,2,1,0:T(8,128)(2,1)S(1)} collective-permute-done((bf16[2,4,25,16,128]{4,3,2,1,0:T(8,128)(2,1)S(1)}, bf16[2,4,25,16,128]{4,3,2,1,0:T(8,128)(2,1)S(1)}, u32[]{:S(2)}, u32[]{:S(2)}) %collective-permute-start.84) | collective-permute-done | bytes 819232 | tf_op jit(solution)/shard_map/ppermute | solution.py:325
  736.6 26.0 %even_product.11.refs_5_ = f32[2,512,640]{2,1,0:T(8,128)S(1)} custom-call(s32[2]{0:T(128)S(1)} %copy-done.68, bf16[2,4,25,16,128]{4,3,2,1,0:T(8,128)(2,1)} %get-tuple-element.228.refs_0_.refs_4_, bf16[2,4,25,16,128]{4,3,2,1,0:T(8,128)(2,1)} %collective-permute-done.58.refs_1_.refs_5_, ...), custom_call_target="tpu_custom_call" | custom-call | flops 14092861440 | bytes 20971520 | tf_op jit(solution)/shard_map/even_product/pallas_call | solution.py:183
  774.9 9.8 %collective-permute-done.86 = bf16[8,64,320]{2,1,0:T(8,128)(2,1)S(1)} collective-permute-done((bf16[8,64,320]{2,1,0:T(8,128)(2,1)S(1)}, bf16[8,64,320]{2,1,0:T(8,128)(2,1)S(1)}, u32[]{:S(2)}, u32[]{:S(2)}) %collective-permute-start.86) | collective-permute-done | bytes 327712 | tf_op jit(solution)/shard_map/ppermute | solution.py:425
  784.7 7.5 collective-permute-done.87
  (447 shorter events, 347.9 us)
Async XLA Ops:
  9.9 71.2 %collective-permute-start.20 = (bf16[3,40,16,80]{3,2,1,0:T(8,128)(2,1)}, bf16[3,40,16,80]{3,2,1,0:T(8,128)(2,1)}, u32[]{:S(2)}, u32[]{:S(2)}) collective-permute-start(bf16[3,40,16,80]{3,2,1,0:T(8,128)(2,1)} %get-tuple-element.297), channel_id=1, source_target_pairs={{0,8},{8,0},{16,24},{24,16},{1,9},{9,1},{17,25},{25,17},{2,10},{10... | collective-permute-start | bytes 921608 | tf_op jit(solution)/shard_map/ppermute | solution.py:310
  10.4 75.3 %collective-permute-start.21 = (bf16[3,40,16,80]{3,2,1,0:T(8,128)(2,1)}, bf16[3,40,16,80]{3,2,1,0:T(8,128)(2,1)}, u32[]{:S(2)}, u32[]{:S(2)}) collective-permute-start(bf16[3,40,16,80]{3,2,1,0:T(8,128)(2,1)} %get-tuple-element.296), channel_id=1, source_target_pairs={{0,16},{8,24},{16,0},{24,8},{1,17},{9,25},{17,1},{25,9},{2,18},{10... | collective-permute-start | bytes 921608 | tf_op jit(solution)/shard_map/ppermute | solution.py:310
  14.1 57.1 %collective-permute-start = (bf16[3,40,16,80]{3,2,1,0:T(8,128)(2,1)}, bf16[3,40,16,80]{3,2,1,0:T(8,128)(2,1)S(1)}, u32[]{:S(2)}, u32[]{:S(2)}) collective-permute-start(bf16[3,40,16,80]{3,2,1,0:T(8,128)(2,1)} %get-tuple-element.305), channel_id=1, source_target_pairs={{0,8},{8,0},{16,24},{24,16},{1,9},{9,1},{17,25},{25,17},{2,10},{10... | collective-permute-start | bytes 921608 | tf_op jit(solution)/shard_map/ppermute | solution.py:310
  14.3 57.3 %collective-permute-start.1 = (bf16[3,40,16,80]{3,2,1,0:T(8,128)(2,1)}, bf16[3,40,16,80]{3,2,1,0:T(8,128)(2,1)S(1)}, u32[]{:S(2)}, u32[]{:S(2)}) collective-permute-start(bf16[3,40,16,80]{3,2,1,0:T(8,128)(2,1)} %get-tuple-element.304), channel_id=1, source_target_pairs={{0,16},{8,24},{16,0},{24,8},{1,17},{9,25},{17,1},{25,9},{2,18},{10... | collective-permute-start | bytes 921608 | tf_op jit(solution)/shard_map/ppermute | solution.py:310
  14.6 57.9 %collective-permute-start.2 = (bf16[3,40,16,80]{3,2,1,0:T(8,128)(2,1)}, bf16[3,40,16,80]{3,2,1,0:T(8,128)(2,1)S(1)}, u32[]{:S(2)}, u32[]{:S(2)}) collective-permute-start(bf16[3,40,16,80]{3,2,1,0:T(8,128)(2,1)} %get-tuple-element.303), channel_id=1, source_target_pairs={{0,24},{8,16},{16,8},{24,0},{1,25},{9,17},{17,9},{25,1},{2,26},{10... | collective-permute-start | bytes 921608 | tf_op jit(solution)/shard_map/ppermute | solution.py:310
  144.9 275.2 %collective-permute-start.32 = (bf16[40,80,640]{2,1,0:T(8,128)(2,1)}, bf16[40,80,640]{2,1,0:T(8,128)(2,1)}, u32[]{:S(2)}, u32[]{:S(2)}) collective-permute-start(bf16[40,80,640]{2,1,0:T(8,128)(2,1)} %mul.117), channel_id=1, source_target_pairs={{0,1},{3,2},{4,5},{7,6},{8,9},{11,10},{12,13},{15,14},{16,17},{19,... | collective-permute-start | bytes 12288008 | tf_op jit(solution)/shard_map/ppermute | solution.py:325
  148.1 115.2 %collective-permute-start.13 = (bf16[2,4,25,16,128]{4,3,2,1,0:T(8,128)(2,1)S(1)}, bf16[2,4,25,16,128]{4,3,2,1,0:T(8,128)(2,1)S(1)}, u32[]{:S(2)}, u32[]{:S(2)}) collective-permute-start(bf16[2,4,25,16,128]{4,3,2,1,0:T(8,128)(2,1)S(1)} %get-tuple-element.151.refs_0_.refs_4_), channel_id=1, source_target_pairs={{0,1},{1,0},{2,3},{3,2},{4,5},{5,4},{6,7},{7,6},{8,9},{9,8},{10,11... | collective-permute-start | bytes 2457608 | tf_op jit(solution)/shard_map/ppermute | solution.py:325
  148.1 116.5 %collective-permute-start.15 = (bf16[2,4,25,16,128]{4,3,2,1,0:T(8,128)(2,1)S(1)}, bf16[2,4,25,16,128]{4,3,2,1,0:T(8,128)(2,1)S(1)}, u32[]{:S(2)}, u32[]{:S(2)}) collective-permute-start(bf16[2,4,25,16,128]{4,3,2,1,0:T(8,128)(2,1)S(1)} %get-tuple-element.151.refs_0_.refs_4_), channel_id=1, source_target_pairs={{1,2},{2,1},{5,6},{6,5},{9,10},{10,9},{13,14},{14,13},{17,18},{18,... | collective-permute-start | bytes 2457608 | tf_op jit(solution)/shard_map/ppermute | solution.py:325
  148.8 111.8 %collective-permute-start.14 = (bf16[1,4,25,16,128]{4,3,2,1,0:T(8,128)(2,1)S(1)}, bf16[1,4,25,16,128]{4,3,2,1,0:T(8,128)(2,1)S(1)}, u32[]{:S(2)}, u32[]{:S(2)}) collective-permute-start(bf16[1,4,25,16,128]{4,3,2,1,0:T(8,128)(2,1)S(1)} %get-tuple-element.152.refs_0_), channel_id=1, source_target_pairs={{0,1},{3,2},{4,5},{7,6},{8,9},{11,10},{12,13},{15,14},{16,17},{19,... | collective-permute-start | bytes 1228808 | tf_op jit(solution)/shard_map/ppermute | solution.py:325
  155.5 105.4 %collective-permute-start.16 = (bf16[1,4,25,16,128]{4,3,2,1,0:T(8,128)(2,1)S(1)}, bf16[1,4,25,16,128]{4,3,2,1,0:T(8,128)(2,1)S(1)}, u32[]{:S(2)}, u32[]{:S(2)}) collective-permute-start(bf16[1,4,25,16,128]{4,3,2,1,0:T(8,128)(2,1)S(1)} %get-tuple-element.152.refs_0_), channel_id=1, source_target_pairs={{1,2},{2,1},{5,6},{6,5},{9,10},{10,9},{13,14},{14,13},{17,18},{18,... | collective-permute-start | bytes 1228808 | tf_op jit(solution)/shard_map/ppermute | solution.py:325
  261.7 56.2 %collective-permute-start.17 = (bf16[2,4,25,16,128]{4,3,2,1,0:T(8,128)(2,1)}, bf16[2,4,25,16,128]{4,3,2,1,0:T(8,128)(2,1)}, u32[]{:S(2)}, u32[]{:S(2)}) collective-permute-start(bf16[2,4,25,16,128]{4,3,2,1,0:T(8,128)(2,1)} %collective-permute-done.9.refs_1_.refs_5_), channel_id=1, source_target_pairs={{1,2},{2,1},{5,6},{6,5},{9,10},{10,9},{13,14},{14,13},{17,18},{18,... | collective-permute-start | bytes 2457608 | tf_op jit(solution)/shard_map/ppermute | solution.py:325
  263.3 59.6 %collective-permute-start.19 = (bf16[2,4,25,16,128]{4,3,2,1,0:T(8,128)(2,1)S(1)}, bf16[2,4,25,16,128]{4,3,2,1,0:T(8,128)(2,1)S(1)}, u32[]{:S(2)}, u32[]{:S(2)}) collective-permute-start(bf16[2,4,25,16,128]{4,3,2,1,0:T(8,128)(2,1)S(1)} %collective-permute-done.11.refs_2_.refs_6_), channel_id=1, source_target_pairs={{1,0},{2,3},{5,4},{6,7},{9,8},{10,11},{13,12},{14,15},{17,16},{18,... | collective-permute-start | bytes 2457608 | tf_op jit(solution)/shard_map/ppermute | solution.py:325
  353.3 64.3 %collective-permute-start.43 = (bf16[2,4,25,16,128]{4,3,2,1,0:T(8,128)(2,1)S(1)}, bf16[2,4,25,16,128]{4,3,2,1,0:T(8,128)(2,1)S(1)}, u32[]{:S(2)}, u32[]{:S(2)}) collective-permute-start(bf16[2,4,25,16,128]{4,3,2,1,0:T(8,128)(2,1)S(1)} %copy-done.3), channel_id=1, source_target_pairs={{0,1},{1,0},{2,3},{3,2},{4,5},{5,4},{6,7},{7,6},{8,9},{9,8},{10,11... | collective-permute-start | bytes 2457608 | tf_op jit(solution)/shard_map/ppermute | solution.py:325
  420.1 84.5 %collective-permute-start.58 = (bf16[2,4,25,16,128]{4,3,2,1,0:T(8,128)(2,1)}, bf16[2,4,25,16,128]{4,3,2,1,0:T(8,128)(2,1)}, u32[]{:S(2)}, u32[]{:S(2)}) collective-permute-start(bf16[2,4,25,16,128]{4,3,2,1,0:T(8,128)(2,1)} %get-tuple-element.228.refs_0_.refs_4_), channel_id=1, source_target_pairs={{0,1},{1,0},{2,3},{3,2},{4,5},{5,4},{6,7},{7,6},{8,9},{9,8},{10,11... | collective-permute-start | bytes 2457608 | tf_op jit(solution)/shard_map/ppermute | solution.py:325
  444.6 61.4 %collective-permute-start.60 = (bf16[2,4,25,16,128]{4,3,2,1,0:T(8,128)(2,1)}, bf16[2,4,25,16,128]{4,3,2,1,0:T(8,128)(2,1)}, u32[]{:S(2)}, u32[]{:S(2)}) collective-permute-start(bf16[2,4,25,16,128]{4,3,2,1,0:T(8,128)(2,1)} %get-tuple-element.228.refs_0_.refs_4_), channel_id=1, source_target_pairs={{1,2},{2,1},{5,6},{6,5},{9,10},{10,9},{13,14},{14,13},{17,18},{18,... | collective-permute-start | bytes 2457608 | tf_op jit(solution)/shard_map/ppermute | solution.py:325
  446.2 55.8 %collective-permute-start.59 = (bf16[1,4,25,16,128]{4,3,2,1,0:T(8,128)(2,1)S(1)}, bf16[1,4,25,16,128]{4,3,2,1,0:T(8,128)(2,1)S(1)}, u32[]{:S(2)}, u32[]{:S(2)}) collective-permute-start(bf16[1,4,25,16,128]{4,3,2,1,0:T(8,128)(2,1)S(1)} %get-tuple-element.229.refs_0_), channel_id=1, source_target_pairs={{0,1},{3,2},{4,5},{7,6},{8,9},{11,10},{12,13},{15,14},{16,17},{19,... | collective-permute-start | bytes 1228808 | tf_op jit(solution)/shard_map/ppermute | solution.py:325
  504.6 59.2 %collective-permute-start.65 = (bf16[2,4,25,16,128]{4,3,2,1,0:T(8,128)(2,1)}, bf16[2,4,25,16,128]{4,3,2,1,0:T(8,128)(2,1)S(1)}, u32[]{:S(2)}, u32[]{:S(2)}) collective-permute-start(bf16[2,4,25,16,128]{4,3,2,1,0:T(8,128)(2,1)} %copy-done.19), channel_id=1, source_target_pairs={{1,0},{2,3},{5,4},{6,7},{9,8},{10,11},{13,12},{14,15},{17,16},{18,... | collective-permute-start | bytes 2457608 | tf_op jit(solution)/shard_map/ppermute | solution.py:325
  506.0 57.7 %collective-permute-start.62 = (bf16[2,4,25,16,128]{4,3,2,1,0:T(8,128)(2,1)}, bf16[2,4,25,16,128]{4,3,2,1,0:T(8,128)(2,1)S(1)}, u32[]{:S(2)}, u32[]{:S(2)}) collective-permute-start(bf16[2,4,25,16,128]{4,3,2,1,0:T(8,128)(2,1)} %copy-done.5), channel_id=1, source_target_pairs={{1,2},{2,1},{5,6},{6,5},{9,10},{10,9},{13,14},{14,13},{17,18},{18,... | collective-permute-start | bytes 2457608 | tf_op jit(solution)/shard_map/ppermute | solution.py:325
  545.9 52.8 %collective-permute-start.36 = (bf16[8,4,8,320]{3,0,2,1:T(8,128)(2,1)S(1)}, bf16[8,4,8,320]{3,0,2,1:T(8,128)(2,1)S(1)}, u32[]{:S(2)}, u32[]{:S(2)}) collective-permute-start(bf16[8,4,8,320]{3,0,2,1:T(8,128)(2,1)S(1)} %copy.80), channel_id=1, source_target_pairs={{0,4},{4,0},{1,5},{5,1},{2,6},{6,2},{3,7},{7,3},{8,12},{12,8},{9,1... | collective-permute-start | bytes 491528 | tf_op jit(solution)/shard_map/ppermute | solution.py:436
  547.7 70.6 %collective-permute-start.55 = (bf16[8,1,8,320]{3,0,2,1:T(8,128)(2,1)S(1)}, bf16[8,1,8,320]{3,0,2,1:T(8,128)(2,1)S(1)}, u32[]{:S(2)}, u32[]{:S(2)}) collective-permute-start(bf16[8,1,8,320]{3,0,2,1:T(8,128)(2,1)S(1)} %get-tuple-element.323), channel_id=1, source_target_pairs={{0,1},{1,0},{2,3},{3,2},{4,5},{5,4},{6,7},{7,6},{8,9},{9,8},{10,11... | collective-permute-start | bytes 122888 | tf_op jit(solution)/shard_map/ppermute | solution.py:442
  563.7 56.1 %collective-permute-start.56 = (bf16[8,1,8,320]{3,0,2,1:T(8,128)(2,1)S(1)}, bf16[8,1,8,320]{3,0,2,1:T(8,128)(2,1)S(1)}, u32[]{:S(2)}, u32[]{:S(2)}) collective-permute-start(bf16[8,1,8,320]{3,0,2,1:T(8,128)(2,1)S(1)} %get-tuple-element.325), channel_id=1, source_target_pairs={{0,2},{1,3},{2,0},{3,1},{4,6},{5,7},{6,4},{7,5},{8,10},{9,11},{10,... | collective-permute-start | bytes 122888 | tf_op jit(solution)/shard_map/ppermute | solution.py:442
  609.9 54.0 %collective-permute-start.76 = (bf16[2,4,25,16,128]{4,3,2,1,0:T(8,128)(2,1)S(1)}, bf16[2,4,25,16,128]{4,3,2,1,0:T(8,128)(2,1)S(1)}, u32[]{:S(2)}, u32[]{:S(2)}) collective-permute-start(bf16[2,4,25,16,128]{4,3,2,1,0:T(8,128)(2,1)S(1)} %collective-permute-done.62.refs_3_), channel_id=1, source_target_pairs={{1,0},{2,3},{5,4},{6,7},{9,8},{10,11},{13,12},{14,15},{17,16},{18,... | collective-permute-start | bytes 2457608 | tf_op jit(solution)/shard_map/ppermute | solution.py:325
  627.0 77.2 %collective-permute-start.37 = (bf16[8,1,8,320]{3,0,2,1:T(8,128)(2,1)S(1)}, bf16[8,1,8,320]{3,0,2,1:T(8,128)(2,1)S(1)}, u32[]{:S(2)}, u32[]{:S(2)}) collective-permute-start(bf16[8,1,8,320]{3,0,2,1:T(8,128)(2,1)S(1)} %get-tuple-element.320), channel_id=1, source_target_pairs={{0,1},{1,0},{2,3},{3,2},{4,5},{5,4},{6,7},{7,6},{8,9},{9,8},{10,11... | collective-permute-start | bytes 122888 | tf_op jit(solution)/shard_map/ppermute | solution.py:442
  642.5 63.2 %collective-permute-start.38 = (bf16[8,1,8,320]{3,0,2,1:T(8,128)(2,1)S(1)}, bf16[8,1,8,320]{3,0,2,1:T(8,128)(2,1)S(1)}, u32[]{:S(2)}, u32[]{:S(2)}) collective-permute-start(bf16[8,1,8,320]{3,0,2,1:T(8,128)(2,1)S(1)} %get-tuple-element.322), channel_id=1, source_target_pairs={{0,2},{1,3},{2,0},{3,1},{4,6},{5,7},{6,4},{7,5},{8,10},{9,11},{10,... | collective-permute-start | bytes 122888 | tf_op jit(solution)/shard_map/ppermute | solution.py:442
  (163 other events, 3624.2 us)

commit v3 on v2

v3 whole, which is shorter than its diff:
```python
import functools

import jax
import jax.numpy as jnp
from jax import lax
from jax.experimental import pallas as pl
from jax.experimental.pallas import tpu as pltpu
from jax.sharding import PartitionSpec as P

LANES = 128
ROWS = 16


def split_sizes(total, count):
    best = 1
    for n in range(1, count + 1):
        if count % n == 0 and total % n == 0 and (total // n) % ROWS == 0:
            best = n
    return best


def group_size(depth):
    best = depth
    for size in range(2, 11, 2):
        if depth % size == 0:
            best = size
    return best


def pack_kernel(group, parts, given, spot_ref, *refs):
    pieces, crossed_ref, low_ref = refs[:parts], refs[parts], refs[parts + 1]
    sent_ref, own_ref, mark_ref, sem = refs[-4:] if parts else (refs[-3], None, refs[-2], refs[-1])
    here = spot_ref[0]
    sides = given["sides"]
    inner = jnp.logical_and(here > 0, here < sides - 1)
    groups, back_at, low_at, low_count, kind_at = (
        given["groups"], given["back"], given["low"], given["count"], given["kind"]
    )
    mark_ref[0] = spot_ref[0]
    mark_ref[1] = spot_ref[1]

    def back():
        return pltpu.make_async_copy(
            crossed_ref.at[0:2 * groups], sent_ref.at[back_at:back_at + 2 * groups], sem
        )

    def lower():
        return pltpu.make_async_copy(
            low_ref.at[low_at:low_at + low_count], sent_ref.at[kind_at:kind_at + low_count], sem
        )

    if given["has_back"]:
        @pl.when(inner)
        def _():
            back().start()
    if low_count:
        @pl.when(jnp.logical_not(inner))
        def _():
            lower().start()

    if parts:
        kinds, depth, rows, width = pieces[0].shape
        total = width * parts
        mains = total // LANES
        rest = total - mains * LANES
        half = (group + 1) // 2

        def place(slot, shift):
            shape = (width, (mains + 1) * LANES)
            target = slot * width + lax.broadcasted_iota(jnp.int32, shape, 0)
            target = jnp.where(target >= mains * LANES, target + shift, target)
            hit = lax.broadcasted_iota(jnp.int32, shape, 1) == target
            return jnp.where(hit, 1.0, 0.0).astype(jnp.bfloat16)

        tables = [[place(s, shift) for s in range(parts)] for shift in (0, rest)]
        for kind in range(kinds):
            base = (0, 2, 1)[kind] * groups

            def put(lo, hi, value):
                value = value.astype(jnp.bfloat16)
                own_ref[base:base + groups, lo:hi] = value
                if kind != 1:
                    sent_ref[base:base + groups, lo:hi] = value
                else:
                    @pl.when(jnp.logical_not(inner))
                    def _():
                        sent_ref[base:base + groups, lo:hi] = value

            tails = []
            for part, (lo, hi) in enumerate(((0, half), (half, group))):
                if lo == hi:
                    continue
                got = 0.0
                for slot, ref in enumerate(pieces):
                    block = ref[kind].reshape(groups, group, rows, width)[:, lo:hi]
                    got = got + jnp.dot(
                        block.reshape(groups * (hi - lo) * rows, width),
                        tables[part][slot],
                        preferred_element_type=jnp.float32,
                    )
                got = got.reshape(groups, hi - lo, rows, (mains + 1) * LANES)
                for main in range(mains):
                    put(main * group + lo, main * group + hi, got[..., main * LANES:(main + 1) * LANES])
                tails.append(got[..., mains * LANES:])
            start = mains * group
            first = tails[0]
            if len(tails) == 1:
                put(start, start + half, first)
            else:
                both = tails[1].shape[1]
                put(start, start + both, first[:, :both] + tails[1])
                if both < half:
                    put(start + both, start + half, first[:, both:])

    if given["has_back"]:
        @pl.when(inner)
        def _():
            back().wait()
    if low_count:
        @pl.when(jnp.logical_not(inner))
        def _():
            lower().wait()


def pack(spot, pieces, crossed, low, deps, given, group, plane, length):
    has_back = crossed is not None
    given = dict(given, has_back=has_back)
    groups = given["groups"]
    out = [jax.ShapeDtypeStruct((length,) + plane, jnp.bfloat16)]
    specs = [pl.BlockSpec(memory_space=pltpu.VMEM)]
    if pieces:
        out.append(jax.ShapeDtypeStruct((3 * groups,) + plane, jnp.bfloat16))
        specs.append(pl.BlockSpec(memory_space=pltpu.VMEM))
    out.append(jax.ShapeDtypeStruct((2,), jnp.int32))
    specs.append(pl.BlockSpec(memory_space=pltpu.SMEM))
    anywhere = pl.BlockSpec(memory_space=pl.ANY)
    operands = [crossed if has_back else low, low] + list(deps)
    got = pl.pallas_call(
        functools.partial(pack_kernel, group, len(pieces), given),
        out_shape=out,
        in_specs=[pl.BlockSpec(memory_space=pltpu.SMEM)]
        + [pl.BlockSpec(memory_space=pltpu.VMEM)] * len(pieces)
        + [anywhere] * len(operands),
        out_specs=specs,
        scratch_shapes=[pltpu.SemaphoreType.DMA],
        compiler_params=pltpu.CompilerParams(vmem_limit_bytes=32 * 2 ** 20),
        cost_estimate=pl.CostEstimate(flops=2 * 10 ** 9, bytes_accessed=6 * 2 ** 20, transcendentals=0),
        name="pack",
    )(spot, *pieces, *operands)
    return (got[0], got[1], got[2]) if pieces else (got[0], None, got[1])


def pass_kernel(given, spot_ref, *refs):
    received_ref, crossed_ref, low_ref = refs[:3]
    outs, sems = refs[given["inputs"]:-1], refs[-1]
    here = spot_ref[0]
    sides, groups = given["sides"], given["groups"]
    inner = jnp.logical_and(here > 0, here < sides - 1)
    low_at, low_count = given["low"], given["count"]
    copies = []
    if given["cross"]:
        copies.append((None, pltpu.make_async_copy(received_ref.at[0:3 * groups], outs[0], sems.at[0])))
    if given["back"]:
        copies.append((inner, pltpu.make_async_copy(crossed_ref.at[0:2 * groups], outs[-1], sems.at[1])))
    if low_count:
        copies.append(
            (
                jnp.logical_not(inner),
                pltpu.make_async_copy(
                    low_ref.at[low_at:low_at + low_count], outs[-1].at[0:low_count], sems.at[2]
                ),
            )
        )
    for act in ("start", "wait"):
        for where, copy in copies:
            if where is None:
                getattr(copy, act)()
            else:
                pl.when(where)(getattr(copy, act))


def pass_on(spot, received, crossed, low, deps, given, plane):
    groups = given["groups"]
    given = dict(given, back=crossed is not None, inputs=3 + len(deps))
    out = []
    if given["cross"]:
        out.append(jax.ShapeDtypeStruct((3 * groups,) + plane, jnp.bfloat16))
    if given["back"]:
        out.append(jax.ShapeDtypeStruct((2 * groups,) + plane, jnp.bfloat16))
    anywhere = pl.BlockSpec(memory_space=pl.ANY)
    operands = [received, crossed if crossed is not None else low, low] + list(deps)
    return pl.pallas_call(
        functools.partial(pass_kernel, given),
        out_shape=out,
        in_specs=[pl.BlockSpec(memory_space=pltpu.SMEM)] + [anywhere] * len(operands),
        out_specs=[anywhere] * len(out),
        scratch_shapes=[pltpu.SemaphoreType.DMA((3,))],
        cost_estimate=pl.CostEstimate(flops=0, bytes_accessed=4 * 2 ** 20, transcendentals=0),
        name="pass_on",
    )(spot, *operands)


def fetch(src, dst, sem):
    pltpu.make_async_copy(src, dst, sem).start()


def expand(source, step, group, groups, tables, spread):
    sides, _, plane, rows, _ = source.shape
    kinds = source.shape[1] // groups
    half = (group + 1) // 2
    mains = (plane - half) // group
    windows = spread[0].shape[0]
    for part, (lo, hi) in enumerate(((0, half), (half, group))):
        if lo == hi:
            continue
        count = hi - lo
        spans = [(main * group + lo, main * group + hi) for main in range(mains)]
        spans.append((mains * group, mains * group + count))
        wide = jnp.concatenate(
            [
                jnp.concatenate(
                    [
                        source[:, kind * groups + step, first:stop].reshape(sides * count * rows, LANES)
                        for first, stop in spans
                    ],
                    axis=1,
                )
                for kind in range(kinds)
            ],
            axis=0,
        )
        for slot, table in enumerate(tables):
            got = jnp.dot(wide, table[part], preferred_element_type=jnp.float32).astype(jnp.bfloat16)
            got = got.reshape(kinds, sides, count, rows, windows * LANES)
            for kind in range(kinds):
                for k in range(count):
                    for a in range(windows):
                        spread[slot + kind][a, :, (lo + k) * LANES:(lo + k + 1) * LANES] = got[
                            kind, :, k, :, a * LANES:(a + 1) * LANES
                        ].reshape(sides * rows, LANES)


def flat(ref):
    windows, rows, lanes = ref.shape
    return ref[...].reshape(windows * rows, lanes)


def even_kernel(sides, group, groups, use_ends, use_inner, starts, spot_ref, *refs):
    views = [ref.at[at:at + 2 * groups] for ref, at in zip(refs[:2 * sides], starts)]
    inner_blocks, end_blocks = views[:sides], views[sides:]
    left_ref, first_ref, last_ref = refs[2 * sides:2 * sides + 3]
    total, even, spread_a, spread_b, sems = refs[-5:]
    here = spot_ref[0]
    step = pl.program_id(0)
    inner = jnp.logical_and(here > 0, here < sides - 1)
    work = jnp.logical_or(jnp.logical_and(inner, use_inner), jnp.logical_and(jnp.logical_not(inner), use_ends))

    @pl.when(work)
    def _():
        @pl.when(step == 0)
        def _():
            total[...] = jnp.zeros_like(total)

            @pl.when(inner)
            def _():
                for at, turn in enumerate((0, 1, 3, 2)):
                    fetch(inner_blocks[at], even.at[here ^ turn], sems.at[at])

            @pl.when(jnp.logical_not(inner))
            def _():
                for at, turn in enumerate((0, 1, 2, 3)):
                    fetch(end_blocks[at], even.at[here ^ turn], sems.at[at])

            for at in range(sides):
                pltpu.make_async_copy(inner_blocks[at], even.at[at], sems.at[at]).wait()

        expand(even, step, group, groups, (left_ref,), (spread_a, spread_b))
        first = first_ref[...].reshape(group * LANES, first_ref.shape[-1])
        last = last_ref[...].reshape(group * LANES, last_ref.shape[-1])
        total[0] += jnp.dot(flat(spread_a), first, preferred_element_type=jnp.float32)
        total[1] += jnp.dot(flat(spread_b), first, preferred_element_type=jnp.float32)
        total[1] += jnp.dot(flat(spread_a), last, preferred_element_type=jnp.float32)

    @pl.when(jnp.logical_and(step == 0, jnp.logical_not(work)))
    def _():
        total[...] = jnp.zeros_like(total)


def even_product(spot, inner_blocks, end_blocks, deps, table, first, last, sides, group, groups):
    some = inner_blocks or end_blocks
    use_inner, use_ends = inner_blocks is not None, end_blocks is not None
    blocks = (inner_blocks or some) + (end_blocks or some)
    starts = [at for _, at in blocks]
    _, planes, rows, _ = some[0][0].shape
    windows = table.shape[2] // LANES
    full = first.shape[-1]
    count = windows * sides * rows
    whole = lambda arr: pl.BlockSpec(arr.shape, lambda g, s: (0,) * len(arr.shape))
    low = pl.BlockSpec((group,) + first.shape[1:], lambda g, s: (g, 0, 0))
    out = jax.ShapeDtypeStruct((2, count, full), jnp.float32)
    depth = groups * group
    flops = 2 * count * depth * LANES * 3 * full + 4 * sides * rows * depth * 3 * LANES * windows * LANES
    return pl.pallas_call(
        functools.partial(even_kernel, sides, group, groups, use_ends, use_inner, starts),
        out_shape=out,
        grid_spec=pltpu.PrefetchScalarGridSpec(
            num_scalar_prefetch=1,
            grid=(groups,),
            in_specs=[pl.BlockSpec(memory_space=pl.ANY)] * (2 * sides)
            + [whole(table), low, low]
            + [pl.BlockSpec(memory_space=pl.ANY)] * len(deps),
            out_specs=whole(out),
            scratch_shapes=[
                pltpu.VMEM((sides, 2 * groups, planes, rows, LANES), jnp.bfloat16),
                pltpu.VMEM((windows, sides * rows, group * LANES), jnp.bfloat16),
                pltpu.VMEM((windows, sides * rows, group * LANES), jnp.bfloat16),
                pltpu.SemaphoreType.DMA((sides,)),
            ],
        ),
        compiler_params=pltpu.CompilerParams(vmem_limit_bytes=40 * 2 ** 20),
        cost_estimate=pl.CostEstimate(flops=flops, bytes_accessed=20 * 2 ** 20, transcendentals=0),
        name="even_product",
    )(spot, *[ref for ref, _ in blocks], table, first, last, *deps)


def odd_kernel(sides, group, groups, outs, starts, spot_ref, *refs):
    blocks = [ref.at[at:at + groups] for ref, at in zip(refs[:sides], starts)]
    inner_part, end_part = refs[sides:sides + 2]
    left_ref, next_left_ref, low_ref, next_low_ref = refs[sides + 2:sides + 6]
    out_refs = refs[-5 - outs:-5]
    odd, spread_a, spread_b, total, sems = refs[-5:]
    here, role = spot_ref[0], spot_ref[1]
    step, last = pl.program_id(0), pl.num_programs(0) - 1
    inner = jnp.logical_and(here > 0, here < sides - 1)

    @pl.when(step == 0)
    def _():
        @pl.when(inner)
        def _():
            fetch(inner_part, total, sems.at[sides])
            for at, turn in enumerate((0, 1, 3, 2)):
                fetch(blocks[at], odd.at[here ^ turn], sems.at[at])
            for at in range(sides):
                pltpu.make_async_copy(blocks[at], odd.at[at], sems.at[at]).wait()

        @pl.when(jnp.logical_not(inner))
        def _():
            fetch(end_part, total, sems.at[sides])

        pltpu.make_async_copy(inner_part, total, sems.at[sides]).wait()

    @pl.when(inner)
    def _():
        expand(odd, step, group, groups, (left_ref, next_left_ref), (spread_a, spread_b))
        low = low_ref[...].reshape(group * LANES, low_ref.shape[-1])
        next_low = next_low_ref[...].reshape(group * LANES, low_ref.shape[-1])
        total[1] += jnp.dot(flat(spread_a), low, preferred_element_type=jnp.float32)
        total[1] += jnp.dot(flat(spread_b), next_low, preferred_element_type=jnp.float32)

    @pl.when(step == last)
    def _():
        for offset in range(outs):
            which = offset ^ role
            value = total[which // 2]
            width = value.shape[1] // 2
            value = jnp.where(which % 2 == 1, value[:, width:], value[:, :width])
            out_refs[offset][...] = value.reshape(out_refs[offset].shape).astype(jnp.bfloat16)


def odd_product(spot, blocks, inner_part, end_part, deps, tables, lows, sides, group, groups, outs):
    starts = [at for _, at in blocks]
    _, planes, rows, _ = blocks[0][0].shape
    table, next_table = tables
    low, next_low = lows
    windows = table.shape[2] // LANES
    full = low.shape[-1]
    count = windows * sides * rows
    whole = lambda arr: pl.BlockSpec(arr.shape, lambda g, s: (0,) * len(arr.shape))
    part = pl.BlockSpec((group,) + low.shape[1:], lambda g, s: (g, 0, 0))
    out = [jax.ShapeDtypeStruct((windows, sides * rows, full // 2), jnp.bfloat16)] * outs
    depth = groups * group
    flops = 2 * count * depth * LANES * 2 * full + 4 * sides * rows * depth * 3 * LANES * windows * LANES
    return pl.pallas_call(
        functools.partial(odd_kernel, sides, group, groups, outs, starts),
        out_shape=out,
        grid_spec=pltpu.PrefetchScalarGridSpec(
            num_scalar_prefetch=1,
            grid=(groups,),
            in_specs=[pl.BlockSpec(memory_space=pl.ANY)] * (sides + 2)
            + [whole(table), whole(next_table), part, part]
            + [pl.BlockSpec(memory_space=pl.ANY)] * len(deps),
            out_specs=[whole(o) for o in out],
            scratch_shapes=[
                pltpu.VMEM((sides, groups, planes, rows, LANES), jnp.bfloat16),
                pltpu.VMEM((windows, sides * rows, group * LANES), jnp.bfloat16),
                pltpu.VMEM((windows, sides * rows, group * LANES), jnp.bfloat16),
                pltpu.VMEM((2, count, full), jnp.float32),
                pltpu.SemaphoreType.DMA((sides + 1,)),
            ],
        ),
        compiler_params=pltpu.CompilerParams(vmem_limit_bytes=40 * 2 ** 20),
        cost_estimate=pl.CostEstimate(flops=flops, bytes_accessed=20 * 2 ** 20, transcendentals=0),
        name="odd_product",
    )(spot, *[ref for ref, _ in blocks], inner_part, end_part, table, next_table, low, next_low, *deps)


def on_device(sizes, tops, bottoms, left_iso, right_iso):
    roles, contrs, sides = sizes
    role = lax.axis_index("role")
    here = lax.axis_index("horiz")
    kinds, depth_all, rows_all, width = tops.shape
    depth = depth_all // roles
    group = group_size(depth)
    groups = depth // group
    share = right_iso.shape[0]
    chunks = split_sizes(rows_all, share)
    unit = share // chunks
    rows = rows_all // chunks
    windows = left_iso.shape[1]
    slab = left_iso.shape[2]
    downs, full = bottoms.shape[3], bottoms.shape[4]
    spot = jnp.stack([here, role]).astype(jnp.int32)

    cut = tops.reshape(kinds, depth_all, contrs, chunks, unit, width)

    def exchange(t, place):
        pieces = []
        for s in range(roles):
            piece = lax.dynamic_slice(
                cut, (0, (place ^ s) * depth, 0, t, 0, 0), (kinds, depth, contrs, 1, unit, width)
            ).reshape(kinds, depth, rows, width)
            if s:
                piece = lax.ppermute(piece, "role", [(j, j ^ s) for j in range(roles)])
            pieces.append(piece)
        return pieces

    def lower(kind, place):
        low = lax.dynamic_slice_in_dim(bottoms[kind], place * depth, depth, 0)
        return low.reshape(depth, slab, downs * full)

    def padded(low):
        return jnp.pad(low, ((0, 0), (0, LANES - slab), (0, 0)))

    pairs = [(z, z ^ 1) for z in range(sides)]
    hand = [(z, z ^ 1) for z in (0, sides - 1)]
    cross = [(z, z ^ 3) for z in range(1, sides - 1)]
    move = lambda value, perm: lax.ppermute(value, "horiz", perm)

    pieces = {0: exchange(0, role)}
    left_all = jnp.concatenate(
        [lax.dynamic_slice_in_dim(left_iso, (role ^ s) * width, width, 0) for s in range(roles)], axis=0
    )
    total = left_all.shape[0]
    mains = total // LANES
    rest = total - mains * LANES
    plane = (mains * group + (group + 1) // 2, rows, LANES)

    def table(flat_left):
        wide = jnp.pad(
            flat_left.reshape(total, windows, slab), ((0, 0), (0, 0), (0, LANES - slab))
        ).reshape(total, windows * LANES)
        first = jnp.pad(wide, ((0, LANES - rest), (0, 0)))
        blank = jnp.zeros((rest, windows * LANES), wide.dtype)
        second = jnp.concatenate([wide[:mains * LANES], blank, wide[mains * LANES:]], axis=0)
        second = jnp.pad(second, ((0, LANES - 2 * rest), (0, 0)))
        return jnp.stack([first, second])

    flat_left = left_all.reshape(total, windows * slab)
    middle = lower(1, role) * jnp.asarray(2, bottoms.dtype)
    tiles = (slab // rows, downs * full // LANES)
    count = depth * tiles[0] * tiles[1]
    units = -(-count // plane[0])
    carried = middle.reshape(depth, tiles[0], rows, tiles[1], LANES).transpose(0, 1, 3, 2, 4)
    carried = jnp.pad(carried.reshape(count, rows, LANES), ((0, units * plane[0] - count), (0, 0), (0, 0)))
    carried = carried.reshape((units,) + plane)
    taken = 0

    def take(most):
        nonlocal taken
        at, size = taken, min(most, units - taken)
        taken += size
        return at, size

    own, sent, straight, turned, last = {}, {}, {}, {}, {}
    sums, shares, reduced = {}, {}, {}
    parts = []
    lows = tables = next_low = None
    done = None

    def reduce_roles(t):
        summed = shares[t][0].astype(jnp.float32)
        for s in range(1, roles):
            got = lax.ppermute(shares[t][s], "role", [(j, j ^ s) for j in range(roles)])
            summed = summed + got.astype(jnp.float32)
        summed = summed.reshape(windows, sides * contrs, unit, full)
        size = sides * contrs
        step = contrs // 2
        place = lax.axis_index("contr")
        while step:
            size //= 2
            bit = (place // step) % 2
            keep = lax.dynamic_slice_in_dim(summed, bit * size, size, 1)
            give = lax.dynamic_slice_in_dim(summed, (1 - bit) * size, size, 1).astype(jnp.bfloat16)
            got = lax.ppermute(give, "contr", [(j, j ^ step) for j in range(contrs)])
            summed = keep + got.astype(jnp.float32)
            step //= 2
        return summed

    for r in range(chunks + 3):
        if r <= chunks:
            fresh = r < chunks
            base = 3 * groups if fresh else 0
            extra = {0: 2, 1: 3}.get(r, 1) * groups if fresh else 0
            at, size = take(extra)
            length = max(base + size, 4 * groups) if fresh else 2 * groups
            given = dict(
                sides=sides, groups=groups, back=2 * groups if fresh else 0, kind=base, low=at, count=size
            )
            deps = [sent[r - 1]] if r else []
            deps += [sums[r - 1]] if r - 1 in sums else []
            out, mine, mark = pack(
                spot, pieces.pop(r) if fresh else [], straight.get(r - 1), carried, deps, given, group,
                plane, length,
            )
            sent[r] = move(out, pairs)
            if size:
                parts.append((at, sent[r], base, size))
            if fresh:
                own[r] = mine
                straight[r] = move(mine, cross)
            done = out
            for t in {0: (1, 2), 1: (3,), 2: (4,)}.get(r, (r + 2,)):
                if t < chunks:
                    pieces[t] = exchange(t, mark[1])
            if r == 0:
                late = mark[1]
                lows = (padded(lower(0, late)), padded(lower(2, late)), padded(middle))
                tables = (table(flat_left), table(move(flat_left, hand)))
        t = r - 4
        if 0 <= t < chunks:
            if next_low is None:
                arrived = [got[first:first + size] for _, got, first, size in sorted(parts, key=lambda p: p[0])]
                arrived = jnp.concatenate(arrived, axis=0).reshape(-1, rows, LANES)[:count]
                arrived = arrived.reshape(depth, tiles[0], tiles[1], rows, LANES).transpose(0, 1, 3, 2, 4)
                next_low = padded(arrived.reshape(depth, slab, downs * full))
            blocks = [(own[t], 2 * groups), (sent[t], 2 * groups), (straight[t], 2 * groups), (turned[t + 1], 2 * groups)]
            shares[t] = odd_product(
                spot, blocks, sums[t + 2], sums[t + 3], [done], tables, (lows[2], next_low),
                sides, group, groups, roles,
            )
            done = shares[t][0]
        if 1 <= r <= chunks + 1:
            at, size = take(2 * groups) if 2 <= r else (0, 0)
            given = dict(sides=sides, groups=groups, cross=r <= chunks, low=at, count=size)
            deps = [done] + ([last[r - 1]] if r - 1 in last else [])
            if r - 5 in shares:
                reduced[r - 5] = reduce_roles(r - 5)
                deps.append(reduced[r - 5])
            outs = pass_on(spot, sent[r - 1], turned.get(r - 1), carried, deps, given, plane)
            if r <= chunks:
                turned[r] = move(outs[0], cross)
            if r - 1 in turned:
                last[r] = move(outs[-1], pairs)
                if size:
                    parts.append((at, last[r], 0, size))
            done = outs[0]
        if r >= 2:
            t = r - 2
            inner_blocks = end_blocks = None
            if t < chunks:
                inner_blocks = [(own[t], 0), (sent[t], 0), (straight[t], 0), (turned[t + 1], 0)]
            t = r - 3
            if 0 <= t:
                end_blocks = [
                    (own[t], 0), (sent[t], 0), (sent[t + 1], 2 * groups if t + 1 < chunks else 0), (last[t + 2], 0)
                ]
            sums[r] = even_product(
                spot, inner_blocks, end_blocks, [done], tables[0], lows[0], lows[1], sides, group, groups
            )
            done = sums[r]
    t = chunks - 1
    blocks = [(own[t], 2 * groups), (sent[t], 2 * groups), (straight[t], 2 * groups), (turned[t + 1], 2 * groups)]
    shares[t] = odd_product(
        spot, blocks, sums[t + 2], sums[t + 3], [done], tables, (lows[2], next_low), sides, group, groups, roles
    )

    for t in range(chunks):
        if t not in reduced:
            reduced[t] = reduce_roles(t)
    summed = jnp.concatenate([reduced[t] for t in range(chunks)], axis=2)
    mine = lax.dynamic_slice_in_dim(summed, here, 1, 1)
    for s in range(1, sides):
        give = lax.dynamic_slice_in_dim(summed, here ^ s, 1, 1).astype(jnp.bfloat16)
        got = lax.ppermute(give, "horiz", [(z, z ^ s) for z in range(sides)])
        mine = mine + got.astype(jnp.float32)
    mine = mine.reshape(windows, share, full).astype(jnp.bfloat16)
    projected = jnp.einsum("aur,urb->ab", mine, right_iso, preferred_element_type=jnp.float32)
    projected = projected * jnp.where(role >= downs, 0.25, 1.0)
    for axis, size in (("contr", contrs), ("horiz", sides)):
        s = 1
        while s < size:
            projected = projected + lax.ppermute(projected, axis, [(j, j ^ s) for j in range(size)])
            s *= 2
    found = [projected] + [
        lax.ppermute(projected, "role", [(j, j ^ s) for j in range(roles)]) for s in range(1, roles)
    ]
    found = jnp.stack(found)
    order = [lax.dynamic_index_in_dim(found, q ^ role, 0, keepdims=False) for q in range(roles)]
    return jnp.stack(order).reshape(roles // downs, downs, windows, -1)


def solution(mesh):
    placed = (
        P(None, "contr", "horiz", "role"),
        P(None, "contr", "horiz", None, None),
        P(None, None, "horiz"),
        P(("contr", "horiz"), None, None),
    )
    sizes = tuple(mesh.shape[axis] for axis in ("role", "contr", "horiz"))
    body = functools.partial(on_device, sizes)
    return jax.shard_map(body, mesh=mesh, in_specs=placed, out_specs=P(), check_vma=False)
```

time: 839 us -> 1030 us (1.23)
  Pallas kernels: 185 us -> 444 us
  waiting for transfers between devices: 221 us -> 107 us
  local copies, waits for them, and re-layouts: 178 us -> 215 us
    pallas_call x16 -> x23, Pallas kernels: 185 us -> 444 us  [the longest x6 233 us: pass_on(): pl.pallas_call(functools.partial(pass_kernel, given), out_shape=out, in_s...]
    ppermute x42 -> x22, waiting for transfers between devices: 118 us -> 19.2 us  [on_device(): move = lambda value, perm: lax.ppermute(value, 'horiz', perm)]
    ppermute x42 -> x22, starting transfers between devices: 119 us -> 189 us  [on_device(): move = lambda value, perm: lax.ppermute(value, 'horiz', perm)]
    ppermute x15 -> x3, starting transfers between devices: 68.1 us -> 3.55 us  [on_device(): got = lax.ppermute(give, 'horiz', [(z, z ^ s) for z in range(sides)])]
    ppermute x20, waiting for transfers between devices: 81.6 us -> 31.1 us  [the longest x15 16.5 us: reduce_roles(): got = lax.ppermute(shares[t][s], 'role', [(j, j ^ s) for j in range(roles)])]
    reshape x0 -> x4, local copies, waits for them, and re-layouts: none -> 20.4 us  [the longest x3 10.4 us: exchange(): piece = lax.dynamic_slice(cut, (0, (place ^ s) * depth, 0, t, 0, 0), (kin...]
    ppermute x15 -> x3, waiting for transfers between devices: 2.28 us -> 21.2 us  [on_device(): got = lax.ppermute(give, 'horiz', [(z, z ^ s) for z in range(sides)])]
    ppermute x15, waiting for transfers between devices: 6.31 us -> 22.2 us  [exchange(): piece = lax.ppermute(piece, 'role', [(j, j ^ s) for j in range(roles)])]
  transfers between devices with their start and end apart: 98 -> 66, of which waited for: 23 -> 17; matrix products, arithmetic and copies ran while one was open for 20% -> 20% of each run, Pallas kernels for 22% -> 42%
where the time goes in v3:
time: 1030 us; the launch traced here: 1020 us
  Pallas kernels  444 us (43%)
  starting transfers between devices  220 us (21%)
  local copies, waits for them, and re-layouts  215 us (21%)
  waiting for transfers between devices  107 us (10%)
  other arithmetic  23.5 us (2%)
    pallas_call x6, Pallas kernels, pass_on(): pl.pallas_call(functools.partial(pass_kernel, given), out_shape=out, in_s...  233 us
    ppermute x22, starting transfers between devices, on_device(): move = lambda value, perm: lax.ppermute(value, 'horiz', perm)  189 us
    pallas_call x6, Pallas kernels, even_product(): pl.pallas_call(functools.partial(even_kernel, sides, group, groups, use_e...  142 us
    pallas_call x5, Pallas kernels, odd_product(): pl.pallas_call(functools.partial(odd_kernel, sides, group, groups, outs,...  44.3 us
    slice x1, local copies, waits for them, and re-layouts, lower(): low = lax.dynamic_slice_in_dim(bottoms[kind], place * depth, depth, 0)  44 us
    unnamed x149, local copies, waits for them, and re-layouts  36.5 us
    mul x2, local copies, waits for them, and re-layouts, on_device(): middle = lower(1, role) * jnp.asarray(2, bottoms.dtype)  24.3 us
    pallas_call x6, Pallas kernels, pack(): pl.pallas_call(functools.partial(pack_kernel, group, len(pieces), given),...  23.7 us
  transfers between devices with their start and end apart: 66, of which 17 were waited for; matrix products, arithmetic and copies ran while one was open for 20% of the time, Pallas kernels for 42%

profile of v3, /device:TPU:0, one launch (start us, length us, event | category | flops | bytes accessed | tf_op | source)
XLA Modules:
  0.0 1023.3 jit_solution(10725271964517438833)
XLA Ops:
  5.0 44.0 %fusion.3 = (bf16[1,160,80,2,320]{4,3,2,1,0:T(2,128)(2,1)}, bf16[1,160,80,2,320]{4,3,2,1,0:T(2,128)(2,1)}, bf16[1,160,80,2,320]{4,3,2,1,0:T(2,128)(2,1)}) fusion(bf16[3,160,80,2,320]{4,3,2,1,0:T(2,128)(2,1)} %param.5), kind=kLoop, calls=%fused_computation.77 | loop fusion | bytes 98304000 | tf_op jit(solution)/shard_map/slice | solution.py:438
  57.6 13.8 %mul.142 = bf16[40,5,16,5,128]{4,3,2,1,0:T(8,128)(2,1)} reshape(bf16[1,40,80,2,320]{4,3,2,1,0:T(2,128)(2,1)} %dynamic-slice_multiply_fusion) | data formatting | bytes 8192000 | tf_op jit(solution)/shard_map/mul | solution.py:469
  92.6 11.5 %collective-permute-done.7.refs_3_ = bf16[3,40,16,80]{3,2,1,0:T(8,128)(2,1)S(1)} collective-permute-done((bf16[3,40,16,80]{3,2,1,0:T(8,128)(2,1)S(1)}, bf16[3,40,16,80]{3,2,1,0:T(8,128)(2,1)S(1)}, u32[]{:S(2)}, u32[]{:S(2)}) %collective-permute-start.7) | collective-permute-done | bytes 307232 | tf_op jit(solution)/shard_map/ppermute | solution.py:433
  104.1 10.6 %collective-permute-done.6.refs_2_ = bf16[3,40,16,80]{3,2,1,0:T(8,128)(2,1)S(1)} collective-permute-done((bf16[3,40,16,80]{3,2,1,0:T(8,128)(2,1)S(1)}, bf16[3,40,16,80]{3,2,1,0:T(8,128)(2,1)S(1)}, u32[]{:S(2)}, u32[]{:S(2)}) %collective-permute-start.6) | collective-permute-done | bytes 307232 | tf_op jit(solution)/shard_map/ppermute | solution.py:433
  114.8 12.3 %collective-permute-done.3.refs_6_.refs_0_.refs_1_.refs_5_ = bf16[20,25,16,128]{3,2,1,0:T(8,128)(2,1)S(1)} collective-permute-done((bf16[20,25,16,128]{3,2,1,0:T(8,128)(2,1)}, bf16[20,25,16,128]{3,2,1,0:T(8,128)(2,1)S(1)}, u32[]{:S(2)}, u32[]{:S(2)}) %collective-permute-start.3) | collective-permute-done | bytes 2048032 | tf_op jit(solution)/shard_map/ppermute | solution.py:447
  137.9 10.5 %mul.163 = bf16[40,80,640]{2,1,0:T(8,128)(2,1)} reshape(bf16[1,40,80,2,320]{4,3,2,1,0:T(2,128)(2,1)} %dynamic-slice_multiply_fusion) | data formatting | bytes 8192000 | tf_op jit(solution)/shard_map/mul | solution.py:469
  176.5 10.5 %reshape.180 = bf16[40,80,640]{2,1,0:T(8,128)(2,1)} reshape(bf16[1,40,80,2,320]{4,3,2,1,0:T(2,128)(2,1)} %get-tuple-element.129) | data formatting | bytes 8192000 | tf_op jit(solution)/shard_map/reshape | solution.py:439
  194.3 10.5 %reshape.179 = bf16[40,80,640]{2,1,0:T(8,128)(2,1)} reshape(bf16[1,40,80,2,320]{4,3,2,1,0:T(2,128)(2,1)} %get-tuple-element.130) | data formatting | bytes 8192000 | tf_op jit(solution)/shard_map/reshape | solution.py:439
  218.4 39.0 %pass_on.6 = bf16[12,25,16,128]{3,2,1,0:T(8,128)(2,1)} custom-call(s32[2]{0:T(128)} %copy-done.46, bf16[20,25,16,128]{3,2,1,0:T(8,128)(2,1)} %copy-done.8, bf16[40,25,16,128]{3,2,1,0:T(8,128)(2,1)} %bitcast.141, bf16[40,25,16,128]{3,2,1,0:T(8,128)(2,1)} %bitcast.142, bf16[24,25,16,128]{3,2,1,0:T(8,128)(2,1)} %get-tuple-element.50.refs_3_), custom_call_target="tpu_custom_call" | custom-call | bytes 4194304 | tf_op jit(solution)/shard_map/pass_on/pallas_call | solution.py:192
  297.4 63.8 %pass_on.7 = (bf16[12,25,16,128]{3,2,1,0:T(8,128)(2,1)}, bf16[8,25,16,128]{3,2,1,0:T(8,128)(2,1)}) custom-call(s32[2]{0:T(128)} %copy-done.46, bf16[24,25,16,128]{3,2,1,0:T(8,128)(2,1)} %copy-done.6, bf16[12,25,16,128]{3,2,1,0:T(8,128)(2,1)} %collective-permute-done.8.refs_1_.refs_3_.refs_7_, bf16[40,25,16,128]{3,2,1,0:T(8,128)(2,1)} %bitcast.143, ...), custom_call_target="tpu_custom_call" | custom-call | bytes 4194304 | tf_op jit(solution)/shard_map/pass_on/pallas_call | solution.py:192
  387.9 23.1 %collective-permute-start.22 = (bf16[16,25,16,128]{3,2,1,0:T(8,128)(2,1)}, bf16[16,25,16,128]{3,2,1,0:T(8,128)(2,1)}, u32[]{:S(2)}, u32[]{:S(2)}) collective-permute-start(bf16[16,25,16,128]{3,2,1,0:T(8,128)(2,1)} %get-tuple-element.57.refs_3_), channel_id=1, source_target_pairs={{0,1},{1,0},{2,3},{3,2},{4,5},{5,4},{6,7},{7,6},{8,9},{9,8},{10,11... | collective-permute-start | bytes 4915208 | tf_op jit(solution)/shard_map/ppermute | solution.py:447
  410.9 51.4 %pass_on.8 = (bf16[12,25,16,128]{3,2,1,0:T(8,128)(2,1)}, bf16[8,25,16,128]{3,2,1,0:T(8,128)(2,1)}) custom-call(s32[2]{0:T(128)} %copy-done.46, bf16[16,25,16,128]{3,2,1,0:T(8,128)(2,1)} %collective-permute-done.16.refs_6_.refs_0_.refs_1_.refs_5_, bf16[12,25,16,128]{3,2,1,0:T(8,128)(2,1)} %collective-permute-done.14.refs_1_.refs_3_, ...), custom_call_target="tpu_custom_call" | custom-call | bytes 4194304 | tf_op jit(solution)/shard_map/pass_on/pallas_call | solution.py:192
  462.4 13.3 %collective-permute-start.23 = (bf16[8,25,16,128]{3,2,1,0:T(8,128)(2,1)}, bf16[8,25,16,128]{3,2,1,0:T(8,128)(2,1)S(1)}, u32[]{:S(2)}, u32[]{:S(2)}) collective-permute-start(bf16[8,25,16,128]{3,2,1,0:T(8,128)(2,1)} %get-tuple-element.59), channel_id=1, source_target_pairs={{0,1},{1,0},{2,3},{3,2},{4,5},{5,4},{6,7},{7,6},{8,9},{9,8},{10,11... | collective-permute-start | bytes 2457608 | tf_op jit(solution)/shard_map/ppermute | solution.py:447
  479.8 28.0 %even_product.7.refs_7_.refs_5_.refs_4_ = f32[2,512,640]{2,1,0:T(8,128)} custom-call(s32[2]{0:T(128)S(1)} %copy-done.49, bf16[12,25,16,128]{3,2,1,0:T(8,128)(2,1)} %get-tuple-element.51.refs_0_.refs_4_, bf16[24,25,16,128]{3,2,1,0:T(8,128)(2,1)S(1)} %copy-done.7, bf16[12,25,16,128]{3,2,1,0:T(8,128)(2,1)} %collective-permute-done.13.refs_4_.refs_2_, ...), custom_call_target="tpu_custom_call" | custom-call | flops 14092861440 | bytes 20971520 | tf_op jit(solution)/shard_map/even_product/pallas_call | solution.py:303
  550.7 12.6 %collective-permute-start.34 = (bf16[16,25,16,128]{3,2,1,0:T(8,128)(2,1)}, bf16[16,25,16,128]{3,2,1,0:T(8,128)(2,1)}, u32[]{:S(2)}, u32[]{:S(2)}) collective-permute-start(bf16[16,25,16,128]{3,2,1,0:T(8,128)(2,1)} %copy-done.53), channel_id=1, source_target_pairs={{0,1},{1,0},{2,3},{3,2},{4,5},{5,4},{6,7},{7,6},{8,9},{9,8},{10,11... | collective-permute-start | bytes 4915208 | tf_op jit(solution)/shard_map/ppermute | solution.py:447
  565.0 39.1 %pass_on.9 = (bf16[12,25,16,128]{3,2,1,0:T(8,128)(2,1)}, bf16[8,25,16,128]{3,2,1,0:T(8,128)(2,1)}) custom-call(s32[2]{0:T(128)} %copy-done.46, bf16[16,25,16,128]{3,2,1,0:T(8,128)(2,1)} %collective-permute-done.22.refs_6_.refs_0_.refs_1_.refs_5_, bf16[12,25,16,128]{3,2,1,0:T(8,128)(2,1)} %collective-permute-done.32.refs_1_.refs_3_, ...), custom_call_target="tpu_custom_call" | custom-call | bytes 4194304 | tf_op jit(solution)/shard_map/pass_on/pallas_call | solution.py:192
  604.2 26.8 %collective-permute-start.40 = (bf16[8,25,16,128]{3,2,1,0:T(8,128)(2,1)}, bf16[8,25,16,128]{3,2,1,0:T(8,128)(2,1)S(1)}, u32[]{:S(2)}, u32[]{:S(2)}) collective-permute-start(bf16[8,25,16,128]{3,2,1,0:T(8,128)(2,1)} %get-tuple-element.74), channel_id=1, source_target_pairs={{0,1},{1,0},{2,3},{3,2},{4,5},{5,4},{6,7},{7,6},{8,9},{9,8},{10,11... | collective-permute-start | bytes 2457608 | tf_op jit(solution)/shard_map/ppermute | solution.py:447
  636.0 28.0 %even_product.8.refs_3_.refs_5_.refs_4_ = f32[2,512,640]{2,1,0:T(8,128)} custom-call(s32[2]{0:T(128)S(1)} %copy-done.50, bf16[12,25,16,128]{3,2,1,0:T(8,128)(2,1)} %get-tuple-element.56.refs_0_.refs_4_, bf16[16,25,16,128]{3,2,1,0:T(8,128)(2,1)} %collective-permute-done.16.refs_6_.refs_0_.refs_1_.refs_5_, ...), custom_call_target="tpu_custom_call" | custom-call | flops 14092861440 | bytes 20971520 | tf_op jit(solution)/shard_map/even_product/pallas_call | solution.py:303
  685.1 39.1 %pass_on.10 = (bf16[12,25,16,128]{3,2,1,0:T(8,128)(2,1)}, bf16[8,25,16,128]{3,2,1,0:T(8,128)(2,1)}) custom-call(s32[2]{0:T(128)} %copy-done.46, bf16[16,25,16,128]{3,2,1,0:T(8,128)(2,1)} %collective-permute-done.34.refs_2_.refs_0_.refs_1_.refs_6_.refs_5_, bf16[12,25,16,128]{3,2,1,0:T(8,128)(2,1)} %copy-done.36, bf16[40,25,16,128]{3,2,1,0:T(8,128)(2,1)} %bitcast.146, ...), custom_call_target="tpu_custom_call" | custom-call | bytes 4194304 | tf_op jit(solution)/shard_map/pass_on/pallas_call | solution.py:192
  730.0 26.6 %even_product.9.refs_5_.refs_10_.refs_4_ = f32[2,512,640]{2,1,0:T(8,128)S(1)} custom-call(s32[2]{0:T(128)S(1)} %copy-done.51, bf16[12,25,16,128]{3,2,1,0:T(8,128)(2,1)} %get-tuple-element.61.refs_0_.refs_4_, bf16[16,25,16,128]{3,2,1,0:T(8,128)(2,1)} %collective-permute-done.22.refs_6_.refs_0_.refs_1_.refs_5_, ...), custom_call_target="tpu_custom_call" | custom-call | flops 14092861440 | bytes 20971520 | tf_op jit(solution)/shard_map/even_product/pallas_call | solution.py:303
  770.1 49.1 %collective-permute-start.46 = (bf16[8,25,16,128]{3,2,1,0:T(8,128)(2,1)S(1)}, bf16[8,25,16,128]{3,2,1,0:T(8,128)(2,1)}, u32[]{:S(2)}, u32[]{:S(2)}) collective-permute-start(bf16[8,25,16,128]{3,2,1,0:T(8,128)(2,1)S(1)} %copy-done.71), channel_id=1, source_target_pairs={{0,1},{1,0},{2,3},{3,2},{4,5},{5,4},{6,7},{7,6},{8,9},{9,8},{10,11... | collective-permute-start | bytes 2457608 | tf_op jit(solution)/shard_map/ppermute | solution.py:447
  838.9 31.8 %collective-permute-start.52 = (bf16[8,25,16,128]{3,2,1,0:T(8,128)(2,1)}, bf16[8,25,16,128]{3,2,1,0:T(8,128)(2,1)S(1)}, u32[]{:S(2)}, u32[]{:S(2)}) collective-permute-start(bf16[8,25,16,128]{3,2,1,0:T(8,128)(2,1)} %pass_on.11.refs_11_), channel_id=1, source_target_pairs={{0,1},{1,0},{2,3},{3,2},{4,5},{5,4},{6,7},{7,6},{8,9},{9,8},{10,11... | collective-permute-start | bytes 2457608 | tf_op jit(solution)/shard_map/ppermute | solution.py:447
  873.2 27.1 %even_product.10.refs_5_.refs_10_.refs_4_ = f32[2,512,640]{2,1,0:T(8,128)S(1)} custom-call(s32[2]{0:T(128)S(1)} %copy-done.52, bf16[12,25,16,128]{3,2,1,0:T(8,128)(2,1)S(1)} %copy-done.55, bf16[16,25,16,128]{3,2,1,0:T(8,128)(2,1)} %collective-permute-done.34.refs_2_.refs_0_.refs_1_.refs_6_.refs_5_, ...), custom_call_target="tpu_custom_call" | custom-call | flops 14092861440 | bytes 20971520 | tf_op jit(solution)/shard_map/even_product/pallas_call | solution.py:303
  912.3 26.7 %even_product.11.refs_5_.refs_10_ = f32[2,512,640]{2,1,0:T(8,128)S(1)} custom-call(s32[2]{0:T(128)S(1)} %copy-done.52, bf16[12,25,16,128]{3,2,1,0:T(8,128)(2,1)S(1)} %copy-done.55, bf16[16,25,16,128]{3,2,1,0:T(8,128)(2,1)} %collective-permute-done.34.refs_2_.refs_0_.refs_1_.refs_6_.refs_5_, ...), custom_call_target="tpu_custom_call" | custom-call | flops 14092861440 | bytes 20971520 | tf_op jit(solution)/shard_map/even_product/pallas_call | solution.py:303
  (347 shorter events, 365.1 us)
Async XLA Ops:
  1.9 73.6 %collective-permute-start.2 = (bf16[3,40,16,80]{3,2,1,0:T(8,128)(2,1)S(1)}, bf16[3,40,16,80]{3,2,1,0:T(8,128)(2,1)S(1)}, u32[]{:S(2)}, u32[]{:S(2)}) collective-permute-start(bf16[3,40,16,80]{3,2,1,0:T(8,128)(2,1)S(1)} %get-tuple-element.112), channel_id=1, source_target_pairs={{0,24},{8,16},{16,8},{24,0},{1,25},{9,17},{17,9},{25,1},{2,26},{10... | collective-permute-start | bytes 921608 | tf_op jit(solution)/shard_map/ppermute | solution.py:433
  131.6 141.5 %collective-permute-start.9 = (bf16[24,25,16,128]{3,2,1,0:T(8,128)(2,1)}, bf16[24,25,16,128]{3,2,1,0:T(8,128)(2,1)S(1)}, u32[]{:S(2)}, u32[]{:S(2)}) collective-permute-start(bf16[24,25,16,128]{3,2,1,0:T(8,128)(2,1)} %get-tuple-element.50.refs_3_), channel_id=1, source_target_pairs={{0,1},{1,0},{2,3},{3,2},{4,5},{5,4},{6,7},{7,6},{8,9},{9,8},{10,11... | collective-permute-start | bytes 7372808 | tf_op jit(solution)/shard_map/ppermute | solution.py:447
  134.3 76.4 %collective-permute-start.21 = (bf16[320,640]{0,1:T(8,128)(2,1)}, bf16[320,640]{0,1:T(8,128)(2,1)}, u32[]{:S(2)}, u32[]{:S(2)}) collective-permute-start(bf16[320,640]{0,1:T(8,128)(2,1)} %bitcast.34), channel_id=1, source_target_pairs={{0,1},{3,2},{4,5},{7,6},{8,9},{11,10},{12,13},{15,14},{16,17},{19,... | collective-permute-start | bytes 1228808 | tf_op jit(solution)/shard_map/ppermute | solution.py:447
  165.2 92.3 %collective-permute-start.12 = (bf16[3,40,16,80]{3,2,1,0:T(8,128)(2,1)}, bf16[3,40,16,80]{3,2,1,0:T(8,128)(2,1)S(1)}, u32[]{:S(2)}, u32[]{:S(2)}) collective-permute-start(bf16[3,40,16,80]{3,2,1,0:T(8,128)(2,1)} %get-tuple-element.104), channel_id=1, source_target_pairs={{0,24},{8,16},{16,8},{24,0},{1,25},{9,17},{17,9},{25,1},{2,26},{10... | collective-permute-start | bytes 921608 | tf_op jit(solution)/shard_map/ppermute | solution.py:433
  165.2 107.9 %collective-permute-start.13 = (bf16[12,25,16,128]{3,2,1,0:T(8,128)(2,1)}, bf16[12,25,16,128]{3,2,1,0:T(8,128)(2,1)}, u32[]{:S(2)}, u32[]{:S(2)}) collective-permute-start(bf16[12,25,16,128]{3,2,1,0:T(8,128)(2,1)} %get-tuple-element.51.refs_0_.refs_4_), channel_id=1, source_target_pairs={{1,2},{2,1},{5,6},{6,5},{9,10},{10,9},{13,14},{14,13},{17,18},{18,... | collective-permute-start | bytes 3686408 | tf_op jit(solution)/shard_map/ppermute | solution.py:447
  192.9 80.2 %collective-permute-start.11 = (bf16[3,40,16,80]{3,2,1,0:T(8,128)(2,1)}, bf16[3,40,16,80]{3,2,1,0:T(8,128)(2,1)}, u32[]{:S(2)}, u32[]{:S(2)}) collective-permute-start(bf16[3,40,16,80]{3,2,1,0:T(8,128)(2,1)} %get-tuple-element.105), channel_id=1, source_target_pairs={{0,16},{8,24},{16,0},{24,8},{1,17},{9,25},{17,1},{25,9},{2,18},{10... | collective-permute-start | bytes 921608 | tf_op jit(solution)/shard_map/ppermute | solution.py:433
  288.8 75.9 %collective-permute-start.19 = (bf16[3,40,16,80]{3,2,1,0:T(8,128)(2,1)S(1)}, bf16[3,40,16,80]{3,2,1,0:T(8,128)(2,1)S(1)}, u32[]{:S(2)}, u32[]{:S(2)}) collective-permute-start(bf16[3,40,16,80]{3,2,1,0:T(8,128)(2,1)S(1)} %get-tuple-element.100), channel_id=1, source_target_pairs={{0,24},{8,16},{16,8},{24,0},{1,25},{9,17},{17,9},{25,1},{2,26},{10... | collective-permute-start | bytes 921608 | tf_op jit(solution)/shard_map/ppermute | solution.py:433
  289.7 77.4 %collective-permute-start.18 = (bf16[3,40,16,80]{3,2,1,0:T(8,128)(2,1)S(1)}, bf16[3,40,16,80]{3,2,1,0:T(8,128)(2,1)S(1)}, u32[]{:S(2)}, u32[]{:S(2)}) collective-permute-start(bf16[3,40,16,80]{3,2,1,0:T(8,128)(2,1)S(1)} %get-tuple-element.101), channel_id=1, source_target_pairs={{0,16},{8,24},{16,0},{24,8},{1,17},{9,25},{17,1},{25,9},{2,18},{10... | collective-permute-start | bytes 921608 | tf_op jit(solution)/shard_map/ppermute | solution.py:433
  291.8 89.9 %collective-permute-start.16 = (bf16[16,25,16,128]{3,2,1,0:T(8,128)(2,1)}, bf16[16,25,16,128]{3,2,1,0:T(8,128)(2,1)}, u32[]{:S(2)}, u32[]{:S(2)}) collective-permute-start(bf16[16,25,16,128]{3,2,1,0:T(8,128)(2,1)} %get-tuple-element.52.refs_3_), channel_id=1, source_target_pairs={{0,1},{1,0},{2,3},{3,2},{4,5},{5,4},{6,7},{7,6},{8,9},{9,8},{10,11... | collective-permute-start | bytes 4915208 | tf_op jit(solution)/shard_map/ppermute | solution.py:447
  295.5 85.5 %collective-permute-start.20 = (bf16[12,25,16,128]{3,2,1,0:T(8,128)(2,1)}, bf16[12,25,16,128]{3,2,1,0:T(8,128)(2,1)}, u32[]{:S(2)}, u32[]{:S(2)}) collective-permute-start(bf16[12,25,16,128]{3,2,1,0:T(8,128)(2,1)} %get-tuple-element.56.refs_0_.refs_4_), channel_id=1, source_target_pairs={{1,2},{2,1},{5,6},{6,5},{9,10},{10,9},{13,14},{14,13},{17,18},{18,... | collective-permute-start | bytes 3686408 | tf_op jit(solution)/shard_map/ppermute | solution.py:447
  379.7 153.7 %collective-permute-start.26 = (bf16[3,40,16,80]{3,2,1,0:T(8,128)(2,1)}, bf16[3,40,16,80]{3,2,1,0:T(8,128)(2,1)}, u32[]{:S(2)}, u32[]{:S(2)}) collective-permute-start(bf16[3,40,16,80]{3,2,1,0:T(8,128)(2,1)} %get-tuple-element.96), channel_id=1, source_target_pairs={{0,24},{8,16},{16,8},{24,0},{1,25},{9,17},{17,9},{25,1},{2,26},{10... | collective-permute-start | bytes 921608 | tf_op jit(solution)/shard_map/ppermute | solution.py:433
  381.0 152.4 %collective-permute-start.25 = (bf16[3,40,16,80]{3,2,1,0:T(8,128)(2,1)}, bf16[3,40,16,80]{3,2,1,0:T(8,128)(2,1)}, u32[]{:S(2)}, u32[]{:S(2)}) collective-permute-start(bf16[3,40,16,80]{3,2,1,0:T(8,128)(2,1)} %get-tuple-element.97), channel_id=1, source_target_pairs={{0,16},{8,24},{16,0},{24,8},{1,17},{9,25},{17,1},{25,9},{2,18},{10... | collective-permute-start | bytes 921608 | tf_op jit(solution)/shard_map/ppermute | solution.py:433
  386.0 147.5 %collective-permute-start.27 = (bf16[12,25,16,128]{3,2,1,0:T(8,128)(2,1)}, bf16[12,25,16,128]{3,2,1,0:T(8,128)(2,1)}, u32[]{:S(2)}, u32[]{:S(2)}) collective-permute-start(bf16[12,25,16,128]{3,2,1,0:T(8,128)(2,1)} %get-tuple-element.61.refs_0_.refs_4_), channel_id=1, source_target_pairs={{1,2},{2,1},{5,6},{6,5},{9,10},{10,9},{13,14},{14,13},{17,18},{18,... | collective-permute-start | bytes 3686408 | tf_op jit(solution)/shard_map/ppermute | solution.py:447
  387.9 121.3 %collective-permute-start.22 = (bf16[16,25,16,128]{3,2,1,0:T(8,128)(2,1)}, bf16[16,25,16,128]{3,2,1,0:T(8,128)(2,1)}, u32[]{:S(2)}, u32[]{:S(2)}) collective-permute-start(bf16[16,25,16,128]{3,2,1,0:T(8,128)(2,1)} %get-tuple-element.57.refs_3_), channel_id=1, source_target_pairs={{0,1},{1,0},{2,3},{3,2},{4,5},{5,4},{6,7},{7,6},{8,9},{9,8},{10,11... | collective-permute-start | bytes 4915208 | tf_op jit(solution)/shard_map/ppermute | solution.py:447
  549.4 81.6 %collective-permute-start.29 = (bf16[8,64,320]{2,1,0:T(8,128)(2,1)}, bf16[8,64,320]{2,1,0:T(8,128)(2,1)}, u32[]{:S(2)}, u32[]{:S(2)}) collective-permute-start(bf16[8,64,320]{2,1,0:T(8,128)(2,1)} %get-tuple-element.65), channel_id=1, source_target_pairs={{0,16},{8,24},{16,0},{24,8},{1,17},{9,25},{17,1},{25,9},{2,18},{10... | collective-permute-start | bytes 983048 | tf_op jit(solution)/shard_map/ppermute | solution.py:493
  550.7 81.0 %collective-permute-start.30 = (bf16[8,64,320]{2,1,0:T(8,128)(2,1)S(1)}, bf16[8,64,320]{2,1,0:T(8,128)(2,1)}, u32[]{:S(2)}, u32[]{:S(2)}) collective-permute-start(bf16[8,64,320]{2,1,0:T(8,128)(2,1)S(1)} %get-tuple-element.66), channel_id=1, source_target_pairs={{0,24},{8,16},{16,8},{24,0},{1,25},{9,17},{17,9},{25,1},{2,26},{10... | collective-permute-start | bytes 983048 | tf_op jit(solution)/shard_map/ppermute | solution.py:493
  550.7 114.3 %collective-permute-start.34 = (bf16[16,25,16,128]{3,2,1,0:T(8,128)(2,1)}, bf16[16,25,16,128]{3,2,1,0:T(8,128)(2,1)}, u32[]{:S(2)}, u32[]{:S(2)}) collective-permute-start(bf16[16,25,16,128]{3,2,1,0:T(8,128)(2,1)} %copy-done.53), channel_id=1, source_target_pairs={{0,1},{1,0},{2,3},{3,2},{4,5},{5,4},{6,7},{7,6},{8,9},{9,8},{10,11... | collective-permute-start | bytes 4915208 | tf_op jit(solution)/shard_map/ppermute | solution.py:447
  563.3 101.7 %collective-permute-start.33 = (bf16[12,25,16,128]{3,2,1,0:T(8,128)(2,1)}, bf16[12,25,16,128]{3,2,1,0:T(8,128)(2,1)}, u32[]{:S(2)}, u32[]{:S(2)}) collective-permute-start(bf16[12,25,16,128]{3,2,1,0:T(8,128)(2,1)} %copy-done.54), channel_id=1, source_target_pairs={{1,2},{2,1},{5,6},{6,5},{9,10},{10,9},{13,14},{14,13},{17,18},{18,... | collective-permute-start | bytes 3686408 | tf_op jit(solution)/shard_map/ppermute | solution.py:447
  604.2 79.1 %collective-permute-start.40 = (bf16[8,25,16,128]{3,2,1,0:T(8,128)(2,1)}, bf16[8,25,16,128]{3,2,1,0:T(8,128)(2,1)S(1)}, u32[]{:S(2)}, u32[]{:S(2)}) collective-permute-start(bf16[8,25,16,128]{3,2,1,0:T(8,128)(2,1)} %get-tuple-element.74), channel_id=1, source_target_pairs={{0,1},{1,0},{2,3},{3,2},{4,5},{5,4},{6,7},{7,6},{8,9},{9,8},{10,11... | collective-permute-start | bytes 2457608 | tf_op jit(solution)/shard_map/ppermute | solution.py:447
  668.3 162.8 %collective-permute-start.47 = (bf16[8,25,16,128]{3,2,1,0:T(8,128)(2,1)}, bf16[8,25,16,128]{3,2,1,0:T(8,128)(2,1)}, u32[]{:S(2)}, u32[]{:S(2)}) collective-permute-start(bf16[8,25,16,128]{3,2,1,0:T(8,128)(2,1)} %get-tuple-element.69.refs_10_), channel_id=1, source_target_pairs={{0,1},{1,0},{2,3},{3,2},{4,5},{5,4},{6,7},{7,6},{8,9},{9,8},{10,11... | collective-permute-start | bytes 2457608 | tf_op jit(solution)/shard_map/ppermute | solution.py:447
  682.2 84.5 %collective-permute-start.35 = (bf16[8,64,320]{2,1,0:T(8,128)(2,1)}, bf16[8,64,320]{2,1,0:T(8,128)(2,1)}, u32[]{:S(2)}, u32[]{:S(2)}) collective-permute-start(bf16[8,64,320]{2,1,0:T(8,128)(2,1)} %get-tuple-element.71), channel_id=1, source_target_pairs={{0,8},{8,0},{16,24},{24,16},{1,9},{9,1},{17,25},{25,17},{2,10},{10... | collective-permute-start | bytes 983048 | tf_op jit(solution)/shard_map/ppermute | solution.py:493
  682.2 84.9 %collective-permute-start.36 = (bf16[8,64,320]{2,1,0:T(8,128)(2,1)}, bf16[8,64,320]{2,1,0:T(8,128)(2,1)}, u32[]{:S(2)}, u32[]{:S(2)}) collective-permute-start(bf16[8,64,320]{2,1,0:T(8,128)(2,1)} %get-tuple-element.72), channel_id=1, source_target_pairs={{0,16},{8,24},{16,0},{24,8},{1,17},{9,25},{17,1},{25,9},{2,18},{10... | collective-permute-start | bytes 983048 | tf_op jit(solution)/shard_map/ppermute | solution.py:493
  683.3 84.9 %collective-permute-start.37 = (bf16[8,64,320]{2,1,0:T(8,128)(2,1)S(1)}, bf16[8,64,320]{2,1,0:T(8,128)(2,1)}, u32[]{:S(2)}, u32[]{:S(2)}) collective-permute-start(bf16[8,64,320]{2,1,0:T(8,128)(2,1)S(1)} %get-tuple-element.73), channel_id=1, source_target_pairs={{0,24},{8,16},{16,8},{24,0},{1,25},{9,17},{17,9},{25,1},{2,26},{10... | collective-permute-start | bytes 983048 | tf_op jit(solution)/shard_map/ppermute | solution.py:493
  724.2 113.8 %collective-permute-start.45 = (bf16[12,25,16,128]{3,2,1,0:T(8,128)(2,1)}, bf16[12,25,16,128]{3,2,1,0:T(8,128)(2,1)}, u32[]{:S(2)}, u32[]{:S(2)}) collective-permute-start(bf16[12,25,16,128]{3,2,1,0:T(8,128)(2,1)} %get-tuple-element.75.refs_11_), channel_id=1, source_target_pairs={{1,2},{2,1},{5,6},{6,5},{9,10},{10,9},{13,14},{14,13},{17,18},{18,... | collective-permute-start | bytes 3686408 | tf_op jit(solution)/shard_map/ppermute | solution.py:447
  (114 other events, 2299.3 us)

commit v4 on v3

--- a/solution.py
+++ b/solution.py
@@ -21,7 +21,7 @@
 
 def group_size(depth):
     best = depth
-    for size in range(2, 11, 2):
+    for size in range(2, 21, 2):
         if depth % size == 0:
             best = size
     return best
@@ -193,8 +193,9 @@
         functools.partial(pass_kernel, given),
         out_shape=out,
         in_specs=[pl.BlockSpec(memory_space=pltpu.SMEM)] + [anywhere] * len(operands),
-        out_specs=[anywhere] * len(out),
+        out_specs=[pl.BlockSpec(memory_space=pltpu.VMEM)] * len(out),
         scratch_shapes=[pltpu.SemaphoreType.DMA((3,))],
+        compiler_params=pltpu.CompilerParams(vmem_limit_bytes=32 * 2 ** 20),
         cost_estimate=pl.CostEstimate(flops=0, bytes_accessed=4 * 2 ** 20, transcendentals=0),
         name="pass_on",
     )(spot, *operands)
@@ -209,7 +210,7 @@
     kinds = source.shape[1] // groups
     half = (group + 1) // 2
     mains = (plane - half) // group
-    windows = spread[0].shape[0]
+    windows = spread.shape[1]
     for part, (lo, hi) in enumerate(((0, half), (half, group))):
         if lo == hi:
             continue
@@ -235,21 +236,40 @@
             for kind in range(kinds):
                 for k in range(count):
                     for a in range(windows):
-                        spread[slot + kind][a, :, (lo + k) * LANES:(lo + k + 1) * LANES] = got[
+                        spread[slot + kind, a, :, (lo + k) * LANES:(lo + k + 1) * LANES] = got[
                             kind, :, k, :, a * LANES:(a + 1) * LANES
                         ].reshape(sides * rows, LANES)
 
 
-def flat(ref):
-    windows, rows, lanes = ref.shape
-    return ref[...].reshape(windows * rows, lanes)
+def set_tables(ref, table_ref, rest):
+    total, lanes = table_ref.shape
+    mains = total - rest
+    ref[...] = jnp.zeros_like(ref)
+    for part in range(2):
+        ref[part, 0:mains] = table_ref[0:mains]
+        ref[part, mains + part * rest:mains + (part + 1) * rest] = table_ref[mains:total]
+
+
+def set_low(ref, low_ref):
+    for k in range(low_ref.shape[0]):
+        ref[k * LANES:k * LANES + low_ref.shape[1]] = low_ref[k]
+
+
+def set_low_planes(ref, low_ref, depth, tiles):
+    rows = low_ref.shape[-2]
+    for k in range(depth):
+        for i in range(tiles[0]):
+            for j in range(tiles[1]):
+                ref[k * LANES + i * rows:k * LANES + (i + 1) * rows, j * LANES:(j + 1) * LANES] = low_ref[
+                    (k * tiles[0] + i) * tiles[1] + j
+                ]
 
 
 def even_kernel(sides, group, groups, use_ends, use_inner, starts, spot_ref, *refs):
     views = [ref.at[at:at + 2 * groups] for ref, at in zip(refs[:2 * sides], starts)]
     inner_blocks, end_blocks = views[:sides], views[sides:]
     left_ref, first_ref, last_ref = refs[2 * sides:2 * sides + 3]
-    total, even, spread_a, spread_b, sems = refs[-5:]
+    total, even, spread, tables, first, last, sems = refs[-7:]
     here = spot_ref[0]
     step = pl.program_id(0)
     inner = jnp.logical_and(here > 0, here < sides - 1)
@@ -259,8 +279,6 @@
     def _():
         @pl.when(step == 0)
         def _():
-            total[...] = jnp.zeros_like(total)
-
             @pl.when(inner)
             def _():
                 for at, turn in enumerate((0, 1, 3, 2)):
@@ -271,15 +289,20 @@
                 for at, turn in enumerate((0, 1, 2, 3)):
                     fetch(end_blocks[at], even.at[here ^ turn], sems.at[at])
 
+            total[...] = jnp.zeros_like(total)
+            first[...] = jnp.zeros_like(first)
+            last[...] = jnp.zeros_like(last)
+            set_tables(tables, left_ref, tables.shape[1] - left_ref.shape[0])
             for at in range(sides):
                 pltpu.make_async_copy(inner_blocks[at], even.at[at], sems.at[at]).wait()
 
-        expand(even, step, group, groups, (left_ref,), (spread_a, spread_b))
-        first = first_ref[...].reshape(group * LANES, first_ref.shape[-1])
-        last = last_ref[...].reshape(group * LANES, last_ref.shape[-1])
-        total[0] += jnp.dot(flat(spread_a), first, preferred_element_type=jnp.float32)
-        total[1] += jnp.dot(flat(spread_b), first, preferred_element_type=jnp.float32)
-        total[1] += jnp.dot(flat(spread_a), last, preferred_element_type=jnp.float32)
+        expand(even, step, group, groups, (tables,), spread)
+        set_low(first, first_ref)
+        set_low(last, last_ref)
+        count = spread.shape[1] * spread.shape[2]
+        both = spread[...].reshape(2 * count, group * LANES)
+        total[...] += jnp.dot(both, first[...], preferred_element_type=jnp.float32).reshape(total.shape)
+        total[1] += jnp.dot(both[:count], last[...], preferred_element_type=jnp.float32)
 
     @pl.when(jnp.logical_and(step == 0, jnp.logical_not(work)))
     def _():
@@ -292,7 +315,7 @@
     blocks = (inner_blocks or some) + (end_blocks or some)
     starts = [at for _, at in blocks]
     _, planes, rows, _ = some[0][0].shape
-    windows = table.shape[2] // LANES
+    windows = table.shape[1] // LANES
     full = first.shape[-1]
     count = windows * sides * rows
     whole = lambda arr: pl.BlockSpec(arr.shape, lambda g, s: (0,) * len(arr.shape))
@@ -312,23 +335,25 @@
             out_specs=whole(out),
             scratch_shapes=[
                 pltpu.VMEM((sides, 2 * groups, planes, rows, LANES), jnp.bfloat16),
-                pltpu.VMEM((windows, sides * rows, group * LANES), jnp.bfloat16),
-                pltpu.VMEM((windows, sides * rows, group * LANES), jnp.bfloat16),
+                pltpu.VMEM((2, windows, sides * rows, group * LANES), jnp.bfloat16),
+                pltpu.VMEM((2, -(-table.shape[0] // LANES) * LANES, table.shape[1]), jnp.bfloat16),
+                pltpu.VMEM((group * LANES, full), jnp.bfloat16),
+                pltpu.VMEM((group * LANES, full), jnp.bfloat16),
                 pltpu.SemaphoreType.DMA((sides,)),
             ],
         ),
-        compiler_params=pltpu.CompilerParams(vmem_limit_bytes=40 * 2 ** 20),
+        compiler_params=pltpu.CompilerParams(vmem_limit_bytes=56 * 2 ** 20),
         cost_estimate=pl.CostEstimate(flops=flops, bytes_accessed=20 * 2 ** 20, transcendentals=0),
         name="even_product",
     )(spot, *[ref for ref, _ in blocks], table, first, last, *deps)
 
 
-def odd_kernel(sides, group, groups, outs, starts, spot_ref, *refs):
+def odd_kernel(sides, group, groups, outs, tiles, starts, spot_ref, *refs):
     blocks = [ref.at[at:at + groups] for ref, at in zip(refs[:sides], starts)]
     inner_part, end_part = refs[sides:sides + 2]
     left_ref, next_left_ref, low_ref, next_low_ref = refs[sides + 2:sides + 6]
-    out_refs = refs[-5 - outs:-5]
-    odd, spread_a, spread_b, total, sems = refs[-5:]
+    out_refs = refs[-8 - outs:-8]
+    odd, spread, tables, next_tables, low, next_low, total, sems = refs[-8:]
     here, role = spot_ref[0], spot_ref[1]
     step, last = pl.program_id(0), pl.num_programs(0) - 1
     inner = jnp.logical_and(here > 0, here < sides - 1)
@@ -340,6 +365,10 @@
             fetch(inner_part, total, sems.at[sides])
             for at, turn in enumerate((0, 1, 3, 2)):
                 fetch(blocks[at], odd.at[here ^ turn], sems.at[at])
+            low[...] = jnp.zeros_like(low)
+            next_low[...] = jnp.zeros_like(next_low)
+            set_tables(tables, left_ref, tables.shape[1] - left_ref.shape[0])
+            set_tables(next_tables, next_left_ref, tables.shape[1] - left_ref.shape[0])
             for at in range(sides):
                 pltpu.make_async_copy(blocks[at], odd.at[at], sems.at[at]).wait()
 
@@ -351,11 +380,13 @@
 
     @pl.when(inner)
     def _():
-        expand(odd, step, group, groups, (left_ref, next_left_ref), (spread_a, spread_b))
-        low = low_ref[...].reshape(group * LANES, low_ref.shape[-1])
-        next_low = next_low_ref[...].reshape(group * LANES, low_ref.shape[-1])
-        total[1] += jnp.dot(flat(spread_a), low, preferred_element_type=jnp.float32)
-        total[1] += jnp.dot(flat(spread_b), next_low, preferred_element_type=jnp.float32)
+        expand(odd, step, group, groups, (tables, next_tables), spread)
+        set_low_planes(low, low_ref, group, tiles)
+        set_low_planes(next_low, next_low_ref, group, tiles)
+        count = spread.shape[1] * spread.shape[2]
+        rows = spread[...].reshape(2, count, group * LANES)
+        total[1] += jnp.dot(rows[0], low[...], preferred_element_type=jnp.float32)
+        total[1] += jnp.dot(rows[1], next_low[...], preferred_element_type=jnp.float32)
 
     @pl.when(step == last)
     def _():
@@ -367,21 +398,21 @@
             out_refs[offset][...] = value.reshape(out_refs[offset].shape).astype(jnp.bfloat16)
 
 
-def odd_product(spot, blocks, inner_part, end_part, deps, tables, lows, sides, group, groups, outs):
+def odd_product(spot, blocks, inner_part, end_part, deps, tables, lows, sides, group, groups, outs, tiles):
     starts = [at for _, at in blocks]
     _, planes, rows, _ = blocks[0][0].shape
     table, next_table = tables
     low, next_low = lows
-    windows = table.shape[2] // LANES
-    full = low.shape[-1]
+    windows = table.shape[1] // LANES
+    full = tiles[1] * LANES
     count = windows * sides * rows
     whole = lambda arr: pl.BlockSpec(arr.shape, lambda g, s: (0,) * len(arr.shape))
-    part = pl.BlockSpec((group,) + low.shape[1:], lambda g, s: (g, 0, 0))
+    part = pl.BlockSpec((group * tiles[0] * tiles[1],) + low.shape[1:], lambda g, s: (g, 0, 0))
     out = [jax.ShapeDtypeStruct((windows, sides * rows, full // 2), jnp.bfloat16)] * outs
     depth = groups * group
     flops = 2 * count * depth * LANES * 2 * full + 4 * sides * rows * depth * 3 * LANES * windows * LANES
     return pl.pallas_call(
-        functools.partial(odd_kernel, sides, group, groups, outs, starts),
+        functools.partial(odd_kernel, sides, group, groups, outs, tiles, starts),
         out_shape=out,
         grid_spec=pltpu.PrefetchScalarGridSpec(
             num_scalar_prefetch=1,
@@ -392,13 +423,16 @@
             out_specs=[whole(o) for o in out],
             scratch_shapes=[
                 pltpu.VMEM((sides, groups, planes, rows, LANES), jnp.bfloat16),
-                pltpu.VMEM((windows, sides * rows, group * LANES), jnp.bfloat16),
-                pltpu.VMEM((windows, sides * rows, group * LANES), jnp.bfloat16),
+                pltpu.VMEM((2, windows, sides * rows, group * LANES), jnp.bfloat16),
+                pltpu.VMEM((2, -(-table.shape[0] // LANES) * LANES, table.shape[1]), jnp.bfloat16),
+                pltpu.VMEM((2, -(-table.shape[0] // LANES) * LANES, table.shape[1]), jnp.bfloat16),
+                pltpu.VMEM((group * LANES, full), jnp.bfloat16),
+                pltpu.VMEM((group * LANES, full), jnp.bfloat16),
                 pltpu.VMEM((2, count, full), jnp.float32),
                 pltpu.SemaphoreType.DMA((sides + 1,)),
             ],
         ),
-        compiler_params=pltpu.CompilerParams(vmem_limit_bytes=40 * 2 ** 20),
+        compiler_params=pltpu.CompilerParams(vmem_limit_bytes=56 * 2 ** 20),
         cost_estimate=pl.CostEstimate(flops=flops, bytes_accessed=20 * 2 ** 20, transcendentals=0),
         name="odd_product",
     )(spot, *[ref for ref, _ in blocks], inner_part, end_part, table, next_table, low, next_low, *deps)
@@ -435,11 +469,10 @@
         return pieces
 
     def lower(kind, place):
-        low = lax.dynamic_slice_in_dim(bottoms[kind], place * depth, depth, 0)
+        low = lax.dynamic_slice(
+            bottoms, (kind, place * depth, 0, 0, 0), (1, depth, slab, downs, full)
+        )
         return low.reshape(depth, slab, downs * full)
-
-    def padded(low):
-        return jnp.pad(low, ((0, 0), (0, LANES - slab), (0, 0)))
 
     pairs = [(z, z ^ 1) for z in range(sides)]
     hand = [(z, z ^ 1) for z in (0, sides - 1)]
@@ -456,14 +489,8 @@
     plane = (mains * group + (group + 1) // 2, rows, LANES)
 
     def table(flat_left):
-        wide = jnp.pad(
-            flat_left.reshape(total, windows, slab), ((0, 0), (0, 0), (0, LANES - slab))
-        ).reshape(total, windows * LANES)
-        first = jnp.pad(wide, ((0, LANES - rest), (0, 0)))
-        blank = jnp.zeros((rest, windows * LANES), wide.dtype)
-        second = jnp.concatenate([wide[:mains * LANES], blank, wide[mains * LANES:]], axis=0)
-        second = jnp.pad(second, ((0, LANES - 2 * rest), (0, 0)))
-        return jnp.stack([first, second])
+        wide = flat_left.reshape(total, windows, slab)
+        return jnp.pad(wide, ((0, 0), (0, 0), (0, LANES - slab))).reshape(total, windows * LANES)
 
     flat_left = left_all.reshape(total, windows * slab)
     middle = lower(1, role) * jnp.asarray(2, bottoms.dtype)
@@ -471,7 +498,8 @@
     count = depth * tiles[0] * tiles[1]
     units = -(-count // plane[0])
     carried = middle.reshape(depth, tiles[0], rows, tiles[1], LANES).transpose(0, 1, 3, 2, 4)
-    carried = jnp.pad(carried.reshape(count, rows, LANES), ((0, units * plane[0] - count), (0, 0), (0, 0)))
+    carried = middle_planes = carried.reshape(count, rows, LANES)
+    carried = jnp.pad(carried, ((0, units * plane[0] - count), (0, 0), (0, 0)))
     carried = carried.reshape((units,) + plane)
     taken = 0
 
@@ -487,11 +515,11 @@
     lows = tables = next_low = None
     done = None
 
-    def reduce_roles(t):
-        summed = shares[t][0].astype(jnp.float32)
-        for s in range(1, roles):
-            got = lax.ppermute(shares[t][s], "role", [(j, j ^ s) for j in range(roles)])
-            summed = summed + got.astype(jnp.float32)
+    def reduce(t):
+        ones = [lax.ppermute(shares[t][s], "role", [(j, j ^ 1) for j in range(roles)]) for s in (1, 3)]
+        kept = [shares[t][s].astype(jnp.float32) + got.astype(jnp.float32) for s, got in zip((0, 2), ones)]
+        got = lax.ppermute(kept[1].astype(jnp.bfloat16), "role", [(j, j ^ 2) for j in range(roles)])
+        summed = kept[0] + got.astype(jnp.float32)
         summed = summed.reshape(windows, sides * contrs, unit, full)
         size = sides * contrs
         step = contrs // 2
@@ -504,7 +532,15 @@
             got = lax.ppermute(give, "contr", [(j, j ^ step) for j in range(contrs)])
             summed = keep + got.astype(jnp.float32)
             step //= 2
-        return summed
+        mine = lax.dynamic_slice_in_dim(summed, here, 1, 1)
+        for s in range(1, sides):
+            give = lax.dynamic_slice_in_dim(summed, here ^ s, 1, 1).astype(jnp.bfloat16)
+            got = lax.ppermute(give, "horiz", [(z, z ^ s) for z in range(sides)])
+            mine = mine + got.astype(jnp.float32)
+        mine = mine.reshape(windows, unit, full).astype(jnp.bfloat16)
+        return jnp.einsum(
+            "aur,urb->ab", mine, right_iso[t * unit:(t + 1) * unit], preferred_element_type=jnp.float32
+        )
 
     for r in range(chunks + 3):
         if r <= chunks:
@@ -534,19 +570,17 @@
                     pieces[t] = exchange(t, mark[1])
             if r == 0:
                 late = mark[1]
-                lows = (padded(lower(0, late)), padded(lower(2, late)), padded(middle))
+                lows = (lower(0, late), lower(2, late))
                 tables = (table(flat_left), table(move(flat_left, hand)))
         t = r - 4
         if 0 <= t < chunks:
             if next_low is None:
                 arrived = [got[first:first + size] for _, got, first, size in sorted(parts, key=lambda p: p[0])]
-                arrived = jnp.concatenate(arrived, axis=0).reshape(-1, rows, LANES)[:count]
-                arrived = arrived.reshape(depth, tiles[0], tiles[1], rows, LANES).transpose(0, 1, 3, 2, 4)
-                next_low = padded(arrived.reshape(depth, slab, downs * full))
+                next_low = jnp.concatenate(arrived, axis=0).reshape(-1, rows, LANES)
             blocks = [(own[t], 2 * groups), (sent[t], 2 * groups), (straight[t], 2 * groups), (turned[t + 1], 2 * groups)]
             shares[t] = odd_product(
-                spot, blocks, sums[t + 2], sums[t + 3], [done], tables, (lows[2], next_low),
-                sides, group, groups, roles,
+                spot, blocks, sums[t + 2], sums[t + 3], [done], tables, (middle_planes, next_low),
+                sides, group, groups, roles, tiles,
             )
             done = shares[t][0]
         if 1 <= r <= chunks + 1:
@@ -554,7 +588,7 @@
             given = dict(sides=sides, groups=groups, cross=r <= chunks, low=at, count=size)
             deps = [done] + ([last[r - 1]] if r - 1 in last else [])
             if r - 5 in shares:
-                reduced[r - 5] = reduce_roles(r - 5)
+                reduced[r - 5] = reduce(r - 5)
                 deps.append(reduced[r - 5])
             outs = pass_on(spot, sent[r - 1], turned.get(r - 1), carried, deps, given, plane)
             if r <= chunks:
@@ -581,20 +615,13 @@
     t = chunks - 1
     blocks = [(own[t], 2 * groups), (sent[t], 2 * groups), (straight[t], 2 * groups), (turned[t + 1], 2 * groups)]
     shares[t] = odd_product(
-        spot, blocks, sums[t + 2], sums[t + 3], [done], tables, (lows[2], next_low), sides, group, groups, roles
+        spot, blocks, sums[t + 2], sums[t + 3], [done], tables, (middle_planes, next_low), sides, group, groups, roles,
+        tiles,
     )
 
+    projected = 0.0
     for t in range(chunks):
-        if t not in reduced:
-            reduced[t] = reduce_roles(t)
-    summed = jnp.concatenate([reduced[t] for t in range(chunks)], axis=2)
-    mine = lax.dynamic_slice_in_dim(summed, here, 1, 1)
-    for s in range(1, sides):
-        give = lax.dynamic_slice_in_dim(summed, here ^ s, 1, 1).astype(jnp.bfloat16)
-        got = lax.ppermute(give, "horiz", [(z, z ^ s) for z in range(sides)])
-        mine = mine + got.astype(jnp.float32)
-    mine = mine.reshape(windows, share, full).astype(jnp.bfloat16)
-    projected = jnp.einsum("aur,urb->ab", mine, right_iso, preferred_element_type=jnp.float32)
+        projected = projected + (reduced[t] if t in reduced else reduce(t))
     projected = projected * jnp.where(role >= downs, 0.25, 1.0)
     for axis, size in (("contr", contrs), ("horiz", sides)):
         s = 1

time: 1030 us -> 727 us (0.71)
  Pallas kernels: 444 us -> 233 us
  local copies, waits for them, and re-layouts: 215 us -> 101 us
  waiting for transfers between devices: 107 us -> 160 us
  starting transfers between devices: 220 us -> 185 us
    pallas_call x6, Pallas kernels: 233 us -> 9.7 us  [pass_on(): pl.pallas_call(functools.partial(pass_kernel, given), out_shape=out, in_s...]
    ppermute x22, starting transfers between devices: 189 us -> 101 us  [on_device(): move = lambda value, perm: lax.ppermute(value, 'horiz', perm)]
    slice x9 -> x0, local copies, waits for them, and re-layouts: 56.8 us -> none  [the longest x1 44 us: lower(): low = lax.dynamic_slice_in_dim(bottoms[kind], place * depth, depth, 0)]
    ppermute x22, waiting for transfers between devices: 19.2 us -> 75.6 us  [on_device(): move = lambda value, perm: lax.ppermute(value, 'horiz', perm)]
    ppermute x23 -> x35, starting transfers between devices: 17.9 us -> 68.2 us  [the longest x15 54 us: reduce(): got = lax.ppermute(give, 'horiz', [(z, z ^ s) for z in range(sides)])]
    pad x6 -> x2, local copies, waits for them, and re-layouts: 27.7 us -> 3.07 us  [table(): jnp.pad(wide, ((0, 0), (0, 0), (0, LANES - slab)))]
    pallas_call x6, Pallas kernels: 142 us -> 160 us  [even_product(): pl.pallas_call(functools.partial(even_kernel, sides, group, groups, use_e...]
    reshape x3 -> x2, local copies, waits for them, and re-layouts: 14.5 us -> 3.36 us  [table(): jnp.pad(wide, ((0, 0), (0, 0), (0, LANES - slab)))]
  transfers between devices with their start and end apart: 66 -> 78, of which waited for: 17 -> 25; matrix products, arithmetic and copies ran while one was open for 20% -> 14% of each run, Pallas kernels for 42% -> 30%
where the time goes in v4:
time: 727 us; the launch traced here: 716 us
  Pallas kernels  233 us (32%)
  starting transfers between devices  185 us (25%)
  waiting for transfers between devices  160 us (22%)
  local copies, waits for them, and re-layouts  101 us (14%)
  other arithmetic  18.1 us (2%)
  matrix products  9.91 us (1%)
  between operations  9.59 us (1%)
    pallas_call x6, Pallas kernels, even_product(): pl.pallas_call(functools.partial(even_kernel, sides, group, groups, use_e...  160 us
    ppermute x22, starting transfers between devices, on_device(): move = lambda value, perm: lax.ppermute(value, 'horiz', perm)  101 us
    ppermute x22, waiting for transfers between devices, on_device(): move = lambda value, perm: lax.ppermute(value, 'horiz', perm)  75.6 us
    ppermute x15, starting transfers between devices, reduce(): got = lax.ppermute(give, 'horiz', [(z, z ^ s) for z in range(sides)])  54 us
    pallas_call x5, Pallas kernels, odd_product(): pl.pallas_call(functools.partial(odd_kernel, sides, group, groups, outs,...  39.8 us
    unnamed x140, local copies, waits for them, and re-layouts  30.7 us
    ppermute x5, waiting for transfers between devices, reduce(): lax.ppermute(kept[1].astype(jnp.bfloat16), 'role', [(j, j ^ 2) for j in r...  24.1 us
    pallas_call x6, Pallas kernels, pack(): pl.pallas_call(functools.partial(pack_kernel, group, len(pieces), given),...  23.8 us
  transfers between devices with their start and end apart: 78, of which 25 were waited for; matrix products, arithmetic and copies ran while one was open for 14% of the time, Pallas kernels for 30%

profile of v4, /device:TPU:0, one launch (start us, length us, event | category | flops | bytes accessed | tf_op | source)
XLA Modules:
  0.0 716.4 jit_solution(18138383526989058407)
XLA Ops:
  5.0 8.6 %dynamic-slice_multiply_fusion = bf16[1,40,80,2,320]{4,3,2,1,0:T(2,128)(2,1)} fusion(bf16[3,160,80,2,320]{4,3,2,1,0:T(2,128)(2,1)} %param.5, s32[]{:T(128)S(6)} %select_n.147), kind=kLoop, calls=%fused_computation | loop fusion | flops 2048000 | bytes 8192004 | tf_op jit(solution)/shard_map/mul | solution.py:496
  13.7 13.9 %mul.139 = bf16[40,5,16,5,128]{4,3,2,1,0:T(8,128)(2,1)} reshape(bf16[1,40,80,2,320]{4,3,2,1,0:T(2,128)(2,1)} %dynamic-slice_multiply_fusion) | data formatting | bytes 8192000 | tf_op jit(solution)/shard_map/mul | solution.py:496
  48.9 11.5 %collective-permute-done.7.refs_3_ = bf16[3,40,16,80]{3,2,1,0:T(8,128)(2,1)S(1)} collective-permute-done((bf16[3,40,16,80]{3,2,1,0:T(8,128)(2,1)S(1)}, bf16[3,40,16,80]{3,2,1,0:T(8,128)(2,1)S(1)}, u32[]{:S(2)}, u32[]{:S(2)}) %collective-permute-start.7) | collective-permute-done | bytes 307232 | tf_op jit(solution)/shard_map/ppermute | solution.py:467
  60.5 10.6 %collective-permute-done.6.refs_2_ = bf16[3,40,16,80]{3,2,1,0:T(8,128)(2,1)S(1)} collective-permute-done((bf16[3,40,16,80]{3,2,1,0:T(8,128)(2,1)S(1)}, bf16[3,40,16,80]{3,2,1,0:T(8,128)(2,1)S(1)}, u32[]{:S(2)}, u32[]{:S(2)}) %collective-permute-start.6) | collective-permute-done | bytes 307232 | tf_op jit(solution)/shard_map/ppermute | solution.py:467
  71.1 12.0 %collective-permute-done.3.refs_6_.refs_0_.refs_1_.refs_5_ = bf16[10,50,16,128]{3,2,1,0:T(8,128)(2,1)S(1)} collective-permute-done((bf16[10,50,16,128]{3,2,1,0:T(8,128)(2,1)}, bf16[10,50,16,128]{3,2,1,0:T(8,128)(2,1)S(1)}, u32[]{:S(2)}, u32[]{:S(2)}) %collective-permute-start.3) | collective-permute-done | bytes 2048032 | tf_op jit(solution)/shard_map/ppermute | solution.py:480
  117.3 26.0 %collective-permute-done.9.refs_6_.refs_0_.refs_1_.refs_5_ = bf16[12,50,16,128]{3,2,1,0:T(8,128)(2,1)S(1)} collective-permute-done((bf16[12,50,16,128]{3,2,1,0:T(8,128)(2,1)}, bf16[12,50,16,128]{3,2,1,0:T(8,128)(2,1)S(1)}, u32[]{:S(2)}, u32[]{:S(2)}) %collective-permute-start.9) | collective-permute-done | bytes 2457632 | tf_op jit(solution)/shard_map/ppermute | solution.py:480
  158.8 9.6 %constant_dynamic-slice_fusion.14 = (bf16[1,40,80,2,320]{4,3,2,1,0:T(2,128)(2,1)}, bf16[1,40,80,2,320]{4,3,2,1,0:T(2,128)(2,1)}) fusion(bf16[3,160,80,2,320]{4,3,2,1,0:T(2,128)(2,1)} %param.5, s32[]{:T(128)S(6)} %select_n.151), kind=kLoop, calls=%fused_computation.112 | loop fusion | bytes 16384004 | tf_op jit(solution)/shard_map/dynamic_slice | solution.py:472
  168.5 10.5 %reshape.178.refs_10_ = bf16[40,80,640]{2,1,0:T(8,128)(2,1)} reshape(bf16[1,40,80,2,320]{4,3,2,1,0:T(2,128)(2,1)} %get-tuple-element.89) | data formatting | bytes 8192000 | tf_op jit(solution)/shard_map/reshape | solution.py:475
  179.0 10.5 %reshape.177.refs_9_ = bf16[40,80,640]{2,1,0:T(8,128)(2,1)} reshape(bf16[1,40,80,2,320]{4,3,2,1,0:T(2,128)(2,1)} %get-tuple-element.90) | data formatting | bytes 8192000 | tf_op jit(solution)/shard_map/reshape | solution.py:475
  217.6 13.3 %collective-permute-done.16.refs_6_.refs_0_.refs_1_.refs_5_ = bf16[8,50,16,128]{3,2,1,0:T(8,128)(2,1)} collective-permute-done((bf16[8,50,16,128]{3,2,1,0:T(8,128)(2,1)}, bf16[8,50,16,128]{3,2,1,0:T(8,128)(2,1)}, u32[]{:S(2)}, u32[]{:S(2)}) %collective-permute-start.16) | collective-permute-done | bytes 1638432 | tf_op jit(solution)/shard_map/ppermute | solution.py:480
  239.5 8.6 %collective-permute-done.15.refs_4_.refs_7_ = bf16[4,50,16,128]{3,2,1,0:T(8,128)(2,1)S(1)} collective-permute-done((bf16[4,50,16,128]{3,2,1,0:T(8,128)(2,1)}, bf16[4,50,16,128]{3,2,1,0:T(8,128)(2,1)S(1)}, u32[]{:S(2)}, u32[]{:S(2)}) %collective-permute-start.15) | collective-permute-done | bytes 819232 | tf_op jit(solution)/shard_map/ppermute | solution.py:480
  258.0 30.5 %even_product.7.refs_7_.refs_5_.refs_4_ = f32[2,512,640]{2,1,0:T(8,128)} custom-call(s32[2]{0:T(128)} %copy-done.35, bf16[6,50,16,128]{3,2,1,0:T(8,128)(2,1)} %get-tuple-element.51.refs_0_.refs_4_, bf16[12,50,16,128]{3,2,1,0:T(8,128)(2,1)} %copy-done.9, bf16[6,50,16,128]{3,2,1,0:T(8,128)(2,1)} %collective-permute-done.13.refs_4_.refs_2_, ...), custom_call_target="tpu_custom_call" | custom-call | flops 14092861440 | bytes 20971520 | tf_op jit(solution)/shard_map/even_product/pallas_call | solution.py:326
  292.4 13.8 %collective-permute-done.23.refs_4_.refs_7_ = bf16[4,50,16,128]{3,2,1,0:T(8,128)(2,1)S(1)} collective-permute-done((bf16[4,50,16,128]{3,2,1,0:T(8,128)(2,1)}, bf16[4,50,16,128]{3,2,1,0:T(8,128)(2,1)S(1)}, u32[]{:S(2)}, u32[]{:S(2)}) %collective-permute-start.23) | collective-permute-done | bytes 819232 | tf_op jit(solution)/shard_map/ppermute | solution.py:480
  324.6 10.2 %collective-permute-done.30 = bf16[8,64,320]{2,1,0:T(8,128)(2,1)S(1)} collective-permute-done((bf16[8,64,320]{2,1,0:T(8,128)(2,1)S(1)}, bf16[8,64,320]{2,1,0:T(8,128)(2,1)S(1)}, u32[]{:S(2)}, u32[]{:S(2)}) %collective-permute-start.30) | collective-permute-done | bytes 327712 | tf_op jit(solution)/shard_map/ppermute | solution.py:521
  338.4 20.1 %collective-permute-start.37 = (bf16[8,50,16,128]{3,2,1,0:T(8,128)(2,1)}, bf16[8,50,16,128]{3,2,1,0:T(8,128)(2,1)S(1)}, u32[]{:S(2)}, u32[]{:S(2)}) collective-permute-start(bf16[8,50,16,128]{3,2,1,0:T(8,128)(2,1)} %copy-done.42), channel_id=1, source_target_pairs={{0,1},{1,0},{2,3},{3,2},{4,5},{5,4},{6,7},{7,6},{8,9},{9,8},{10,11... | collective-permute-start | bytes 4915208 | tf_op jit(solution)/shard_map/ppermute | solution.py:480
  365.6 13.2 %collective-permute-start.32 = (bf16[8,1,8,320]{3,0,2,1:T(8,128)(2,1)S(1)}, bf16[8,1,8,320]{3,0,2,1:T(8,128)(2,1)S(1)}, u32[]{:S(2)}, u32[]{:S(2)}) collective-permute-start(bf16[8,1,8,320]{3,0,2,1:T(8,128)(2,1)S(1)} %get-tuple-element.127), channel_id=1, source_target_pairs={{0,1},{1,0},{2,3},{3,2},{4,5},{5,4},{6,7},{7,6},{8,9},{9,8},{10,11... | collective-permute-start | bytes 122888 | tf_op jit(solution)/shard_map/ppermute | solution.py:538
  380.4 30.9 %even_product.8.refs_3_.refs_5_.refs_4_ = f32[2,512,640]{2,1,0:T(8,128)} custom-call(s32[2]{0:T(128)} %copy-done.35, bf16[6,50,16,128]{3,2,1,0:T(8,128)(2,1)} %copy-done.44, bf16[8,50,16,128]{3,2,1,0:T(8,128)(2,1)} %collective-permute-done.16.refs_6_.refs_0_.refs_1_.refs_5_, bf16[6,50,16,128]{3,2,1,0:T(8,128)(2,1)} %collective-permute-done.20.refs_4_.refs_2_, ...), custom_call_target="tpu_custom_call" | custom-call | flops 14092861440 | bytes 20971520 | tf_op jit(solution)/shard_map/even_product/pallas_call | solution.py:326
  422.9 8.3 %odd_product.6 = (bf16[8,64,320]{2,1,0:T(8,128)(2,1)}, bf16[8,64,320]{2,1,0:T(8,128)(2,1)}, bf16[8,64,320]{2,1,0:T(8,128)(2,1)}, bf16[8,64,320]{2,1,0:T(8,128)(2,1)}) custom-call(s32[2]{0:T(128)} %copy-done.35, bf16[6,50,16,128]{3,2,1,0:T(8,128)(2,1)} %get-tuple-element.51.refs_0_.refs_4_, bf16[12,50,16,128]{3,2,1,0:T(8,128)(2,1)} %copy-done.9, ...), custom_call_target="tpu_custom_call" | custom-call | flops 10737418240 | bytes 20971520 | tf_op jit(solution)/shard_map/odd_product/pallas_call | solution.py:414
  437.1 30.6 %even_product.9.refs_5_.refs_10_.refs_4_ = f32[2,512,640]{2,1,0:T(8,128)} custom-call(s32[2]{0:T(128)} %copy-done.35, bf16[6,50,16,128]{3,2,1,0:T(8,128)(2,1)} %get-tuple-element.61.refs_0_.refs_4_, bf16[8,50,16,128]{3,2,1,0:T(8,128)(2,1)} %copy-done.12, bf16[6,50,16,128]{3,2,1,0:T(8,128)(2,1)} %collective-permute-done.27.refs_4_.refs_2_, ...), custom_call_target="tpu_custom_call" | custom-call | flops 14092861440 | bytes 20971520 | tf_op jit(solution)/shard_map/even_product/pallas_call | solution.py:326
  478.6 35.1 %collective-permute-start.56 = (bf16[4,50,16,128]{3,2,1,0:T(8,128)(2,1)S(1)}, bf16[4,50,16,128]{3,2,1,0:T(8,128)(2,1)S(1)}, u32[]{:S(2)}, u32[]{:S(2)}) collective-permute-start(bf16[4,50,16,128]{3,2,1,0:T(8,128)(2,1)S(1)} %copy-done.49), channel_id=1, source_target_pairs={{0,1},{1,0},{2,3},{3,2},{4,5},{5,4},{6,7},{7,6},{8,9},{9,8},{10,11... | collective-permute-start | bytes 2457608 | tf_op jit(solution)/shard_map/ppermute | solution.py:480
  539.8 11.1 %collective-permute-done.42 = bf16[8,1,8,320]{3,0,2,1:T(8,128)(2,1)S(1)} collective-permute-done((bf16[8,1,8,320]{3,0,2,1:T(8,128)(2,1)S(1)}, bf16[8,1,8,320]{3,0,2,1:T(8,128)(2,1)S(1)}, u32[]{:S(2)}, u32[]{:S(2)}) %collective-permute-start.42) | collective-permute-done | bytes 40992 | tf_op jit(solution)/shard_map/ppermute | solution.py:538
  561.7 30.9 %even_product.10.refs_5_.refs_10_.refs_4_ = f32[2,512,640]{2,1,0:T(8,128)} custom-call(s32[2]{0:T(128)} %copy-done.35, bf16[6,50,16,128]{3,2,1,0:T(8,128)(2,1)} %copy-done.43, bf16[8,50,16,128]{3,2,1,0:T(8,128)(2,1)} %copy-done.13, bf16[6,50,16,128]{3,2,1,0:T(8,128)(2,1)} %copy-done.29, bf16[6,50,16,128]{3,2,1,0:T(8,128)(2,1)} %copy-done.30, ...), custom_call_target="tpu_custom_call" | custom-call | flops 14092861440 | bytes 20971520 | tf_op jit(solution)/shard_map/even_product/pallas_call | solution.py:326
  600.5 18.7 %collective-permute-start.51 = (bf16[8,1,8,320]{3,0,2,1:T(8,128)(2,1)S(1)}, bf16[8,1,8,320]{3,0,2,1:T(8,128)(2,1)S(1)}, u32[]{:S(2)}, u32[]{:S(2)}) collective-permute-start(bf16[8,1,8,320]{3,0,2,1:T(8,128)(2,1)S(1)} %get-tuple-element.124), channel_id=1, source_target_pairs={{0,1},{1,0},{2,3},{3,2},{4,5},{5,4},{6,7},{7,6},{8,9},{9,8},{10,11... | collective-permute-start | bytes 122888 | tf_op jit(solution)/shard_map/ppermute | solution.py:538
  630.4 30.6 %even_product.11.refs_5_.refs_10_ = f32[2,512,640]{2,1,0:T(8,128)} custom-call(s32[2]{0:T(128)} %copy-done.35, bf16[6,50,16,128]{3,2,1,0:T(8,128)(2,1)} %copy-done.43, bf16[8,50,16,128]{3,2,1,0:T(8,128)(2,1)} %copy-done.13, bf16[4,50,16,128]{3,2,1,0:T(8,128)(2,1)} %copy-done.31, bf16[4,50,16,128]{3,2,1,0:T(8,128)(2,1)} %collective-permute-done.64.refs_3_.refs_7_, ...), custom_call_target="tpu_custom_call" | custom-call | flops 14092861440 | bytes 20971520 | tf_op jit(solution)/shard_map/even_product/pallas_call | solution.py:326
  (356 shorter events, 287.6 us)
Async XLA Ops:
  35.9 47.2 %collective-permute-start.3 = (bf16[10,50,16,128]{3,2,1,0:T(8,128)(2,1)}, bf16[10,50,16,128]{3,2,1,0:T(8,128)(2,1)S(1)}, u32[]{:S(2)}, u32[]{:S(2)}) collective-permute-start(bf16[10,50,16,128]{3,2,1,0:T(8,128)(2,1)} %get-tuple-element.48), channel_id=1, source_target_pairs={{0,1},{1,0},{2,3},{3,2},{4,5},{5,4},{6,7},{7,6},{8,9},{9,8},{10,11... | collective-permute-start | bytes 6144008 | tf_op jit(solution)/shard_map/ppermute | solution.py:480
  88.0 55.3 %collective-permute-start.9 = (bf16[12,50,16,128]{3,2,1,0:T(8,128)(2,1)}, bf16[12,50,16,128]{3,2,1,0:T(8,128)(2,1)S(1)}, u32[]{:S(2)}, u32[]{:S(2)}) collective-permute-start(bf16[12,50,16,128]{3,2,1,0:T(8,128)(2,1)} %get-tuple-element.50.refs_3_), channel_id=1, source_target_pairs={{0,1},{1,0},{2,3},{3,2},{4,5},{5,4},{6,7},{7,6},{8,9},{9,8},{10,11... | collective-permute-start | bytes 7372808 | tf_op jit(solution)/shard_map/ppermute | solution.py:480
  109.1 80.4 %collective-permute-start.21 = (bf16[320,640]{0,1:T(8,128)(2,1)}, bf16[320,640]{0,1:T(8,128)(2,1)}, u32[]{:S(2)}, u32[]{:S(2)}) collective-permute-start(bf16[320,640]{0,1:T(8,128)(2,1)} %bitcast.30), channel_id=1, source_target_pairs={{0,1},{3,2},{4,5},{7,6},{8,9},{11,10},{12,13},{15,14},{16,17},{19,... | collective-permute-start | bytes 1228808 | tf_op jit(solution)/shard_map/ppermute | solution.py:480
  115.6 82.2 %collective-permute-start.8 = (bf16[6,50,16,128]{3,2,1,0:T(8,128)(2,1)}, bf16[6,50,16,128]{3,2,1,0:T(8,128)(2,1)}, u32[]{:S(2)}, u32[]{:S(2)}) collective-permute-start(bf16[6,50,16,128]{3,2,1,0:T(8,128)(2,1)} %pass_on.6), channel_id=1, source_target_pairs={{1,2},{2,1},{5,6},{6,5},{9,10},{10,9},{13,14},{14,13},{17,18},{18,... | collective-permute-start | bytes 3686408 | tf_op jit(solution)/shard_map/ppermute | solution.py:480
  157.4 48.3 %collective-permute-start.19 = (bf16[3,40,16,80]{3,2,1,0:T(8,128)(2,1)}, bf16[3,40,16,80]{3,2,1,0:T(8,128)(2,1)}, u32[]{:S(2)}, u32[]{:S(2)}) collective-permute-start(bf16[3,40,16,80]{3,2,1,0:T(8,128)(2,1)} %get-tuple-element.95), channel_id=1, source_target_pairs={{0,24},{8,16},{16,8},{24,0},{1,25},{9,17},{17,9},{25,1},{2,26},{10... | collective-permute-start | bytes 921608 | tf_op jit(solution)/shard_map/ppermute | solution.py:467
  157.4 50.4 %collective-permute-start.18 = (bf16[3,40,16,80]{3,2,1,0:T(8,128)(2,1)}, bf16[3,40,16,80]{3,2,1,0:T(8,128)(2,1)}, u32[]{:S(2)}, u32[]{:S(2)}) collective-permute-start(bf16[3,40,16,80]{3,2,1,0:T(8,128)(2,1)} %get-tuple-element.96), channel_id=1, source_target_pairs={{0,16},{8,24},{16,0},{24,8},{1,17},{9,25},{17,1},{25,9},{2,18},{10... | collective-permute-start | bytes 921608 | tf_op jit(solution)/shard_map/ppermute | solution.py:467
  202.2 45.9 %collective-permute-start.15 = (bf16[4,50,16,128]{3,2,1,0:T(8,128)(2,1)}, bf16[4,50,16,128]{3,2,1,0:T(8,128)(2,1)S(1)}, u32[]{:S(2)}, u32[]{:S(2)}) collective-permute-start(bf16[4,50,16,128]{3,2,1,0:T(8,128)(2,1)} %get-tuple-element.54), channel_id=1, source_target_pairs={{0,1},{1,0},{2,3},{3,2},{4,5},{5,4},{6,7},{7,6},{8,9},{9,8},{10,11... | collective-permute-start | bytes 2457608 | tf_op jit(solution)/shard_map/ppermute | solution.py:480
  205.6 47.4 %collective-permute-start.14 = (bf16[6,50,16,128]{3,2,1,0:T(8,128)(2,1)}, bf16[6,50,16,128]{3,2,1,0:T(8,128)(2,1)}, u32[]{:S(2)}, u32[]{:S(2)}) collective-permute-start(bf16[6,50,16,128]{3,2,1,0:T(8,128)(2,1)} %get-tuple-element.53.refs_11_), channel_id=1, source_target_pairs={{1,2},{2,1},{5,6},{6,5},{9,10},{10,9},{13,14},{14,13},{17,18},{18,... | collective-permute-start | bytes 3686408 | tf_op jit(solution)/shard_map/ppermute | solution.py:480
  215.5 91.6 %collective-permute-start.26 = (bf16[3,40,16,80]{3,2,1,0:T(8,128)(2,1)}, bf16[3,40,16,80]{3,2,1,0:T(8,128)(2,1)}, u32[]{:S(2)}, u32[]{:S(2)}) collective-permute-start(bf16[3,40,16,80]{3,2,1,0:T(8,128)(2,1)} %get-tuple-element.91), channel_id=1, source_target_pairs={{0,24},{8,16},{16,8},{24,0},{1,25},{9,17},{17,9},{25,1},{2,26},{10... | collective-permute-start | bytes 921608 | tf_op jit(solution)/shard_map/ppermute | solution.py:467
  216.3 90.8 %collective-permute-start.25 = (bf16[3,40,16,80]{3,2,1,0:T(8,128)(2,1)}, bf16[3,40,16,80]{3,2,1,0:T(8,128)(2,1)}, u32[]{:S(2)}, u32[]{:S(2)}) collective-permute-start(bf16[3,40,16,80]{3,2,1,0:T(8,128)(2,1)} %get-tuple-element.92), channel_id=1, source_target_pairs={{0,16},{8,24},{16,0},{24,8},{1,17},{9,25},{17,1},{25,9},{2,18},{10... | collective-permute-start | bytes 921608 | tf_op jit(solution)/shard_map/ppermute | solution.py:467
  237.7 69.4 %collective-permute-start.27 = (bf16[6,50,16,128]{3,2,1,0:T(8,128)(2,1)}, bf16[6,50,16,128]{3,2,1,0:T(8,128)(2,1)}, u32[]{:S(2)}, u32[]{:S(2)}) collective-permute-start(bf16[6,50,16,128]{3,2,1,0:T(8,128)(2,1)} %get-tuple-element.61.refs_0_.refs_4_), channel_id=1, source_target_pairs={{1,2},{2,1},{5,6},{6,5},{9,10},{10,9},{13,14},{14,13},{17,18},{18,... | collective-permute-start | bytes 3686408 | tf_op jit(solution)/shard_map/ppermute | solution.py:480
  248.1 43.5 %collective-permute-start.22 = (bf16[8,50,16,128]{3,2,1,0:T(8,128)(2,1)}, bf16[8,50,16,128]{3,2,1,0:T(8,128)(2,1)S(1)}, u32[]{:S(2)}, u32[]{:S(2)}) collective-permute-start(bf16[8,50,16,128]{3,2,1,0:T(8,128)(2,1)} %get-tuple-element.57.refs_3_), channel_id=1, source_target_pairs={{0,1},{1,0},{2,3},{3,2},{4,5},{5,4},{6,7},{7,6},{8,9},{9,8},{10,11... | collective-permute-start | bytes 4915208 | tf_op jit(solution)/shard_map/ppermute | solution.py:480
  256.2 50.0 %collective-permute-start.23 = (bf16[4,50,16,128]{3,2,1,0:T(8,128)(2,1)}, bf16[4,50,16,128]{3,2,1,0:T(8,128)(2,1)S(1)}, u32[]{:S(2)}, u32[]{:S(2)}) collective-permute-start(bf16[4,50,16,128]{3,2,1,0:T(8,128)(2,1)} %get-tuple-element.59), channel_id=1, source_target_pairs={{0,1},{1,0},{2,3},{3,2},{4,5},{5,4},{6,7},{7,6},{8,9},{9,8},{10,11... | collective-permute-start | bytes 2457608 | tf_op jit(solution)/shard_map/ppermute | solution.py:480
  338.4 80.1 %collective-permute-start.37 = (bf16[8,50,16,128]{3,2,1,0:T(8,128)(2,1)}, bf16[8,50,16,128]{3,2,1,0:T(8,128)(2,1)S(1)}, u32[]{:S(2)}, u32[]{:S(2)}) collective-permute-start(bf16[8,50,16,128]{3,2,1,0:T(8,128)(2,1)} %copy-done.42), channel_id=1, source_target_pairs={{0,1},{1,0},{2,3},{3,2},{4,5},{5,4},{6,7},{7,6},{8,9},{9,8},{10,11... | collective-permute-start | bytes 4915208 | tf_op jit(solution)/shard_map/ppermute | solution.py:480
  358.5 60.0 %collective-permute-start.36 = (bf16[6,50,16,128]{3,2,1,0:T(8,128)(2,1)}, bf16[6,50,16,128]{3,2,1,0:T(8,128)(2,1)S(1)}, u32[]{:S(2)}, u32[]{:S(2)}) collective-permute-start(bf16[6,50,16,128]{3,2,1,0:T(8,128)(2,1)} %copy-done.43), channel_id=1, source_target_pairs={{1,2},{2,1},{5,6},{6,5},{9,10},{10,9},{13,14},{14,13},{17,18},{18,... | collective-permute-start | bytes 3686408 | tf_op jit(solution)/shard_map/ppermute | solution.py:480
  365.6 45.7 %collective-permute-start.32 = (bf16[8,1,8,320]{3,0,2,1:T(8,128)(2,1)S(1)}, bf16[8,1,8,320]{3,0,2,1:T(8,128)(2,1)S(1)}, u32[]{:S(2)}, u32[]{:S(2)}) collective-permute-start(bf16[8,1,8,320]{3,0,2,1:T(8,128)(2,1)S(1)} %get-tuple-element.127), channel_id=1, source_target_pairs={{0,1},{1,0},{2,3},{3,2},{4,5},{5,4},{6,7},{7,6},{8,9},{9,8},{10,11... | collective-permute-start | bytes 122888 | tf_op jit(solution)/shard_map/ppermute | solution.py:538
  431.2 45.2 %collective-permute-start.39 = (bf16[8,64,320]{2,1,0:T(8,128)(2,1)}, bf16[8,64,320]{2,1,0:T(8,128)(2,1)}, u32[]{:S(2)}, u32[]{:S(2)}) collective-permute-start(bf16[8,64,320]{2,1,0:T(8,128)(2,1)} %get-tuple-element.73), channel_id=1, source_target_pairs={{0,8},{8,0},{16,24},{24,16},{1,9},{9,1},{17,25},{25,17},{2,10},{10... | collective-permute-start | bytes 983048 | tf_op jit(solution)/shard_map/ppermute | solution.py:519
  475.9 42.6 %collective-permute-start.38 = (bf16[8,64,320]{2,1,0:T(8,128)(2,1)S(1)}, bf16[8,64,320]{2,1,0:T(8,128)(2,1)S(1)}, u32[]{:S(2)}, u32[]{:S(2)}) collective-permute-start(bf16[8,64,320]{2,1,0:T(8,128)(2,1)S(1)} %copy-done.63), channel_id=1, source_target_pairs={{0,8},{8,0},{16,24},{24,16},{1,9},{9,1},{17,25},{25,17},{2,10},{10... | collective-permute-start | bytes 983048 | tf_op jit(solution)/shard_map/ppermute | solution.py:519
  477.5 41.1 %collective-permute-start.40 = (bf16[8,64,320]{2,1,0:T(8,128)(2,1)S(1)}, bf16[8,64,320]{2,1,0:T(8,128)(2,1)S(1)}, u32[]{:S(2)}, u32[]{:S(2)}) collective-permute-start(bf16[8,64,320]{2,1,0:T(8,128)(2,1)S(1)} %add_convert_fusion.3), channel_id=1, source_target_pairs={{0,16},{8,24},{16,0},{24,8},{1,17},{9,25},{17,1},{25,9},{2,18},{10... | collective-permute-start | bytes 983048 | tf_op jit(solution)/shard_map/ppermute | solution.py:521
  478.6 79.8 %collective-permute-start.56 = (bf16[4,50,16,128]{3,2,1,0:T(8,128)(2,1)S(1)}, bf16[4,50,16,128]{3,2,1,0:T(8,128)(2,1)S(1)}, u32[]{:S(2)}, u32[]{:S(2)}) collective-permute-start(bf16[4,50,16,128]{3,2,1,0:T(8,128)(2,1)S(1)} %copy-done.49), channel_id=1, source_target_pairs={{0,1},{1,0},{2,3},{3,2},{4,5},{5,4},{6,7},{7,6},{8,9},{9,8},{10,11... | collective-permute-start | bytes 2457608 | tf_op jit(solution)/shard_map/ppermute | solution.py:480
  513.7 44.7 %collective-permute-start.54 = (bf16[6,50,16,128]{3,2,1,0:T(8,128)(2,1)S(1)}, bf16[6,50,16,128]{3,2,1,0:T(8,128)(2,1)S(1)}, u32[]{:S(2)}, u32[]{:S(2)}) collective-permute-start(bf16[6,50,16,128]{3,2,1,0:T(8,128)(2,1)S(1)} %copy-done.46), channel_id=1, source_target_pairs={{1,2},{2,1},{5,6},{6,5},{9,10},{10,9},{13,14},{14,13},{17,18},{18,... | collective-permute-start | bytes 3686408 | tf_op jit(solution)/shard_map/ppermute | solution.py:480
  514.5 43.9 %collective-permute-start.55 = (bf16[4,50,16,128]{3,2,1,0:T(8,128)(2,1)S(1)}, bf16[4,50,16,128]{3,2,1,0:T(8,128)(2,1)S(1)}, u32[]{:S(2)}, u32[]{:S(2)}) collective-permute-start(bf16[4,50,16,128]{3,2,1,0:T(8,128)(2,1)S(1)} %copy-done.51), channel_id=1, source_target_pairs={{0,1},{1,0},{2,3},{3,2},{4,5},{5,4},{6,7},{7,6},{8,9},{9,8},{10,11... | collective-permute-start | bytes 2457608 | tf_op jit(solution)/shard_map/ppermute | solution.py:480
  559.9 70.4 %collective-permute-start.64 = (bf16[4,50,16,128]{3,2,1,0:T(8,128)(2,1)S(1)}, bf16[4,50,16,128]{3,2,1,0:T(8,128)(2,1)}, u32[]{:S(2)}, u32[]{:S(2)}) collective-permute-start(bf16[4,50,16,128]{3,2,1,0:T(8,128)(2,1)S(1)} %pass_on.11.refs_11_), channel_id=1, source_target_pairs={{0,1},{1,0},{2,3},{3,2},{4,5},{5,4},{6,7},{7,6},{8,9},{9,8},{10,11... | collective-permute-start | bytes 2457608 | tf_op jit(solution)/shard_map/ppermute | solution.py:480
  629.1 40.2 %collective-permute-start.57 = (bf16[8,64,320]{2,1,0:T(8,128)(2,1)}, bf16[8,64,320]{2,1,0:T(8,128)(2,1)S(1)}, u32[]{:S(2)}, u32[]{:S(2)}) collective-permute-start(bf16[8,64,320]{2,1,0:T(8,128)(2,1)} %get-tuple-element.82), channel_id=1, source_target_pairs={{0,8},{8,0},{16,24},{24,16},{1,9},{9,1},{17,25},{25,17},{2,10},{10... | collective-permute-start | bytes 983048 | tf_op jit(solution)/shard_map/ppermute | solution.py:519
  (119 other events, 2048.0 us)

commit v5 on v3

--- a/solution.py
+++ b/solution.py
@@ -193,8 +193,9 @@
         functools.partial(pass_kernel, given),
         out_shape=out,
         in_specs=[pl.BlockSpec(memory_space=pltpu.SMEM)] + [anywhere] * len(operands),
-        out_specs=[anywhere] * len(out),
+        out_specs=[pl.BlockSpec(memory_space=pltpu.VMEM)] * len(out),
         scratch_shapes=[pltpu.SemaphoreType.DMA((3,))],
+        compiler_params=pltpu.CompilerParams(vmem_limit_bytes=32 * 2 ** 20),
         cost_estimate=pl.CostEstimate(flops=0, bytes_accessed=4 * 2 ** 20, transcendentals=0),
         name="pass_on",
     )(spot, *operands)
@@ -209,7 +210,7 @@
     kinds = source.shape[1] // groups
     half = (group + 1) // 2
     mains = (plane - half) // group
-    windows = spread[0].shape[0]
+    windows = spread.shape[1]
     for part, (lo, hi) in enumerate(((0, half), (half, group))):
         if lo == hi:
             continue
@@ -235,21 +236,125 @@
             for kind in range(kinds):
                 for k in range(count):
                     for a in range(windows):
-                        spread[slot + kind][a, :, (lo + k) * LANES:(lo + k + 1) * LANES] = got[
+                        spread[slot + kind, a, :, (lo + k) * LANES:(lo + k + 1) * LANES] = got[
                             kind, :, k, :, a * LANES:(a + 1) * LANES
                         ].reshape(sides * rows, LANES)
 
 
-def flat(ref):
-    windows, rows, lanes = ref.shape
-    return ref[...].reshape(windows * rows, lanes)
+def table_kernel(rest, table_ref, *refs):
+    out_ref = refs[-1]
+    total = table_ref.shape[0]
+    mains = total - rest
+    out_ref[...] = jnp.zeros_like(out_ref)
+    for part in range(2):
+        out_ref[part, 0:mains] = table_ref[0:mains]
+        out_ref[part, mains + part * rest:mains + (part + 1) * rest] = table_ref[mains:total]
+
+
+def make_table(table, deps, rest):
+    total, lanes = table.shape
+    vmem = pl.BlockSpec(memory_space=pltpu.VMEM)
+    return pl.pallas_call(
+        functools.partial(table_kernel, rest),
+        out_shape=jax.ShapeDtypeStruct((2, total - rest + LANES, lanes), table.dtype),
+        in_specs=[vmem] + [pl.BlockSpec(memory_space=pl.ANY)] * len(deps),
+        out_specs=vmem,
+        name="make_table",
+    )(table, *deps)
+
+
+def low_kernel(one_ref, two_ref, out_ref):
+    group, slab, lanes = one_ref.shape
+    out_ref[...] = jnp.zeros_like(out_ref)
+    for k in range(group):
+        for half, ref in enumerate((one_ref, two_ref)):
+            out_ref[k * LANES:k * LANES + slab, half * lanes:(half + 1) * lanes] = ref[k]
+
+
+def make_lows(one, two, group):
+    depth, slab, lanes = one.shape
+    block = pl.BlockSpec((group, slab, lanes), lambda g: (g, 0, 0))
+    return pl.pallas_call(
+        low_kernel,
+        out_shape=jax.ShapeDtypeStruct((depth * LANES, 2 * lanes), one.dtype),
+        grid=(depth // group,),
+        in_specs=[block, block],
+        out_specs=pl.BlockSpec((group * LANES, 2 * lanes), lambda g: (g, 0)),
+        compiler_params=pltpu.CompilerParams(vmem_limit_bytes=32 * 2 ** 20),
+        name="make_lows",
+    )(one, two)
+
+
+def planes_kernel(spans, depth, tiles, *refs):
+    parts = refs[:len(spans)]
+    out_ref, held, sems = refs[-3:]
+    copies = [
+        pltpu.make_async_copy(ref.at[first:first + size], held.at[at:at + size], sems.at[i])
+        for i, (ref, (at, first, size)) in enumerate(zip(parts, spans))
+    ]
+    for copy in copies:
+        copy.start()
+    out_ref[...] = jnp.zeros_like(out_ref)
+    for copy in copies:
+        copy.wait()
+    planes, rows = held.shape[1], held.shape[2]
+
+    def one(k, _):
+        for i in range(tiles[0]):
+            for j in range(tiles[1]):
+                plane = (k * tiles[0] + i) * tiles[1] + j
+                out_ref[
+                    pl.ds(pl.multiple_of(k * LANES + i * rows, rows), rows), j * LANES:(j + 1) * LANES
+                ] = held[plane // planes, plane % planes]
+        return 0
+
+    lax.fori_loop(0, depth, one, 0)
+
+
+def low_of_planes(parts, deps, units, depth, tiles):
+    spans = [(at, first, size) for at, _, first, size in parts]
+    shape = parts[0][1].shape[1:]
+    anywhere = pl.BlockSpec(memory_space=pl.ANY)
+    return pl.pallas_call(
+        functools.partial(planes_kernel, spans, depth, tiles),
+        out_shape=jax.ShapeDtypeStruct((depth * LANES, tiles[1] * LANES), jnp.bfloat16),
+        in_specs=[anywhere] * (len(parts) + len(deps)),
+        out_specs=pl.BlockSpec(memory_space=pltpu.VMEM),
+        scratch_shapes=[
+            pltpu.VMEM((units,) + shape, jnp.bfloat16),
+            pltpu.SemaphoreType.DMA((len(parts),)),
+        ],
+        compiler_params=pltpu.CompilerParams(vmem_limit_bytes=40 * 2 ** 20),
+        name="low_of_planes",
+    )(*[got for _, got, _, _ in parts], *deps)
+
+
+def join_kernel(count, *refs):
+    outs = refs[-count:]
+    for i in range(count):
+        outs[i][...] = (refs[2 * i][...].astype(jnp.float32) + refs[2 * i + 1][...].astype(jnp.float32)).astype(
+            outs[i].dtype
+        )
+
+
+def join(pairs, deps):
+    vmem = pl.BlockSpec(memory_space=pltpu.VMEM)
+    types = [jnp.float32] + [jnp.bfloat16] * (len(pairs) - 1)
+    return pl.pallas_call(
+        functools.partial(join_kernel, len(pairs)),
+        out_shape=[jax.ShapeDtypeStruct(a.shape, kind) for (a, _), kind in zip(pairs, types)],
+        in_specs=[vmem] * (2 * len(pairs)) + [pl.BlockSpec(memory_space=pl.ANY)] * len(deps),
+        out_specs=[vmem] * len(pairs),
+        compiler_params=pltpu.CompilerParams(vmem_limit_bytes=32 * 2 ** 20),
+        name="join",
+    )(*[x for pair in pairs for x in pair], *deps)
 
 
 def even_kernel(sides, group, groups, use_ends, use_inner, starts, spot_ref, *refs):
     views = [ref.at[at:at + 2 * groups] for ref, at in zip(refs[:2 * sides], starts)]
     inner_blocks, end_blocks = views[:sides], views[sides:]
-    left_ref, first_ref, last_ref = refs[2 * sides:2 * sides + 3]
-    total, even, spread_a, spread_b, sems = refs[-5:]
+    tables, low_ref = refs[2 * sides:2 * sides + 2]
+    total, even, spread, sems = refs[-4:]
     here = spot_ref[0]
     step = pl.program_id(0)
     inner = jnp.logical_and(here > 0, here < sides - 1)
@@ -259,8 +364,6 @@
     def _():
         @pl.when(step == 0)
         def _():
-            total[...] = jnp.zeros_like(total)
-
             @pl.when(inner)
             def _():
                 for at, turn in enumerate((0, 1, 3, 2)):
@@ -271,32 +374,34 @@
                 for at, turn in enumerate((0, 1, 2, 3)):
                     fetch(end_blocks[at], even.at[here ^ turn], sems.at[at])
 
+            total[...] = jnp.zeros_like(total)
             for at in range(sides):
                 pltpu.make_async_copy(inner_blocks[at], even.at[at], sems.at[at]).wait()
 
-        expand(even, step, group, groups, (left_ref,), (spread_a, spread_b))
-        first = first_ref[...].reshape(group * LANES, first_ref.shape[-1])
-        last = last_ref[...].reshape(group * LANES, last_ref.shape[-1])
-        total[0] += jnp.dot(flat(spread_a), first, preferred_element_type=jnp.float32)
-        total[1] += jnp.dot(flat(spread_b), first, preferred_element_type=jnp.float32)
-        total[1] += jnp.dot(flat(spread_a), last, preferred_element_type=jnp.float32)
+        expand(even, step, group, groups, (tables,), spread)
+        count = spread.shape[1] * spread.shape[2]
+        full = total.shape[2]
+        both = spread[...].reshape(2, count, group * LANES)
+        got = jnp.dot(both[0], low_ref[...], preferred_element_type=jnp.float32)
+        total[0] += got[:, :full]
+        total[1] += got[:, full:] + jnp.dot(both[1], low_ref[:, :full], preferred_element_type=jnp.float32)
 
     @pl.when(jnp.logical_and(step == 0, jnp.logical_not(work)))
     def _():
         total[...] = jnp.zeros_like(total)
 
 
-def even_product(spot, inner_blocks, end_blocks, deps, table, first, last, sides, group, groups):
+def even_product(spot, inner_blocks, end_blocks, deps, table, low, sides, group, groups):
     some = inner_blocks or end_blocks
     use_inner, use_ends = inner_blocks is not None, end_blocks is not None
     blocks = (inner_blocks or some) + (end_blocks or some)
     starts = [at for _, at in blocks]
     _, planes, rows, _ = some[0][0].shape
     windows = table.shape[2] // LANES
-    full = first.shape[-1]
+    full = low.shape[-1] // 2
     count = windows * sides * rows
     whole = lambda arr: pl.BlockSpec(arr.shape, lambda g, s: (0,) * len(arr.shape))
-    low = pl.BlockSpec((group,) + first.shape[1:], lambda g, s: (g, 0, 0))
+    part = pl.BlockSpec((group * LANES, 2 * full), lambda g, s: (g, 0))
     out = jax.ShapeDtypeStruct((2, count, full), jnp.float32)
     depth = groups * group
     flops = 2 * count * depth * LANES * 3 * full + 4 * sides * rows * depth * 3 * LANES * windows * LANES
@@ -307,28 +412,27 @@
             num_scalar_prefetch=1,
             grid=(groups,),
             in_specs=[pl.BlockSpec(memory_space=pl.ANY)] * (2 * sides)
-            + [whole(table), low, low]
+            + [whole(table), part]
             + [pl.BlockSpec(memory_space=pl.ANY)] * len(deps),
             out_specs=whole(out),
             scratch_shapes=[
                 pltpu.VMEM((sides, 2 * groups, planes, rows, LANES), jnp.bfloat16),
-                pltpu.VMEM((windows, sides * rows, group * LANES), jnp.bfloat16),
-                pltpu.VMEM((windows, sides * rows, group * LANES), jnp.bfloat16),
+                pltpu.VMEM((2, windows, sides * rows, group * LANES), jnp.bfloat16),
                 pltpu.SemaphoreType.DMA((sides,)),
             ],
         ),
-        compiler_params=pltpu.CompilerParams(vmem_limit_bytes=40 * 2 ** 20),
+        compiler_params=pltpu.CompilerParams(vmem_limit_bytes=56 * 2 ** 20),
         cost_estimate=pl.CostEstimate(flops=flops, bytes_accessed=20 * 2 ** 20, transcendentals=0),
         name="even_product",
-    )(spot, *[ref for ref, _ in blocks], table, first, last, *deps)
+    )(spot, *[ref for ref, _ in blocks], table, low, *deps)
 
 
 def odd_kernel(sides, group, groups, outs, starts, spot_ref, *refs):
     blocks = [ref.at[at:at + groups] for ref, at in zip(refs[:sides], starts)]
     inner_part, end_part = refs[sides:sides + 2]
-    left_ref, next_left_ref, low_ref, next_low_ref = refs[sides + 2:sides + 6]
-    out_refs = refs[-5 - outs:-5]
-    odd, spread_a, spread_b, total, sems = refs[-5:]
+    tables, next_tables, low_ref, next_low_ref = refs[sides + 2:sides + 6]
+    out_refs = refs[-4 - outs:-4]
+    odd, spread, total, sems = refs[-4:]
     here, role = spot_ref[0], spot_ref[1]
     step, last = pl.program_id(0), pl.num_programs(0) - 1
     inner = jnp.logical_and(here > 0, here < sides - 1)
@@ -351,11 +455,11 @@
 
     @pl.when(inner)
     def _():
-        expand(odd, step, group, groups, (left_ref, next_left_ref), (spread_a, spread_b))
-        low = low_ref[...].reshape(group * LANES, low_ref.shape[-1])
-        next_low = next_low_ref[...].reshape(group * LANES, low_ref.shape[-1])
-        total[1] += jnp.dot(flat(spread_a), low, preferred_element_type=jnp.float32)
-        total[1] += jnp.dot(flat(spread_b), next_low, preferred_element_type=jnp.float32)
+        expand(odd, step, group, groups, (tables, next_tables), spread)
+        count = spread.shape[1] * spread.shape[2]
+        rows = spread[...].reshape(2, count, group * LANES)
+        got = jnp.dot(rows[0], low_ref[...], preferred_element_type=jnp.float32)
+        total[1] += got + jnp.dot(rows[1], next_low_ref[...], preferred_element_type=jnp.float32)
 
     @pl.when(step == last)
     def _():
@@ -376,7 +480,7 @@
     full = low.shape[-1]
     count = windows * sides * rows
     whole = lambda arr: pl.BlockSpec(arr.shape, lambda g, s: (0,) * len(arr.shape))
-    part = pl.BlockSpec((group,) + low.shape[1:], lambda g, s: (g, 0, 0))
+    part = pl.BlockSpec((group * LANES, full), lambda g, s: (g, 0))
     out = [jax.ShapeDtypeStruct((windows, sides * rows, full // 2), jnp.bfloat16)] * outs
     depth = groups * group
     flops = 2 * count * depth * LANES * 2 * full + 4 * sides * rows * depth * 3 * LANES * windows * LANES
@@ -392,13 +496,12 @@
             out_specs=[whole(o) for o in out],
             scratch_shapes=[
                 pltpu.VMEM((sides, groups, planes, rows, LANES), jnp.bfloat16),
-                pltpu.VMEM((windows, sides * rows, group * LANES), jnp.bfloat16),
-                pltpu.VMEM((windows, sides * rows, group * LANES), jnp.bfloat16),
+                pltpu.VMEM((2, windows, sides * rows, group * LANES), jnp.bfloat16),
                 pltpu.VMEM((2, count, full), jnp.float32),
                 pltpu.SemaphoreType.DMA((sides + 1,)),
             ],
         ),
-        compiler_params=pltpu.CompilerParams(vmem_limit_bytes=40 * 2 ** 20),
+        compiler_params=pltpu.CompilerParams(vmem_limit_bytes=56 * 2 ** 20),
         cost_estimate=pl.CostEstimate(flops=flops, bytes_accessed=20 * 2 ** 20, transcendentals=0),
         name="odd_product",
     )(spot, *[ref for ref, _ in blocks], inner_part, end_part, table, next_table, low, next_low, *deps)
@@ -435,11 +538,10 @@
         return pieces
 
     def lower(kind, place):
-        low = lax.dynamic_slice_in_dim(bottoms[kind], place * depth, depth, 0)
+        low = lax.dynamic_slice(
+            bottoms, (kind, place * depth, 0, 0, 0), (1, depth, slab, downs, full)
+        )
         return low.reshape(depth, slab, downs * full)
-
-    def padded(low):
-        return jnp.pad(low, ((0, 0), (0, LANES - slab), (0, 0)))
 
     pairs = [(z, z ^ 1) for z in range(sides)]
     hand = [(z, z ^ 1) for z in (0, sides - 1)]
@@ -456,14 +558,8 @@
     plane = (mains * group + (group + 1) // 2, rows, LANES)
 
     def table(flat_left):
-        wide = jnp.pad(
-            flat_left.reshape(total, windows, slab), ((0, 0), (0, 0), (0, LANES - slab))
-        ).reshape(total, windows * LANES)
-        first = jnp.pad(wide, ((0, LANES - rest), (0, 0)))
-        blank = jnp.zeros((rest, windows * LANES), wide.dtype)
-        second = jnp.concatenate([wide[:mains * LANES], blank, wide[mains * LANES:]], axis=0)
-        second = jnp.pad(second, ((0, LANES - 2 * rest), (0, 0)))
-        return jnp.stack([first, second])
+        wide = flat_left.reshape(total, windows, slab)
+        return jnp.pad(wide, ((0, 0), (0, 0), (0, LANES - slab))).reshape(total, windows * LANES)
 
     flat_left = left_all.reshape(total, windows * slab)
     middle = lower(1, role) * jnp.asarray(2, bottoms.dtype)
@@ -471,7 +567,8 @@
     count = depth * tiles[0] * tiles[1]
     units = -(-count // plane[0])
     carried = middle.reshape(depth, tiles[0], rows, tiles[1], LANES).transpose(0, 1, 3, 2, 4)
-    carried = jnp.pad(carried.reshape(count, rows, LANES), ((0, units * plane[0] - count), (0, 0), (0, 0)))
+    carried = carried.reshape(count, rows, LANES)
+    carried = jnp.pad(carried, ((0, units * plane[0] - count), (0, 0), (0, 0)))
     carried = carried.reshape((units,) + plane)
     taken = 0
 
@@ -484,34 +581,45 @@
     own, sent, straight, turned, last = {}, {}, {}, {}, {}
     sums, shares, reduced = {}, {}, {}
     parts = []
-    lows = tables = next_low = None
+    near_low = None
     done = None
 
-    def reduce_roles(t):
-        summed = shares[t][0].astype(jnp.float32)
-        for s in range(1, roles):
-            got = lax.ppermute(shares[t][s], "role", [(j, j ^ s) for j in range(roles)])
-            summed = summed + got.astype(jnp.float32)
-        summed = summed.reshape(windows, sides * contrs, unit, full)
-        size = sides * contrs
-        step = contrs // 2
-        place = lax.axis_index("contr")
+    def send_core(t):
+        stages[t] = [lax.ppermute(shares[t][s], "role", [(j, j ^ 1) for j in range(roles)]) for s in (1, 3)]
+
+    def join_core(t, deps):
+        kept, give = join([(shares[t][0], stages[t][0]), (shares[t][2], stages[t][1])], deps)
+        stages[t] = [kept, lax.ppermute(give, "role", [(j, j ^ 2) for j in range(roles)])]
+        return kept
+
+    def join_chip(t, deps):
+        summed = join([tuple(stages[t])], deps)[0]
+        size, step = sides * contrs, contrs // 2
+        stages[t] = halve(summed.reshape(windows, size, unit, full), size, step) + (size // 2, step // 2)
+        return summed
+
+    def halve(summed, size, step):
+        bit = (lax.axis_index("contr") // step) % 2
+        keep = lax.dynamic_slice_in_dim(summed, bit * (size // 2), size // 2, 1)
+        give = lax.dynamic_slice_in_dim(summed, (1 - bit) * (size // 2), size // 2, 1).astype(jnp.bfloat16)
+        return keep, lax.ppermute(give, "contr", [(j, j ^ step) for j in range(contrs)])
+
+    def join_contr(t, deps):
+        keep, got, size, step = stages[t]
+        summed = join([(keep, got)], deps)[0]
         while step:
-            size //= 2
-            bit = (place // step) % 2
-            keep = lax.dynamic_slice_in_dim(summed, bit * size, size, 1)
-            give = lax.dynamic_slice_in_dim(summed, (1 - bit) * size, size, 1).astype(jnp.bfloat16)
-            got = lax.ppermute(give, "contr", [(j, j ^ step) for j in range(contrs)])
-            summed = keep + got.astype(jnp.float32)
-            step //= 2
+            summed = join([halve(summed, size, step)], [])[0]
+            size, step = size // 2, step // 2
+        reduced[t] = summed
         return summed
 
+    stages, extra = {}, []
     for r in range(chunks + 3):
         if r <= chunks:
             fresh = r < chunks
             base = 3 * groups if fresh else 0
-            extra = {0: 2, 1: 3}.get(r, 1) * groups if fresh else 0
-            at, size = take(extra)
+            most = {0: 2, 1: 3}.get(r, 1) * groups if fresh else 0
+            at, size = take(most)
             length = max(base + size, 4 * groups) if fresh else 2 * groups
             given = dict(
                 sides=sides, groups=groups, back=2 * groups if fresh else 0, kind=base, low=at, count=size
@@ -519,9 +627,10 @@
             deps = [sent[r - 1]] if r else []
             deps += [sums[r - 1]] if r - 1 in sums else []
             out, mine, mark = pack(
-                spot, pieces.pop(r) if fresh else [], straight.get(r - 1), carried, deps, given, group,
-                plane, length,
+                spot, pieces.pop(r) if fresh else [], straight.get(r - 1), carried, deps + extra, given,
+                group, plane, length,
             )
+            extra = []
             sent[r] = move(out, pairs)
             if size:
                 parts.append((at, sent[r], base, size))
@@ -534,29 +643,34 @@
                     pieces[t] = exchange(t, mark[1])
             if r == 0:
                 late = mark[1]
-                lows = (padded(lower(0, late)), padded(lower(2, late)), padded(middle))
-                tables = (table(flat_left), table(move(flat_left, hand)))
+                first_table = make_table(table(flat_left), [out], rest)
+                low = make_lows(lower(0, late), lower(2, late), group)
+                near_left = move(flat_left, hand)
+                extra = [low, first_table]
+            if r == 1:
+                near_table = make_table(table(near_left), [out], rest)
+                middle_low = low_of_planes([(0, carried, 0, units)], [out], units, depth, tiles)
+                extra = [near_table, middle_low]
         t = r - 4
         if 0 <= t < chunks:
-            if next_low is None:
-                arrived = [got[first:first + size] for _, got, first, size in sorted(parts, key=lambda p: p[0])]
-                arrived = jnp.concatenate(arrived, axis=0).reshape(-1, rows, LANES)[:count]
-                arrived = arrived.reshape(depth, tiles[0], tiles[1], rows, LANES).transpose(0, 1, 3, 2, 4)
-                next_low = padded(arrived.reshape(depth, slab, downs * full))
+            if near_low is None:
+                near_low = low_of_planes(sorted(parts, key=lambda p: p[0]), [done], units, depth, tiles)
             blocks = [(own[t], 2 * groups), (sent[t], 2 * groups), (straight[t], 2 * groups), (turned[t + 1], 2 * groups)]
             shares[t] = odd_product(
-                spot, blocks, sums[t + 2], sums[t + 3], [done], tables, (lows[2], next_low),
-                sides, group, groups, roles,
+                spot, blocks, sums[t + 2], sums[t + 3], [done] + extra, (first_table, near_table),
+                (middle_low, near_low), sides, group, groups, roles,
             )
             done = shares[t][0]
+            extra = []
+            send_core(t)
+            if t - 1 in stages:
+                extra.append(join_chip(t - 1, [done]))
         if 1 <= r <= chunks + 1:
             at, size = take(2 * groups) if 2 <= r else (0, 0)
             given = dict(sides=sides, groups=groups, cross=r <= chunks, low=at, count=size)
             deps = [done] + ([last[r - 1]] if r - 1 in last else [])
-            if r - 5 in shares:
-                reduced[r - 5] = reduce_roles(r - 5)
-                deps.append(reduced[r - 5])
-            outs = pass_on(spot, sent[r - 1], turned.get(r - 1), carried, deps, given, plane)
+            outs = pass_on(spot, sent[r - 1], turned.get(r - 1), carried, deps + extra, given, plane)
+            extra = []
             if r <= chunks:
                 turned[r] = move(outs[0], cross)
             if r - 1 in turned:
@@ -575,18 +689,27 @@
                     (own[t], 0), (sent[t], 0), (sent[t + 1], 2 * groups if t + 1 < chunks else 0), (last[t + 2], 0)
                 ]
             sums[r] = even_product(
-                spot, inner_blocks, end_blocks, [done], tables[0], lows[0], lows[1], sides, group, groups
+                spot, inner_blocks, end_blocks, [done] + extra, first_table, low, sides, group, groups
             )
             done = sums[r]
+            extra = []
+            if r - 4 in shares:
+                extra.append(join_core(r - 4, [done]))
+            if r - 5 in shares:
+                extra.append(join_contr(r - 5, [done]))
     t = chunks - 1
     blocks = [(own[t], 2 * groups), (sent[t], 2 * groups), (straight[t], 2 * groups), (turned[t + 1], 2 * groups)]
     shares[t] = odd_product(
-        spot, blocks, sums[t + 2], sums[t + 3], [done], tables, (lows[2], next_low), sides, group, groups, roles
+        spot, blocks, sums[t + 2], sums[t + 3], [done] + extra, (first_table, near_table),
+        (middle_low, near_low), sides, group, groups, roles,
     )
-
-    for t in range(chunks):
-        if t not in reduced:
-            reduced[t] = reduce_roles(t)
+    send_core(t)
+    join_chip(t - 1, [shares[t][0]])
+    join_core(t, [])
+    join_contr(t - 1, [])
+    join_chip(t, [])
+    join_contr(t, [])
+
     summed = jnp.concatenate([reduced[t] for t in range(chunks)], axis=2)
     mine = lax.dynamic_slice_in_dim(summed, here, 1, 1)
     for s in range(1, sides):

time: 1030 us -> 698 us (0.68)
  Pallas kernels: 444 us -> 252 us
  local copies, waits for them, and re-layouts: 215 us -> 133 us
  starting transfers between devices: 220 us -> 138 us
  waiting for transfers between devices: 107 us -> 140 us
  other arithmetic: 23.5 us -> 10.9 us
    pallas_call x6, Pallas kernels: 233 us -> 14.2 us  [pass_on(): pl.pallas_call(functools.partial(pass_kernel, given), out_shape=out, in_s...]
    ppermute x22, starting transfers between devices: 189 us -> 93.6 us  [on_device(): move = lambda value, perm: lax.ppermute(value, 'horiz', perm)]
    slice x9 -> x0, local copies, waits for them, and re-layouts: 56.8 us -> none  [the longest x1 44 us: lower(): low = lax.dynamic_slice_in_dim(bottoms[kind], place * depth, depth, 0)]
    ppermute x22, waiting for transfers between devices: 19.2 us -> 68.6 us  [on_device(): move = lambda value, perm: lax.ppermute(value, 'horiz', perm)]
    pallas_call x0 -> x20, Pallas kernels: none -> 32.5 us  [the longest x2 21.2 us: low_of_planes(): pl.pallas_call(functools.partial(planes_kernel, spans, depth, tiles), out...]
    unnamed x149 -> x178, local copies, waits for them, and re-layouts: 36.5 us -> 65.1 us
    pad x6 -> x2, local copies, waits for them, and re-layouts: 27.7 us -> 1.07 us  [table(): jnp.pad(wide, ((0, 0), (0, 0), (0, LANES - slab)))]
    pallas_call x6, Pallas kernels: 142 us -> 127 us  [even_product(): pl.pallas_call(functools.partial(even_kernel, sides, group, groups, use_e...]
  transfers between devices with their start and end apart: 66 -> 66, of which waited for: 17 -> 20; matrix products, arithmetic and copies ran while one was open for 20% -> 11% of each run, Pallas kernels for 42% -> 33%
where the time goes in v5:
time: 698 us; the launch traced here: 687 us
  Pallas kernels  252 us (36%)
  waiting for transfers between devices  140 us (20%)
  starting transfers between devices  138 us (20%)
  local copies, waits for them, and re-layouts  133 us (19%)
  other arithmetic  10.9 us (2%)
  between operations  8.82 us (1%)
    pallas_call x6, Pallas kernels, even_product(): pl.pallas_call(functools.partial(even_kernel, sides, group, groups, use_e...  127 us
    ppermute x22, starting transfers between devices, on_device(): move = lambda value, perm: lax.ppermute(value, 'horiz', perm)  93.6 us
    ppermute x22, waiting for transfers between devices, on_device(): move = lambda value, perm: lax.ppermute(value, 'horiz', perm)  68.6 us
    unnamed x178, local copies, waits for them, and re-layouts  65.1 us
    pallas_call x5, Pallas kernels, odd_product(): pl.pallas_call(functools.partial(odd_kernel, sides, group, groups, outs,...  53.9 us
    ppermute x15, waiting for transfers between devices, exchange(): piece = lax.ppermute(piece, 'role', [(j, j ^ s) for j in range(roles)])  25.6 us
    pallas_call x6, Pallas kernels, pack(): pl.pallas_call(functools.partial(pack_kernel, group, len(pieces), given),...  24.2 us
    pallas_call x2, Pallas kernels, low_of_planes(): pl.pallas_call(functools.partial(planes_kernel, spans, depth, tiles), out...  21.2 us
  transfers between devices with their start and end apart: 66, of which 20 were waited for; matrix products, arithmetic and copies ran while one was open for 11% of the time, Pallas kernels for 33%

profile of v5, /device:TPU:0, one launch (start us, length us, event | category | flops | bytes accessed | tf_op | source)
XLA Modules:
  0.0 687.5 jit_solution(10508348422536930990)
XLA Ops:
  5.1 8.6 %dynamic-slice_multiply_fusion = bf16[1,40,80,2,320]{4,3,2,1,0:T(2,128)(2,1)} fusion(bf16[3,160,80,2,320]{4,3,2,1,0:T(2,128)(2,1)} %param.5, s32[]{:T(128)S(6)} %select_n.131), kind=kLoop, calls=%fused_computation | loop fusion | flops 2048000 | bytes 8192004 | tf_op jit(solution)/shard_map/mul | solution.py:565
  13.7 13.8 %mul.139 = bf16[40,5,16,5,128]{4,3,2,1,0:T(8,128)(2,1)} reshape(bf16[1,40,80,2,320]{4,3,2,1,0:T(2,128)(2,1)} %dynamic-slice_multiply_fusion) | data formatting | bytes 8192000 | tf_op jit(solution)/shard_map/mul | solution.py:565
  55.8 9.7 %constant_dynamic-slice_fusion.13 = (bf16[1,40,80,2,320]{4,3,2,1,0:T(2,128)(2,1)}, bf16[1,40,80,2,320]{4,3,2,1,0:T(2,128)(2,1)}) fusion(bf16[3,160,80,2,320]{4,3,2,1,0:T(2,128)(2,1)} %param.5, s32[]{:T(128)S(6)} %select_n.135), kind=kLoop, calls=%fused_computation.55 | loop fusion | bytes 16384004 | tf_op jit(solution)/shard_map/dynamic_slice | solution.py:541
  65.5 10.5 %reshape.163.one_ref = bf16[40,80,640]{2,1,0:T(8,128)(2,1)} reshape(bf16[1,40,80,2,320]{4,3,2,1,0:T(2,128)(2,1)} %get-tuple-element.110) | data formatting | bytes 8192000 | tf_op jit(solution)/shard_map/reshape | solution.py:544
  76.0 10.5 %reshape.164.two_ref = bf16[40,80,640]{2,1,0:T(8,128)(2,1)} reshape(bf16[1,40,80,2,320]{4,3,2,1,0:T(2,128)(2,1)} %get-tuple-element.109) | data formatting | bytes 8192000 | tf_op jit(solution)/shard_map/reshape | solution.py:544
  113.1 59.4 %collective-permute-done.8 = bf16[320,640]{0,1:T(8,128)(2,1)S(1)} collective-permute-done((bf16[320,640]{0,1:T(8,128)(2,1)S(1)}, bf16[320,640]{0,1:T(8,128)(2,1)S(1)}, u32[]{:S(2)}, u32[]{:S(2)}) %collective-permute-start.8) | collective-permute-done | bytes 409632 | tf_op jit(solution)/shard_map/ppermute | solution.py:549
  177.9 8.9 %low_of_planes.2.refs_5_.refs_8_ = bf16[5120,640]{1,0:T(8,128)(2,1)S(1)} custom-call(bf16[40,25,16,128]{3,2,1,0:T(8,128)(2,1)S(1)} %bitcast.121, bf16[24,25,16,128]{3,2,1,0:T(8,128)(2,1)} %get-tuple-element.60.refs_0_.refs_1_.refs_3_), custom_call_target="tpu_custom_call" | custom-call | tf_op jit(solution)/shard_map/low_of_planes/pallas_call | solution.py:318
  208.0 10.1 %collective-permute-done.12.refs_2_ = bf16[3,40,16,80]{3,2,1,0:T(8,128)(2,1)} collective-permute-done((bf16[3,40,16,80]{3,2,1,0:T(8,128)(2,1)}, bf16[3,40,16,80]{3,2,1,0:T(8,128)(2,1)}, u32[]{:S(2)}, u32[]{:S(2)}) %collective-permute-start.12) | collective-permute-done | bytes 307232 | tf_op jit(solution)/shard_map/ppermute | solution.py:536
  302.3 12.7 %collective-permute-start.23 = (bf16[8,25,16,128]{3,2,1,0:T(8,128)(2,1)}, bf16[8,25,16,128]{3,2,1,0:T(8,128)(2,1)}, u32[]{:S(2)}, u32[]{:S(2)}) collective-permute-start(bf16[8,25,16,128]{3,2,1,0:T(8,128)(2,1)} %get-tuple-element.69), channel_id=1, source_target_pairs={{0,1},{1,0},{2,3},{3,2},{4,5},{5,4},{6,7},{7,6},{8,9},{9,8},{10,11... | collective-permute-start | bytes 2457608 | tf_op jit(solution)/shard_map/ppermute | solution.py:549
  316.7 24.3 %even_product.7.refs_7_.refs_5_.refs_4_ = f32[2,512,640]{2,1,0:T(8,128)} custom-call(s32[2]{0:T(128)} %copy-done.73, bf16[12,25,16,128]{3,2,1,0:T(8,128)(2,1)} %get-tuple-element.61.refs_0_.refs_4_, bf16[24,25,16,128]{3,2,1,0:T(8,128)(2,1)} %copy-done.11, bf16[12,25,16,128]{3,2,1,0:T(8,128)(2,1)} %collective-permute-done.14.refs_4_.refs_2_, ...), custom_call_target="tpu_custom_call" | custom-call | flops 14092861440 | bytes 20971520 | tf_op jit(solution)/shard_map/even_product/pallas_call | solution.py:408
  353.4 12.2 %low_of_planes.3.refs_9_ = bf16[5120,640]{1,0:T(8,128)(2,1)} custom-call(bf16[20,25,16,128]{3,2,1,0:T(8,128)(2,1)S(1)} %copy-done.15, bf16[24,25,16,128]{3,2,1,0:T(8,128)(2,1)S(1)} %copy-done.12, bf16[16,25,16,128]{3,2,1,0:T(8,128)(2,1)} %collective-permute-done.17.refs_6_.refs_0_.refs_2_.refs_1_.refs_5_, bf16[8,25,16,128]{3,2,1,0:T(8,128)(2,1)S(1)} %copy-done.33, ...), custom_call_target="tpu_custom_call" | custom-call | tf_op jit(solution)/shard_map/low_of_planes/pallas_call | solution.py:318
  365.6 10.7 %odd_product.5 = (bf16[8,64,320]{2,1,0:T(8,128)(2,1)}, bf16[8,64,320]{2,1,0:T(8,128)(2,1)}, bf16[8,64,320]{2,1,0:T(8,128)(2,1)}, bf16[8,64,320]{2,1,0:T(8,128)(2,1)}) custom-call(s32[2]{0:T(128)} %copy-done.73, bf16[12,25,16,128]{3,2,1,0:T(8,128)(2,1)} %get-tuple-element.57.refs_0_.refs_4_, bf16[20,25,16,128]{3,2,1,0:T(8,128)(2,1)} %copy-done.13, ...), custom_call_target="tpu_custom_call" | custom-call | flops 10737418240 | bytes 20971520 | tf_op jit(solution)/shard_map/odd_product/pallas_call | solution.py:487
  383.7 23.7 %even_product.8.refs_4_.refs_3_.refs_5_ = f32[2,512,640]{2,1,0:T(8,128)} custom-call(s32[2]{0:T(128)} %copy-done.73, bf16[12,25,16,128]{3,2,1,0:T(8,128)(2,1)} %get-tuple-element.66.refs_0_.refs_4_, bf16[16,25,16,128]{3,2,1,0:T(8,128)(2,1)} %collective-permute-done.17.refs_6_.refs_0_.refs_2_.refs_1_.refs_5_, ...), custom_call_target="tpu_custom_call" | custom-call | flops 14092861440 | bytes 20971520 | tf_op jit(solution)/shard_map/even_product/pallas_call | solution.py:408
  407.5 17.0 %collective-permute-start.36 = (bf16[8,25,16,128]{3,2,1,0:T(8,128)(2,1)}, bf16[8,25,16,128]{3,2,1,0:T(8,128)(2,1)}, u32[]{:S(2)}, u32[]{:S(2)}) collective-permute-start(bf16[8,25,16,128]{3,2,1,0:T(8,128)(2,1)} %get-tuple-element.83), channel_id=1, source_target_pairs={{0,1},{1,0},{2,3},{3,2},{4,5},{5,4},{6,7},{7,6},{8,9},{9,8},{10,11... | collective-permute-start | bytes 2457608 | tf_op jit(solution)/shard_map/ppermute | solution.py:549
  432.4 10.7 %odd_product.6 = (bf16[8,64,320]{2,1,0:T(8,128)(2,1)}, bf16[8,64,320]{2,1,0:T(8,128)(2,1)}, bf16[8,64,320]{2,1,0:T(8,128)(2,1)}, bf16[8,64,320]{2,1,0:T(8,128)(2,1)}) custom-call(s32[2]{0:T(128)} %copy-done.73, bf16[12,25,16,128]{3,2,1,0:T(8,128)(2,1)} %get-tuple-element.61.refs_0_.refs_4_, bf16[24,25,16,128]{3,2,1,0:T(8,128)(2,1)} %copy-done.11, ...), custom_call_target="tpu_custom_call" | custom-call | flops 10737418240 | bytes 20971520 | tf_op jit(solution)/shard_map/odd_product/pallas_call | solution.py:487
  451.1 23.8 %even_product.9.refs_2_.refs_4_.refs_5_.refs_10_ = f32[2,512,640]{2,1,0:T(8,128)} custom-call(s32[2]{0:T(128)} %copy-done.73, bf16[12,25,16,128]{3,2,1,0:T(8,128)(2,1)} %copy-done.80, bf16[16,25,16,128]{3,2,1,0:T(8,128)(2,1)} %copy-done.18, bf16[12,25,16,128]{3,2,1,0:T(8,128)(2,1)} %collective-permute-done.27.refs_4_.refs_2_, ...), custom_call_target="tpu_custom_call" | custom-call | flops 14092861440 | bytes 20971520 | tf_op jit(solution)/shard_map/even_product/pallas_call | solution.py:408
  475.0 14.5 %collective-permute-start.42 = (bf16[8,25,16,128]{3,2,1,0:T(8,128)(2,1)}, bf16[8,25,16,128]{3,2,1,0:T(8,128)(2,1)S(1)}, u32[]{:S(2)}, u32[]{:S(2)}) collective-permute-start(bf16[8,25,16,128]{3,2,1,0:T(8,128)(2,1)} %copy-done.82), channel_id=1, source_target_pairs={{0,1},{1,0},{2,3},{3,2},{4,5},{5,4},{6,7},{7,6},{8,9},{9,8},{10,11... | collective-permute-start | bytes 2457608 | tf_op jit(solution)/shard_map/ppermute | solution.py:549
  495.7 10.7 %odd_product.7 = (bf16[8,64,320]{2,1,0:T(8,128)(2,1)}, bf16[8,64,320]{2,1,0:T(8,128)(2,1)}, bf16[8,64,320]{2,1,0:T(8,128)(2,1)}, bf16[8,64,320]{2,1,0:T(8,128)(2,1)}) custom-call(s32[2]{0:T(128)} %copy-done.73, bf16[12,25,16,128]{3,2,1,0:T(8,128)(2,1)} %get-tuple-element.66.refs_0_.refs_4_, ...), custom_call_target="tpu_custom_call" | custom-call | flops 10737418240 | bytes 20971520 | tf_op jit(solution)/shard_map/odd_product/pallas_call | solution.py:487
  511.7 12.2 %collective-permute-start.48 = (bf16[8,25,16,128]{3,2,1,0:T(8,128)(2,1)}, bf16[8,25,16,128]{3,2,1,0:T(8,128)(2,1)}, u32[]{:S(2)}, u32[]{:S(2)}) collective-permute-start(bf16[8,25,16,128]{3,2,1,0:T(8,128)(2,1)} %pass_on.11.refs_10_), channel_id=1, source_target_pairs={{0,1},{1,0},{2,3},{3,2},{4,5},{5,4},{6,7},{7,6},{8,9},{9,8},{10,11... | collective-permute-start | bytes 2457608 | tf_op jit(solution)/shard_map/ppermute | solution.py:549
  523.8 23.7 %even_product.10.refs_2_.refs_4_.refs_5_.refs_10_ = f32[2,512,640]{2,1,0:T(8,128)} custom-call(s32[2]{0:T(128)} %copy-done.73, bf16[12,25,16,128]{3,2,1,0:T(8,128)(2,1)} %copy-done.81, bf16[16,25,16,128]{3,2,1,0:T(8,128)(2,1)} %collective-permute-done.33.refs_2_.refs_0_.refs_1_.refs_6_.refs_5_, ...), custom_call_target="tpu_custom_call" | custom-call | flops 14092861440 | bytes 20971520 | tf_op jit(solution)/shard_map/even_product/pallas_call | solution.py:408
  553.1 10.8 %odd_product.8 = (bf16[8,64,320]{2,1,0:T(8,128)(2,1)}, bf16[8,64,320]{2,1,0:T(8,128)(2,1)}, bf16[8,64,320]{2,1,0:T(8,128)(2,1)}, bf16[8,64,320]{2,1,0:T(8,128)(2,1)}) custom-call(s32[2]{0:T(128)} %copy-done.73, bf16[12,25,16,128]{3,2,1,0:T(8,128)(2,1)} %copy-done.80, bf16[16,25,16,128]{3,2,1,0:T(8,128)(2,1)} %copy-done.18, ...), custom_call_target="tpu_custom_call" | custom-call | flops 10737418240 | bytes 20971520 | tf_op jit(solution)/shard_map/odd_product/pallas_call | solution.py:487
  567.2 23.8 %even_product.11.refs_2_.refs_4_.refs_5_.refs_10_ = f32[2,512,640]{2,1,0:T(8,128)} custom-call(s32[2]{0:T(128)} %copy-done.73, bf16[12,25,16,128]{3,2,1,0:T(8,128)(2,1)} %copy-done.81, bf16[16,25,16,128]{3,2,1,0:T(8,128)(2,1)} %collective-permute-done.33.refs_2_.refs_0_.refs_1_.refs_6_.refs_5_, bf16[8,25,16,128]{3,2,1,0:T(8,128)(2,1)} %copy-done.54, ...), custom_call_target="tpu_custom_call" | custom-call | flops 14092861440 | bytes 20971520 | tf_op jit(solution)/shard_map/even_product/pallas_call | solution.py:408
  595.9 11.1 %odd_product.9 = (bf16[8,64,320]{2,1,0:T(8,128)(2,1)}, bf16[8,64,320]{2,1,0:T(8,128)(2,1)}, bf16[8,64,320]{2,1,0:T(8,128)(2,1)}, bf16[8,64,320]{2,1,0:T(8,128)(2,1)}) custom-call(s32[2]{0:T(128)} %copy-done.73, bf16[12,25,16,128]{3,2,1,0:T(8,128)(2,1)} %copy-done.81, ...), custom_call_target="tpu_custom_call" | custom-call | flops 10737418240 | bytes 20971520 | tf_op jit(solution)/shard_map/odd_product/pallas_call | solution.py:487
  650.8 12.1 %collective-permute-done.58 = bf16[8,1,40,320]{3,2,1,0:T(8,128)(2,1)S(1)} collective-permute-done((bf16[8,1,40,320]{3,2,1,0:T(8,128)(2,1)S(1)}, bf16[8,1,40,320]{3,2,1,0:T(8,128)(2,1)S(1)}, u32[]{:S(2)}, u32[]{:S(2)}) %collective-permute-start.58) | collective-permute-done | bytes 204832 | tf_op jit(solution)/shard_map/ppermute | solution.py:717
  (368 shorter events, 293.0 us)
Async XLA Ops:
  40.1 59.2 %collective-permute-start.3 = (bf16[20,25,16,128]{3,2,1,0:T(8,128)(2,1)}, bf16[20,25,16,128]{3,2,1,0:T(8,128)(2,1)S(1)}, u32[]{:S(2)}, u32[]{:S(2)}) collective-permute-start(bf16[20,25,16,128]{3,2,1,0:T(8,128)(2,1)} %get-tuple-element.58.refs_0_), channel_id=1, source_target_pairs={{0,1},{1,0},{2,3},{3,2},{4,5},{5,4},{6,7},{7,6},{8,9},{9,8},{10,11... | collective-permute-start | bytes 6144008 | tf_op jit(solution)/shard_map/ppermute | solution.py:549
  41.8 57.5 %collective-permute-start.4 = (bf16[12,25,16,128]{3,2,1,0:T(8,128)(2,1)}, bf16[12,25,16,128]{3,2,1,0:T(8,128)(2,1)}, u32[]{:S(2)}, u32[]{:S(2)}) collective-permute-start(bf16[12,25,16,128]{3,2,1,0:T(8,128)(2,1)} %get-tuple-element.57.refs_0_.refs_4_), channel_id=1, source_target_pairs={{1,2},{2,1},{5,6},{6,5},{9,10},{10,9},{13,14},{14,13},{17,18},{18,... | collective-permute-start | bytes 3686408 | tf_op jit(solution)/shard_map/ppermute | solution.py:549
  54.0 45.3 %collective-permute-start.5 = (bf16[3,40,16,80]{3,2,1,0:T(8,128)(2,1)}, bf16[3,40,16,80]{3,2,1,0:T(8,128)(2,1)}, u32[]{:S(2)}, u32[]{:S(2)}) collective-permute-start(bf16[3,40,16,80]{3,2,1,0:T(8,128)(2,1)} %get-tuple-element.125), channel_id=1, source_target_pairs={{0,8},{8,0},{16,24},{24,16},{1,9},{9,1},{17,25},{25,17},{2,10},{10... | collective-permute-start | bytes 921608 | tf_op jit(solution)/shard_map/ppermute | solution.py:536
  54.0 45.3 %collective-permute-start.6 = (bf16[3,40,16,80]{3,2,1,0:T(8,128)(2,1)}, bf16[3,40,16,80]{3,2,1,0:T(8,128)(2,1)}, u32[]{:S(2)}, u32[]{:S(2)}) collective-permute-start(bf16[3,40,16,80]{3,2,1,0:T(8,128)(2,1)} %get-tuple-element.124), channel_id=1, source_target_pairs={{0,16},{8,24},{16,0},{24,8},{1,17},{9,25},{17,1},{25,9},{2,18},{10... | collective-permute-start | bytes 921608 | tf_op jit(solution)/shard_map/ppermute | solution.py:536
  105.5 120.6 %collective-permute-start.10 = (bf16[24,25,16,128]{3,2,1,0:T(8,128)(2,1)}, bf16[24,25,16,128]{3,2,1,0:T(8,128)(2,1)S(1)}, u32[]{:S(2)}, u32[]{:S(2)}) collective-permute-start(bf16[24,25,16,128]{3,2,1,0:T(8,128)(2,1)} %get-tuple-element.60.refs_0_.refs_1_.refs_3_), channel_id=1, source_target_pairs={{0,1},{1,0},{2,3},{3,2},{4,5},{5,4},{6,7},{7,6},{8,9},{9,8},{10,11... | collective-permute-start | bytes 7372808 | tf_op jit(solution)/shard_map/ppermute | solution.py:549
  108.7 117.4 %collective-permute-start.14 = (bf16[12,25,16,128]{3,2,1,0:T(8,128)(2,1)}, bf16[12,25,16,128]{3,2,1,0:T(8,128)(2,1)}, u32[]{:S(2)}, u32[]{:S(2)}) collective-permute-start(bf16[12,25,16,128]{3,2,1,0:T(8,128)(2,1)} %get-tuple-element.61.refs_0_.refs_4_), channel_id=1, source_target_pairs={{1,2},{2,1},{5,6},{6,5},{9,10},{10,9},{13,14},{14,13},{17,18},{18,... | collective-permute-start | bytes 3686408 | tf_op jit(solution)/shard_map/ppermute | solution.py:549
  110.4 62.1 %collective-permute-start.8 = (bf16[320,640]{0,1:T(8,128)(2,1)S(1)}, bf16[320,640]{0,1:T(8,128)(2,1)S(1)}, u32[]{:S(2)}, u32[]{:S(2)}) collective-permute-start(bf16[320,640]{0,1:T(8,128)(2,1)S(1)} %bitcast.149), channel_id=1, source_target_pairs={{0,1},{3,2},{4,5},{7,6},{8,9},{11,10},{12,13},{15,14},{16,17},{19,... | collective-permute-start | bytes 1228808 | tf_op jit(solution)/shard_map/ppermute | solution.py:549
  113.0 92.1 %collective-permute-start.11 = (bf16[3,40,16,80]{3,2,1,0:T(8,128)(2,1)}, bf16[3,40,16,80]{3,2,1,0:T(8,128)(2,1)S(1)}, u32[]{:S(2)}, u32[]{:S(2)}) collective-permute-start(bf16[3,40,16,80]{3,2,1,0:T(8,128)(2,1)} %get-tuple-element.121), channel_id=1, source_target_pairs={{0,8},{8,0},{16,24},{24,16},{1,9},{9,1},{17,25},{25,17},{2,10},{10... | collective-permute-start | bytes 921608 | tf_op jit(solution)/shard_map/ppermute | solution.py:536
  201.9 45.3 %collective-permute-start.9 = (bf16[12,25,16,128]{3,2,1,0:T(8,128)(2,1)}, bf16[12,25,16,128]{3,2,1,0:T(8,128)(2,1)}, u32[]{:S(2)}, u32[]{:S(2)}) collective-permute-start(bf16[12,25,16,128]{3,2,1,0:T(8,128)(2,1)} %pass_on.6), channel_id=1, source_target_pairs={{1,2},{2,1},{5,6},{6,5},{9,10},{10,9},{13,14},{14,13},{17,18},{18,... | collective-permute-start | bytes 3686408 | tf_op jit(solution)/shard_map/ppermute | solution.py:549
  251.2 44.0 %collective-permute-start.15 = (bf16[12,25,16,128]{3,2,1,0:T(8,128)(2,1)}, bf16[12,25,16,128]{3,2,1,0:T(8,128)(2,1)}, u32[]{:S(2)}, u32[]{:S(2)}) collective-permute-start(bf16[12,25,16,128]{3,2,1,0:T(8,128)(2,1)} %get-tuple-element.63.refs_10_), channel_id=1, source_target_pairs={{1,2},{2,1},{5,6},{6,5},{9,10},{10,9},{13,14},{14,13},{17,18},{18,... | collective-permute-start | bytes 3686408 | tf_op jit(solution)/shard_map/ppermute | solution.py:549
  284.2 57.7 %collective-permute-start.22 = (bf16[16,25,16,128]{3,2,1,0:T(8,128)(2,1)}, bf16[16,25,16,128]{3,2,1,0:T(8,128)(2,1)S(1)}, u32[]{:S(2)}, u32[]{:S(2)}) collective-permute-start(bf16[16,25,16,128]{3,2,1,0:T(8,128)(2,1)} %get-tuple-element.67.refs_3_), channel_id=1, source_target_pairs={{0,1},{1,0},{2,3},{3,2},{4,5},{5,4},{6,7},{7,6},{8,9},{9,8},{10,11... | collective-permute-start | bytes 4915208 | tf_op jit(solution)/shard_map/ppermute | solution.py:549
  294.5 46.6 %collective-permute-start.26 = (bf16[3,40,16,80]{3,2,1,0:T(8,128)(2,1)}, bf16[3,40,16,80]{3,2,1,0:T(8,128)(2,1)S(1)}, u32[]{:S(2)}, u32[]{:S(2)}) collective-permute-start(bf16[3,40,16,80]{3,2,1,0:T(8,128)(2,1)} %get-tuple-element.111), channel_id=1, source_target_pairs={{0,24},{8,16},{16,8},{24,0},{1,25},{9,17},{17,9},{25,1},{2,26},{10... | collective-permute-start | bytes 921608 | tf_op jit(solution)/shard_map/ppermute | solution.py:536
  295.2 46.7 %collective-permute-start.27 = (bf16[12,25,16,128]{3,2,1,0:T(8,128)(2,1)}, bf16[12,25,16,128]{3,2,1,0:T(8,128)(2,1)}, u32[]{:S(2)}, u32[]{:S(2)}) collective-permute-start(bf16[12,25,16,128]{3,2,1,0:T(8,128)(2,1)} %copy-done.80), channel_id=1, source_target_pairs={{1,2},{2,1},{5,6},{6,5},{9,10},{10,9},{13,14},{14,13},{17,18},{18,... | collective-permute-start | bytes 3686408 | tf_op jit(solution)/shard_map/ppermute | solution.py:549
  302.3 51.1 %collective-permute-start.23 = (bf16[8,25,16,128]{3,2,1,0:T(8,128)(2,1)}, bf16[8,25,16,128]{3,2,1,0:T(8,128)(2,1)}, u32[]{:S(2)}, u32[]{:S(2)}) collective-permute-start(bf16[8,25,16,128]{3,2,1,0:T(8,128)(2,1)} %get-tuple-element.69), channel_id=1, source_target_pairs={{0,1},{1,0},{2,3},{3,2},{4,5},{5,4},{6,7},{7,6},{8,9},{9,8},{10,11... | collective-permute-start | bytes 2457608 | tf_op jit(solution)/shard_map/ppermute | solution.py:549
  314.9 63.7 %collective-permute-start.30 = (bf16[12,25,16,128]{3,2,1,0:T(8,128)(2,1)}, bf16[12,25,16,128]{3,2,1,0:T(8,128)(2,1)}, u32[]{:S(2)}, u32[]{:S(2)}) collective-permute-start(bf16[12,25,16,128]{3,2,1,0:T(8,128)(2,1)} %get-tuple-element.68.refs_10_), channel_id=1, source_target_pairs={{1,2},{2,1},{5,6},{6,5},{9,10},{10,9},{13,14},{14,13},{17,18},{18,... | collective-permute-start | bytes 3686408 | tf_op jit(solution)/shard_map/ppermute | solution.py:549
  352.8 76.9 %collective-permute-start.33 = (bf16[16,25,16,128]{3,2,1,0:T(8,128)(2,1)S(1)}, bf16[16,25,16,128]{3,2,1,0:T(8,128)(2,1)}, u32[]{:S(2)}, u32[]{:S(2)}) collective-permute-start(bf16[16,25,16,128]{3,2,1,0:T(8,128)(2,1)S(1)} %get-tuple-element.72.refs_6_.refs_10_), channel_id=1, source_target_pairs={{0,1},{1,0},{2,3},{3,2},{4,5},{5,4},{6,7},{7,6},{8,9},{9,8},{10,11... | collective-permute-start | bytes 4915208 | tf_op jit(solution)/shard_map/ppermute | solution.py:549
  376.4 48.0 %collective-permute-start.29 = (bf16[8,64,320]{2,1,0:T(8,128)(2,1)}, bf16[8,64,320]{2,1,0:T(8,128)(2,1)}, u32[]{:S(2)}, u32[]{:S(2)}) collective-permute-start(bf16[8,64,320]{2,1,0:T(8,128)(2,1)} %get-tuple-element.76), channel_id=1, source_target_pairs={{0,8},{8,0},{16,24},{24,16},{1,9},{9,1},{17,25},{25,17},{2,10},{10... | collective-permute-start | bytes 983048 | tf_op jit(solution)/shard_map/ppermute | solution.py:588
  376.9 52.8 %collective-permute-start.32 = (bf16[12,25,16,128]{3,2,1,0:T(8,128)(2,1)}, bf16[12,25,16,128]{3,2,1,0:T(8,128)(2,1)}, u32[]{:S(2)}, u32[]{:S(2)}) collective-permute-start(bf16[12,25,16,128]{3,2,1,0:T(8,128)(2,1)} %copy-done.81), channel_id=1, source_target_pairs={{1,2},{2,1},{5,6},{6,5},{9,10},{10,9},{13,14},{14,13},{17,18},{18,... | collective-permute-start | bytes 3686408 | tf_op jit(solution)/shard_map/ppermute | solution.py:549
  381.8 64.6 %collective-permute-start.35 = (bf16[12,25,16,128]{3,2,1,0:T(8,128)(2,1)}, bf16[12,25,16,128]{3,2,1,0:T(8,128)(2,1)}, u32[]{:S(2)}, u32[]{:S(2)}) collective-permute-start(bf16[12,25,16,128]{3,2,1,0:T(8,128)(2,1)} %get-tuple-element.77.refs_10_), channel_id=1, source_target_pairs={{1,2},{2,1},{5,6},{6,5},{9,10},{10,9},{13,14},{14,13},{17,18},{18,... | collective-permute-start | bytes 3686408 | tf_op jit(solution)/shard_map/ppermute | solution.py:549
  431.2 78.7 %collective-permute-start.43 = (bf16[8,25,16,128]{3,2,1,0:T(8,128)(2,1)}, bf16[8,25,16,128]{3,2,1,0:T(8,128)(2,1)S(1)}, u32[]{:S(2)}, u32[]{:S(2)}) collective-permute-start(bf16[8,25,16,128]{3,2,1,0:T(8,128)(2,1)} %get-tuple-element.81.refs_10_), channel_id=1, source_target_pairs={{0,1},{1,0},{2,3},{3,2},{4,5},{5,4},{6,7},{7,6},{8,9},{9,8},{10,11... | collective-permute-start | bytes 2457608 | tf_op jit(solution)/shard_map/ppermute | solution.py:549
  443.1 48.2 %collective-permute-start.37 = (bf16[8,64,320]{2,1,0:T(8,128)(2,1)}, bf16[8,64,320]{2,1,0:T(8,128)(2,1)S(1)}, u32[]{:S(2)}, u32[]{:S(2)}) collective-permute-start(bf16[8,64,320]{2,1,0:T(8,128)(2,1)} %get-tuple-element.85), channel_id=1, source_target_pairs={{0,8},{8,0},{16,24},{24,16},{1,9},{9,1},{17,25},{25,17},{2,10},{10... | collective-permute-start | bytes 983048 | tf_op jit(solution)/shard_map/ppermute | solution.py:588
  443.2 48.1 %collective-permute-start.38 = (bf16[8,64,320]{2,1,0:T(8,128)(2,1)}, bf16[8,64,320]{2,1,0:T(8,128)(2,1)}, u32[]{:S(2)}, u32[]{:S(2)}) collective-permute-start(bf16[8,64,320]{2,1,0:T(8,128)(2,1)} %get-tuple-element.87), channel_id=1, source_target_pairs={{0,8},{8,0},{16,24},{24,16},{1,9},{9,1},{17,25},{25,17},{2,10},{10... | collective-permute-start | bytes 983048 | tf_op jit(solution)/shard_map/ppermute | solution.py:588
  450.2 59.7 %collective-permute-start.41 = (bf16[12,25,16,128]{3,2,1,0:T(8,128)(2,1)}, bf16[12,25,16,128]{3,2,1,0:T(8,128)(2,1)S(1)}, u32[]{:S(2)}, u32[]{:S(2)}) collective-permute-start(bf16[12,25,16,128]{3,2,1,0:T(8,128)(2,1)} %get-tuple-element.84.refs_10_), channel_id=1, source_target_pairs={{1,2},{2,1},{5,6},{6,5},{9,10},{10,9},{13,14},{14,13},{17,18},{18,... | collective-permute-start | bytes 3686408 | tf_op jit(solution)/shard_map/ppermute | solution.py:549
  511.7 55.5 %collective-permute-start.48 = (bf16[8,25,16,128]{3,2,1,0:T(8,128)(2,1)}, bf16[8,25,16,128]{3,2,1,0:T(8,128)(2,1)}, u32[]{:S(2)}, u32[]{:S(2)}) collective-permute-start(bf16[8,25,16,128]{3,2,1,0:T(8,128)(2,1)} %pass_on.11.refs_10_), channel_id=1, source_target_pairs={{0,1},{1,0},{2,3},{3,2},{4,5},{5,4},{6,7},{7,6},{8,9},{9,8},{10,11... | collective-permute-start | bytes 2457608 | tf_op jit(solution)/shard_map/ppermute | solution.py:549
  (129 other events, 1710.5 us)

commit v6 on v5

--- a/solution.py
+++ b/solution.py
@@ -9,6 +9,7 @@
 
 LANES = 128
 ROWS = 16
+VMEM_BYTES = 60 * 2 ** 20
 
 
 def split_sizes(total, count):
@@ -124,6 +125,7 @@
 
 def pack(spot, pieces, crossed, low, deps, given, group, plane, length):
     has_back = crossed is not None
+    pieces, turn = pieces
     given = dict(given, has_back=has_back)
     groups = given["groups"]
     out = [jax.ShapeDtypeStruct((length,) + plane, jnp.bfloat16)]
@@ -138,12 +140,13 @@
     got = pl.pallas_call(
         functools.partial(pack_kernel, group, len(pieces), given),
         out_shape=out,
+        grid=(1,),
         in_specs=[pl.BlockSpec(memory_space=pltpu.SMEM)]
-        + [pl.BlockSpec(memory_space=pltpu.VMEM)] * len(pieces)
+        + [pl.BlockSpec((None,) + piece.shape[1:], lambda g: (turn, 0, 0, 0, 0)) for piece in pieces]
         + [anywhere] * len(operands),
         out_specs=specs,
         scratch_shapes=[pltpu.SemaphoreType.DMA],
-        compiler_params=pltpu.CompilerParams(vmem_limit_bytes=32 * 2 ** 20),
+        compiler_params=pltpu.CompilerParams(vmem_limit_bytes=VMEM_BYTES),
         cost_estimate=pl.CostEstimate(flops=2 * 10 ** 9, bytes_accessed=6 * 2 ** 20, transcendentals=0),
         name="pack",
     )(spot, *pieces, *operands)
@@ -195,7 +198,7 @@
         in_specs=[pl.BlockSpec(memory_space=pltpu.SMEM)] + [anywhere] * len(operands),
         out_specs=[pl.BlockSpec(memory_space=pltpu.VMEM)] * len(out),
         scratch_shapes=[pltpu.SemaphoreType.DMA((3,))],
-        compiler_params=pltpu.CompilerParams(vmem_limit_bytes=32 * 2 ** 20),
+        compiler_params=pltpu.CompilerParams(vmem_limit_bytes=VMEM_BYTES),
         cost_estimate=pl.CostEstimate(flops=0, bytes_accessed=4 * 2 ** 20, transcendentals=0),
         name="pass_on",
     )(spot, *operands)
@@ -259,72 +262,105 @@
         out_shape=jax.ShapeDtypeStruct((2, total - rest + LANES, lanes), table.dtype),
         in_specs=[vmem] + [pl.BlockSpec(memory_space=pl.ANY)] * len(deps),
         out_specs=vmem,
+        compiler_params=pltpu.CompilerParams(vmem_limit_bytes=VMEM_BYTES),
         name="make_table",
     )(table, *deps)
 
 
-def low_kernel(one_ref, two_ref, out_ref):
-    group, slab, lanes = one_ref.shape
+def low_kernel(*refs):
+    parts, out_ref = refs[:-1], refs[-1]
+    group, slab, lanes = parts[0].shape
     out_ref[...] = jnp.zeros_like(out_ref)
     for k in range(group):
-        for half, ref in enumerate((one_ref, two_ref)):
-            out_ref[k * LANES:k * LANES + slab, half * lanes:(half + 1) * lanes] = ref[k]
-
-
-def make_lows(one, two, group):
-    depth, slab, lanes = one.shape
+        for at, ref in enumerate(parts):
+            out_ref[k * LANES:k * LANES + slab, at * lanes:(at + 1) * lanes] = ref[k]
+
+
+def make_lows(parts, group):
+    depth, slab, lanes = parts[0].shape
     block = pl.BlockSpec((group, slab, lanes), lambda g: (g, 0, 0))
     return pl.pallas_call(
         low_kernel,
-        out_shape=jax.ShapeDtypeStruct((depth * LANES, 2 * lanes), one.dtype),
+        out_shape=jax.ShapeDtypeStruct((depth * LANES, len(parts) * lanes), parts[0].dtype),
         grid=(depth // group,),
-        in_specs=[block, block],
-        out_specs=pl.BlockSpec((group * LANES, 2 * lanes), lambda g: (g, 0)),
-        compiler_params=pltpu.CompilerParams(vmem_limit_bytes=32 * 2 ** 20),
+        in_specs=[block] * len(parts),
+        out_specs=pl.BlockSpec((group * LANES, len(parts) * lanes), lambda g: (g, 0)),
+        compiler_params=pltpu.CompilerParams(vmem_limit_bytes=VMEM_BYTES),
         name="make_lows",
-    )(one, two)
-
-
-def planes_kernel(spans, depth, tiles, *refs):
+    )(*parts)
+
+
+def split_kernel(tiles, low_ref, out_ref):
+    group, rows = low_ref.shape[0], out_ref.shape[1]
+    for k in range(group):
+        for i in range(tiles[0]):
+            for j in range(tiles[1]):
+                out_ref[(k * tiles[0] + i) * tiles[1] + j] = low_ref[
+                    k, i * rows:(i + 1) * rows, j * LANES:(j + 1) * LANES
+                ]
+
+
+def make_planes(low, group, tiles, rows, planes):
+    depth, slab, lanes = low.shape
+    each = group * tiles[0] * tiles[1]
+    return pl.pallas_call(
+        functools.partial(split_kernel, tiles),
+        out_shape=jax.ShapeDtypeStruct((planes, rows, LANES), low.dtype),
+        grid=(depth // group,),
+        in_specs=[pl.BlockSpec((group, slab, lanes), lambda g: (g, 0, 0))],
+        out_specs=pl.BlockSpec((each, rows, LANES), lambda g: (g, 0, 0)),
+        compiler_params=pltpu.CompilerParams(vmem_limit_bytes=VMEM_BYTES),
+        name="make_planes",
+    )(low)
+
+
+def planes_kernel(spans, group, groups, tiles, *refs):
     parts = refs[:len(spans)]
     out_ref, held, sems = refs[-3:]
-    copies = [
-        pltpu.make_async_copy(ref.at[first:first + size], held.at[at:at + size], sems.at[i])
-        for i, (ref, (at, first, size)) in enumerate(zip(parts, spans))
-    ]
-    for copy in copies:
-        copy.start()
+    step = pl.program_id(0)
+
+    @pl.when(step == 0)
+    def _():
+        copies = [
+            pltpu.make_async_copy(ref.at[first:first + size], held.at[at:at + size], sems.at[i])
+            for i, (ref, (at, first, size)) in enumerate(zip(parts, spans))
+        ]
+        for copy in copies:
+            copy.start()
+        for copy in copies:
+            copy.wait()
+
     out_ref[...] = jnp.zeros_like(out_ref)
-    for copy in copies:
-        copy.wait()
     planes, rows = held.shape[1], held.shape[2]
-
-    def one(k, _):
+    each = group * tiles[0] * tiles[1]
+    for k in range(group):
         for i in range(tiles[0]):
             for j in range(tiles[1]):
-                plane = (k * tiles[0] + i) * tiles[1] + j
-                out_ref[
-                    pl.ds(pl.multiple_of(k * LANES + i * rows, rows), rows), j * LANES:(j + 1) * LANES
-                ] = held[plane // planes, plane % planes]
-        return 0
-
-    lax.fori_loop(0, depth, one, 0)
-
-
-def low_of_planes(parts, deps, units, depth, tiles):
+                at = (k * tiles[0] + i) * tiles[1] + j
+                if groups == 1:
+                    plane = held[at // planes, at % planes]
+                elif each % planes == 0:
+                    plane = held[step * (each // planes) + at // planes, at % planes]
+                else:
+                    plane = held[(step * each + at) // planes, (step * each + at) % planes]
+                out_ref[k * LANES + i * rows:k * LANES + (i + 1) * rows, j * LANES:(j + 1) * LANES] = plane
+
+
+def low_of_planes(parts, deps, units, group, groups, tiles):
     spans = [(at, first, size) for at, _, first, size in parts]
     shape = parts[0][1].shape[1:]
     anywhere = pl.BlockSpec(memory_space=pl.ANY)
     return pl.pallas_call(
-        functools.partial(planes_kernel, spans, depth, tiles),
-        out_shape=jax.ShapeDtypeStruct((depth * LANES, tiles[1] * LANES), jnp.bfloat16),
+        functools.partial(planes_kernel, spans, group, groups, tiles),
+        out_shape=jax.ShapeDtypeStruct((groups * group * LANES, tiles[1] * LANES), jnp.bfloat16),
+        grid=(groups,),
         in_specs=[anywhere] * (len(parts) + len(deps)),
-        out_specs=pl.BlockSpec(memory_space=pltpu.VMEM),
+        out_specs=pl.BlockSpec((group * LANES, tiles[1] * LANES), lambda g: (g, 0)),
         scratch_shapes=[
             pltpu.VMEM((units,) + shape, jnp.bfloat16),
             pltpu.SemaphoreType.DMA((len(parts),)),
         ],
-        compiler_params=pltpu.CompilerParams(vmem_limit_bytes=40 * 2 ** 20),
+        compiler_params=pltpu.CompilerParams(vmem_limit_bytes=VMEM_BYTES),
         name="low_of_planes",
     )(*[got for _, got, _, _ in parts], *deps)
 
@@ -345,7 +381,7 @@
         out_shape=[jax.ShapeDtypeStruct(a.shape, kind) for (a, _), kind in zip(pairs, types)],
         in_specs=[vmem] * (2 * len(pairs)) + [pl.BlockSpec(memory_space=pl.ANY)] * len(deps),
         out_specs=[vmem] * len(pairs),
-        compiler_params=pltpu.CompilerParams(vmem_limit_bytes=32 * 2 ** 20),
+        compiler_params=pltpu.CompilerParams(vmem_limit_bytes=VMEM_BYTES),
         name="join",
     )(*[x for pair in pairs for x in pair], *deps)
 
@@ -401,7 +437,12 @@
     full = low.shape[-1] // 2
     count = windows * sides * rows
     whole = lambda arr: pl.BlockSpec(arr.shape, lambda g, s: (0,) * len(arr.shape))
-    part = pl.BlockSpec((group * LANES, 2 * full), lambda g, s: (g, 0))
+
+    def busy(spot_ref):
+        end = jnp.logical_or(spot_ref[0] == 0, spot_ref[0] == sides - 1)
+        return jnp.where(jnp.where(end, use_ends, use_inner), 1, 0)
+
+    part = pl.BlockSpec((group * LANES, 2 * full), lambda g, s: (g * busy(s), 0))
     out = jax.ShapeDtypeStruct((2, count, full), jnp.float32)
     depth = groups * group
     flops = 2 * count * depth * LANES * 3 * full + 4 * sides * rows * depth * 3 * LANES * windows * LANES
@@ -421,7 +462,7 @@
                 pltpu.SemaphoreType.DMA((sides,)),
             ],
         ),
-        compiler_params=pltpu.CompilerParams(vmem_limit_bytes=56 * 2 ** 20),
+        compiler_params=pltpu.CompilerParams(vmem_limit_bytes=VMEM_BYTES),
         cost_estimate=pl.CostEstimate(flops=flops, bytes_accessed=20 * 2 ** 20, transcendentals=0),
         name="even_product",
     )(spot, *[ref for ref, _ in blocks], table, low, *deps)
@@ -458,8 +499,8 @@
         expand(odd, step, group, groups, (tables, next_tables), spread)
         count = spread.shape[1] * spread.shape[2]
         rows = spread[...].reshape(2, count, group * LANES)
-        got = jnp.dot(rows[0], low_ref[...], preferred_element_type=jnp.float32)
-        total[1] += got + jnp.dot(rows[1], next_low_ref[...], preferred_element_type=jnp.float32)
+        total[1] += jnp.dot(rows[0], low_ref[...], preferred_element_type=jnp.float32)
+        total[1] += jnp.dot(rows[1], next_low_ref[...], preferred_element_type=jnp.float32)
 
     @pl.when(step == last)
     def _():
@@ -480,7 +521,11 @@
     full = low.shape[-1]
     count = windows * sides * rows
     whole = lambda arr: pl.BlockSpec(arr.shape, lambda g, s: (0,) * len(arr.shape))
-    part = pl.BlockSpec((group * LANES, full), lambda g, s: (g, 0))
+
+    def busy(spot_ref):
+        return jnp.where(jnp.logical_or(spot_ref[0] == 0, spot_ref[0] == sides - 1), 0, 1)
+
+    part = pl.BlockSpec((group * LANES, full), lambda g, s: (g * busy(s), 0))
     out = [jax.ShapeDtypeStruct((windows, sides * rows, full // 2), jnp.bfloat16)] * outs
     depth = groups * group
     flops = 2 * count * depth * LANES * 2 * full + 4 * sides * rows * depth * 3 * LANES * windows * LANES
@@ -501,7 +546,7 @@
                 pltpu.SemaphoreType.DMA((sides + 1,)),
             ],
         ),
-        compiler_params=pltpu.CompilerParams(vmem_limit_bytes=56 * 2 ** 20),
+        compiler_params=pltpu.CompilerParams(vmem_limit_bytes=VMEM_BYTES),
         cost_estimate=pl.CostEstimate(flops=flops, bytes_accessed=20 * 2 ** 20, transcendentals=0),
         name="odd_product",
     )(spot, *[ref for ref, _ in blocks], inner_part, end_part, table, next_table, low, next_low, *deps)
@@ -526,16 +571,17 @@
 
     cut = tops.reshape(kinds, depth_all, contrs, chunks, unit, width)
 
-    def exchange(t, place):
-        pieces = []
+    def exchange(first, count, place):
+        got = []
         for s in range(roles):
             piece = lax.dynamic_slice(
-                cut, (0, (place ^ s) * depth, 0, t, 0, 0), (kinds, depth, contrs, 1, unit, width)
-            ).reshape(kinds, depth, rows, width)
+                cut, (0, (place ^ s) * depth, 0, first, 0, 0), (kinds, depth, contrs, count, unit, width)
+            ).transpose(3, 0, 1, 2, 4, 5).reshape(count, kinds, depth, rows, width)
             if s:
                 piece = lax.ppermute(piece, "role", [(j, j ^ s) for j in range(roles)])
-            pieces.append(piece)
-        return pieces
+            got.append(piece)
+        for t in range(count):
+            pieces[first + t] = (got, t)
 
     def lower(kind, place):
         low = lax.dynamic_slice(
@@ -548,7 +594,8 @@
     cross = [(z, z ^ 3) for z in range(1, sides - 1)]
     move = lambda value, perm: lax.ppermute(value, "horiz", perm)
 
-    pieces = {0: exchange(0, role)}
+    pieces = {}
+    exchange(0, 1, role)
     left_all = jnp.concatenate(
         [lax.dynamic_slice_in_dim(left_iso, (role ^ s) * width, width, 0) for s in range(roles)], axis=0
     )
@@ -566,10 +613,7 @@
     tiles = (slab // rows, downs * full // LANES)
     count = depth * tiles[0] * tiles[1]
     units = -(-count // plane[0])
-    carried = middle.reshape(depth, tiles[0], rows, tiles[1], LANES).transpose(0, 1, 3, 2, 4)
-    carried = carried.reshape(count, rows, LANES)
-    carried = jnp.pad(carried, ((0, units * plane[0] - count), (0, 0), (0, 0)))
-    carried = carried.reshape((units,) + plane)
+    carried = make_planes(middle, group, tiles, rows, units * plane[0]).reshape((units,) + plane)
     taken = 0
 
     def take(most):
@@ -627,7 +671,7 @@
             deps = [sent[r - 1]] if r else []
             deps += [sums[r - 1]] if r - 1 in sums else []
             out, mine, mark = pack(
-                spot, pieces.pop(r) if fresh else [], straight.get(r - 1), carried, deps + extra, given,
+                spot, pieces.pop(r) if fresh else ([], 0), straight.get(r - 1), carried, deps + extra, given,
                 group, plane, length,
             )
             extra = []
@@ -638,23 +682,20 @@
                 own[r] = mine
                 straight[r] = move(mine, cross)
             done = out
-            for t in {0: (1, 2), 1: (3,), 2: (4,)}.get(r, (r + 2,)):
-                if t < chunks:
-                    pieces[t] = exchange(t, mark[1])
+            if 2 * r + 1 < chunks:
+                exchange(2 * r + 1, min(2, chunks - 2 * r - 1), mark[1])
             if r == 0:
                 late = mark[1]
                 first_table = make_table(table(flat_left), [out], rest)
-                low = make_lows(lower(0, late), lower(2, late), group)
+                low = make_lows([lower(0, late), lower(2, late)], group)
                 near_left = move(flat_left, hand)
-                extra = [low, first_table]
-            if r == 1:
-                near_table = make_table(table(near_left), [out], rest)
-                middle_low = low_of_planes([(0, carried, 0, units)], [out], units, depth, tiles)
-                extra = [near_table, middle_low]
         t = r - 4
         if 0 <= t < chunks:
             if near_low is None:
-                near_low = low_of_planes(sorted(parts, key=lambda p: p[0]), [done], units, depth, tiles)
+                near_low = low_of_planes(
+                    sorted(parts, key=lambda p: p[0]), [done], units, group, groups, tiles
+                )
+                near_table = make_table(table(near_left), [done], rest)
             blocks = [(own[t], 2 * groups), (sent[t], 2 * groups), (straight[t], 2 * groups), (turned[t + 1], 2 * groups)]
             shares[t] = odd_product(
                 spot, blocks, sums[t + 2], sums[t + 3], [done] + extra, (first_table, near_table),
@@ -678,6 +719,10 @@
                 if size:
                     parts.append((at, last[r], 0, size))
             done = outs[0]
+        if r == 1:
+            extra = [low, first_table]
+        if r == 2:
+            middle_low = make_lows([middle], group)
         if r >= 2:
             t = r - 2
             inner_blocks = end_blocks = None

time: 698 us -> 661 us (0.947)
  waiting for transfers between devices: 140 us -> 99.1 us
  local copies, waits for them, and re-layouts: 133 us -> 105 us
  Pallas kernels: 252 us -> 269 us
  starting transfers between devices: 138 us -> 154 us
    ppermute x22, waiting for transfers between devices: 68.6 us -> 3.94 us  [on_device(): move = lambda value, perm: lax.ppermute(value, 'horiz', perm)]
    unnamed x178 -> x94, local copies, waits for them, and re-layouts: 65.1 us -> 30.3 us
    ppermute x15 -> x9, waiting for transfers between devices: 25.6 us -> 53 us  [exchange(): piece = lax.ppermute(piece, 'role', [(j, j ^ s) for j in range(roles)])]
    pallas_call x15, Pallas kernels: 5.34 us -> 32.4 us  [join(): pl.pallas_call(functools.partial(join_kernel, len(pairs)), out_shape=[jax...]
    ppermute x22, starting transfers between devices: 93.6 us -> 119 us  [on_device(): move = lambda value, perm: lax.ppermute(value, 'horiz', perm)]
    pallas_call x5, Pallas kernels: 53.9 us -> 38.3 us  [odd_product(): pl.pallas_call(functools.partial(odd_kernel, sides, group, groups, outs,...]
    pallas_call x1 -> x2, Pallas kernels: 1.32 us -> 14.3 us  [make_lows(): pl.pallas_call(low_kernel, out_shape=jax.ShapeDtypeStruct((depth * LANES,...]
    pallas_call x2, Pallas kernels: 21.2 us -> 10.4 us  [the longest x1 5.53 us: low_of_planes(): pl.pallas_call(functools.partial(planes_kernel, spans, group, groups, til...]
  transfers between devices with their start and end apart: 66 -> 60, of which waited for: 20 -> 16; matrix products, arithmetic and copies ran while one was open for 11% -> 13% of each run, Pallas kernels for 33% -> 38%
where the time goes in v6:
time: 661 us; the launch traced here: 649 us
  Pallas kernels  269 us (41%)
  starting transfers between devices  154 us (23%)
  local copies, waits for them, and re-layouts  105 us (16%)
  waiting for transfers between devices  99.1 us (15%)
  other arithmetic  11.1 us (2%)
    pallas_call x6, Pallas kernels, even_product(): pl.pallas_call(functools.partial(even_kernel, sides, group, groups, use_e...  124 us
    ppermute x22, starting transfers between devices, on_device(): move = lambda value, perm: lax.ppermute(value, 'horiz', perm)  119 us
    ppermute x9, waiting for transfers between devices, exchange(): piece = lax.ppermute(piece, 'role', [(j, j ^ s) for j in range(roles)])  53 us
    pallas_call x5, Pallas kernels, odd_product(): pl.pallas_call(functools.partial(odd_kernel, sides, group, groups, outs,...  38.3 us
    pallas_call x15, Pallas kernels, join(): pl.pallas_call(functools.partial(join_kernel, len(pairs)), out_shape=[jax...  32.4 us
    unnamed x94, local copies, waits for them, and re-layouts  30.3 us
    pallas_call x6, Pallas kernels, pack(): pl.pallas_call(functools.partial(pack_kernel, group, len(pieces), given),...  26.9 us
    reshape x2, local copies, waits for them, and re-layouts, lower(): return low.reshape(depth, slab, downs * full)  21.1 us
  transfers between devices with their start and end apart: 60, of which 16 were waited for; matrix products, arithmetic and copies ran while one was open for 13% of the time, Pallas kernels for 38%

profile of v6, /device:TPU:0, one launch (start us, length us, event | category | flops | bytes accessed | tf_op | source)
XLA Modules:
  0.0 649.0 jit_solution(11680654714451885316)
XLA Ops:
  5.8 8.6 %dynamic-slice_multiply_fusion = bf16[1,40,80,2,320]{4,3,2,1,0:T(2,128)(2,1)} fusion(bf16[3,160,80,2,320]{4,3,2,1,0:T(2,128)(2,1)} %param.5, s32[]{:T(128)S(6)} %select_n.115), kind=kLoop, calls=%fused_computation | loop fusion | flops 2048000 | bytes 8192004 | tf_op jit(solution)/shard_map/mul | solution.py:612
  14.4 10.5 %mul.109.low_ref.refs_0_ = bf16[40,80,640]{2,1,0:T(8,128)(2,1)} reshape(bf16[1,40,80,2,320]{4,3,2,1,0:T(2,128)(2,1)} %dynamic-slice_multiply_fusion) | data formatting | bytes 8192000 | tf_op jit(solution)/shard_map/mul | solution.py:612
  50.4 21.3 %collective-permute-done.6.refs_2_ = bf16[2,3,40,16,80]{4,3,2,1,0:T(8,128)(2,1)S(1)} collective-permute-done((bf16[2,3,40,16,80]{4,3,2,1,0:T(8,128)(2,1)S(1)}, bf16[2,3,40,16,80]{4,3,2,1,0:T(8,128)(2,1)S(1)}, u32[]{:S(2)}, u32[]{:S(2)}) %collective-permute-start.6) | collective-permute-done | bytes 614432 | tf_op jit(solution)/shard_map/ppermute | solution.py:581
  71.8 20.3 %collective-permute-done.7.refs_3_ = bf16[2,3,40,16,80]{4,3,2,1,0:T(8,128)(2,1)S(1)} collective-permute-done((bf16[2,3,40,16,80]{4,3,2,1,0:T(8,128)(2,1)S(1)}, bf16[2,3,40,16,80]{4,3,2,1,0:T(8,128)(2,1)S(1)}, u32[]{:S(2)}, u32[]{:S(2)}) %collective-permute-start.7) | collective-permute-done | bytes 614432 | tf_op jit(solution)/shard_map/ppermute | solution.py:581
  125.8 9.6 %constant_dynamic-slice_fusion.13 = (bf16[1,40,80,2,320]{4,3,2,1,0:T(2,128)(2,1)}, bf16[1,40,80,2,320]{4,3,2,1,0:T(2,128)(2,1)}) fusion(bf16[3,160,80,2,320]{4,3,2,1,0:T(2,128)(2,1)} %param.5, s32[]{:T(128)S(6)} %select_n.119), kind=kLoop, calls=%fused_computation.47 | loop fusion | bytes 16384004 | tf_op jit(solution)/shard_map/dynamic_slice | solution.py:587
  137.8 10.5 %reshape.106.refs_0_ = bf16[40,80,640]{2,1,0:T(8,128)(2,1)} reshape(bf16[1,40,80,2,320]{4,3,2,1,0:T(2,128)(2,1)} %get-tuple-element.108) | data formatting | bytes 8192000 | tf_op jit(solution)/shard_map/reshape | solution.py:590
  148.3 10.5 %reshape.107.refs_1_ = bf16[40,80,640]{2,1,0:T(8,128)(2,1)} reshape(bf16[1,40,80,2,320]{4,3,2,1,0:T(2,128)(2,1)} %get-tuple-element.107) | data formatting | bytes 8192000 | tf_op jit(solution)/shard_map/reshape | solution.py:590
  158.9 8.8 %make_lows.2.refs_7_.refs_9_ = bf16[5120,1280]{1,0:T(8,128)(2,1)} custom-call(bf16[40,80,640]{2,1,0:T(8,128)(2,1)} %reshape.106.refs_0_, bf16[40,80,640]{2,1,0:T(8,128)(2,1)} %reshape.107.refs_1_), custom_call_target="tpu_custom_call" | custom-call | tf_op jit(solution)/shard_map/make_lows/pallas_call | solution.py:282
  192.9 11.5 %collective-permute-done.16.refs_3_ = bf16[2,3,40,16,80]{4,3,2,1,0:T(8,128)(2,1)S(1)} collective-permute-done((bf16[2,3,40,16,80]{4,3,2,1,0:T(8,128)(2,1)}, bf16[2,3,40,16,80]{4,3,2,1,0:T(8,128)(2,1)S(1)}, u32[]{:S(2)}, u32[]{:S(2)}) %collective-permute-start.16) | collective-permute-done | bytes 614432 | tf_op jit(solution)/shard_map/ppermute | solution.py:581
  204.3 12.7 %collective-permute-start.18 = (bf16[320,640]{0,1:T(8,128)(2,1)}, bf16[320,640]{0,1:T(8,128)(2,1)}, u32[]{:S(2)}, u32[]{:S(2)}) collective-permute-start(bf16[320,640]{0,1:T(8,128)(2,1)} %bitcast.34), channel_id=1, source_target_pairs={{0,1},{3,2},{4,5},{7,6},{8,9},{11,10},{12,13},{15,14},{16,17},{19,... | collective-permute-start | bytes 1228808 | tf_op jit(solution)/shard_map/ppermute | solution.py:595
  223.2 24.9 %collective-permute-start.20 = (bf16[16,25,16,128]{3,2,1,0:T(8,128)(2,1)}, bf16[16,25,16,128]{3,2,1,0:T(8,128)(2,1)S(1)}, u32[]{:S(2)}, u32[]{:S(2)}) collective-permute-start(bf16[16,25,16,128]{3,2,1,0:T(8,128)(2,1)} %get-tuple-element.66.refs_3_), channel_id=1, source_target_pairs={{0,1},{1,0},{2,3},{3,2},{4,5},{5,4},{6,7},{7,6},{8,9},{9,8},{10,11... | collective-permute-start | bytes 4915208 | tf_op jit(solution)/shard_map/ppermute | solution.py:595
  264.2 23.8 %even_product.7.refs_7_.refs_5_.refs_4_ = f32[2,512,640]{2,1,0:T(8,128)} custom-call(s32[2]{0:T(128)} %pad_add_fusion.spot_ref, bf16[12,25,16,128]{3,2,1,0:T(8,128)(2,1)} %get-tuple-element.60.refs_0_.refs_4_, bf16[24,25,16,128]{3,2,1,0:T(8,128)(2,1)} %copy-done, bf16[12,25,16,128]{3,2,1,0:T(8,128)(2,1)} %collective-permute-done.10.refs_4_.refs_2_, ...), custom_call_target="tpu_custom_call" | custom-call | flops 14092861440 | bytes 20971520 | tf_op jit(solution)/shard_map/even_product/pallas_call | solution.py:449
  322.0 23.8 %even_product.8.refs_4_.refs_3_.refs_5_ = f32[2,512,640]{2,1,0:T(8,128)} custom-call(s32[2]{0:T(128)} %pad_add_fusion.spot_ref, bf16[12,25,16,128]{3,2,1,0:T(8,128)(2,1)} %get-tuple-element.65.refs_0_.refs_4_, bf16[16,25,16,128]{3,2,1,0:T(8,128)(2,1)} %copy-done.2, bf16[12,25,16,128]{3,2,1,0:T(8,128)(2,1)} %collective-permute-done.17.refs_4_.refs_2_, ...), custom_call_target="tpu_custom_call" | custom-call | flops 14092861440 | bytes 20971520 | tf_op jit(solution)/shard_map/even_product/pallas_call | solution.py:449
  345.8 21.8 %collective-permute-start.30 = (bf16[8,25,16,128]{3,2,1,0:T(8,128)(2,1)}, bf16[8,25,16,128]{3,2,1,0:T(8,128)(2,1)}, u32[]{:S(2)}, u32[]{:S(2)}) collective-permute-start(bf16[8,25,16,128]{3,2,1,0:T(8,128)(2,1)} %get-tuple-element.81), channel_id=1, source_target_pairs={{0,1},{1,0},{2,3},{3,2},{4,5},{5,4},{6,7},{7,6},{8,9},{9,8},{10,11... | collective-permute-start | bytes 2457608 | tf_op jit(solution)/shard_map/ppermute | solution.py:595
  375.9 7.5 %odd_product.6 = (bf16[8,64,320]{2,1,0:T(8,128)(2,1)}, bf16[8,64,320]{2,1,0:T(8,128)(2,1)}, bf16[8,64,320]{2,1,0:T(8,128)(2,1)}, bf16[8,64,320]{2,1,0:T(8,128)(2,1)}) custom-call(s32[2]{0:T(128)} %pad_add_fusion.spot_ref, bf16[12,25,16,128]{3,2,1,0:T(8,128)(2,1)} %get-tuple-element.60.refs_0_.refs_4_, bf16[24,25,16,128]{3,2,1,0:T(8,128)(2,1)} %copy-done, ...), custom_call_target="tpu_custom_call" | custom-call | flops 10737418240 | bytes 20971520 | tf_op jit(solution)/shard_map/odd_product/pallas_call | solution.py:532
  394.8 23.7 %even_product.9.refs_2_.refs_4_.refs_5_.refs_10_ = f32[2,512,640]{2,1,0:T(8,128)} custom-call(s32[2]{0:T(128)} %pad_add_fusion.spot_ref, bf16[12,25,16,128]{3,2,1,0:T(8,128)(2,1)} %get-tuple-element.68.refs_0_.refs_4_, bf16[16,25,16,128]{3,2,1,0:T(8,128)(2,1)} %copy-done.3, bf16[12,25,16,128]{3,2,1,0:T(8,128)(2,1)} %collective-permute-done.19.refs_4_.refs_2_, ...), custom_call_target="tpu_custom_call" | custom-call | flops 14092861440 | bytes 20971520 | tf_op jit(solution)/shard_map/even_product/pallas_call | solution.py:449
  419.3 17.6 %collective-permute-start.36 = (bf16[8,25,16,128]{3,2,1,0:T(8,128)(2,1)}, bf16[8,25,16,128]{3,2,1,0:T(8,128)(2,1)S(1)}, u32[]{:S(2)}, u32[]{:S(2)}) collective-permute-start(bf16[8,25,16,128]{3,2,1,0:T(8,128)(2,1)} %get-tuple-element.89), channel_id=1, source_target_pairs={{0,1},{1,0},{2,3},{3,2},{4,5},{5,4},{6,7},{7,6},{8,9},{9,8},{10,11... | collective-permute-start | bytes 2457608 | tf_op jit(solution)/shard_map/ppermute | solution.py:595
  463.4 14.2 %collective-permute-start.42 = (bf16[8,25,16,128]{3,2,1,0:T(8,128)(2,1)}, bf16[8,25,16,128]{3,2,1,0:T(8,128)(2,1)S(1)}, u32[]{:S(2)}, u32[]{:S(2)}) collective-permute-start(bf16[8,25,16,128]{3,2,1,0:T(8,128)(2,1)} %pass_on.11.refs_10_), channel_id=1, source_target_pairs={{0,1},{1,0},{2,3},{3,2},{4,5},{5,4},{6,7},{7,6},{8,9},{9,8},{10,11... | collective-permute-start | bytes 2457608 | tf_op jit(solution)/shard_map/ppermute | solution.py:595
  477.6 23.7 %even_product.10.refs_2_.refs_4_.refs_5_.refs_10_ = f32[2,512,640]{2,1,0:T(8,128)} custom-call(s32[2]{0:T(128)} %pad_add_fusion.spot_ref, bf16[12,25,16,128]{3,2,1,0:T(8,128)(2,1)} %get-tuple-element.78.refs_0_.refs_4_, bf16[16,25,16,128]{3,2,1,0:T(8,128)(2,1)} %copy-done.4, bf16[12,25,16,128]{3,2,1,0:T(8,128)(2,1)} %copy-done.18, ...), custom_call_target="tpu_custom_call" | custom-call | flops 14092861440 | bytes 20971520 | tf_op jit(solution)/shard_map/even_product/pallas_call | solution.py:449
  508.8 7.8 %odd_product.8 = (bf16[8,64,320]{2,1,0:T(8,128)(2,1)}, bf16[8,64,320]{2,1,0:T(8,128)(2,1)}, bf16[8,64,320]{2,1,0:T(8,128)(2,1)}, bf16[8,64,320]{2,1,0:T(8,128)(2,1)}) custom-call(s32[2]{0:T(128)} %pad_add_fusion.spot_ref, bf16[12,25,16,128]{3,2,1,0:T(8,128)(2,1)} %get-tuple-element.68.refs_0_.refs_4_, bf16[16,25,16,128]{3,2,1,0:T(8,128)(2,1)} %copy-done.3, ...), custom_call_target="tpu_custom_call" | custom-call | flops 10737418240 | bytes 20971520 | tf_op jit(solution)/shard_map/odd_product/pallas_call | solution.py:532
  525.3 23.7 %even_product.11.refs_2_.refs_4_.refs_5_.refs_10_ = f32[2,512,640]{2,1,0:T(8,128)} custom-call(s32[2]{0:T(128)} %pad_add_fusion.spot_ref, bf16[12,25,16,128]{3,2,1,0:T(8,128)(2,1)} %get-tuple-element.78.refs_0_.refs_4_, bf16[16,25,16,128]{3,2,1,0:T(8,128)(2,1)} %copy-done.4, bf16[8,25,16,128]{3,2,1,0:T(8,128)(2,1)} %copy-done.19, ...), custom_call_target="tpu_custom_call" | custom-call | flops 14092861440 | bytes 20971520 | tf_op jit(solution)/shard_map/even_product/pallas_call | solution.py:449
  554.9 7.9 %odd_product.9 = (bf16[8,64,320]{2,1,0:T(8,128)(2,1)}, bf16[8,64,320]{2,1,0:T(8,128)(2,1)}, bf16[8,64,320]{2,1,0:T(8,128)(2,1)}, bf16[8,64,320]{2,1,0:T(8,128)(2,1)}) custom-call(s32[2]{0:T(128)} %pad_add_fusion.spot_ref, bf16[12,25,16,128]{3,2,1,0:T(8,128)(2,1)} %get-tuple-element.78.refs_0_.refs_4_, bf16[16,25,16,128]{3,2,1,0:T(8,128)(2,1)} %copy-done.4, ...), custom_call_target="tpu_custom_call" | custom-call | flops 10737418240 | bytes 20971520 | tf_op jit(solution)/shard_map/odd_product/pallas_call | solution.py:532
  603.9 10.1 %collective-permute-start.52 = (bf16[8,1,40,320]{3,2,1,0:T(8,128)(2,1)S(1)}, bf16[8,1,40,320]{3,2,1,0:T(8,128)(2,1)S(1)}, u32[]{:S(2)}, u32[]{:S(2)}) collective-permute-start(bf16[8,1,40,320]{3,2,1,0:T(8,128)(2,1)S(1)} %get-tuple-element.123), channel_id=1, source_target_pairs={{0,2},{1,3},{2,0},{3,1},{4,6},{5,7},{6,4},{7,5},{8,10},{9,11},{10,... | collective-permute-start | bytes 614408 | tf_op jit(solution)/shard_map/ppermute | solution.py:762
  614.3 12.4 %collective-permute-done.52 = bf16[8,1,40,320]{3,2,1,0:T(8,128)(2,1)S(1)} collective-permute-done((bf16[8,1,40,320]{3,2,1,0:T(8,128)(2,1)S(1)}, bf16[8,1,40,320]{3,2,1,0:T(8,128)(2,1)S(1)}, u32[]{:S(2)}, u32[]{:S(2)}) %collective-permute-start.52) | collective-permute-done | bytes 204832 | tf_op jit(solution)/shard_map/ppermute | solution.py:762
  (271 shorter events, 275.4 us)
Async XLA Ops:
  36.5 55.5 %collective-permute-start.3 = (bf16[20,25,16,128]{3,2,1,0:T(8,128)(2,1)}, bf16[20,25,16,128]{3,2,1,0:T(8,128)(2,1)S(1)}, u32[]{:S(2)}, u32[]{:S(2)}) collective-permute-start(bf16[20,25,16,128]{3,2,1,0:T(8,128)(2,1)} %get-tuple-element.57.refs_0_), channel_id=1, source_target_pairs={{0,1},{1,0},{2,3},{3,2},{4,5},{5,4},{6,7},{7,6},{8,9},{9,8},{10,11... | collective-permute-start | bytes 6144008 | tf_op jit(solution)/shard_map/ppermute | solution.py:595
  38.4 53.7 %collective-permute-start.4 = (bf16[12,25,16,128]{3,2,1,0:T(8,128)(2,1)}, bf16[12,25,16,128]{3,2,1,0:T(8,128)(2,1)}, u32[]{:S(2)}, u32[]{:S(2)}) collective-permute-start(bf16[12,25,16,128]{3,2,1,0:T(8,128)(2,1)} %get-tuple-element.56.refs_0_.refs_4_), channel_id=1, source_target_pairs={{1,2},{2,1},{5,6},{6,5},{9,10},{10,9},{13,14},{14,13},{17,18},{18,... | collective-permute-start | bytes 3686408 | tf_op jit(solution)/shard_map/ppermute | solution.py:595
  99.6 68.0 %collective-permute-start.9 = (bf16[24,25,16,128]{3,2,1,0:T(8,128)(2,1)}, bf16[24,25,16,128]{3,2,1,0:T(8,128)(2,1)S(1)}, u32[]{:S(2)}, u32[]{:S(2)}) collective-permute-start(bf16[24,25,16,128]{3,2,1,0:T(8,128)(2,1)} %get-tuple-element.59.refs_3_), channel_id=1, source_target_pairs={{0,1},{1,0},{2,3},{3,2},{4,5},{5,4},{6,7},{7,6},{8,9},{9,8},{10,11... | collective-permute-start | bytes 7372808 | tf_op jit(solution)/shard_map/ppermute | solution.py:595
  103.1 64.6 %collective-permute-start.10 = (bf16[12,25,16,128]{3,2,1,0:T(8,128)(2,1)}, bf16[12,25,16,128]{3,2,1,0:T(8,128)(2,1)}, u32[]{:S(2)}, u32[]{:S(2)}) collective-permute-start(bf16[12,25,16,128]{3,2,1,0:T(8,128)(2,1)} %get-tuple-element.60.refs_0_.refs_4_), channel_id=1, source_target_pairs={{1,2},{2,1},{5,6},{6,5},{9,10},{10,9},{13,14},{14,13},{17,18},{18,... | collective-permute-start | bytes 3686408 | tf_op jit(solution)/shard_map/ppermute | solution.py:595
  116.4 63.9 %collective-permute-start.8 = (bf16[12,25,16,128]{3,2,1,0:T(8,128)(2,1)}, bf16[12,25,16,128]{3,2,1,0:T(8,128)(2,1)}, u32[]{:S(2)}, u32[]{:S(2)}) collective-permute-start(bf16[12,25,16,128]{3,2,1,0:T(8,128)(2,1)} %pass_on.6), channel_id=1, source_target_pairs={{1,2},{2,1},{5,6},{6,5},{9,10},{10,9},{13,14},{14,13},{17,18},{18,... | collective-permute-start | bytes 3686408 | tf_op jit(solution)/shard_map/ppermute | solution.py:595
  123.2 62.3 %collective-permute-start.14 = (bf16[2,3,40,16,80]{4,3,2,1,0:T(8,128)(2,1)}, bf16[2,3,40,16,80]{4,3,2,1,0:T(8,128)(2,1)}, u32[]{:S(2)}, u32[]{:S(2)}) collective-permute-start(bf16[2,3,40,16,80]{4,3,2,1,0:T(8,128)(2,1)} %bitcast.83), channel_id=1, source_target_pairs={{0,8},{8,0},{16,24},{24,16},{1,9},{9,1},{17,25},{25,17},{2,10},{10... | collective-permute-start | bytes 1843208 | tf_op jit(solution)/shard_map/ppermute | solution.py:581
  124.3 61.9 %collective-permute-start.15 = (bf16[2,3,40,16,80]{4,3,2,1,0:T(8,128)(2,1)}, bf16[2,3,40,16,80]{4,3,2,1,0:T(8,128)(2,1)}, u32[]{:S(2)}, u32[]{:S(2)}) collective-permute-start(bf16[2,3,40,16,80]{4,3,2,1,0:T(8,128)(2,1)} %bitcast.82), channel_id=1, source_target_pairs={{0,16},{8,24},{16,0},{24,8},{1,17},{9,25},{17,1},{25,9},{2,18},{10... | collective-permute-start | bytes 1843208 | tf_op jit(solution)/shard_map/ppermute | solution.py:581
  183.8 73.7 %collective-permute-start.11 = (bf16[12,25,16,128]{3,2,1,0:T(8,128)(2,1)}, bf16[12,25,16,128]{3,2,1,0:T(8,128)(2,1)}, u32[]{:S(2)}, u32[]{:S(2)}) collective-permute-start(bf16[12,25,16,128]{3,2,1,0:T(8,128)(2,1)} %get-tuple-element.62.refs_10_), channel_id=1, source_target_pairs={{1,2},{2,1},{5,6},{6,5},{9,10},{10,9},{13,14},{14,13},{17,18},{18,... | collective-permute-start | bytes 3686408 | tf_op jit(solution)/shard_map/ppermute | solution.py:595
  185.5 72.0 %collective-permute-start.12 = (bf16[8,25,16,128]{3,2,1,0:T(8,128)(2,1)}, bf16[8,25,16,128]{3,2,1,0:T(8,128)(2,1)S(1)}, u32[]{:S(2)}, u32[]{:S(2)}) collective-permute-start(bf16[8,25,16,128]{3,2,1,0:T(8,128)(2,1)} %get-tuple-element.63), channel_id=1, source_target_pairs={{0,1},{1,0},{2,3},{3,2},{4,5},{5,4},{6,7},{7,6},{8,9},{9,8},{10,11... | collective-permute-start | bytes 2457608 | tf_op jit(solution)/shard_map/ppermute | solution.py:595
  204.3 49.2 %collective-permute-start.18 = (bf16[320,640]{0,1:T(8,128)(2,1)}, bf16[320,640]{0,1:T(8,128)(2,1)}, u32[]{:S(2)}, u32[]{:S(2)}) collective-permute-start(bf16[320,640]{0,1:T(8,128)(2,1)} %bitcast.34), channel_id=1, source_target_pairs={{0,1},{3,2},{4,5},{7,6},{8,9},{11,10},{12,13},{15,14},{16,17},{19,... | collective-permute-start | bytes 1228808 | tf_op jit(solution)/shard_map/ppermute | solution.py:595
  223.2 64.8 %collective-permute-start.20 = (bf16[16,25,16,128]{3,2,1,0:T(8,128)(2,1)}, bf16[16,25,16,128]{3,2,1,0:T(8,128)(2,1)S(1)}, u32[]{:S(2)}, u32[]{:S(2)}) collective-permute-start(bf16[16,25,16,128]{3,2,1,0:T(8,128)(2,1)} %get-tuple-element.66.refs_3_), channel_id=1, source_target_pairs={{0,1},{1,0},{2,3},{3,2},{4,5},{5,4},{6,7},{7,6},{8,9},{9,8},{10,11... | collective-permute-start | bytes 4915208 | tf_op jit(solution)/shard_map/ppermute | solution.py:595
  262.5 55.3 %collective-permute-start.24 = (bf16[12,25,16,128]{3,2,1,0:T(8,128)(2,1)}, bf16[12,25,16,128]{3,2,1,0:T(8,128)(2,1)}, u32[]{:S(2)}, u32[]{:S(2)}) collective-permute-start(bf16[12,25,16,128]{3,2,1,0:T(8,128)(2,1)} %get-tuple-element.67.refs_10_), channel_id=1, source_target_pairs={{1,2},{2,1},{5,6},{6,5},{9,10},{10,9},{13,14},{14,13},{17,18},{18,... | collective-permute-start | bytes 3686408 | tf_op jit(solution)/shard_map/ppermute | solution.py:595
  294.2 77.4 %collective-permute-start.27 = (bf16[16,25,16,128]{3,2,1,0:T(8,128)(2,1)}, bf16[16,25,16,128]{3,2,1,0:T(8,128)(2,1)S(1)}, u32[]{:S(2)}, u32[]{:S(2)}) collective-permute-start(bf16[16,25,16,128]{3,2,1,0:T(8,128)(2,1)} %get-tuple-element.69.refs_0_.refs_6_.refs_10_), channel_id=1, source_target_pairs={{0,1},{1,0},{2,3},{3,2},{4,5},{5,4},{6,7},{7,6},{8,9},{9,8},{10,11... | collective-permute-start | bytes 4915208 | tf_op jit(solution)/shard_map/ppermute | solution.py:595
  316.5 51.1 %collective-permute-start.23 = (bf16[8,64,320]{2,1,0:T(8,128)(2,1)}, bf16[8,64,320]{2,1,0:T(8,128)(2,1)}, u32[]{:S(2)}, u32[]{:S(2)}) collective-permute-start(bf16[8,64,320]{2,1,0:T(8,128)(2,1)} %get-tuple-element.74), channel_id=1, source_target_pairs={{0,8},{8,0},{16,24},{24,16},{1,9},{9,1},{17,25},{25,17},{2,10},{10... | collective-permute-start | bytes 983048 | tf_op jit(solution)/shard_map/ppermute | solution.py:632
  317.0 54.5 %collective-permute-start.26 = (bf16[12,25,16,128]{3,2,1,0:T(8,128)(2,1)}, bf16[12,25,16,128]{3,2,1,0:T(8,128)(2,1)S(1)}, u32[]{:S(2)}, u32[]{:S(2)}) collective-permute-start(bf16[12,25,16,128]{3,2,1,0:T(8,128)(2,1)} %get-tuple-element.78.refs_0_.refs_4_), channel_id=1, source_target_pairs={{1,2},{2,1},{5,6},{6,5},{9,10},{10,9},{13,14},{14,13},{17,18},{18,... | collective-permute-start | bytes 3686408 | tf_op jit(solution)/shard_map/ppermute | solution.py:595
  321.1 68.3 %collective-permute-start.29 = (bf16[12,25,16,128]{3,2,1,0:T(8,128)(2,1)}, bf16[12,25,16,128]{3,2,1,0:T(8,128)(2,1)S(1)}, u32[]{:S(2)}, u32[]{:S(2)}) collective-permute-start(bf16[12,25,16,128]{3,2,1,0:T(8,128)(2,1)} %get-tuple-element.75.refs_10_), channel_id=1, source_target_pairs={{1,2},{2,1},{5,6},{6,5},{9,10},{10,9},{13,14},{14,13},{17,18},{18,... | collective-permute-start | bytes 3686408 | tf_op jit(solution)/shard_map/ppermute | solution.py:595
  374.7 85.1 %collective-permute-start.37 = (bf16[8,25,16,128]{3,2,1,0:T(8,128)(2,1)}, bf16[8,25,16,128]{3,2,1,0:T(8,128)(2,1)S(1)}, u32[]{:S(2)}, u32[]{:S(2)}) collective-permute-start(bf16[8,25,16,128]{3,2,1,0:T(8,128)(2,1)} %get-tuple-element.79.refs_10_), channel_id=1, source_target_pairs={{0,1},{1,0},{2,3},{3,2},{4,5},{5,4},{6,7},{7,6},{8,9},{9,8},{10,11... | collective-permute-start | bytes 2457608 | tf_op jit(solution)/shard_map/ppermute | solution.py:595
  388.9 49.9 %collective-permute-start.31 = (bf16[8,64,320]{2,1,0:T(8,128)(2,1)}, bf16[8,64,320]{2,1,0:T(8,128)(2,1)S(1)}, u32[]{:S(2)}, u32[]{:S(2)}) collective-permute-start(bf16[8,64,320]{2,1,0:T(8,128)(2,1)} %get-tuple-element.83), channel_id=1, source_target_pairs={{0,8},{8,0},{16,24},{24,16},{1,9},{9,1},{17,25},{25,17},{2,10},{10... | collective-permute-start | bytes 983048 | tf_op jit(solution)/shard_map/ppermute | solution.py:632
  388.9 49.9 %collective-permute-start.32 = (bf16[8,64,320]{2,1,0:T(8,128)(2,1)}, bf16[8,64,320]{2,1,0:T(8,128)(2,1)S(1)}, u32[]{:S(2)}, u32[]{:S(2)}) collective-permute-start(bf16[8,64,320]{2,1,0:T(8,128)(2,1)} %get-tuple-element.85), channel_id=1, source_target_pairs={{0,8},{8,0},{16,24},{24,16},{1,9},{9,1},{17,25},{25,17},{2,10},{10... | collective-permute-start | bytes 983048 | tf_op jit(solution)/shard_map/ppermute | solution.py:632
  393.7 66.1 %collective-permute-start.35 = (bf16[12,25,16,128]{3,2,1,0:T(8,128)(2,1)}, bf16[12,25,16,128]{3,2,1,0:T(8,128)(2,1)S(1)}, u32[]{:S(2)}, u32[]{:S(2)}) collective-permute-start(bf16[12,25,16,128]{3,2,1,0:T(8,128)(2,1)} %get-tuple-element.82.refs_10_), channel_id=1, source_target_pairs={{1,2},{2,1},{5,6},{6,5},{9,10},{10,9},{13,14},{14,13},{17,18},{18,... | collective-permute-start | bytes 3686408 | tf_op jit(solution)/shard_map/ppermute | solution.py:595
  450.2 51.2 %collective-permute-start.38 = (bf16[8,64,320]{2,1,0:T(8,128)(2,1)}, bf16[8,64,320]{2,1,0:T(8,128)(2,1)S(1)}, u32[]{:S(2)}, u32[]{:S(2)}) collective-permute-start(bf16[8,64,320]{2,1,0:T(8,128)(2,1)} %get-tuple-element.90), channel_id=1, source_target_pairs={{0,8},{8,0},{16,24},{24,16},{1,9},{9,1},{17,25},{25,17},{2,10},{10... | collective-permute-start | bytes 983048 | tf_op jit(solution)/shard_map/ppermute | solution.py:632
  453.6 47.8 %collective-permute-start.39 = (bf16[8,64,320]{2,1,0:T(8,128)(2,1)}, bf16[8,64,320]{2,1,0:T(8,128)(2,1)S(1)}, u32[]{:S(2)}, u32[]{:S(2)}) collective-permute-start(bf16[8,64,320]{2,1,0:T(8,128)(2,1)} %get-tuple-element.92), channel_id=1, source_target_pairs={{0,8},{8,0},{16,24},{24,16},{1,9},{9,1},{17,25},{25,17},{2,10},{10... | collective-permute-start | bytes 983048 | tf_op jit(solution)/shard_map/ppermute | solution.py:632
  459.3 47.0 %collective-permute-start.34 = (bf16[8,4,8,320]{3,2,1,0:T(8,128)(2,1)}, bf16[8,4,8,320]{3,2,1,0:T(8,128)(2,1)S(1)}, u32[]{:S(2)}, u32[]{:S(2)}) collective-permute-start(bf16[8,4,8,320]{3,2,1,0:T(8,128)(2,1)} %dynamic-slice_convert_fusion.6), channel_id=1, source_target_pairs={{0,4},{4,0},{1,5},{5,1},{2,6},{6,2},{3,7},{7,3},{8,12},{12,8},{9,1... | collective-permute-start | bytes 491528 | tf_op jit(solution)/shard_map/ppermute | solution.py:649
  463.4 61.0 %collective-permute-start.42 = (bf16[8,25,16,128]{3,2,1,0:T(8,128)(2,1)}, bf16[8,25,16,128]{3,2,1,0:T(8,128)(2,1)S(1)}, u32[]{:S(2)}, u32[]{:S(2)}) collective-permute-start(bf16[8,25,16,128]{3,2,1,0:T(8,128)(2,1)} %pass_on.11.refs_10_), channel_id=1, source_target_pairs={{0,1},{1,0},{2,3},{3,2},{4,5},{5,4},{6,7},{7,6},{8,9},{9,8},{10,11... | collective-permute-start | bytes 2457608 | tf_op jit(solution)/shard_map/ppermute | solution.py:595
  (77 other events, 889.6 us)

commit v7 on v6

--- a/solution.py
+++ b/solution.py
@@ -22,10 +22,19 @@
 
 def group_size(depth):
     best = depth
-    for size in range(2, 11, 2):
+    for size in range(2, 21, 2):
         if depth % size == 0:
             best = size
     return best
+
+
+def row_of(k, slab):
+    each = 2 * LANES // slab
+    return k // each * 2 * LANES + k % each * slab
+
+
+def rows_of(group, slab):
+    return -(-(row_of(group - 1, slab) + slab) // LANES) * LANES
 
 
 def pack_kernel(group, parts, given, spot_ref, *refs):
@@ -208,63 +217,81 @@
     pltpu.make_async_copy(src, dst, sem).start()
 
 
-def expand(source, step, group, groups, tables, spread):
+def expand(source, step, group, groups, tables, spread, slab):
     sides, _, plane, rows, _ = source.shape
     kinds = source.shape[1] // groups
     half = (group + 1) // 2
     mains = (plane - half) // group
     windows = spread.shape[1]
-    for part, (lo, hi) in enumerate(((0, half), (half, group))):
-        if lo == hi:
-            continue
-        count = hi - lo
-        spans = [(main * group + lo, main * group + hi) for main in range(mains)]
-        spans.append((mains * group, mains * group + count))
-        wide = jnp.concatenate(
-            [
-                jnp.concatenate(
-                    [
-                        source[:, kind * groups + step, first:stop].reshape(sides * count * rows, LANES)
-                        for first, stop in spans
-                    ],
-                    axis=1,
-                )
-                for kind in range(kinds)
-            ],
-            axis=0,
+    each = tables[0].shape[0]
+    rest = tables[0].shape[1] - mains * LANES - LANES // 2
+    lane = lax.broadcasted_iota(jnp.int32, (sides * rows, LANES), 1)
+    keeps = [jnp.where(side, 1.0, 0.0).astype(jnp.bfloat16) for side in (lane < rest, lane >= rest)]
+
+    def row(kind, k):
+        def block(at):
+            return source[:, kind * groups + step, at].reshape(sides * rows, LANES)
+
+        last = block(mains * group + (k if k < half else k - half)) * keeps[0 if k < half else 1]
+        return jnp.concatenate([block(main * group + k) for main in range(mains)] + [last], axis=1)
+
+    wides = []
+    for turn in range(min(each, group)):
+        wides.append(
+            jnp.concatenate([row(kind, k) for kind in range(kinds) for k in range(turn, group, each)], axis=0)
         )
-        for slot, table in enumerate(tables):
-            got = jnp.dot(wide, table[part], preferred_element_type=jnp.float32).astype(jnp.bfloat16)
-            got = got.reshape(kinds, sides, count, rows, windows * LANES)
-            for kind in range(kinds):
-                for k in range(count):
-                    for a in range(windows):
-                        spread[slot + kind, a, :, (lo + k) * LANES:(lo + k + 1) * LANES] = got[
-                            kind, :, k, :, a * LANES:(a + 1) * LANES
-                        ].reshape(sides * rows, LANES)
-
-
-def table_kernel(rest, table_ref, *refs):
+    for slot, table in enumerate(tables):
+        got = [
+            jnp.dot(wide, table[turn], preferred_element_type=jnp.float32).reshape(
+                kinds, -1, sides * rows, windows * LANES
+            )
+            for turn, wide in enumerate(wides)
+        ]
+        for kind in range(kinds):
+            for first in range(0, group, each):
+                members = range(first, min(first + each, group))
+                for a in range(windows):
+                    window = slice(a * LANES, (a + 1) * LANES)
+                    for tile in range(2):
+                        value = None
+                        for k in members:
+                            start = (k - first) * slab - tile * LANES
+                            if start + slab <= 0 or start >= LANES:
+                                continue
+                            mine = got[k - first][kind, k // each, :, window]
+                            value = mine if value is None else jnp.where(lane >= start, mine, value)
+                        if value is not None:
+                            at = first // each * 2 * LANES + tile * LANES
+                            spread[slot + kind, a, :, at:at + LANES] = value.astype(jnp.bfloat16)
+
+
+def table_kernel(windows, slab, left_ref, *refs):
     out_ref = refs[-1]
-    total = table_ref.shape[0]
+    total, lanes = left_ref.shape
+    rest = LANES // 2
     mains = total - rest
-    out_ref[...] = jnp.zeros_like(out_ref)
-    for part in range(2):
-        out_ref[part, 0:mains] = table_ref[0:mains]
-        out_ref[part, mains + part * rest:mains + (part + 1) * rest] = table_ref[mains:total]
-
-
-def make_table(table, deps, rest):
-    total, lanes = table.shape
+    shape = (lanes, windows * LANES)
+    source = lax.broadcasted_iota(jnp.int32, shape, 0)
+    target = lax.broadcasted_iota(jnp.int32, shape, 1)
+    for turn in range(out_ref.shape[0]):
+        column = (source // slab) * LANES + (source % slab + turn * slab) % LANES
+        select = jnp.where(column == target, 1.0, 0.0).astype(jnp.bfloat16)
+        got = jnp.dot(left_ref[...], select, preferred_element_type=jnp.float32).astype(jnp.bfloat16)
+        out_ref[turn, 0:total] = got
+        out_ref[turn, total:total + rest] = got[mains:total]
+
+
+def make_table(left, deps, windows, slab):
+    total, lanes = left.shape
     vmem = pl.BlockSpec(memory_space=pltpu.VMEM)
     return pl.pallas_call(
-        functools.partial(table_kernel, rest),
-        out_shape=jax.ShapeDtypeStruct((2, total - rest + LANES, lanes), table.dtype),
+        functools.partial(table_kernel, windows, slab),
+        out_shape=jax.ShapeDtypeStruct((2 * LANES // slab, total + LANES // 2, windows * LANES), left.dtype),
         in_specs=[vmem] + [pl.BlockSpec(memory_space=pl.ANY)] * len(deps),
         out_specs=vmem,
         compiler_params=pltpu.CompilerParams(vmem_limit_bytes=VMEM_BYTES),
         name="make_table",
-    )(table, *deps)
+    )(left, *deps)
 
 
 def low_kernel(*refs):
@@ -273,7 +300,8 @@
     out_ref[...] = jnp.zeros_like(out_ref)
     for k in range(group):
         for at, ref in enumerate(parts):
-            out_ref[k * LANES:k * LANES + slab, at * lanes:(at + 1) * lanes] = ref[k]
+            row = row_of(k, slab)
+            out_ref[row:row + slab, at * lanes:(at + 1) * lanes] = ref[k]
 
 
 def make_lows(parts, group):
@@ -281,10 +309,10 @@
     block = pl.BlockSpec((group, slab, lanes), lambda g: (g, 0, 0))
     return pl.pallas_call(
         low_kernel,
-        out_shape=jax.ShapeDtypeStruct((depth * LANES, len(parts) * lanes), parts[0].dtype),
+        out_shape=jax.ShapeDtypeStruct((depth // group * rows_of(group, slab), len(parts) * lanes), parts[0].dtype),
         grid=(depth // group,),
         in_specs=[block] * len(parts),
-        out_specs=pl.BlockSpec((group * LANES, len(parts) * lanes), lambda g: (g, 0)),
+        out_specs=pl.BlockSpec((rows_of(group, slab), len(parts) * lanes), lambda g: (g, 0)),
         compiler_params=pltpu.CompilerParams(vmem_limit_bytes=VMEM_BYTES),
         name="make_lows",
     )(*parts)
@@ -343,19 +371,21 @@
                     plane = held[step * (each // planes) + at // planes, at % planes]
                 else:
                     plane = held[(step * each + at) // planes, (step * each + at) % planes]
-                out_ref[k * LANES + i * rows:k * LANES + (i + 1) * rows, j * LANES:(j + 1) * LANES] = plane
+                row = row_of(k, tiles[0] * rows) + i * rows
+                out_ref[row:row + rows, j * LANES:(j + 1) * LANES] = plane
 
 
 def low_of_planes(parts, deps, units, group, groups, tiles):
     spans = [(at, first, size) for at, _, first, size in parts]
     shape = parts[0][1].shape[1:]
+    height = rows_of(group, tiles[0] * shape[1])
     anywhere = pl.BlockSpec(memory_space=pl.ANY)
     return pl.pallas_call(
         functools.partial(planes_kernel, spans, group, groups, tiles),
-        out_shape=jax.ShapeDtypeStruct((groups * group * LANES, tiles[1] * LANES), jnp.bfloat16),
+        out_shape=jax.ShapeDtypeStruct((groups * height, tiles[1] * LANES), jnp.bfloat16),
         grid=(groups,),
         in_specs=[anywhere] * (len(parts) + len(deps)),
-        out_specs=pl.BlockSpec((group * LANES, tiles[1] * LANES), lambda g: (g, 0)),
+        out_specs=pl.BlockSpec((height, tiles[1] * LANES), lambda g: (g, 0)),
         scratch_shapes=[
             pltpu.VMEM((units,) + shape, jnp.bfloat16),
             pltpu.SemaphoreType.DMA((len(parts),)),
@@ -386,7 +416,7 @@
     )(*[x for pair in pairs for x in pair], *deps)
 
 
-def even_kernel(sides, group, groups, use_ends, use_inner, starts, spot_ref, *refs):
+def even_kernel(sides, group, groups, slab, use_ends, use_inner, starts, spot_ref, *refs):
     views = [ref.at[at:at + 2 * groups] for ref, at in zip(refs[:2 * sides], starts)]
     inner_blocks, end_blocks = views[:sides], views[sides:]
     tables, low_ref = refs[2 * sides:2 * sides + 2]
@@ -414,51 +444,53 @@
             for at in range(sides):
                 pltpu.make_async_copy(inner_blocks[at], even.at[at], sems.at[at]).wait()
 
-        expand(even, step, group, groups, (tables,), spread)
+        expand(even, step, group, groups, (tables,), spread, slab)
         count = spread.shape[1] * spread.shape[2]
         full = total.shape[2]
-        both = spread[...].reshape(2, count, group * LANES)
-        got = jnp.dot(both[0], low_ref[...], preferred_element_type=jnp.float32)
+        one = spread[0].reshape(count, spread.shape[3])
+        two = spread[1].reshape(count, spread.shape[3])
+        got = jnp.dot(one, low_ref[...], preferred_element_type=jnp.float32)
         total[0] += got[:, :full]
-        total[1] += got[:, full:] + jnp.dot(both[1], low_ref[:, :full], preferred_element_type=jnp.float32)
+        total[1] += got[:, full:] + jnp.dot(two, low_ref[:, :full], preferred_element_type=jnp.float32)
 
     @pl.when(jnp.logical_and(step == 0, jnp.logical_not(work)))
     def _():
         total[...] = jnp.zeros_like(total)
 
 
-def even_product(spot, inner_blocks, end_blocks, deps, table, low, sides, group, groups):
+def even_product(spot, inner_blocks, end_blocks, deps, table, low, sides, group, groups, slab):
     some = inner_blocks or end_blocks
     use_inner, use_ends = inner_blocks is not None, end_blocks is not None
     blocks = (inner_blocks or some) + (end_blocks or some)
     starts = [at for _, at in blocks]
     _, planes, rows, _ = some[0][0].shape
+    height = rows_of(group, slab)
     windows = table.shape[2] // LANES
     full = low.shape[-1] // 2
     count = windows * sides * rows
-    whole = lambda arr: pl.BlockSpec(arr.shape, lambda g, s: (0,) * len(arr.shape))
+    whole = lambda arr, **mode: pl.BlockSpec(arr.shape, lambda g, s: (0,) * len(arr.shape), **mode)
+    once = dict(pipeline_mode=pl.Buffered(1))
 
     def busy(spot_ref):
         end = jnp.logical_or(spot_ref[0] == 0, spot_ref[0] == sides - 1)
         return jnp.where(jnp.where(end, use_ends, use_inner), 1, 0)
 
-    part = pl.BlockSpec((group * LANES, 2 * full), lambda g, s: (g * busy(s), 0))
+    part = pl.BlockSpec((height, 2 * full), lambda g, s: (g * busy(s), 0))
     out = jax.ShapeDtypeStruct((2, count, full), jnp.float32)
-    depth = groups * group
-    flops = 2 * count * depth * LANES * 3 * full + 4 * sides * rows * depth * 3 * LANES * windows * LANES
+    flops = 2 * count * groups * height * 3 * full + 4 * sides * rows * groups * group * 3 * LANES * windows * LANES
     return pl.pallas_call(
-        functools.partial(even_kernel, sides, group, groups, use_ends, use_inner, starts),
+        functools.partial(even_kernel, sides, group, groups, slab, use_ends, use_inner, starts),
         out_shape=out,
         grid_spec=pltpu.PrefetchScalarGridSpec(
             num_scalar_prefetch=1,
             grid=(groups,),
             in_specs=[pl.BlockSpec(memory_space=pl.ANY)] * (2 * sides)
-            + [whole(table), part]
+            + [whole(table, **once), part]
             + [pl.BlockSpec(memory_space=pl.ANY)] * len(deps),
             out_specs=whole(out),
             scratch_shapes=[
                 pltpu.VMEM((sides, 2 * groups, planes, rows, LANES), jnp.bfloat16),
-                pltpu.VMEM((2, windows, sides * rows, group * LANES), jnp.bfloat16),
+                pltpu.VMEM((2, windows, sides * rows, height), jnp.bfloat16),
                 pltpu.SemaphoreType.DMA((sides,)),
             ],
         ),
@@ -468,7 +500,7 @@
     )(spot, *[ref for ref, _ in blocks], table, low, *deps)
 
 
-def odd_kernel(sides, group, groups, outs, starts, spot_ref, *refs):
+def odd_kernel(sides, group, groups, slab, outs, starts, spot_ref, *refs):
     blocks = [ref.at[at:at + groups] for ref, at in zip(refs[:sides], starts)]
     inner_part, end_part = refs[sides:sides + 2]
     tables, next_tables, low_ref, next_low_ref = refs[sides + 2:sides + 6]
@@ -496,11 +528,12 @@
 
     @pl.when(inner)
     def _():
-        expand(odd, step, group, groups, (tables, next_tables), spread)
+        expand(odd, step, group, groups, (tables, next_tables), spread, slab)
         count = spread.shape[1] * spread.shape[2]
-        rows = spread[...].reshape(2, count, group * LANES)
-        total[1] += jnp.dot(rows[0], low_ref[...], preferred_element_type=jnp.float32)
-        total[1] += jnp.dot(rows[1], next_low_ref[...], preferred_element_type=jnp.float32)
+        one = spread[0].reshape(count, spread.shape[3])
+        two = spread[1].reshape(count, spread.shape[3])
+        total[1] += jnp.dot(one, low_ref[...], preferred_element_type=jnp.float32)
+        total[1] += jnp.dot(two, next_low_ref[...], preferred_element_type=jnp.float32)
 
     @pl.when(step == last)
     def _():
@@ -512,36 +545,37 @@
             out_refs[offset][...] = value.reshape(out_refs[offset].shape).astype(jnp.bfloat16)
 
 
-def odd_product(spot, blocks, inner_part, end_part, deps, tables, lows, sides, group, groups, outs):
+def odd_product(spot, blocks, inner_part, end_part, deps, tables, lows, sides, group, groups, slab, outs):
     starts = [at for _, at in blocks]
     _, planes, rows, _ = blocks[0][0].shape
     table, next_table = tables
     low, next_low = lows
+    height = rows_of(group, slab)
     windows = table.shape[2] // LANES
     full = low.shape[-1]
     count = windows * sides * rows
-    whole = lambda arr: pl.BlockSpec(arr.shape, lambda g, s: (0,) * len(arr.shape))
+    whole = lambda arr, **mode: pl.BlockSpec(arr.shape, lambda g, s: (0,) * len(arr.shape), **mode)
+    once = dict(pipeline_mode=pl.Buffered(1))
 
     def busy(spot_ref):
         return jnp.where(jnp.logical_or(spot_ref[0] == 0, spot_ref[0] == sides - 1), 0, 1)
 
-    part = pl.BlockSpec((group * LANES, full), lambda g, s: (g * busy(s), 0))
+    part = pl.BlockSpec((height, full), lambda g, s: (g * busy(s), 0))
     out = [jax.ShapeDtypeStruct((windows, sides * rows, full // 2), jnp.bfloat16)] * outs
-    depth = groups * group
-    flops = 2 * count * depth * LANES * 2 * full + 4 * sides * rows * depth * 3 * LANES * windows * LANES
+    flops = 2 * count * groups * height * 2 * full + 4 * sides * rows * groups * group * 3 * LANES * windows * LANES
     return pl.pallas_call(
-        functools.partial(odd_kernel, sides, group, groups, outs, starts),
+        functools.partial(odd_kernel, sides, group, groups, slab, outs, starts),
         out_shape=out,
         grid_spec=pltpu.PrefetchScalarGridSpec(
             num_scalar_prefetch=1,
             grid=(groups,),
             in_specs=[pl.BlockSpec(memory_space=pl.ANY)] * (sides + 2)
-            + [whole(table), whole(next_table), part, part]
+            + [whole(table, **once), whole(next_table, **once), part, part]
             + [pl.BlockSpec(memory_space=pl.ANY)] * len(deps),
             out_specs=[whole(o) for o in out],
             scratch_shapes=[
                 pltpu.VMEM((sides, groups, planes, rows, LANES), jnp.bfloat16),
-                pltpu.VMEM((2, windows, sides * rows, group * LANES), jnp.bfloat16),
+                pltpu.VMEM((2, windows, sides * rows, height), jnp.bfloat16),
                 pltpu.VMEM((2, count, full), jnp.float32),
                 pltpu.SemaphoreType.DMA((sides + 1,)),
             ],
@@ -601,12 +635,7 @@
     )
     total = left_all.shape[0]
     mains = total // LANES
-    rest = total - mains * LANES
     plane = (mains * group + (group + 1) // 2, rows, LANES)
-
-    def table(flat_left):
-        wide = flat_left.reshape(total, windows, slab)
-        return jnp.pad(wide, ((0, 0), (0, 0), (0, LANES - slab))).reshape(total, windows * LANES)
 
     flat_left = left_all.reshape(total, windows * slab)
     middle = lower(1, role) * jnp.asarray(2, bottoms.dtype)
@@ -682,24 +711,24 @@
                 own[r] = mine
                 straight[r] = move(mine, cross)
             done = out
-            if 2 * r + 1 < chunks:
-                exchange(2 * r + 1, min(2, chunks - 2 * r - 1), mark[1])
+            for first, size in {0: ((1, 1), (2, 1)), 1: ((3, chunks - 3),)}.get(r, ()):
+                if size > 0 and first < chunks:
+                    exchange(first, size, mark[1])
             if r == 0:
                 late = mark[1]
-                first_table = make_table(table(flat_left), [out], rest)
-                low = make_lows([lower(0, late), lower(2, late)], group)
                 near_left = move(flat_left, hand)
+                outer = [lower(0, late), lower(2, late)]
+                extra = list(outer)
         t = r - 4
         if 0 <= t < chunks:
             if near_low is None:
                 near_low = low_of_planes(
                     sorted(parts, key=lambda p: p[0]), [done], units, group, groups, tiles
                 )
-                near_table = make_table(table(near_left), [done], rest)
             blocks = [(own[t], 2 * groups), (sent[t], 2 * groups), (straight[t], 2 * groups), (turned[t + 1], 2 * groups)]
             shares[t] = odd_product(
                 spot, blocks, sums[t + 2], sums[t + 3], [done] + extra, (first_table, near_table),
-                (middle_low, near_low), sides, group, groups, roles,
+                (middle_low, near_low), sides, group, groups, slab, roles,
             )
             done = shares[t][0]
             extra = []
@@ -720,6 +749,8 @@
                     parts.append((at, last[r], 0, size))
             done = outs[0]
         if r == 1:
+            first_table = make_table(flat_left, [done], windows, slab)
+            low = make_lows(outer, group)
             extra = [low, first_table]
         if r == 2:
             middle_low = make_lows([middle], group)
@@ -734,10 +765,13 @@
                     (own[t], 0), (sent[t], 0), (sent[t + 1], 2 * groups if t + 1 < chunks else 0), (last[t + 2], 0)
                 ]
             sums[r] = even_product(
-                spot, inner_blocks, end_blocks, [done] + extra, first_table, low, sides, group, groups
+                spot, inner_blocks, end_blocks, [done] + extra, first_table, low, sides, group, groups, slab
             )
             done = sums[r]
             extra = []
+            if r == 3:
+                near_table = make_table(near_left, [], windows, slab)
+                extra.append(near_table)
             if r - 4 in shares:
                 extra.append(join_core(r - 4, [done]))
             if r - 5 in shares:
@@ -746,7 +780,7 @@
     blocks = [(own[t], 2 * groups), (sent[t], 2 * groups), (straight[t], 2 * groups), (turned[t + 1], 2 * groups)]
     shares[t] = odd_product(
         spot, blocks, sums[t + 2], sums[t + 3], [done] + extra, (first_table, near_table),
-        (middle_low, near_low), sides, group, groups, roles,
+        (middle_low, near_low), sides, group, groups, slab, roles,
     )
     send_core(t)
     join_chip(t - 1, [shares[t][0]])

time: 661 us -> 632 us (0.956)
  starting transfers between devices: 154 us -> 111 us
  waiting for transfers between devices: 99.1 us -> 129 us
  Pallas kernels: 269 us -> 260 us
    ppermute x22, waiting for transfers between devices: 3.94 us -> 75.6 us  [on_device(): move = lambda value, perm: lax.ppermute(value, 'horiz', perm)]
    ppermute x9 -> x12, waiting for transfers between devices: 53 us -> 10.7 us  [exchange(): piece = lax.ppermute(piece, 'role', [(j, j ^ s) for j in range(roles)])]
    ppermute x22, starting transfers between devices: 119 us -> 77.3 us  [on_device(): move = lambda value, perm: lax.ppermute(value, 'horiz', perm)]
    pallas_call x15, Pallas kernels: 181 us -> 173 us  [the longest x6 112 us: even_product(): pl.pallas_call(functools.partial(even_kernel, sides, group, groups, slab,...]
    unnamed x94 -> x96, local copies, waits for them, and re-layouts: 30.3 us -> 30.4 us
  transfers between devices with their start and end apart: 60 -> 63, of which waited for: 16 -> 18; matrix products, arithmetic and copies ran while one was open for 13% -> 13% of each run, Pallas kernels for 38% -> 38%
where the time goes in v7:
time: 632 us; the launch traced here: 623 us
  Pallas kernels  260 us (41%)
  waiting for transfers between devices  129 us (20%)
  starting transfers between devices  111 us (18%)
  local copies, waits for them, and re-layouts  101 us (16%)
  other arithmetic  10.4 us (2%)
    pallas_call x6, Pallas kernels, even_product(): pl.pallas_call(functools.partial(even_kernel, sides, group, groups, slab,...  112 us
    ppermute x22, starting transfers between devices, on_device(): move = lambda value, perm: lax.ppermute(value, 'horiz', perm)  77.3 us
    ppermute x22, waiting for transfers between devices, on_device(): move = lambda value, perm: lax.ppermute(value, 'horiz', perm)  75.6 us
    pallas_call x5, Pallas kernels, odd_product(): pl.pallas_call(functools.partial(odd_kernel, sides, group, groups, slab,...  42.2 us
    pallas_call x15, Pallas kernels, join(): pl.pallas_call(functools.partial(join_kernel, len(pairs)), out_shape=[jax...  32.5 us
    unnamed x96, local copies, waits for them, and re-layouts  30.4 us
    pallas_call x6, Pallas kernels, pack(): pl.pallas_call(functools.partial(pack_kernel, group, len(pieces), given),...  27.3 us
    reshape x2, local copies, waits for them, and re-layouts, lower(): return low.reshape(depth, slab, downs * full)  21.1 us
  transfers between devices with their start and end apart: 63, of which 18 were waited for; matrix products, arithmetic and copies ran while one was open for 13% of the time, Pallas kernels for 38%

profile of v7, /device:TPU:0, one launch (start us, length us, event | category | flops | bytes accessed | tf_op | source)
XLA Modules:
  0.0 623.1 jit_solution(14508846285540533672)
XLA Ops:
  5.8 8.6 %dynamic-slice_multiply_fusion = bf16[1,40,80,2,320]{4,3,2,1,0:T(2,128)(2,1)} fusion(bf16[3,160,80,2,320]{4,3,2,1,0:T(2,128)(2,1)} %param.5, s32[]{:T(128)S(6)} %select_n.119), kind=kLoop, calls=%fused_computation | loop fusion | flops 2048000 | bytes 8192004 | tf_op jit(solution)/shard_map/mul | solution.py:641
  14.4 10.5 %mul.113.low_ref.refs_0_ = bf16[40,80,640]{2,1,0:T(8,128)(2,1)} reshape(bf16[1,40,80,2,320]{4,3,2,1,0:T(2,128)(2,1)} %dynamic-slice_multiply_fusion) | data formatting | bytes 8192000 | tf_op jit(solution)/shard_map/mul | solution.py:641
  48.9 9.6 %constant_dynamic-slice_fusion.17 = (bf16[1,40,80,2,320]{4,3,2,1,0:T(2,128)(2,1)}, bf16[1,40,80,2,320]{4,3,2,1,0:T(2,128)(2,1)}) fusion(bf16[3,160,80,2,320]{4,3,2,1,0:T(2,128)(2,1)} %param.5, s32[]{:T(128)S(6)} %select_n.123), kind=kLoop, calls=%fused_computation.55 | loop fusion | bytes 16384004 | tf_op jit(solution)/shard_map/dynamic_slice | solution.py:621
  58.5 10.5 %reshape.80.refs_7_.refs_0_ = bf16[40,80,640]{2,1,0:T(8,128)(2,1)} reshape(bf16[1,40,80,2,320]{4,3,2,1,0:T(2,128)(2,1)} %get-tuple-element.108) | data formatting | bytes 8192000 | tf_op jit(solution)/shard_map/reshape | solution.py:624
  69.1 10.5 %reshape.81.refs_8_.refs_1_ = bf16[40,80,640]{2,1,0:T(8,128)(2,1)} reshape(bf16[1,40,80,2,320]{4,3,2,1,0:T(2,128)(2,1)} %get-tuple-element.107) | data formatting | bytes 8192000 | tf_op jit(solution)/shard_map/reshape | solution.py:624
  123.8 21.3 %collective-permute-done.9.refs_6_.refs_0_.refs_1_.refs_5_ = bf16[12,50,16,128]{3,2,1,0:T(8,128)(2,1)S(1)} collective-permute-done((bf16[12,50,16,128]{3,2,1,0:T(8,128)(2,1)}, bf16[12,50,16,128]{3,2,1,0:T(8,128)(2,1)S(1)}, u32[]{:S(2)}, u32[]{:S(2)}) %collective-permute-start.9) | collective-permute-done | bytes 2457632 | tf_op jit(solution)/shard_map/ppermute | solution.py:629
  172.7 10.4 %collective-permute-done.19.refs_3_ = bf16[2,3,40,16,80]{4,3,2,1,0:T(8,128)(2,1)S(1)} collective-permute-done((bf16[2,3,40,16,80]{4,3,2,1,0:T(8,128)(2,1)}, bf16[2,3,40,16,80]{4,3,2,1,0:T(8,128)(2,1)S(1)}, u32[]{:S(2)}, u32[]{:S(2)}) %collective-permute-start.19) | collective-permute-done | bytes 614432 | tf_op jit(solution)/shard_map/ppermute | solution.py:615
  183.1 7.7 %collective-permute-done.16.refs_6_.refs_0_.refs_2_.refs_1_.refs_5_ = bf16[8,50,16,128]{3,2,1,0:T(8,128)(2,1)S(1)} collective-permute-done((bf16[8,50,16,128]{3,2,1,0:T(8,128)(2,1)}, bf16[8,50,16,128]{3,2,1,0:T(8,128)(2,1)S(1)}, u32[]{:S(2)}, u32[]{:S(2)}) %collective-permute-start.16) | collective-permute-done | bytes 1638432 | tf_op jit(solution)/shard_map/ppermute | solution.py:629
  206.7 43.3 %collective-permute-done.21.left_ref = bf16[320,640]{1,0:T(8,128)(2,1)S(1)} collective-permute-done((bf16[320,640]{1,0:T(8,128)(2,1)}, bf16[320,640]{1,0:T(8,128)(2,1)S(1)}, u32[]{:S(2)}, u32[]{:S(2)}) %collective-permute-start.21) | collective-permute-done | bytes 409632 | tf_op jit(solution)/shard_map/ppermute | solution.py:629
  264.1 21.2 %even_product.7.refs_7_.refs_5_.refs_4_ = f32[2,512,640]{2,1,0:T(8,128)} custom-call(s32[2]{0:T(128)} %pad_add_fusion.spot_ref, bf16[6,50,16,128]{3,2,1,0:T(8,128)(2,1)} %get-tuple-element.60.refs_0_.refs_4_, bf16[12,50,16,128]{3,2,1,0:T(8,128)(2,1)} %copy-done, bf16[6,50,16,128]{3,2,1,0:T(8,128)(2,1)} %collective-permute-done.13.refs_4_.refs_2_, ...), custom_call_target="tpu_custom_call" | custom-call | flops 11072962560 | bytes 20971520 | tf_op jit(solution)/shard_map/even_product/pallas_call | solution.py:481
  301.2 8.4 %odd_product.5 = (bf16[8,64,320]{2,1,0:T(8,128)(2,1)}, bf16[8,64,320]{2,1,0:T(8,128)(2,1)}, bf16[8,64,320]{2,1,0:T(8,128)(2,1)}, bf16[8,64,320]{2,1,0:T(8,128)(2,1)}) custom-call(s32[2]{0:T(128)} %pad_add_fusion.spot_ref, bf16[6,50,16,128]{3,2,1,0:T(8,128)(2,1)} %get-tuple-element.56.refs_0_.refs_4_, bf16[10,50,16,128]{3,2,1,0:T(8,128)(2,1)} %copy-done.1, ...), custom_call_target="tpu_custom_call" | custom-call | flops 8724152320 | bytes 20971520 | tf_op jit(solution)/shard_map/odd_product/pallas_call | solution.py:566
  314.6 21.1 %even_product.8.refs_4_.refs_3_.refs_5_ = f32[2,512,640]{2,1,0:T(8,128)} custom-call(s32[2]{0:T(128)} %pad_add_fusion.spot_ref, bf16[6,50,16,128]{3,2,1,0:T(8,128)(2,1)} %get-tuple-element.65.refs_0_.refs_4_, bf16[8,50,16,128]{3,2,1,0:T(8,128)(2,1)} %copy-done.2, bf16[6,50,16,128]{3,2,1,0:T(8,128)(2,1)} %collective-permute-done.20.refs_4_.refs_2_, ...), custom_call_target="tpu_custom_call" | custom-call | flops 11072962560 | bytes 20971520 | tf_op jit(solution)/shard_map/even_product/pallas_call | solution.py:481
  335.8 14.1 %collective-permute-start.33 = (bf16[4,50,16,128]{3,2,1,0:T(8,128)(2,1)}, bf16[4,50,16,128]{3,2,1,0:T(8,128)(2,1)}, u32[]{:S(2)}, u32[]{:S(2)}) collective-permute-start(bf16[4,50,16,128]{3,2,1,0:T(8,128)(2,1)} %get-tuple-element.81), channel_id=1, source_target_pairs={{0,1},{1,0},{2,3},{3,2},{4,5},{5,4},{6,7},{7,6},{8,9},{9,8},{10,11... | collective-permute-start | bytes 2457608 | tf_op jit(solution)/shard_map/ppermute | solution.py:629
  358.8 8.4 %odd_product.6 = (bf16[8,64,320]{2,1,0:T(8,128)(2,1)}, bf16[8,64,320]{2,1,0:T(8,128)(2,1)}, bf16[8,64,320]{2,1,0:T(8,128)(2,1)}, bf16[8,64,320]{2,1,0:T(8,128)(2,1)}) custom-call(s32[2]{0:T(128)} %pad_add_fusion.spot_ref, bf16[6,50,16,128]{3,2,1,0:T(8,128)(2,1)} %get-tuple-element.60.refs_0_.refs_4_, bf16[12,50,16,128]{3,2,1,0:T(8,128)(2,1)} %copy-done, ...), custom_call_target="tpu_custom_call" | custom-call | flops 8724152320 | bytes 20971520 | tf_op jit(solution)/shard_map/odd_product/pallas_call | solution.py:566
  379.4 21.2 %even_product.9.refs_2_.refs_4_.refs_5_.refs_10_ = f32[2,512,640]{2,1,0:T(8,128)} custom-call(s32[2]{0:T(128)} %pad_add_fusion.spot_ref, bf16[6,50,16,128]{3,2,1,0:T(8,128)(2,1)} %get-tuple-element.69.refs_0_.refs_4_, bf16[8,50,16,128]{3,2,1,0:T(8,128)(2,1)} %copy-done.3, bf16[6,50,16,128]{3,2,1,0:T(8,128)(2,1)} %collective-permute-done.24.refs_4_.refs_2_, ...), custom_call_target="tpu_custom_call" | custom-call | flops 11072962560 | bytes 20971520 | tf_op jit(solution)/shard_map/even_product/pallas_call | solution.py:481
  401.4 16.4 %collective-permute-start.39 = (bf16[4,50,16,128]{3,2,1,0:T(8,128)(2,1)}, bf16[4,50,16,128]{3,2,1,0:T(8,128)(2,1)S(1)}, u32[]{:S(2)}, u32[]{:S(2)}) collective-permute-start(bf16[4,50,16,128]{3,2,1,0:T(8,128)(2,1)} %get-tuple-element.89), channel_id=1, source_target_pairs={{0,1},{1,0},{2,3},{3,2},{4,5},{5,4},{6,7},{7,6},{8,9},{9,8},{10,11... | collective-permute-start | bytes 2457608 | tf_op jit(solution)/shard_map/ppermute | solution.py:629
  423.6 8.4 %odd_product.7 = (bf16[8,64,320]{2,1,0:T(8,128)(2,1)}, bf16[8,64,320]{2,1,0:T(8,128)(2,1)}, bf16[8,64,320]{2,1,0:T(8,128)(2,1)}, bf16[8,64,320]{2,1,0:T(8,128)(2,1)}) custom-call(s32[2]{0:T(128)} %pad_add_fusion.spot_ref, bf16[6,50,16,128]{3,2,1,0:T(8,128)(2,1)} %get-tuple-element.65.refs_0_.refs_4_, bf16[8,50,16,128]{3,2,1,0:T(8,128)(2,1)} %copy-done.2, ...), custom_call_target="tpu_custom_call" | custom-call | flops 8724152320 | bytes 20971520 | tf_op jit(solution)/shard_map/odd_product/pallas_call | solution.py:566
  444.2 12.6 %collective-permute-start.45 = (bf16[4,50,16,128]{3,2,1,0:T(8,128)(2,1)}, bf16[4,50,16,128]{3,2,1,0:T(8,128)(2,1)S(1)}, u32[]{:S(2)}, u32[]{:S(2)}) collective-permute-start(bf16[4,50,16,128]{3,2,1,0:T(8,128)(2,1)} %pass_on.11.refs_10_), channel_id=1, source_target_pairs={{0,1},{1,0},{2,3},{3,2},{4,5},{5,4},{6,7},{7,6},{8,9},{9,8},{10,11... | collective-permute-start | bytes 2457608 | tf_op jit(solution)/shard_map/ppermute | solution.py:629
  456.8 21.3 %even_product.10.refs_2_.refs_4_.refs_5_.refs_10_ = f32[2,512,640]{2,1,0:T(8,128)} custom-call(s32[2]{0:T(128)} %pad_add_fusion.spot_ref, bf16[6,50,16,128]{3,2,1,0:T(8,128)(2,1)} %get-tuple-element.78.refs_0_.refs_4_, bf16[8,50,16,128]{3,2,1,0:T(8,128)(2,1)} %copy-done.4, bf16[6,50,16,128]{3,2,1,0:T(8,128)(2,1)} %collective-permute-done.29.refs_0_.refs_2_, ...), custom_call_target="tpu_custom_call" | custom-call | flops 11072962560 | bytes 20971520 | tf_op jit(solution)/shard_map/even_product/pallas_call | solution.py:481
  485.5 8.4 %odd_product.8 = (bf16[8,64,320]{2,1,0:T(8,128)(2,1)}, bf16[8,64,320]{2,1,0:T(8,128)(2,1)}, bf16[8,64,320]{2,1,0:T(8,128)(2,1)}, bf16[8,64,320]{2,1,0:T(8,128)(2,1)}) custom-call(s32[2]{0:T(128)} %pad_add_fusion.spot_ref, bf16[6,50,16,128]{3,2,1,0:T(8,128)(2,1)} %get-tuple-element.69.refs_0_.refs_4_, bf16[8,50,16,128]{3,2,1,0:T(8,128)(2,1)} %copy-done.3, ...), custom_call_target="tpu_custom_call" | custom-call | flops 8724152320 | bytes 20971520 | tf_op jit(solution)/shard_map/odd_product/pallas_call | solution.py:566
  502.7 21.6 %even_product.11.refs_2_.refs_4_.refs_5_.refs_10_ = f32[2,512,640]{2,1,0:T(8,128)} custom-call(s32[2]{0:T(128)} %pad_add_fusion.spot_ref, bf16[6,50,16,128]{3,2,1,0:T(8,128)(2,1)} %get-tuple-element.78.refs_0_.refs_4_, bf16[8,50,16,128]{3,2,1,0:T(8,128)(2,1)} %copy-done.4, bf16[4,50,16,128]{3,2,1,0:T(8,128)(2,1)} %copy-done.17, ...), custom_call_target="tpu_custom_call" | custom-call | flops 11072962560 | bytes 20971520 | tf_op jit(solution)/shard_map/even_product/pallas_call | solution.py:481
  530.1 8.7 %odd_product.9 = (bf16[8,64,320]{2,1,0:T(8,128)(2,1)}, bf16[8,64,320]{2,1,0:T(8,128)(2,1)}, bf16[8,64,320]{2,1,0:T(8,128)(2,1)}, bf16[8,64,320]{2,1,0:T(8,128)(2,1)}) custom-call(s32[2]{0:T(128)} %pad_add_fusion.spot_ref, bf16[6,50,16,128]{3,2,1,0:T(8,128)(2,1)} %get-tuple-element.78.refs_0_.refs_4_, bf16[8,50,16,128]{3,2,1,0:T(8,128)(2,1)} %copy-done.4, ...), custom_call_target="tpu_custom_call" | custom-call | flops 8724152320 | bytes 20971520 | tf_op jit(solution)/shard_map/odd_product/pallas_call | solution.py:566
  578.4 9.6 %collective-permute-start.55 = (bf16[8,1,40,320]{3,2,1,0:T(8,128)(2,1)S(1)}, bf16[8,1,40,320]{3,2,1,0:T(8,128)(2,1)S(1)}, u32[]{:S(2)}, u32[]{:S(2)}) collective-permute-start(bf16[8,1,40,320]{3,2,1,0:T(8,128)(2,1)S(1)} %get-tuple-element.127), channel_id=1, source_target_pairs={{0,2},{1,3},{2,0},{3,1},{4,6},{5,7},{6,4},{7,5},{8,10},{9,11},{10,... | collective-permute-start | bytes 614408 | tf_op jit(solution)/shard_map/ppermute | solution.py:796
  588.0 13.0 %collective-permute-done.55 = bf16[8,1,40,320]{3,2,1,0:T(8,128)(2,1)S(1)} collective-permute-done((bf16[8,1,40,320]{3,2,1,0:T(8,128)(2,1)S(1)}, bf16[8,1,40,320]{3,2,1,0:T(8,128)(2,1)S(1)}, u32[]{:S(2)}, u32[]{:S(2)}) %collective-permute-start.55) | collective-permute-done | bytes 204832 | tf_op jit(solution)/shard_map/ppermute | solution.py:796
  (276 shorter events, 270.5 us)
Async XLA Ops:
  35.8 47.1 %collective-permute-start.3 = (bf16[10,50,16,128]{3,2,1,0:T(8,128)(2,1)}, bf16[10,50,16,128]{3,2,1,0:T(8,128)(2,1)S(1)}, u32[]{:S(2)}, u32[]{:S(2)}) collective-permute-start(bf16[10,50,16,128]{3,2,1,0:T(8,128)(2,1)} %get-tuple-element.57), channel_id=1, source_target_pairs={{0,1},{1,0},{2,3},{3,2},{4,5},{5,4},{6,7},{7,6},{8,9},{9,8},{10,11... | collective-permute-start | bytes 6144008 | tf_op jit(solution)/shard_map/ppermute | solution.py:629
  37.6 42.0 %collective-permute-start.4 = (bf16[6,50,16,128]{3,2,1,0:T(8,128)(2,1)}, bf16[6,50,16,128]{3,2,1,0:T(8,128)(2,1)S(1)}, u32[]{:S(2)}, u32[]{:S(2)}) collective-permute-start(bf16[6,50,16,128]{3,2,1,0:T(8,128)(2,1)} %get-tuple-element.56.refs_0_.refs_4_), channel_id=1, source_target_pairs={{1,2},{2,1},{5,6},{6,5},{9,10},{10,9},{13,14},{14,13},{17,18},{18,... | collective-permute-start | bytes 3686408 | tf_op jit(solution)/shard_map/ppermute | solution.py:629
  89.5 55.6 %collective-permute-start.9 = (bf16[12,50,16,128]{3,2,1,0:T(8,128)(2,1)}, bf16[12,50,16,128]{3,2,1,0:T(8,128)(2,1)S(1)}, u32[]{:S(2)}, u32[]{:S(2)}) collective-permute-start(bf16[12,50,16,128]{3,2,1,0:T(8,128)(2,1)} %get-tuple-element.59.refs_3_), channel_id=1, source_target_pairs={{0,1},{1,0},{2,3},{3,2},{4,5},{5,4},{6,7},{7,6},{8,9},{9,8},{10,11... | collective-permute-start | bytes 7372808 | tf_op jit(solution)/shard_map/ppermute | solution.py:629
  96.1 62.7 %collective-permute-start.8 = (bf16[6,50,16,128]{3,2,1,0:T(8,128)(2,1)}, bf16[6,50,16,128]{3,2,1,0:T(8,128)(2,1)}, u32[]{:S(2)}, u32[]{:S(2)}) collective-permute-start(bf16[6,50,16,128]{3,2,1,0:T(8,128)(2,1)} %pass_on.6.refs_0_), channel_id=1, source_target_pairs={{1,2},{2,1},{5,6},{6,5},{9,10},{10,9},{13,14},{14,13},{17,18},{18,... | collective-permute-start | bytes 3686408 | tf_op jit(solution)/shard_map/ppermute | solution.py:629
  121.8 40.8 %collective-permute-start.17 = (bf16[2,3,40,16,80]{4,3,2,1,0:T(8,128)(2,1)}, bf16[2,3,40,16,80]{4,3,2,1,0:T(8,128)(2,1)}, u32[]{:S(2)}, u32[]{:S(2)}) collective-permute-start(bf16[2,3,40,16,80]{4,3,2,1,0:T(8,128)(2,1)} %bitcast.96), channel_id=1, source_target_pairs={{0,8},{8,0},{16,24},{24,16},{1,9},{9,1},{17,25},{25,17},{2,10},{10... | collective-permute-start | bytes 1843208 | tf_op jit(solution)/shard_map/ppermute | solution.py:615
  122.3 42.0 %collective-permute-start.18 = (bf16[2,3,40,16,80]{4,3,2,1,0:T(8,128)(2,1)}, bf16[2,3,40,16,80]{4,3,2,1,0:T(8,128)(2,1)}, u32[]{:S(2)}, u32[]{:S(2)}) collective-permute-start(bf16[2,3,40,16,80]{4,3,2,1,0:T(8,128)(2,1)} %bitcast.95), channel_id=1, source_target_pairs={{0,16},{8,24},{16,0},{24,8},{1,17},{9,25},{17,1},{25,9},{2,18},{10... | collective-permute-start | bytes 1843208 | tf_op jit(solution)/shard_map/ppermute | solution.py:615
  162.6 92.7 %collective-permute-start.14 = (bf16[6,50,16,128]{3,2,1,0:T(8,128)(2,1)}, bf16[6,50,16,128]{3,2,1,0:T(8,128)(2,1)}, u32[]{:S(2)}, u32[]{:S(2)}) collective-permute-start(bf16[6,50,16,128]{3,2,1,0:T(8,128)(2,1)} %get-tuple-element.62.refs_10_), channel_id=1, source_target_pairs={{1,2},{2,1},{5,6},{6,5},{9,10},{10,9},{13,14},{14,13},{17,18},{18,... | collective-permute-start | bytes 3686408 | tf_op jit(solution)/shard_map/ppermute | solution.py:629
  164.3 91.0 %collective-permute-start.15 = (bf16[4,50,16,128]{3,2,1,0:T(8,128)(2,1)}, bf16[4,50,16,128]{3,2,1,0:T(8,128)(2,1)S(1)}, u32[]{:S(2)}, u32[]{:S(2)}) collective-permute-start(bf16[4,50,16,128]{3,2,1,0:T(8,128)(2,1)} %get-tuple-element.63), channel_id=1, source_target_pairs={{0,1},{1,0},{2,3},{3,2},{4,5},{5,4},{6,7},{7,6},{8,9},{9,8},{10,11... | collective-permute-start | bytes 2457608 | tf_op jit(solution)/shard_map/ppermute | solution.py:629
  197.0 88.3 %collective-permute-start.22 = (bf16[8,50,16,128]{3,2,1,0:T(8,128)(2,1)}, bf16[8,50,16,128]{3,2,1,0:T(8,128)(2,1)S(1)}, u32[]{:S(2)}, u32[]{:S(2)}) collective-permute-start(bf16[8,50,16,128]{3,2,1,0:T(8,128)(2,1)} %get-tuple-element.66.refs_3_), channel_id=1, source_target_pairs={{0,1},{1,0},{2,3},{3,2},{4,5},{5,4},{6,7},{7,6},{8,9},{9,8},{10,11... | collective-permute-start | bytes 4915208 | tf_op jit(solution)/shard_map/ppermute | solution.py:629
  198.8 51.2 %collective-permute-start.21 = (bf16[320,640]{1,0:T(8,128)(2,1)}, bf16[320,640]{1,0:T(8,128)(2,1)S(1)}, u32[]{:S(2)}, u32[]{:S(2)}) collective-permute-start(bf16[320,640]{1,0:T(8,128)(2,1)} %copy.31.left_ref), channel_id=1, source_target_pairs={{0,1},{3,2},{4,5},{7,6},{8,9},{11,10},{12,13},{15,14},{16,17},{19,... | collective-permute-start | bytes 1228808 | tf_op jit(solution)/shard_map/ppermute | solution.py:629
  201.1 84.3 %collective-permute-start.24 = (bf16[6,50,16,128]{3,2,1,0:T(8,128)(2,1)}, bf16[6,50,16,128]{3,2,1,0:T(8,128)(2,1)}, u32[]{:S(2)}, u32[]{:S(2)}) collective-permute-start(bf16[6,50,16,128]{3,2,1,0:T(8,128)(2,1)} %get-tuple-element.69.refs_0_.refs_4_), channel_id=1, source_target_pairs={{1,2},{2,1},{5,6},{6,5},{9,10},{10,9},{13,14},{14,13},{17,18},{18,... | collective-permute-start | bytes 3686408 | tf_op jit(solution)/shard_map/ppermute | solution.py:629
  262.2 48.0 %collective-permute-start.27 = (bf16[6,50,16,128]{3,2,1,0:T(8,128)(2,1)}, bf16[6,50,16,128]{3,2,1,0:T(8,128)(2,1)}, u32[]{:S(2)}, u32[]{:S(2)}) collective-permute-start(bf16[6,50,16,128]{3,2,1,0:T(8,128)(2,1)} %get-tuple-element.67.refs_10_), channel_id=1, source_target_pairs={{1,2},{2,1},{5,6},{6,5},{9,10},{10,9},{13,14},{14,13},{17,18},{18,... | collective-permute-start | bytes 3686408 | tf_op jit(solution)/shard_map/ppermute | solution.py:629
  291.5 63.2 %collective-permute-start.29 = (bf16[6,50,16,128]{3,2,1,0:T(8,128)(2,1)}, bf16[6,50,16,128]{3,2,1,0:T(8,128)(2,1)}, u32[]{:S(2)}, u32[]{:S(2)}) collective-permute-start(bf16[6,50,16,128]{3,2,1,0:T(8,128)(2,1)} %get-tuple-element.78.refs_0_.refs_4_), channel_id=1, source_target_pairs={{1,2},{2,1},{5,6},{6,5},{9,10},{10,9},{13,14},{14,13},{17,18},{18,... | collective-permute-start | bytes 3686408 | tf_op jit(solution)/shard_map/ppermute | solution.py:629
  293.2 61.5 %collective-permute-start.30 = (bf16[8,50,16,128]{3,2,1,0:T(8,128)(2,1)}, bf16[8,50,16,128]{3,2,1,0:T(8,128)(2,1)S(1)}, u32[]{:S(2)}, u32[]{:S(2)}) collective-permute-start(bf16[8,50,16,128]{3,2,1,0:T(8,128)(2,1)} %get-tuple-element.70.refs_6_.refs_10_), channel_id=1, source_target_pairs={{0,1},{1,0},{2,3},{3,2},{4,5},{5,4},{6,7},{7,6},{8,9},{9,8},{10,11... | collective-permute-start | bytes 4915208 | tf_op jit(solution)/shard_map/ppermute | solution.py:629
  309.7 40.2 %collective-permute-start.26 = (bf16[8,64,320]{2,1,0:T(8,128)(2,1)}, bf16[8,64,320]{2,1,0:T(8,128)(2,1)S(1)}, u32[]{:S(2)}, u32[]{:S(2)}) collective-permute-start(bf16[8,64,320]{2,1,0:T(8,128)(2,1)} %get-tuple-element.74), channel_id=1, source_target_pairs={{0,8},{8,0},{16,24},{24,16},{1,9},{9,1},{17,25},{25,17},{2,10},{10... | collective-permute-start | bytes 983048 | tf_op jit(solution)/shard_map/ppermute | solution.py:661
  313.5 60.4 %collective-permute-start.32 = (bf16[6,50,16,128]{3,2,1,0:T(8,128)(2,1)}, bf16[6,50,16,128]{3,2,1,0:T(8,128)(2,1)S(1)}, u32[]{:S(2)}, u32[]{:S(2)}) collective-permute-start(bf16[6,50,16,128]{3,2,1,0:T(8,128)(2,1)} %get-tuple-element.75.refs_10_), channel_id=1, source_target_pairs={{1,2},{2,1},{5,6},{6,5},{9,10},{10,9},{13,14},{14,13},{17,18},{18,... | collective-permute-start | bytes 3686408 | tf_op jit(solution)/shard_map/ppermute | solution.py:629
  357.5 83.1 %collective-permute-start.40 = (bf16[4,50,16,128]{3,2,1,0:T(8,128)(2,1)}, bf16[4,50,16,128]{3,2,1,0:T(8,128)(2,1)S(1)}, u32[]{:S(2)}, u32[]{:S(2)}) collective-permute-start(bf16[4,50,16,128]{3,2,1,0:T(8,128)(2,1)} %get-tuple-element.79.refs_10_), channel_id=1, source_target_pairs={{0,1},{1,0},{2,3},{3,2},{4,5},{5,4},{6,7},{7,6},{8,9},{9,8},{10,11... | collective-permute-start | bytes 2457608 | tf_op jit(solution)/shard_map/ppermute | solution.py:629
  373.4 46.2 %collective-permute-start.34 = (bf16[8,64,320]{2,1,0:T(8,128)(2,1)}, bf16[8,64,320]{2,1,0:T(8,128)(2,1)S(1)}, u32[]{:S(2)}, u32[]{:S(2)}) collective-permute-start(bf16[8,64,320]{2,1,0:T(8,128)(2,1)} %get-tuple-element.83), channel_id=1, source_target_pairs={{0,8},{8,0},{16,24},{24,16},{1,9},{9,1},{17,25},{25,17},{2,10},{10... | collective-permute-start | bytes 983048 | tf_op jit(solution)/shard_map/ppermute | solution.py:661
  373.4 46.2 %collective-permute-start.35 = (bf16[8,64,320]{2,1,0:T(8,128)(2,1)}, bf16[8,64,320]{2,1,0:T(8,128)(2,1)S(1)}, u32[]{:S(2)}, u32[]{:S(2)}) collective-permute-start(bf16[8,64,320]{2,1,0:T(8,128)(2,1)} %get-tuple-element.85), channel_id=1, source_target_pairs={{0,8},{8,0},{16,24},{24,16},{1,9},{9,1},{17,25},{25,17},{2,10},{10... | collective-permute-start | bytes 983048 | tf_op jit(solution)/shard_map/ppermute | solution.py:661
  378.3 62.4 %collective-permute-start.38 = (bf16[6,50,16,128]{3,2,1,0:T(8,128)(2,1)}, bf16[6,50,16,128]{3,2,1,0:T(8,128)(2,1)S(1)}, u32[]{:S(2)}, u32[]{:S(2)}) collective-permute-start(bf16[6,50,16,128]{3,2,1,0:T(8,128)(2,1)} %get-tuple-element.82.refs_10_), channel_id=1, source_target_pairs={{1,2},{2,1},{5,6},{6,5},{9,10},{10,9},{13,14},{14,13},{17,18},{18,... | collective-permute-start | bytes 3686408 | tf_op jit(solution)/shard_map/ppermute | solution.py:629
  432.0 46.1 %collective-permute-start.41 = (bf16[8,64,320]{2,1,0:T(8,128)(2,1)}, bf16[8,64,320]{2,1,0:T(8,128)(2,1)S(1)}, u32[]{:S(2)}, u32[]{:S(2)}) collective-permute-start(bf16[8,64,320]{2,1,0:T(8,128)(2,1)} %get-tuple-element.90), channel_id=1, source_target_pairs={{0,8},{8,0},{16,24},{24,16},{1,9},{9,1},{17,25},{25,17},{2,10},{10... | collective-permute-start | bytes 983048 | tf_op jit(solution)/shard_map/ppermute | solution.py:661
  434.5 43.6 %collective-permute-start.42 = (bf16[8,64,320]{2,1,0:T(8,128)(2,1)}, bf16[8,64,320]{2,1,0:T(8,128)(2,1)S(1)}, u32[]{:S(2)}, u32[]{:S(2)}) collective-permute-start(bf16[8,64,320]{2,1,0:T(8,128)(2,1)} %get-tuple-element.92), channel_id=1, source_target_pairs={{0,8},{8,0},{16,24},{24,16},{1,9},{9,1},{17,25},{25,17},{2,10},{10... | collective-permute-start | bytes 983048 | tf_op jit(solution)/shard_map/ppermute | solution.py:661
  440.2 42.8 %collective-permute-start.37 = (bf16[8,4,8,320]{3,2,1,0:T(8,128)(2,1)}, bf16[8,4,8,320]{3,2,1,0:T(8,128)(2,1)S(1)}, u32[]{:S(2)}, u32[]{:S(2)}) collective-permute-start(bf16[8,4,8,320]{3,2,1,0:T(8,128)(2,1)} %dynamic-slice_convert_fusion.6), channel_id=1, source_target_pairs={{0,4},{4,0},{1,5},{5,1},{2,6},{6,2},{3,7},{7,3},{8,12},{12,8},{9,1... | collective-permute-start | bytes 491528 | tf_op jit(solution)/shard_map/ppermute | solution.py:678
  444.2 57.6 %collective-permute-start.45 = (bf16[4,50,16,128]{3,2,1,0:T(8,128)(2,1)}, bf16[4,50,16,128]{3,2,1,0:T(8,128)(2,1)S(1)}, u32[]{:S(2)}, u32[]{:S(2)}) collective-permute-start(bf16[4,50,16,128]{3,2,1,0:T(8,128)(2,1)} %pass_on.11.refs_10_), channel_id=1, source_target_pairs={{0,1},{1,0},{2,3},{3,2},{4,5},{5,4},{6,7},{7,6},{8,9},{9,8},{10,11... | collective-permute-start | bytes 2457608 | tf_op jit(solution)/shard_map/ppermute | solution.py:629
  (83 other events, 893.0 us)

commit v8 on v7

--- a/solution.py
+++ b/solution.py
@@ -395,25 +395,50 @@
     )(*[got for _, got, _, _ in parts], *deps)
 
 
-def join_kernel(count, *refs):
-    outs = refs[-count:]
-    for i in range(count):
-        outs[i][...] = (refs[2 * i][...].astype(jnp.float32) + refs[2 * i + 1][...].astype(jnp.float32)).astype(
-            outs[i].dtype
-        )
-
-
-def join(pairs, deps):
+def join_kernel(one_ref, two_ref, *refs):
+    refs[-1][...] = one_ref[...] + two_ref[...].astype(jnp.float32)
+
+
+def join(one, two, deps):
     vmem = pl.BlockSpec(memory_space=pltpu.VMEM)
-    types = [jnp.float32] + [jnp.bfloat16] * (len(pairs) - 1)
     return pl.pallas_call(
-        functools.partial(join_kernel, len(pairs)),
-        out_shape=[jax.ShapeDtypeStruct(a.shape, kind) for (a, _), kind in zip(pairs, types)],
-        in_specs=[vmem] * (2 * len(pairs)) + [pl.BlockSpec(memory_space=pl.ANY)] * len(deps),
-        out_specs=[vmem] * len(pairs),
+        join_kernel,
+        out_shape=jax.ShapeDtypeStruct(one.shape, jnp.float32),
+        in_specs=[vmem] * 2 + [pl.BlockSpec(memory_space=pl.ANY)] * len(deps),
+        out_specs=vmem,
         compiler_params=pltpu.CompilerParams(vmem_limit_bytes=VMEM_BYTES),
         name="join",
-    )(*[x for pair in pairs for x in pair], *deps)
+    )(one, two, *deps)
+
+
+def join_roles_kernel(chunks, pieces, spot_ref, *refs):
+    keep_ref, give_ref, held = refs[-3:]
+    half = keep_ref.shape[2]
+    side = spot_ref[2]
+    for t in range(chunks):
+        value = refs[t * pieces][...].astype(jnp.float32)
+        for i in range(1, pieces):
+            value = value + refs[t * pieces + i][...].astype(jnp.float32)
+        held[...] = value
+        keep_ref[t] = held[:, pl.ds(pl.multiple_of(side * half, half), half)]
+        give_ref[t] = held[:, pl.ds(pl.multiple_of((1 - side) * half, half), half)].astype(jnp.bfloat16)
+
+
+def join_roles(spot, groups, deps):
+    windows, rows, full = groups[0][0].shape
+    vmem = pl.BlockSpec(memory_space=pltpu.VMEM)
+    shape = (len(groups), windows, rows // 2, full)
+    return pl.pallas_call(
+        functools.partial(join_roles_kernel, len(groups), len(groups[0])),
+        out_shape=[jax.ShapeDtypeStruct(shape, jnp.float32), jax.ShapeDtypeStruct(shape, jnp.bfloat16)],
+        in_specs=[pl.BlockSpec(memory_space=pltpu.SMEM)]
+        + [vmem] * (len(groups) * len(groups[0]))
+        + [pl.BlockSpec(memory_space=pl.ANY)] * len(deps),
+        out_specs=[vmem] * 2,
+        scratch_shapes=[pltpu.VMEM((windows, rows, full), jnp.float32)],
+        compiler_params=pltpu.CompilerParams(vmem_limit_bytes=VMEM_BYTES),
+        name="join_roles",
+    )(spot, *[x for group in groups for x in group], *deps)
 
 
 def even_kernel(sides, group, groups, slab, use_ends, use_inner, starts, spot_ref, *refs):
@@ -601,7 +626,8 @@
     windows = left_iso.shape[1]
     slab = left_iso.shape[2]
     downs, full = bottoms.shape[3], bottoms.shape[4]
-    spot = jnp.stack([here, role]).astype(jnp.int32)
+    step = max(contrs // 2, 1)
+    spot = jnp.stack([here, role, lax.axis_index("contr") // step]).astype(jnp.int32)
 
     cut = tops.reshape(kinds, depth_all, contrs, chunks, unit, width)
 
@@ -630,14 +656,15 @@
 
     pieces = {}
     exchange(0, 1, role)
-    left_all = jnp.concatenate(
-        [lax.dynamic_slice_in_dim(left_iso, (role ^ s) * width, width, 0) for s in range(roles)], axis=0
-    )
-    total = left_all.shape[0]
+    total = left_iso.shape[0]
     mains = total // LANES
     plane = (mains * group + (group + 1) // 2, rows, LANES)
 
-    flat_left = left_all.reshape(total, windows * slab)
+    def flat_left(left):
+        rows = [lax.dynamic_slice_in_dim(left, (role ^ s) * width, width, 0) for s in range(roles)]
+        return jnp.concatenate(rows, axis=0).reshape(total, windows * slab)
+
+    near_left = move(left_iso, hand)
     middle = lower(1, role) * jnp.asarray(2, bottoms.dtype)
     tiles = (slab // rows, downs * full // LANES)
     count = depth * tiles[0] * tiles[1]
@@ -657,47 +684,57 @@
     near_low = None
     done = None
 
-    def send_core(t):
-        stages[t] = [lax.ppermute(shares[t][s], "role", [(j, j ^ 1) for j in range(roles)]) for s in (1, 3)]
-
-    def join_core(t, deps):
-        kept, give = join([(shares[t][0], stages[t][0]), (shares[t][2], stages[t][1])], deps)
-        stages[t] = [kept, lax.ppermute(give, "role", [(j, j ^ 2) for j in range(roles)])]
-        return kept
-
-    def join_chip(t, deps):
-        summed = join([tuple(stages[t])], deps)[0]
-        size, step = sides * contrs, contrs // 2
-        stages[t] = halve(summed.reshape(windows, size, unit, full), size, step) + (size // 2, step // 2)
+    def send_roles(t):
+        stages[t] = [shares[t][0]] + [
+            lax.ppermute(shares[t][s], "role", [(j, j ^ s) for j in range(roles)]) for s in range(1, roles)
+        ]
+
+    def add_roles(ts, deps):
+        step = contrs // 2
+        keep, give = join_roles(spot, [stages[t] for t in ts], deps)
+        halves[ts] = keep, lax.ppermute(give, "contr", [(j, j ^ step) for j in range(contrs)])
+        return keep
+
+    def add_contr(ts, deps):
+        summed = join(*halves[ts], deps)
+        size, step = sides * contrs // 2, contrs // 4
+        summed = summed.reshape(len(ts), windows, size, unit, full)
+        while step:
+            size //= 2
+            bit = (lax.axis_index("contr") // step) % 2
+            keep = lax.dynamic_slice_in_dim(summed, bit * size, size, 2)
+            give = lax.dynamic_slice_in_dim(summed, (1 - bit) * size, size, 2).astype(jnp.bfloat16)
+            got = lax.ppermute(give, "contr", [(j, j ^ step) for j in range(contrs)])
+            summed = keep + got.astype(jnp.float32)
+            step //= 2
+        reduced[ts] = summed
         return summed
 
-    def halve(summed, size, step):
-        bit = (lax.axis_index("contr") // step) % 2
-        keep = lax.dynamic_slice_in_dim(summed, bit * (size // 2), size // 2, 1)
-        give = lax.dynamic_slice_in_dim(summed, (1 - bit) * (size // 2), size // 2, 1).astype(jnp.bfloat16)
-        return keep, lax.ppermute(give, "contr", [(j, j ^ step) for j in range(contrs)])
-
-    def join_contr(t, deps):
-        keep, got, size, step = stages[t]
-        summed = join([(keep, got)], deps)[0]
-        while step:
-            summed = join([halve(summed, size, step)], [])[0]
-            size, step = size // 2, step // 2
-        reduced[t] = summed
-        return summed
-
+    def project(groups):
+        summed = jnp.concatenate([reduced[ts] for ts in groups], axis=0)
+        first, count = groups[0][0], summed.shape[0]
+        mine = lax.dynamic_slice_in_dim(summed, here, 1, 2)
+        for s in range(1, sides):
+            give = lax.dynamic_slice_in_dim(summed, here ^ s, 1, 2).astype(jnp.bfloat16)
+            got = lax.ppermute(give, "horiz", [(z, z ^ s) for z in range(sides)])
+            mine = mine + got.astype(jnp.float32)
+        mine = mine.reshape(count, windows, unit, full).astype(jnp.bfloat16)
+        iso = right_iso[first * unit:(first + count) * unit].reshape(count, unit, full, right_iso.shape[2])
+        return jnp.einsum("taur,turb->ab", mine, iso, preferred_element_type=jnp.float32)
+
+    halves = {}
     stages, extra = {}, []
     for r in range(chunks + 3):
         if r <= chunks:
             fresh = r < chunks
             base = 3 * groups if fresh else 0
-            most = {0: 2, 1: 3}.get(r, 1) * groups if fresh else 0
+            most = {0: 3, 1: 2}.get(r, 1) * groups if fresh else 0
             at, size = take(most)
             length = max(base + size, 4 * groups) if fresh else 2 * groups
             given = dict(
                 sides=sides, groups=groups, back=2 * groups if fresh else 0, kind=base, low=at, count=size
             )
-            deps = [sent[r - 1]] if r else []
+            deps = [sent[r - 1]] if r else [near_left]
             deps += [sums[r - 1]] if r - 1 in sums else []
             out, mine, mark = pack(
                 spot, pieces.pop(r) if fresh else ([], 0), straight.get(r - 1), carried, deps + extra, given,
@@ -716,7 +753,6 @@
                     exchange(first, size, mark[1])
             if r == 0:
                 late = mark[1]
-                near_left = move(flat_left, hand)
                 outer = [lower(0, late), lower(2, late)]
                 extra = list(outer)
         t = r - 4
@@ -732,9 +768,9 @@
             )
             done = shares[t][0]
             extra = []
-            send_core(t)
+            send_roles(t)
             if t - 1 in stages:
-                extra.append(join_chip(t - 1, [done]))
+                extra.append(add_roles((t - 1,), [done]))
         if 1 <= r <= chunks + 1:
             at, size = take(2 * groups) if 2 <= r else (0, 0)
             given = dict(sides=sides, groups=groups, cross=r <= chunks, low=at, count=size)
@@ -749,7 +785,7 @@
                     parts.append((at, last[r], 0, size))
             done = outs[0]
         if r == 1:
-            first_table = make_table(flat_left, [done], windows, slab)
+            first_table = make_table(flat_left(left_iso), [done], windows, slab)
             low = make_lows(outer, group)
             extra = [low, first_table]
         if r == 2:
@@ -770,33 +806,23 @@
             done = sums[r]
             extra = []
             if r == 3:
-                near_table = make_table(near_left, [], windows, slab)
+                near_table = make_table(flat_left(near_left), [done], windows, slab)
                 extra.append(near_table)
-            if r - 4 in shares:
-                extra.append(join_core(r - 4, [done]))
-            if r - 5 in shares:
-                extra.append(join_contr(r - 5, [done]))
+            if (r - 5,) in halves:
+                extra.append(add_contr((r - 5,), [done]))
     t = chunks - 1
     blocks = [(own[t], 2 * groups), (sent[t], 2 * groups), (straight[t], 2 * groups), (turned[t + 1], 2 * groups)]
     shares[t] = odd_product(
         spot, blocks, sums[t + 2], sums[t + 3], [done] + extra, (first_table, near_table),
         (middle_low, near_low), sides, group, groups, slab, roles,
     )
-    send_core(t)
-    join_chip(t - 1, [shares[t][0]])
-    join_core(t, [])
-    join_contr(t - 1, [])
-    join_chip(t, [])
-    join_contr(t, [])
-
-    summed = jnp.concatenate([reduced[t] for t in range(chunks)], axis=2)
-    mine = lax.dynamic_slice_in_dim(summed, here, 1, 1)
-    for s in range(1, sides):
-        give = lax.dynamic_slice_in_dim(summed, here ^ s, 1, 1).astype(jnp.bfloat16)
-        got = lax.ppermute(give, "horiz", [(z, z ^ s) for z in range(sides)])
-        mine = mine + got.astype(jnp.float32)
-    mine = mine.reshape(windows, share, full).astype(jnp.bfloat16)
-    projected = jnp.einsum("aur,urb->ab", mine, right_iso, preferred_element_type=jnp.float32)
+    send_roles(t)
+    late = tuple(t for t in range(chunks) if (t,) not in halves)
+    done = [(t,) for t in range(chunks) if (t,) in halves]
+    projected = project(done) if done else 0.0
+    add_roles(late, [])
+    add_contr(late, [])
+    projected = projected + project([late])
     projected = projected * jnp.where(role >= downs, 0.25, 1.0)
     for axis, size in (("contr", contrs), ("horiz", sides)):
         s = 1

time: 632 us -> 588 us (0.930)
  waiting for transfers between devices: 129 us -> 103 us
  local copies, waits for them, and re-layouts: 101 us -> 86.8 us
  Pallas kernels: 260 us -> 246 us
  starting transfers between devices: 111 us -> 120 us
    ppermute x22, waiting for transfers between devices: 75.6 us -> 45.9 us  [on_device(): move = lambda value, perm: lax.ppermute(value, 'horiz', perm)]
    pallas_call x15 -> x8, Pallas kernels: 32.5 us -> 18.8 us  [the longest x4 11.1 us: join_roles(): pl.pallas_call(functools.partial(join_roles_kernel, len(groups), len(grou...]
    ppermute x23 -> x25, starting transfers between devices: 22.6 us -> 32.8 us  [the longest x6 19.3 us: project(): got = lax.ppermute(give, 'horiz', [(z, z ^ s) for z in range(sides)])]
    unnamed x96 -> x79, local copies, waits for them, and re-layouts: 30.4 us -> 20.9 us
    ppermute x23 -> x25, waiting for transfers between devices: 29.7 us -> 37.3 us  [the longest x15 24.1 us: send_roles(): lax.ppermute(shares[t][s], 'role', [(j, j ^ s) for j in range(roles)])]
    convert_element_type x6 -> x1, local copies, waits for them, and re-layouts: 6.59 us -> 0.08 us  [project(): give = lax.dynamic_slice_in_dim(summed, here ^ s, 1, 2).astype(jnp.bfloat16)]
  transfers between devices with their start and end apart: 63 -> 65, of which waited for: 18 -> 20; matrix products, arithmetic and copies ran while one was open for 13% -> 14% of each run, Pallas kernels for 38% -> 40%
where the time goes in v8:
time: 588 us; the launch traced here: 579 us
  Pallas kernels  246 us (42%)
  starting transfers between devices  120 us (20%)
  waiting for transfers between devices  103 us (18%)
  local copies, waits for them, and re-layouts  86.8 us (15%)
  other arithmetic  12.8 us (2%)
  between operations  6.26 us (1%)
    pallas_call x6, Pallas kernels, even_product(): pl.pallas_call(functools.partial(even_kernel, sides, group, groups, slab,...  112 us
    ppermute x22, starting transfers between devices, on_device(): move = lambda value, perm: lax.ppermute(value, 'horiz', perm)  72.1 us
    ppermute x22, waiting for transfers between devices, on_device(): move = lambda value, perm: lax.ppermute(value, 'horiz', perm)  45.9 us
    pallas_call x5, Pallas kernels, odd_product(): pl.pallas_call(functools.partial(odd_kernel, sides, group, groups, slab,...  42 us
    pallas_call x6, Pallas kernels, pack(): pl.pallas_call(functools.partial(pack_kernel, group, len(pieces), given),...  27.5 us
    ppermute x15, waiting for transfers between devices, send_roles(): lax.ppermute(shares[t][s], 'role', [(j, j ^ s) for j in range(roles)])  24.1 us
    reshape x2, local copies, waits for them, and re-layouts, lower(): return low.reshape(depth, slab, downs * full)  21.1 us
    unnamed x79, local copies, waits for them, and re-layouts  20.9 us
  transfers between devices with their start and end apart: 65, of which 20 were waited for; matrix products, arithmetic and copies ran while one was open for 14% of the time, Pallas kernels for 40%

profile of v8, /device:TPU:0, one launch (start us, length us, event | category | flops | bytes accessed | tf_op | source)
XLA Modules:
  0.0 578.9 jit_solution(11693456725594087407)
XLA Ops:
  9.8 8.6 %dynamic-slice_multiply_fusion = bf16[1,40,80,2,320]{4,3,2,1,0:T(2,128)(2,1)} fusion(bf16[3,160,80,2,320]{4,3,2,1,0:T(2,128)(2,1)} %param.5, s32[]{:T(128)S(6)} %select_n.95), kind=kLoop, calls=%fused_computation | loop fusion | flops 2048000 | bytes 8192004 | tf_op jit(solution)/shard_map/mul | solution.py:668
  18.4 10.5 %mul.103.low_ref.refs_0_ = bf16[40,80,640]{2,1,0:T(8,128)(2,1)} reshape(bf16[1,40,80,2,320]{4,3,2,1,0:T(2,128)(2,1)} %dynamic-slice_multiply_fusion) | data formatting | bytes 8192000 | tf_op jit(solution)/shard_map/mul | solution.py:668
  53.4 9.7 %constant_dynamic-slice_fusion.20 = (bf16[1,40,80,2,320]{4,3,2,1,0:T(2,128)(2,1)}, bf16[1,40,80,2,320]{4,3,2,1,0:T(2,128)(2,1)}) fusion(bf16[3,160,80,2,320]{4,3,2,1,0:T(2,128)(2,1)} %param.5, s32[]{:T(128)S(6)} %select_n.99), kind=kLoop, calls=%fused_computation.60 | loop fusion | bytes 16384004 | tf_op jit(solution)/shard_map/dynamic_slice | solution.py:647
  63.1 10.5 %reshape.88.refs_7_.refs_0_ = bf16[40,80,640]{2,1,0:T(8,128)(2,1)} reshape(bf16[1,40,80,2,320]{4,3,2,1,0:T(2,128)(2,1)} %get-tuple-element.104) | data formatting | bytes 8192000 | tf_op jit(solution)/shard_map/reshape | solution.py:650
  73.6 10.5 %reshape.89.refs_8_.refs_1_ = bf16[40,80,640]{2,1,0:T(8,128)(2,1)} reshape(bf16[1,40,80,2,320]{4,3,2,1,0:T(2,128)(2,1)} %get-tuple-element.103) | data formatting | bytes 8192000 | tf_op jit(solution)/shard_map/reshape | solution.py:650
  84.1 12.6 %collective-permute-done.4.refs_6_.refs_0_.refs_1_.refs_5_ = bf16[12,50,16,128]{3,2,1,0:T(8,128)(2,1)S(1)} collective-permute-done((bf16[12,50,16,128]{3,2,1,0:T(8,128)(2,1)}, bf16[12,50,16,128]{3,2,1,0:T(8,128)(2,1)S(1)}, u32[]{:S(2)}, u32[]{:S(2)}) %collective-permute-start.4) | collective-permute-done | bytes 2457632 | tf_op jit(solution)/shard_map/ppermute | solution.py:655
  135.9 13.2 %collective-permute-done.10.refs_6_.refs_0_.refs_1_.refs_5_ = bf16[10,50,16,128]{3,2,1,0:T(8,128)(2,1)S(1)} collective-permute-done((bf16[10,50,16,128]{3,2,1,0:T(8,128)(2,1)}, bf16[10,50,16,128]{3,2,1,0:T(8,128)(2,1)S(1)}, u32[]{:S(2)}, u32[]{:S(2)}) %collective-permute-start.10) | collective-permute-done | bytes 2048032 | tf_op jit(solution)/shard_map/ppermute | solution.py:655
  176.7 9.5 %collective-permute-done.20.refs_3_ = bf16[2,3,40,16,80]{4,3,2,1,0:T(8,128)(2,1)S(1)} collective-permute-done((bf16[2,3,40,16,80]{4,3,2,1,0:T(8,128)(2,1)}, bf16[2,3,40,16,80]{4,3,2,1,0:T(8,128)(2,1)S(1)}, u32[]{:S(2)}, u32[]{:S(2)}) %collective-permute-start.20) | collective-permute-done | bytes 614432 | tf_op jit(solution)/shard_map/ppermute | solution.py:641
  186.2 9.0 %collective-permute-done.17.refs_6_.refs_0_.refs_2_.refs_1_.refs_5_ = bf16[8,50,16,128]{3,2,1,0:T(8,128)(2,1)S(1)} collective-permute-done((bf16[8,50,16,128]{3,2,1,0:T(8,128)(2,1)}, bf16[8,50,16,128]{3,2,1,0:T(8,128)(2,1)S(1)}, u32[]{:S(2)}, u32[]{:S(2)}) %collective-permute-start.17) | collective-permute-done | bytes 1638432 | tf_op jit(solution)/shard_map/ppermute | solution.py:655
  222.2 21.2 %even_product.7.refs_0_.refs_7_.refs_5_.refs_4_ = f32[2,512,640]{2,1,0:T(8,128)} custom-call(s32[3]{0:T(128)} %pad_add_fusion.spot_ref, bf16[6,50,16,128]{3,2,1,0:T(8,128)(2,1)} %get-tuple-element.58.refs_0_.refs_4_, bf16[10,50,16,128]{3,2,1,0:T(8,128)(2,1)} %copy-done.1, bf16[6,50,16,128]{3,2,1,0:T(8,128)(2,1)} %collective-permute-done.14.refs_4_.refs_2_, ...), custom_call_target="tpu_custom_call" | custom-call | flops 11072962560 | bytes 20971520 | tf_op jit(solution)/shard_map/even_product/pallas_call | solution.py:506
  271.0 8.3 %odd_product.5 = (bf16[8,64,320]{2,1,0:T(8,128)(2,1)}, bf16[8,64,320]{2,1,0:T(8,128)(2,1)}, bf16[8,64,320]{2,1,0:T(8,128)(2,1)}, bf16[8,64,320]{2,1,0:T(8,128)(2,1)}) custom-call(s32[3]{0:T(128)} %pad_add_fusion.spot_ref, bf16[6,50,16,128]{3,2,1,0:T(8,128)(2,1)} %get-tuple-element.54.refs_0_.refs_4_, bf16[12,50,16,128]{3,2,1,0:T(8,128)(2,1)} %copy-done, ...), custom_call_target="tpu_custom_call" | custom-call | flops 8724152320 | bytes 20971520 | tf_op jit(solution)/shard_map/odd_product/pallas_call | solution.py:591
  285.4 21.1 %even_product.8.refs_3_.refs_5_.refs_4_ = f32[2,512,640]{2,1,0:T(8,128)} custom-call(s32[3]{0:T(128)} %pad_add_fusion.spot_ref, bf16[6,50,16,128]{3,2,1,0:T(8,128)(2,1)} %get-tuple-element.63.refs_0_.refs_4_, bf16[8,50,16,128]{3,2,1,0:T(8,128)(2,1)} %copy-done.2, bf16[6,50,16,128]{3,2,1,0:T(8,128)(2,1)} %collective-permute-done.21.refs_4_.refs_2_, ...), custom_call_target="tpu_custom_call" | custom-call | flops 11072962560 | bytes 20971520 | tf_op jit(solution)/shard_map/even_product/pallas_call | solution.py:506
  306.9 15.8 %collective-permute-start.33 = (bf16[4,50,16,128]{3,2,1,0:T(8,128)(2,1)}, bf16[4,50,16,128]{3,2,1,0:T(8,128)(2,1)S(1)}, u32[]{:S(2)}, u32[]{:S(2)}) collective-permute-start(bf16[4,50,16,128]{3,2,1,0:T(8,128)(2,1)} %get-tuple-element.79), channel_id=1, source_target_pairs={{0,1},{1,0},{2,3},{3,2},{4,5},{5,4},{6,7},{7,6},{8,9},{9,8},{10,11... | collective-permute-start | bytes 2457608 | tf_op jit(solution)/shard_map/ppermute | solution.py:655
  324.3 8.4 %odd_product.6 = (bf16[8,64,320]{2,1,0:T(8,128)(2,1)}, bf16[8,64,320]{2,1,0:T(8,128)(2,1)}, bf16[8,64,320]{2,1,0:T(8,128)(2,1)}, bf16[8,64,320]{2,1,0:T(8,128)(2,1)}) custom-call(s32[3]{0:T(128)} %pad_add_fusion.spot_ref, bf16[6,50,16,128]{3,2,1,0:T(8,128)(2,1)} %get-tuple-element.58.refs_0_.refs_4_, bf16[10,50,16,128]{3,2,1,0:T(8,128)(2,1)} %copy-done.1, ...), custom_call_target="tpu_custom_call" | custom-call | flops 8724152320 | bytes 20971520 | tf_op jit(solution)/shard_map/odd_product/pallas_call | solution.py:591
  332.7 14.8 %collective-permute-start.40 = (bf16[4,50,16,128]{3,2,1,0:T(8,128)(2,1)}, bf16[4,50,16,128]{3,2,1,0:T(8,128)(2,1)S(1)}, u32[]{:S(2)}, u32[]{:S(2)}) collective-permute-start(bf16[4,50,16,128]{3,2,1,0:T(8,128)(2,1)} %get-tuple-element.75.refs_10_), channel_id=1, source_target_pairs={{0,1},{1,0},{2,3},{3,2},{4,5},{5,4},{6,7},{7,6},{8,9},{9,8},{10,11... | collective-permute-start | bytes 2457608 | tf_op jit(solution)/shard_map/ppermute | solution.py:655
  359.9 21.2 %even_product.9.refs_0_.refs_5_.refs_10_.refs_4_ = f32[2,512,640]{2,1,0:T(8,128)} custom-call(s32[3]{0:T(128)} %pad_add_fusion.spot_ref, bf16[6,50,16,128]{3,2,1,0:T(8,128)(2,1)} %get-tuple-element.67.refs_0_.refs_4_, bf16[8,50,16,128]{3,2,1,0:T(8,128)(2,1)} %copy-done.3, bf16[6,50,16,128]{3,2,1,0:T(8,128)(2,1)} %collective-permute-done.24.refs_4_.refs_2_, ...), custom_call_target="tpu_custom_call" | custom-call | flops 11072962560 | bytes 20971520 | tf_op jit(solution)/shard_map/even_product/pallas_call | solution.py:506
  384.6 8.4 %odd_product.7 = (bf16[8,64,320]{2,1,0:T(8,128)(2,1)}, bf16[8,64,320]{2,1,0:T(8,128)(2,1)}, bf16[8,64,320]{2,1,0:T(8,128)(2,1)}, bf16[8,64,320]{2,1,0:T(8,128)(2,1)}) custom-call(s32[3]{0:T(128)} %pad_add_fusion.spot_ref, bf16[6,50,16,128]{3,2,1,0:T(8,128)(2,1)} %get-tuple-element.63.refs_0_.refs_4_, bf16[8,50,16,128]{3,2,1,0:T(8,128)(2,1)} %copy-done.2, ...), custom_call_target="tpu_custom_call" | custom-call | flops 8724152320 | bytes 20971520 | tf_op jit(solution)/shard_map/odd_product/pallas_call | solution.py:591
  407.6 7.9 %collective-permute-start.45 = (bf16[4,50,16,128]{3,2,1,0:T(8,128)(2,1)}, bf16[4,50,16,128]{3,2,1,0:T(8,128)(2,1)S(1)}, u32[]{:S(2)}, u32[]{:S(2)}) collective-permute-start(bf16[4,50,16,128]{3,2,1,0:T(8,128)(2,1)} %pass_on.11.refs_10_), channel_id=1, source_target_pairs={{0,1},{1,0},{2,3},{3,2},{4,5},{5,4},{6,7},{7,6},{8,9},{9,8},{10,11... | collective-permute-start | bytes 2457608 | tf_op jit(solution)/shard_map/ppermute | solution.py:655
  415.5 21.3 %even_product.10.refs_0_.refs_5_.refs_10_.refs_4_ = f32[2,512,640]{2,1,0:T(8,128)} custom-call(s32[3]{0:T(128)} %pad_add_fusion.spot_ref, bf16[6,50,16,128]{3,2,1,0:T(8,128)(2,1)} %get-tuple-element.74.refs_0_.refs_4_, bf16[8,50,16,128]{3,2,1,0:T(8,128)(2,1)} %copy-done.4, bf16[6,50,16,128]{3,2,1,0:T(8,128)(2,1)} %collective-permute-done.29.refs_0_.refs_2_, ...), custom_call_target="tpu_custom_call" | custom-call | flops 11072962560 | bytes 20971520 | tf_op jit(solution)/shard_map/even_product/pallas_call | solution.py:506
  439.3 8.4 %odd_product.8 = (bf16[8,64,320]{2,1,0:T(8,128)(2,1)}, bf16[8,64,320]{2,1,0:T(8,128)(2,1)}, bf16[8,64,320]{2,1,0:T(8,128)(2,1)}, bf16[8,64,320]{2,1,0:T(8,128)(2,1)}) custom-call(s32[3]{0:T(128)} %pad_add_fusion.spot_ref, bf16[6,50,16,128]{3,2,1,0:T(8,128)(2,1)} %get-tuple-element.67.refs_0_.refs_4_, bf16[8,50,16,128]{3,2,1,0:T(8,128)(2,1)} %copy-done.3, ...), custom_call_target="tpu_custom_call" | custom-call | flops 8724152320 | bytes 20971520 | tf_op jit(solution)/shard_map/odd_product/pallas_call | solution.py:591
  454.9 21.6 %even_product.11.refs_0_.refs_5_.refs_10_ = f32[2,512,640]{2,1,0:T(8,128)} custom-call(s32[3]{0:T(128)} %pad_add_fusion.spot_ref, bf16[6,50,16,128]{3,2,1,0:T(8,128)(2,1)} %get-tuple-element.74.refs_0_.refs_4_, bf16[8,50,16,128]{3,2,1,0:T(8,128)(2,1)} %copy-done.4, bf16[4,50,16,128]{3,2,1,0:T(8,128)(2,1)} %copy-done.15, bf16[4,50,16,128]{3,2,1,0:T(8,128)(2,1)} %copy-done.34, ...), custom_call_target="tpu_custom_call" | custom-call | flops 11072962560 | bytes 20971520 | tf_op jit(solution)/shard_map/even_product/pallas_call | solution.py:506
  484.6 8.5 %odd_product.9 = (bf16[8,64,320]{2,1,0:T(8,128)(2,1)}, bf16[8,64,320]{2,1,0:T(8,128)(2,1)}, bf16[8,64,320]{2,1,0:T(8,128)(2,1)}, bf16[8,64,320]{2,1,0:T(8,128)(2,1)}) custom-call(s32[3]{0:T(128)} %pad_add_fusion.spot_ref, bf16[6,50,16,128]{3,2,1,0:T(8,128)(2,1)} %get-tuple-element.74.refs_0_.refs_4_, bf16[8,50,16,128]{3,2,1,0:T(8,128)(2,1)} %copy-done.4, ...), custom_call_target="tpu_custom_call" | custom-call | flops 8724152320 | bytes 20971520 | tf_op jit(solution)/shard_map/odd_product/pallas_call | solution.py:591
  512.5 8.9 %collective-permute-done.54.refs_7_ = bf16[8,64,320]{2,1,0:T(8,128)(2,1)} collective-permute-done((bf16[8,64,320]{2,1,0:T(8,128)(2,1)}, bf16[8,64,320]{2,1,0:T(8,128)(2,1)}, u32[]{:S(2)}, u32[]{:S(2)}) %collective-permute-start.54) | collective-permute-done | bytes 327712 | tf_op jit(solution)/shard_map/ppermute | solution.py:689
  539.4 12.2 %collective-permute-start.56 = (bf16[2,8,1,8,320]{4,1,3,0,2:T(8,128)(2,1)S(1)}, bf16[2,8,1,8,320]{4,1,3,0,2:T(8,128)(2,1)S(1)}, u32[]{:S(2)}, u32[]{:S(2)}) collective-permute-start(bf16[2,8,1,8,320]{4,1,3,0,2:T(8,128)(2,1)S(1)} %copy.120), channel_id=1, source_target_pairs={{0,1},{1,0},{2,3},{3,2},{4,5},{5,4},{6,7},{7,6},{8,9},{9,8},{10,11... | collective-permute-start | bytes 245768 | tf_op jit(solution)/shard_map/ppermute | solution.py:719
  (256 shorter events, 270.6 us)
Async XLA Ops:
  41.2 55.5 %collective-permute-start.4 = (bf16[12,50,16,128]{3,2,1,0:T(8,128)(2,1)}, bf16[12,50,16,128]{3,2,1,0:T(8,128)(2,1)S(1)}, u32[]{:S(2)}, u32[]{:S(2)}) collective-permute-start(bf16[12,50,16,128]{3,2,1,0:T(8,128)(2,1)} %get-tuple-element.55), channel_id=1, source_target_pairs={{0,1},{1,0},{2,3},{3,2},{4,5},{5,4},{6,7},{7,6},{8,9},{9,8},{10,11... | collective-permute-start | bytes 7372808 | tf_op jit(solution)/shard_map/ppermute | solution.py:655
  41.2 42.9 %collective-permute-start.5 = (bf16[6,50,16,128]{3,2,1,0:T(8,128)(2,1)}, bf16[6,50,16,128]{3,2,1,0:T(8,128)(2,1)}, u32[]{:S(2)}, u32[]{:S(2)}) collective-permute-start(bf16[6,50,16,128]{3,2,1,0:T(8,128)(2,1)} %get-tuple-element.54.refs_0_.refs_4_), channel_id=1, source_target_pairs={{1,2},{2,1},{5,6},{6,5},{9,10},{10,9},{13,14},{14,13},{17,18},{18,... | collective-permute-start | bytes 3686408 | tf_op jit(solution)/shard_map/ppermute | solution.py:655
  103.2 45.9 %collective-permute-start.10 = (bf16[10,50,16,128]{3,2,1,0:T(8,128)(2,1)}, bf16[10,50,16,128]{3,2,1,0:T(8,128)(2,1)S(1)}, u32[]{:S(2)}, u32[]{:S(2)}) collective-permute-start(bf16[10,50,16,128]{3,2,1,0:T(8,128)(2,1)} %get-tuple-element.57.refs_3_), channel_id=1, source_target_pairs={{0,1},{1,0},{2,3},{3,2},{4,5},{5,4},{6,7},{7,6},{8,9},{9,8},{10,11... | collective-permute-start | bytes 6144008 | tf_op jit(solution)/shard_map/ppermute | solution.py:655
  108.3 53.7 %collective-permute-start.9 = (bf16[6,50,16,128]{3,2,1,0:T(8,128)(2,1)}, bf16[6,50,16,128]{3,2,1,0:T(8,128)(2,1)}, u32[]{:S(2)}, u32[]{:S(2)}) collective-permute-start(bf16[6,50,16,128]{3,2,1,0:T(8,128)(2,1)} %pass_on.6.refs_0_), channel_id=1, source_target_pairs={{1,2},{2,1},{5,6},{6,5},{9,10},{10,9},{13,14},{14,13},{17,18},{18,... | collective-permute-start | bytes 3686408 | tf_op jit(solution)/shard_map/ppermute | solution.py:655
  165.5 47.2 %collective-permute-start.15 = (bf16[6,50,16,128]{3,2,1,0:T(8,128)(2,1)}, bf16[6,50,16,128]{3,2,1,0:T(8,128)(2,1)}, u32[]{:S(2)}, u32[]{:S(2)}) collective-permute-start(bf16[6,50,16,128]{3,2,1,0:T(8,128)(2,1)} %get-tuple-element.60.refs_10_), channel_id=1, source_target_pairs={{1,2},{2,1},{5,6},{6,5},{9,10},{10,9},{13,14},{14,13},{17,18},{18,... | collective-permute-start | bytes 3686408 | tf_op jit(solution)/shard_map/ppermute | solution.py:655
  167.2 45.5 %collective-permute-start.16 = (bf16[4,50,16,128]{3,2,1,0:T(8,128)(2,1)}, bf16[4,50,16,128]{3,2,1,0:T(8,128)(2,1)S(1)}, u32[]{:S(2)}, u32[]{:S(2)}) collective-permute-start(bf16[4,50,16,128]{3,2,1,0:T(8,128)(2,1)} %get-tuple-element.61), channel_id=1, source_target_pairs={{0,1},{1,0},{2,3},{3,2},{4,5},{5,4},{6,7},{7,6},{8,9},{9,8},{10,11... | collective-permute-start | bytes 2457608 | tf_op jit(solution)/shard_map/ppermute | solution.py:655
  201.3 46.5 %collective-permute-start.22 = (bf16[8,50,16,128]{3,2,1,0:T(8,128)(2,1)}, bf16[8,50,16,128]{3,2,1,0:T(8,128)(2,1)S(1)}, u32[]{:S(2)}, u32[]{:S(2)}) collective-permute-start(bf16[8,50,16,128]{3,2,1,0:T(8,128)(2,1)} %get-tuple-element.64.refs_3_), channel_id=1, source_target_pairs={{0,1},{1,0},{2,3},{3,2},{4,5},{5,4},{6,7},{7,6},{8,9},{9,8},{10,11... | collective-permute-start | bytes 4915208 | tf_op jit(solution)/shard_map/ppermute | solution.py:655
  205.9 41.9 %collective-permute-start.24 = (bf16[6,50,16,128]{3,2,1,0:T(8,128)(2,1)}, bf16[6,50,16,128]{3,2,1,0:T(8,128)(2,1)}, u32[]{:S(2)}, u32[]{:S(2)}) collective-permute-start(bf16[6,50,16,128]{3,2,1,0:T(8,128)(2,1)} %get-tuple-element.67.refs_0_.refs_4_), channel_id=1, source_target_pairs={{1,2},{2,1},{5,6},{6,5},{9,10},{10,9},{13,14},{14,13},{17,18},{18,... | collective-permute-start | bytes 3686408 | tf_op jit(solution)/shard_map/ppermute | solution.py:655
  217.0 48.4 %collective-permute-start.23 = (bf16[4,50,16,128]{3,2,1,0:T(8,128)(2,1)}, bf16[4,50,16,128]{3,2,1,0:T(8,128)(2,1)S(1)}, u32[]{:S(2)}, u32[]{:S(2)}) collective-permute-start(bf16[4,50,16,128]{3,2,1,0:T(8,128)(2,1)} %get-tuple-element.66), channel_id=1, source_target_pairs={{0,1},{1,0},{2,3},{3,2},{4,5},{5,4},{6,7},{7,6},{8,9},{9,8},{10,11... | collective-permute-start | bytes 2457608 | tf_op jit(solution)/shard_map/ppermute | solution.py:655
  220.3 60.7 %collective-permute-start.28 = (bf16[6,50,16,128]{3,2,1,0:T(8,128)(2,1)}, bf16[6,50,16,128]{3,2,1,0:T(8,128)(2,1)}, u32[]{:S(2)}, u32[]{:S(2)}) collective-permute-start(bf16[6,50,16,128]{3,2,1,0:T(8,128)(2,1)} %get-tuple-element.65.refs_10_), channel_id=1, source_target_pairs={{1,2},{2,1},{5,6},{6,5},{9,10},{10,9},{13,14},{14,13},{17,18},{18,... | collective-permute-start | bytes 3686408 | tf_op jit(solution)/shard_map/ppermute | solution.py:655
  254.0 52.8 %collective-permute-start.30 = (bf16[8,50,16,128]{3,2,1,0:T(8,128)(2,1)}, bf16[8,50,16,128]{3,2,1,0:T(8,128)(2,1)S(1)}, u32[]{:S(2)}, u32[]{:S(2)}) collective-permute-start(bf16[8,50,16,128]{3,2,1,0:T(8,128)(2,1)} %get-tuple-element.68.refs_6_.refs_10_), channel_id=1, source_target_pairs={{0,1},{1,0},{2,3},{3,2},{4,5},{5,4},{6,7},{7,6},{8,9},{9,8},{10,11... | collective-permute-start | bytes 4915208 | tf_op jit(solution)/shard_map/ppermute | solution.py:655
  256.0 50.5 %collective-permute-start.29 = (bf16[6,50,16,128]{3,2,1,0:T(8,128)(2,1)}, bf16[6,50,16,128]{3,2,1,0:T(8,128)(2,1)}, u32[]{:S(2)}, u32[]{:S(2)}) collective-permute-start(bf16[6,50,16,128]{3,2,1,0:T(8,128)(2,1)} %get-tuple-element.74.refs_0_.refs_4_), channel_id=1, source_target_pairs={{1,2},{2,1},{5,6},{6,5},{9,10},{10,9},{13,14},{14,13},{17,18},{18,... | collective-permute-start | bytes 3686408 | tf_op jit(solution)/shard_map/ppermute | solution.py:655
  279.3 53.4 %collective-permute-start.25 = (bf16[8,64,320]{2,1,0:T(8,128)(2,1)}, bf16[8,64,320]{2,1,0:T(8,128)(2,1)S(1)}, u32[]{:S(2)}, u32[]{:S(2)}) collective-permute-start(bf16[8,64,320]{2,1,0:T(8,128)(2,1)} %get-tuple-element.70), channel_id=1, source_target_pairs={{0,8},{8,0},{16,24},{24,16},{1,9},{9,1},{17,25},{25,17},{2,10},{10... | collective-permute-start | bytes 983048 | tf_op jit(solution)/shard_map/ppermute | solution.py:689
  279.4 68.1 %collective-permute-start.26 = (bf16[8,64,320]{2,1,0:T(8,128)(2,1)}, bf16[8,64,320]{2,1,0:T(8,128)(2,1)}, u32[]{:S(2)}, u32[]{:S(2)}) collective-permute-start(bf16[8,64,320]{2,1,0:T(8,128)(2,1)} %get-tuple-element.71), channel_id=1, source_target_pairs={{0,16},{8,24},{16,0},{24,8},{1,17},{9,25},{17,1},{25,9},{2,18},{10... | collective-permute-start | bytes 983048 | tf_op jit(solution)/shard_map/ppermute | solution.py:689
  284.2 67.4 %collective-permute-start.32 = (bf16[6,50,16,128]{3,2,1,0:T(8,128)(2,1)}, bf16[6,50,16,128]{3,2,1,0:T(8,128)(2,1)S(1)}, u32[]{:S(2)}, u32[]{:S(2)}) collective-permute-start(bf16[6,50,16,128]{3,2,1,0:T(8,128)(2,1)} %get-tuple-element.73.refs_10_), channel_id=1, source_target_pairs={{1,2},{2,1},{5,6},{6,5},{9,10},{10,9},{13,14},{14,13},{17,18},{18,... | collective-permute-start | bytes 3686408 | tf_op jit(solution)/shard_map/ppermute | solution.py:655
  306.9 44.7 %collective-permute-start.33 = (bf16[4,50,16,128]{3,2,1,0:T(8,128)(2,1)}, bf16[4,50,16,128]{3,2,1,0:T(8,128)(2,1)S(1)}, u32[]{:S(2)}, u32[]{:S(2)}) collective-permute-start(bf16[4,50,16,128]{3,2,1,0:T(8,128)(2,1)} %get-tuple-element.79), channel_id=1, source_target_pairs={{0,1},{1,0},{2,3},{3,2},{4,5},{5,4},{6,7},{7,6},{8,9},{9,8},{10,11... | collective-permute-start | bytes 2457608 | tf_op jit(solution)/shard_map/ppermute | solution.py:655
  332.7 71.7 %collective-permute-start.40 = (bf16[4,50,16,128]{3,2,1,0:T(8,128)(2,1)}, bf16[4,50,16,128]{3,2,1,0:T(8,128)(2,1)S(1)}, u32[]{:S(2)}, u32[]{:S(2)}) collective-permute-start(bf16[4,50,16,128]{3,2,1,0:T(8,128)(2,1)} %get-tuple-element.75.refs_10_), channel_id=1, source_target_pairs={{0,1},{1,0},{2,3},{3,2},{4,5},{5,4},{6,7},{7,6},{8,9},{9,8},{10,11... | collective-permute-start | bytes 2457608 | tf_op jit(solution)/shard_map/ppermute | solution.py:655
  356.2 48.7 %collective-permute-start.38 = (bf16[6,50,16,128]{3,2,1,0:T(8,128)(2,1)}, bf16[6,50,16,128]{3,2,1,0:T(8,128)(2,1)S(1)}, u32[]{:S(2)}, u32[]{:S(2)}) collective-permute-start(bf16[6,50,16,128]{3,2,1,0:T(8,128)(2,1)} %get-tuple-element.80.refs_10_), channel_id=1, source_target_pairs={{1,2},{2,1},{5,6},{6,5},{9,10},{10,9},{13,14},{14,13},{17,18},{18,... | collective-permute-start | bytes 3686408 | tf_op jit(solution)/shard_map/ppermute | solution.py:655
  357.1 46.0 %collective-permute-start.39 = (bf16[4,50,16,128]{3,2,1,0:T(8,128)(2,1)}, bf16[4,50,16,128]{3,2,1,0:T(8,128)(2,1)S(1)}, u32[]{:S(2)}, u32[]{:S(2)}) collective-permute-start(bf16[4,50,16,128]{3,2,1,0:T(8,128)(2,1)} %get-tuple-element.87), channel_id=1, source_target_pairs={{0,1},{1,0},{2,3},{3,2},{4,5},{5,4},{6,7},{7,6},{8,9},{9,8},{10,11... | collective-permute-start | bytes 2457608 | tf_op jit(solution)/shard_map/ppermute | solution.py:655
  394.2 53.6 %collective-permute-start.41 = (bf16[8,64,320]{2,1,0:T(8,128)(2,1)}, bf16[8,64,320]{2,1,0:T(8,128)(2,1)S(1)}, u32[]{:S(2)}, u32[]{:S(2)}) collective-permute-start(bf16[8,64,320]{2,1,0:T(8,128)(2,1)} %get-tuple-element.88), channel_id=1, source_target_pairs={{0,8},{8,0},{16,24},{24,16},{1,9},{9,1},{17,25},{25,17},{2,10},{10... | collective-permute-start | bytes 983048 | tf_op jit(solution)/shard_map/ppermute | solution.py:689
  399.6 48.2 %collective-permute-start.42 = (bf16[8,64,320]{2,1,0:T(8,128)(2,1)}, bf16[8,64,320]{2,1,0:T(8,128)(2,1)S(1)}, u32[]{:S(2)}, u32[]{:S(2)}) collective-permute-start(bf16[8,64,320]{2,1,0:T(8,128)(2,1)} %get-tuple-element.89), channel_id=1, source_target_pairs={{0,16},{8,24},{16,0},{24,8},{1,17},{9,25},{17,1},{25,9},{2,18},{10... | collective-permute-start | bytes 983048 | tf_op jit(solution)/shard_map/ppermute | solution.py:689
  403.2 44.6 %collective-permute-start.43 = (bf16[8,64,320]{2,1,0:T(8,128)(2,1)}, bf16[8,64,320]{2,1,0:T(8,128)(2,1)}, u32[]{:S(2)}, u32[]{:S(2)}) collective-permute-start(bf16[8,64,320]{2,1,0:T(8,128)(2,1)} %get-tuple-element.90), channel_id=1, source_target_pairs={{0,24},{8,16},{16,8},{24,0},{1,25},{9,17},{17,9},{25,1},{2,26},{10... | collective-permute-start | bytes 983048 | tf_op jit(solution)/shard_map/ppermute | solution.py:689
  407.6 46.3 %collective-permute-start.45 = (bf16[4,50,16,128]{3,2,1,0:T(8,128)(2,1)}, bf16[4,50,16,128]{3,2,1,0:T(8,128)(2,1)S(1)}, u32[]{:S(2)}, u32[]{:S(2)}) collective-permute-start(bf16[4,50,16,128]{3,2,1,0:T(8,128)(2,1)} %pass_on.11.refs_10_), channel_id=1, source_target_pairs={{0,1},{1,0},{2,3},{3,2},{4,5},{5,4},{6,7},{7,6},{8,9},{9,8},{10,11... | collective-permute-start | bytes 2457608 | tf_op jit(solution)/shard_map/ppermute | solution.py:655
  452.6 50.3 %collective-permute-start.50 = (bf16[8,64,320]{2,1,0:T(8,128)(2,1)}, bf16[8,64,320]{2,1,0:T(8,128)(2,1)S(1)}, u32[]{:S(2)}, u32[]{:S(2)}) collective-permute-start(bf16[8,64,320]{2,1,0:T(8,128)(2,1)} %get-tuple-element.95), channel_id=1, source_target_pairs={{0,16},{8,24},{16,0},{24,8},{1,17},{9,25},{17,1},{25,9},{2,18},{10... | collective-permute-start | bytes 983048 | tf_op jit(solution)/shard_map/ppermute | solution.py:689
  (78 other events, 1066.2 us)

commit v9 on v8

--- a/solution.py
+++ b/solution.py
@@ -145,7 +145,8 @@
     out.append(jax.ShapeDtypeStruct((2,), jnp.int32))
     specs.append(pl.BlockSpec(memory_space=pltpu.SMEM))
     anywhere = pl.BlockSpec(memory_space=pl.ANY)
-    operands = [crossed if has_back else low, low] + list(deps)
+    some = crossed if has_back else pieces[0]
+    operands = [some, some if low is None else low] + list(deps)
     got = pl.pallas_call(
         functools.partial(pack_kernel, group, len(pieces), given),
         out_shape=out,
@@ -411,14 +412,15 @@
     )(one, two, *deps)
 
 
-def join_roles_kernel(chunks, pieces, spot_ref, *refs):
+def join_roles_kernel(counts, spot_ref, *refs):
     keep_ref, give_ref, held = refs[-3:]
     half = keep_ref.shape[2]
     side = spot_ref[2]
-    for t in range(chunks):
-        value = refs[t * pieces][...].astype(jnp.float32)
-        for i in range(1, pieces):
-            value = value + refs[t * pieces + i][...].astype(jnp.float32)
+    for t, count in enumerate(counts):
+        at = sum(counts[:t])
+        value = refs[at][...].astype(jnp.float32)
+        for i in range(1, count):
+            value = value + refs[at + i][...].astype(jnp.float32)
         held[...] = value
         keep_ref[t] = held[:, pl.ds(pl.multiple_of(side * half, half), half)]
         give_ref[t] = held[:, pl.ds(pl.multiple_of((1 - side) * half, half), half)].astype(jnp.bfloat16)
@@ -429,10 +431,10 @@
     vmem = pl.BlockSpec(memory_space=pltpu.VMEM)
     shape = (len(groups), windows, rows // 2, full)
     return pl.pallas_call(
-        functools.partial(join_roles_kernel, len(groups), len(groups[0])),
+        functools.partial(join_roles_kernel, [len(group) for group in groups]),
         out_shape=[jax.ShapeDtypeStruct(shape, jnp.float32), jax.ShapeDtypeStruct(shape, jnp.bfloat16)],
         in_specs=[pl.BlockSpec(memory_space=pltpu.SMEM)]
-        + [vmem] * (len(groups) * len(groups[0]))
+        + [vmem] * sum(len(group) for group in groups)
         + [pl.BlockSpec(memory_space=pl.ANY)] * len(deps),
         out_specs=[vmem] * 2,
         scratch_shapes=[pltpu.VMEM((windows, rows, full), jnp.float32)],
@@ -665,11 +667,9 @@
         return jnp.concatenate(rows, axis=0).reshape(total, windows * slab)
 
     near_left = move(left_iso, hand)
-    middle = lower(1, role) * jnp.asarray(2, bottoms.dtype)
     tiles = (slab // rows, downs * full // LANES)
-    count = depth * tiles[0] * tiles[1]
-    units = -(-count // plane[0])
-    carried = make_planes(middle, group, tiles, rows, units * plane[0]).reshape((units,) + plane)
+    units = -(-(depth * tiles[0] * tiles[1]) // plane[0])
+    carried = None
     taken = 0
 
     def take(most):
@@ -728,14 +728,16 @@
         if r <= chunks:
             fresh = r < chunks
             base = 3 * groups if fresh else 0
-            most = {0: 3, 1: 2}.get(r, 1) * groups if fresh else 0
+            most = {0: 0, 1: 4, 3: 3}.get(r, 1) * groups if fresh else 0
             at, size = take(most)
-            length = max(base + size, 4 * groups) if fresh else 2 * groups
+            length = max(base + size, 4 * groups if r else 0) if fresh else 2 * groups
             given = dict(
                 sides=sides, groups=groups, back=2 * groups if fresh else 0, kind=base, low=at, count=size
             )
             deps = [sent[r - 1]] if r else [near_left]
             deps += [sums[r - 1]] if r - 1 in sums else []
+            deps += [turned[2], last[2]] if r == 3 else []
+            deps += [got for later in pieces.values() for got in later[0]] if r == 2 else []
             out, mine, mark = pack(
                 spot, pieces.pop(r) if fresh else ([], 0), straight.get(r - 1), carried, deps + extra, given,
                 group, plane, length,
@@ -748,13 +750,14 @@
                 own[r] = mine
                 straight[r] = move(mine, cross)
             done = out
-            for first, size in {0: ((1, 1), (2, 1)), 1: ((3, chunks - 3),)}.get(r, ()):
+            for first, size in {0: ((1, 1), (2, chunks - 2))}.get(r, ()):
                 if size > 0 and first < chunks:
                     exchange(first, size, mark[1])
             if r == 0:
                 late = mark[1]
+                middle = lower(1, late) * jnp.asarray(2, bottoms.dtype)
+                carried = make_planes(middle, group, tiles, rows, units * plane[0]).reshape((units,) + plane)
                 outer = [lower(0, late), lower(2, late)]
-                extra = list(outer)
         t = r - 4
         if 0 <= t < chunks:
             if near_low is None:
@@ -816,7 +819,10 @@
         spot, blocks, sums[t + 2], sums[t + 3], [done] + extra, (first_table, near_table),
         (middle_low, near_low), sides, group, groups, slab, roles,
     )
-    send_roles(t)
+    ones = [lax.ppermute(shares[t][s], "role", [(j, j ^ 1) for j in range(roles)]) for s in (1, 3)]
+    kept = shares[t][0].astype(jnp.float32) + ones[0].astype(jnp.float32)
+    give = (shares[t][2].astype(jnp.float32) + ones[1].astype(jnp.float32)).astype(jnp.bfloat16)
+    stages[t] = [kept, lax.ppermute(give, "role", [(j, j ^ 2) for j in range(roles)])]
     late = tuple(t for t in range(chunks) if (t,) not in halves)
     done = [(t,) for t in range(chunks) if (t,) in halves]
     projected = project(done) if done else 0.0

time: 588 us -> 628 us (1.068)
  waiting for transfers between devices: 103 us -> 151 us
  local copies, waits for them, and re-layouts: 86.8 us -> 74 us
    ppermute x12 -> x9, waiting for transfers between devices: 9.91 us -> 37.5 us  [exchange(): piece = lax.ppermute(piece, 'role', [(j, j ^ s) for j in range(roles)])]
    dynamic_slice x0 -> x1, other arithmetic: none -> 13.5 us  [lower(): lax.dynamic_slice(bottoms, (kind, place * depth, 0, 0, 0), (1, depth, sla...]
    ppermute x22, waiting for transfers between devices: 45.9 us -> 58.5 us  [on_device(): move = lambda value, perm: lax.ppermute(value, 'horiz', perm)]
    dynamic_slice x1 -> x0, local copies, waits for them, and re-layouts: 9.66 us -> none  [lower(): lax.dynamic_slice(bottoms, (kind, place * depth, 0, 0, 0), (1, depth, sla...]
    ppermute x0 -> x3, waiting for transfers between devices: none -> 8.93 us  [the longest x1 8.92 us: on_device(): lax.ppermute(give, 'role', [(j, j ^ 2) for j in range(roles)])]
    ppermute x15 -> x12, waiting for transfers between devices: 24.1 us -> 15.5 us  [send_roles(): lax.ppermute(shares[t][s], 'role', [(j, j ^ s) for j in range(roles)])]
    mul x1 -> x0, other arithmetic: 8.63 us -> none  [on_device(): middle = lower(1, role) * jnp.asarray(2, bottoms.dtype)]
    ppermute x22, starting transfers between devices: 72.1 us -> 80.3 us  [on_device(): move = lambda value, perm: lax.ppermute(value, 'horiz', perm)]
  transfers between devices with their start and end apart: 65 -> 62, of which waited for: 20 -> 22; matrix products, arithmetic and copies ran while one was open for 14% -> 12% of each run, Pallas kernels for 40% -> 35%
where the time goes in v9:
time: 628 us; the launch traced here: 619 us
  Pallas kernels  245 us (39%)
  waiting for transfers between devices  151 us (24%)
  starting transfers between devices  123 us (20%)
  local copies, waits for them, and re-layouts  74 us (12%)
  other arithmetic  16.8 us (3%)
    pallas_call x6, Pallas kernels, even_product(): pl.pallas_call(functools.partial(even_kernel, sides, group, groups, slab,...  111 us
    ppermute x22, starting transfers between devices, on_device(): move = lambda value, perm: lax.ppermute(value, 'horiz', perm)  80.3 us
    ppermute x22, waiting for transfers between devices, on_device(): move = lambda value, perm: lax.ppermute(value, 'horiz', perm)  58.5 us
    pallas_call x5, Pallas kernels, odd_product(): pl.pallas_call(functools.partial(odd_kernel, sides, group, groups, slab,...  42.1 us
    ppermute x9, waiting for transfers between devices, exchange(): piece = lax.ppermute(piece, 'role', [(j, j ^ s) for j in range(roles)])  37.5 us
    pallas_call x6, Pallas kernels, pack(): pl.pallas_call(functools.partial(pack_kernel, group, len(pieces), given),...  27 us
    reshape x2, local copies, waits for them, and re-layouts, lower(): return low.reshape(depth, slab, downs * full)  21.2 us
    unnamed x93, local copies, waits for them, and re-layouts  18.7 us
  transfers between devices with their start and end apart: 62, of which 22 were waited for; matrix products, arithmetic and copies ran while one was open for 12% of the time, Pallas kernels for 35%

profile of v9, /device:TPU:0, one launch (start us, length us, event | category | flops | bytes accessed | tf_op | source)
XLA Modules:
  0.0 618.6 jit_solution(15809905386302506765)
XLA Ops:
  21.7 9.8 %collective-permute-done.2.refs_3_ = bf16[1,3,40,16,80]{4,3,2,1,0:T(8,128)(2,1)S(1)} collective-permute-done((bf16[1,3,40,16,80]{4,3,2,1,0:T(8,128)(2,1)S(1)}, bf16[1,3,40,16,80]{4,3,2,1,0:T(8,128)(2,1)S(1)}, u32[]{:S(2)}, u32[]{:S(2)}) %collective-permute-start.2) | collective-permute-done | bytes 307232 | tf_op jit(solution)/shard_map/ppermute | solution.py:643
  46.8 13.5 %constant_dynamic-slice_fusion.16 = (bf16[1,40,80,2,320]{4,3,2,1,0:T(2,128)(2,1)}, bf16[1,40,80,2,320]{4,3,2,1,0:T(2,128)(2,1)}, bf16[1,40,80,2,320]{4,3,2,1,0:T(2,128)(2,1)}) fusion(bf16[3,160,80,2,320]{4,3,2,1,0:T(2,128)(2,1)} %param.5, s32[]{:T(128)S(6)} %select_n.87), kind=kLoop, calls=%fused_computation.54 | loop fusion | flops 2048000 | bytes 24576004 | tf_op jit(solution)/shard_map/dynamic_slice | solution.py:649
  60.4 10.5 %mul.81.low_ref.refs_0_ = bf16[40,80,640]{2,1,0:T(8,128)(2,1)} reshape(bf16[1,40,80,2,320]{4,3,2,1,0:T(2,128)(2,1)} %get-tuple-element.102) | data formatting | bytes 8192000 | tf_op jit(solution)/shard_map/mul | solution.py:758
  106.0 10.5 %reshape.75.refs_0_ = bf16[40,80,640]{2,1,0:T(8,128)(2,1)} reshape(bf16[1,40,80,2,320]{4,3,2,1,0:T(2,128)(2,1)} %get-tuple-element.103) | data formatting | bytes 8192000 | tf_op jit(solution)/shard_map/reshape | solution.py:652
  116.6 10.7 %reshape.76.refs_1_ = bf16[40,80,640]{2,1,0:T(8,128)(2,1)} reshape(bf16[1,40,80,2,320]{4,3,2,1,0:T(2,128)(2,1)} %get-tuple-element.101) | data formatting | bytes 8192000 | tf_op jit(solution)/shard_map/reshape | solution.py:652
  139.4 22.9 %collective-permute-done.13.refs_3_.refs_10_.refs_14_.refs_18_ = bf16[3,3,40,16,80]{4,3,2,1,0:T(8,128)(2,1)} collective-permute-done((bf16[3,3,40,16,80]{4,3,2,1,0:T(8,128)(2,1)}, bf16[3,3,40,16,80]{4,3,2,1,0:T(8,128)(2,1)}, u32[]{:S(2)}, u32[]{:S(2)}) %collective-permute-start.13) | collective-permute-done | bytes 921632 | tf_op jit(solution)/shard_map/ppermute | solution.py:643
  184.6 38.5 %collective-permute-done.16.refs_9_.refs_4_.refs_7_.refs_2_ = bf16[4,50,16,128]{3,2,1,0:T(8,128)(2,1)S(1)} collective-permute-done((bf16[4,50,16,128]{3,2,1,0:T(8,128)(2,1)}, bf16[4,50,16,128]{3,2,1,0:T(8,128)(2,1)S(1)}, u32[]{:S(2)}, u32[]{:S(2)}) %collective-permute-start.16) | collective-permute-done | bytes 819232 | tf_op jit(solution)/shard_map/ppermute | solution.py:657
  252.4 21.1 %even_product.7.refs_0_.refs_7_.refs_5_.refs_4_ = f32[2,512,640]{2,1,0:T(8,128)} custom-call(s32[3]{0:T(128)} %pad_add_fusion.spot_ref, bf16[6,50,16,128]{3,2,1,0:T(8,128)(2,1)} %get-tuple-element.57.refs_0_.refs_4_, bf16[14,50,16,128]{3,2,1,0:T(8,128)(2,1)} %collective-permute-done.10.refs_6_.refs_0_.refs_1_.refs_5_, ...), custom_call_target="tpu_custom_call" | custom-call | flops 11072962560 | bytes 20971520 | tf_op jit(solution)/shard_map/even_product/pallas_call | solution.py:508
  278.0 13.3 %collective-permute-done.19.refs_6_.refs_3_.refs_0_.refs_1_.refs_5_ = bf16[12,50,16,128]{3,2,1,0:T(8,128)(2,1)S(1)} collective-permute-done((bf16[12,50,16,128]{3,2,1,0:T(8,128)(2,1)}, bf16[12,50,16,128]{3,2,1,0:T(8,128)(2,1)S(1)}, u32[]{:S(2)}, u32[]{:S(2)}) %collective-permute-start.19) | collective-permute-done | bytes 2457632 | tf_op jit(solution)/shard_map/ppermute | solution.py:657
  305.7 8.4 %odd_product.5 = (bf16[8,64,320]{2,1,0:T(8,128)(2,1)}, bf16[8,64,320]{2,1,0:T(8,128)(2,1)}, bf16[8,64,320]{2,1,0:T(8,128)(2,1)}, bf16[8,64,320]{2,1,0:T(8,128)(2,1)}) custom-call(s32[3]{0:T(128)} %pad_add_fusion.spot_ref, bf16[6,50,16,128]{3,2,1,0:T(8,128)(2,1)} %get-tuple-element.53.refs_0_.refs_4_, bf16[6,50,16,128]{3,2,1,0:T(8,128)(2,1)} %copy-done.8, ...), custom_call_target="tpu_custom_call" | custom-call | flops 8724152320 | bytes 20971520 | tf_op jit(solution)/shard_map/odd_product/pallas_call | solution.py:593
  320.0 21.1 %even_product.8.refs_3_.refs_5_.refs_4_ = f32[2,512,640]{2,1,0:T(8,128)} custom-call(s32[3]{0:T(128)} %pad_add_fusion.spot_ref, bf16[6,50,16,128]{3,2,1,0:T(8,128)(2,1)} %get-tuple-element.61.refs_0_.refs_4_, bf16[8,50,16,128]{3,2,1,0:T(8,128)(2,1)} %copy-done.3, bf16[6,50,16,128]{3,2,1,0:T(8,128)(2,1)} %collective-permute-done.18.refs_4_.refs_2_, ...), custom_call_target="tpu_custom_call" | custom-call | flops 11072962560 | bytes 20971520 | tf_op jit(solution)/shard_map/even_product/pallas_call | solution.py:508
  342.2 16.7 %collective-permute-start.30 = (bf16[4,50,16,128]{3,2,1,0:T(8,128)(2,1)}, bf16[4,50,16,128]{3,2,1,0:T(8,128)(2,1)}, u32[]{:S(2)}, u32[]{:S(2)}) collective-permute-start(bf16[4,50,16,128]{3,2,1,0:T(8,128)(2,1)} %get-tuple-element.77), channel_id=1, source_target_pairs={{0,1},{1,0},{2,3},{3,2},{4,5},{5,4},{6,7},{7,6},{8,9},{9,8},{10,11... | collective-permute-start | bytes 2457608 | tf_op jit(solution)/shard_map/ppermute | solution.py:657
  360.5 8.4 %odd_product.6 = (bf16[8,64,320]{2,1,0:T(8,128)(2,1)}, bf16[8,64,320]{2,1,0:T(8,128)(2,1)}, bf16[8,64,320]{2,1,0:T(8,128)(2,1)}, bf16[8,64,320]{2,1,0:T(8,128)(2,1)}) custom-call(s32[3]{0:T(128)} %pad_add_fusion.spot_ref, bf16[6,50,16,128]{3,2,1,0:T(8,128)(2,1)} %get-tuple-element.57.refs_0_.refs_4_, ...), custom_call_target="tpu_custom_call" | custom-call | flops 8724152320 | bytes 20971520 | tf_op jit(solution)/shard_map/odd_product/pallas_call | solution.py:593
  368.9 14.9 %collective-permute-start.37 = (bf16[4,50,16,128]{3,2,1,0:T(8,128)(2,1)}, bf16[4,50,16,128]{3,2,1,0:T(8,128)(2,1)S(1)}, u32[]{:S(2)}, u32[]{:S(2)}) collective-permute-start(bf16[4,50,16,128]{3,2,1,0:T(8,128)(2,1)} %get-tuple-element.73.refs_10_), channel_id=1, source_target_pairs={{0,1},{1,0},{2,3},{3,2},{4,5},{5,4},{6,7},{7,6},{8,9},{9,8},{10,11... | collective-permute-start | bytes 2457608 | tf_op jit(solution)/shard_map/ppermute | solution.py:657
  395.6 21.1 %even_product.9.refs_0_.refs_5_.refs_10_.refs_4_ = f32[2,512,640]{2,1,0:T(8,128)} custom-call(s32[3]{0:T(128)} %pad_add_fusion.spot_ref, bf16[6,50,16,128]{3,2,1,0:T(8,128)(2,1)} %get-tuple-element.64.refs_0_.refs_4_, bf16[12,50,16,128]{3,2,1,0:T(8,128)(2,1)} %copy-done.2, bf16[6,50,16,128]{3,2,1,0:T(8,128)(2,1)} %collective-permute-done.20.refs_4_.refs_2_, ...), custom_call_target="tpu_custom_call" | custom-call | flops 11072962560 | bytes 20971520 | tf_op jit(solution)/shard_map/even_product/pallas_call | solution.py:508
  420.0 8.4 %odd_product.7 = (bf16[8,64,320]{2,1,0:T(8,128)(2,1)}, bf16[8,64,320]{2,1,0:T(8,128)(2,1)}, bf16[8,64,320]{2,1,0:T(8,128)(2,1)}, bf16[8,64,320]{2,1,0:T(8,128)(2,1)}) custom-call(s32[3]{0:T(128)} %pad_add_fusion.spot_ref, bf16[6,50,16,128]{3,2,1,0:T(8,128)(2,1)} %get-tuple-element.61.refs_0_.refs_4_, bf16[8,50,16,128]{3,2,1,0:T(8,128)(2,1)} %copy-done.3, ...), custom_call_target="tpu_custom_call" | custom-call | flops 8724152320 | bytes 20971520 | tf_op jit(solution)/shard_map/odd_product/pallas_call | solution.py:593
  443.8 7.2 %collective-permute-start.42 = (bf16[4,50,16,128]{3,2,1,0:T(8,128)(2,1)}, bf16[4,50,16,128]{3,2,1,0:T(8,128)(2,1)S(1)}, u32[]{:S(2)}, u32[]{:S(2)}) collective-permute-start(bf16[4,50,16,128]{3,2,1,0:T(8,128)(2,1)} %pass_on.11.refs_10_), channel_id=1, source_target_pairs={{0,1},{1,0},{2,3},{3,2},{4,5},{5,4},{6,7},{7,6},{8,9},{9,8},{10,11... | collective-permute-start | bytes 2457608 | tf_op jit(solution)/shard_map/ppermute | solution.py:657
  451.0 21.2 %even_product.10.refs_0_.refs_5_.refs_10_.refs_4_ = f32[2,512,640]{2,1,0:T(8,128)} custom-call(s32[3]{0:T(128)} %pad_add_fusion.spot_ref, bf16[6,50,16,128]{3,2,1,0:T(8,128)(2,1)} %get-tuple-element.72.refs_0_.refs_4_, bf16[8,50,16,128]{3,2,1,0:T(8,128)(2,1)} %copy-done.5, bf16[6,50,16,128]{3,2,1,0:T(8,128)(2,1)} %copy-done.15, ...), custom_call_target="tpu_custom_call" | custom-call | flops 11072962560 | bytes 20971520 | tf_op jit(solution)/shard_map/even_product/pallas_call | solution.py:508
  474.1 8.4 %odd_product.8 = (bf16[8,64,320]{2,1,0:T(8,128)(2,1)}, bf16[8,64,320]{2,1,0:T(8,128)(2,1)}, bf16[8,64,320]{2,1,0:T(8,128)(2,1)}, bf16[8,64,320]{2,1,0:T(8,128)(2,1)}) custom-call(s32[3]{0:T(128)} %pad_add_fusion.spot_ref, bf16[6,50,16,128]{3,2,1,0:T(8,128)(2,1)} %get-tuple-element.64.refs_0_.refs_4_, bf16[12,50,16,128]{3,2,1,0:T(8,128)(2,1)} %copy-done.2, ...), custom_call_target="tpu_custom_call" | custom-call | flops 8724152320 | bytes 20971520 | tf_op jit(solution)/shard_map/odd_product/pallas_call | solution.py:593
  488.5 21.3 %even_product.11.refs_0_.refs_5_.refs_10_ = f32[2,512,640]{2,1,0:T(8,128)} custom-call(s32[3]{0:T(128)} %pad_add_fusion.spot_ref, bf16[6,50,16,128]{3,2,1,0:T(8,128)(2,1)} %get-tuple-element.72.refs_0_.refs_4_, bf16[8,50,16,128]{3,2,1,0:T(8,128)(2,1)} %copy-done.5, bf16[4,50,16,128]{3,2,1,0:T(8,128)(2,1)} %copy-done.19, bf16[4,50,16,128]{3,2,1,0:T(8,128)(2,1)} %copy-done.36, ...), custom_call_target="tpu_custom_call" | custom-call | flops 11072962560 | bytes 20971520 | tf_op jit(solution)/shard_map/even_product/pallas_call | solution.py:508
  512.3 8.6 %odd_product.9 = (bf16[8,64,320]{2,1,0:T(8,128)(2,1)}, bf16[8,64,320]{2,1,0:T(8,128)(2,1)}, bf16[8,64,320]{2,1,0:T(8,128)(2,1)}, bf16[8,64,320]{2,1,0:T(8,128)(2,1)}) custom-call(s32[3]{0:T(128)} %pad_add_fusion.spot_ref, bf16[6,50,16,128]{3,2,1,0:T(8,128)(2,1)} %get-tuple-element.72.refs_0_.refs_4_, bf16[8,50,16,128]{3,2,1,0:T(8,128)(2,1)} %copy-done.5, ...), custom_call_target="tpu_custom_call" | custom-call | flops 8724152320 | bytes 20971520 | tf_op jit(solution)/shard_map/odd_product/pallas_call | solution.py:593
  528.2 9.5 %collective-permute-start.43 = (bf16[3,8,1,8,320]{4,3,2,1,0:T(8,128)(2,1)S(1)}, bf16[3,8,1,8,320]{4,3,2,1,0:T(8,128)(2,1)S(1)}, u32[]{:S(2)}, u32[]{:S(2)}) collective-permute-start(bf16[3,8,1,8,320]{4,3,2,1,0:T(8,128)(2,1)S(1)} %get-tuple-element.116), channel_id=1, source_target_pairs={{0,1},{1,0},{2,3},{3,2},{4,5},{5,4},{6,7},{7,6},{8,9},{9,8},{10,11... | collective-permute-start | bytes 368648 | tf_op jit(solution)/shard_map/ppermute | solution.py:719
  555.8 7.4 %collective-permute-done.48.refs_3_ = bf16[8,64,320]{2,1,0:T(8,128)(2,1)S(1)} collective-permute-done((bf16[8,64,320]{2,1,0:T(8,128)(2,1)S(1)}, bf16[8,64,320]{2,1,0:T(8,128)(2,1)S(1)}, u32[]{:S(2)}, u32[]{:S(2)}) %collective-permute-start.48) | collective-permute-done | bytes 327712 | tf_op jit(solution)/shard_map/ppermute | solution.py:689
  563.2 8.9 %collective-permute-done.51.refs_5_ = bf16[8,64,320]{2,1,0:T(8,128)(2,1)S(1)} collective-permute-done((bf16[8,64,320]{2,1,0:T(8,128)(2,1)S(1)}, bf16[8,64,320]{2,1,0:T(8,128)(2,1)S(1)}, u32[]{:S(2)}, u32[]{:S(2)}) %collective-permute-start.51) | collective-permute-done | bytes 327712 | tf_op jit(solution)/shard_map/ppermute | solution.py:825
  (264 shorter events, 272.3 us)
Async XLA Ops:
  82.5 79.8 %collective-permute-start.10 = (bf16[14,50,16,128]{3,2,1,0:T(8,128)(2,1)}, bf16[14,50,16,128]{3,2,1,0:T(8,128)(2,1)}, u32[]{:S(2)}, u32[]{:S(2)}) collective-permute-start(bf16[14,50,16,128]{3,2,1,0:T(8,128)(2,1)} %get-tuple-element.56.refs_3_), channel_id=1, source_target_pairs={{0,1},{1,0},{2,3},{3,2},{4,5},{5,4},{6,7},{7,6},{8,9},{9,8},{10,11... | collective-permute-start | bytes 8601608 | tf_op jit(solution)/shard_map/ppermute | solution.py:657
  93.0 69.4 %collective-permute-start.14 = (bf16[6,50,16,128]{3,2,1,0:T(8,128)(2,1)}, bf16[6,50,16,128]{3,2,1,0:T(8,128)(2,1)}, u32[]{:S(2)}, u32[]{:S(2)}) collective-permute-start(bf16[6,50,16,128]{3,2,1,0:T(8,128)(2,1)} %get-tuple-element.57.refs_0_.refs_4_), channel_id=1, source_target_pairs={{1,2},{2,1},{5,6},{6,5},{9,10},{10,9},{13,14},{14,13},{17,18},{18,... | collective-permute-start | bytes 3686408 | tf_op jit(solution)/shard_map/ppermute | solution.py:657
  96.1 43.3 %collective-permute-start.12 = (bf16[3,3,40,16,80]{4,3,2,1,0:T(8,128)(2,1)}, bf16[3,3,40,16,80]{4,3,2,1,0:T(8,128)(2,1)S(1)}, u32[]{:S(2)}, u32[]{:S(2)}) collective-permute-start(bf16[3,3,40,16,80]{4,3,2,1,0:T(8,128)(2,1)} %bitcast.90), channel_id=1, source_target_pairs={{0,16},{8,24},{16,0},{24,8},{1,17},{9,25},{17,1},{25,9},{2,18},{10... | collective-permute-start | bytes 2764808 | tf_op jit(solution)/shard_map/ppermute | solution.py:643
  99.0 63.3 %collective-permute-start.13 = (bf16[3,3,40,16,80]{4,3,2,1,0:T(8,128)(2,1)}, bf16[3,3,40,16,80]{4,3,2,1,0:T(8,128)(2,1)}, u32[]{:S(2)}, u32[]{:S(2)}) collective-permute-start(bf16[3,3,40,16,80]{4,3,2,1,0:T(8,128)(2,1)} %bitcast.89), channel_id=1, source_target_pairs={{0,24},{8,16},{16,8},{24,0},{1,25},{9,17},{17,9},{25,1},{2,26},{10... | collective-permute-start | bytes 2764808 | tf_op jit(solution)/shard_map/ppermute | solution.py:643
  102.5 65.3 %collective-permute-start.9 = (bf16[6,50,16,128]{3,2,1,0:T(8,128)(2,1)}, bf16[6,50,16,128]{3,2,1,0:T(8,128)(2,1)}, u32[]{:S(2)}, u32[]{:S(2)}) collective-permute-start(bf16[6,50,16,128]{3,2,1,0:T(8,128)(2,1)} %pass_on.6.refs_0_), channel_id=1, source_target_pairs={{1,2},{2,1},{5,6},{6,5},{9,10},{10,9},{13,14},{14,13},{17,18},{18,... | collective-permute-start | bytes 3686408 | tf_op jit(solution)/shard_map/ppermute | solution.py:657
  167.3 55.8 %collective-permute-start.17 = (bf16[8,50,16,128]{3,2,1,0:T(8,128)(2,1)}, bf16[8,50,16,128]{3,2,1,0:T(8,128)(2,1)S(1)}, u32[]{:S(2)}, u32[]{:S(2)}) collective-permute-start(bf16[8,50,16,128]{3,2,1,0:T(8,128)(2,1)} %get-tuple-element.58.refs_3_), channel_id=1, source_target_pairs={{0,1},{1,0},{2,3},{3,2},{4,5},{5,4},{6,7},{7,6},{8,9},{9,8},{10,11... | collective-permute-start | bytes 4915208 | tf_op jit(solution)/shard_map/ppermute | solution.py:657
  171.3 51.8 %collective-permute-start.15 = (bf16[6,50,16,128]{3,2,1,0:T(8,128)(2,1)}, bf16[6,50,16,128]{3,2,1,0:T(8,128)(2,1)S(1)}, u32[]{:S(2)}, u32[]{:S(2)}) collective-permute-start(bf16[6,50,16,128]{3,2,1,0:T(8,128)(2,1)} %get-tuple-element.59.refs_10_), channel_id=1, source_target_pairs={{1,2},{2,1},{5,6},{6,5},{9,10},{10,9},{13,14},{14,13},{17,18},{18,... | collective-permute-start | bytes 3686408 | tf_op jit(solution)/shard_map/ppermute | solution.py:657
  172.0 51.0 %collective-permute-start.18 = (bf16[6,50,16,128]{3,2,1,0:T(8,128)(2,1)}, bf16[6,50,16,128]{3,2,1,0:T(8,128)(2,1)}, u32[]{:S(2)}, u32[]{:S(2)}) collective-permute-start(bf16[6,50,16,128]{3,2,1,0:T(8,128)(2,1)} %get-tuple-element.61.refs_0_.refs_4_), channel_id=1, source_target_pairs={{1,2},{2,1},{5,6},{6,5},{9,10},{10,9},{13,14},{14,13},{17,18},{18,... | collective-permute-start | bytes 3686408 | tf_op jit(solution)/shard_map/ppermute | solution.py:657
  174.0 49.1 %collective-permute-start.16 = (bf16[4,50,16,128]{3,2,1,0:T(8,128)(2,1)}, bf16[4,50,16,128]{3,2,1,0:T(8,128)(2,1)S(1)}, u32[]{:S(2)}, u32[]{:S(2)}) collective-permute-start(bf16[4,50,16,128]{3,2,1,0:T(8,128)(2,1)} %get-tuple-element.60), channel_id=1, source_target_pairs={{0,1},{1,0},{2,3},{3,2},{4,5},{5,4},{6,7},{7,6},{8,9},{9,8},{10,11... | collective-permute-start | bytes 2457608 | tf_op jit(solution)/shard_map/ppermute | solution.py:657
  230.8 60.5 %collective-permute-start.19 = (bf16[12,50,16,128]{3,2,1,0:T(8,128)(2,1)}, bf16[12,50,16,128]{3,2,1,0:T(8,128)(2,1)S(1)}, u32[]{:S(2)}, u32[]{:S(2)}) collective-permute-start(bf16[12,50,16,128]{3,2,1,0:T(8,128)(2,1)} %get-tuple-element.62.refs_3_), channel_id=1, source_target_pairs={{0,1},{1,0},{2,3},{3,2},{4,5},{5,4},{6,7},{7,6},{8,9},{9,8},{10,11... | collective-permute-start | bytes 7372808 | tf_op jit(solution)/shard_map/ppermute | solution.py:657
  247.4 68.3 %collective-permute-start.24 = (bf16[6,50,16,128]{3,2,1,0:T(8,128)(2,1)}, bf16[6,50,16,128]{3,2,1,0:T(8,128)(2,1)}, u32[]{:S(2)}, u32[]{:S(2)}) collective-permute-start(bf16[6,50,16,128]{3,2,1,0:T(8,128)(2,1)} %get-tuple-element.63.refs_10_), channel_id=1, source_target_pairs={{1,2},{2,1},{5,6},{6,5},{9,10},{10,9},{13,14},{14,13},{17,18},{18,... | collective-permute-start | bytes 3686408 | tf_op jit(solution)/shard_map/ppermute | solution.py:657
  249.5 64.6 %collective-permute-start.25 = (bf16[4,50,16,128]{3,2,1,0:T(8,128)(2,1)}, bf16[4,50,16,128]{3,2,1,0:T(8,128)(2,1)S(1)}, u32[]{:S(2)}, u32[]{:S(2)}) collective-permute-start(bf16[4,50,16,128]{3,2,1,0:T(8,128)(2,1)} %get-tuple-element.70), channel_id=1, source_target_pairs={{0,1},{1,0},{2,3},{3,2},{4,5},{5,4},{6,7},{7,6},{8,9},{9,8},{10,11... | collective-permute-start | bytes 2457608 | tf_op jit(solution)/shard_map/ppermute | solution.py:657
  297.8 44.4 %collective-permute-start.27 = (bf16[8,50,16,128]{3,2,1,0:T(8,128)(2,1)}, bf16[8,50,16,128]{3,2,1,0:T(8,128)(2,1)S(1)}, u32[]{:S(2)}, u32[]{:S(2)}) collective-permute-start(bf16[8,50,16,128]{3,2,1,0:T(8,128)(2,1)} %get-tuple-element.65.refs_4_.refs_10_), channel_id=1, source_target_pairs={{0,1},{1,0},{2,3},{3,2},{4,5},{5,4},{6,7},{7,6},{8,9},{9,8},{10,11... | collective-permute-start | bytes 4915208 | tf_op jit(solution)/shard_map/ppermute | solution.py:657
  314.1 54.8 %collective-permute-start.21 = (bf16[8,64,320]{2,1,0:T(8,128)(2,1)}, bf16[8,64,320]{2,1,0:T(8,128)(2,1)}, u32[]{:S(2)}, u32[]{:S(2)}) collective-permute-start(bf16[8,64,320]{2,1,0:T(8,128)(2,1)} %get-tuple-element.67), channel_id=1, source_target_pairs={{0,8},{8,0},{16,24},{24,16},{1,9},{9,1},{17,25},{25,17},{2,10},{10... | collective-permute-start | bytes 983048 | tf_op jit(solution)/shard_map/ppermute | solution.py:689
  314.2 69.6 %collective-permute-start.22 = (bf16[8,64,320]{2,1,0:T(8,128)(2,1)}, bf16[8,64,320]{2,1,0:T(8,128)(2,1)}, u32[]{:S(2)}, u32[]{:S(2)}) collective-permute-start(bf16[8,64,320]{2,1,0:T(8,128)(2,1)} %get-tuple-element.68), channel_id=1, source_target_pairs={{0,16},{8,24},{16,0},{24,8},{1,17},{9,25},{17,1},{25,9},{2,18},{10... | collective-permute-start | bytes 983048 | tf_op jit(solution)/shard_map/ppermute | solution.py:689
  319.1 68.8 %collective-permute-start.29 = (bf16[6,50,16,128]{3,2,1,0:T(8,128)(2,1)}, bf16[6,50,16,128]{3,2,1,0:T(8,128)(2,1)S(1)}, u32[]{:S(2)}, u32[]{:S(2)}) collective-permute-start(bf16[6,50,16,128]{3,2,1,0:T(8,128)(2,1)} %get-tuple-element.71.refs_10_), channel_id=1, source_target_pairs={{1,2},{2,1},{5,6},{6,5},{9,10},{10,9},{13,14},{14,13},{17,18},{18,... | collective-permute-start | bytes 3686408 | tf_op jit(solution)/shard_map/ppermute | solution.py:657
  342.2 45.6 %collective-permute-start.30 = (bf16[4,50,16,128]{3,2,1,0:T(8,128)(2,1)}, bf16[4,50,16,128]{3,2,1,0:T(8,128)(2,1)}, u32[]{:S(2)}, u32[]{:S(2)}) collective-permute-start(bf16[4,50,16,128]{3,2,1,0:T(8,128)(2,1)} %get-tuple-element.77), channel_id=1, source_target_pairs={{0,1},{1,0},{2,3},{3,2},{4,5},{5,4},{6,7},{7,6},{8,9},{9,8},{10,11... | collective-permute-start | bytes 2457608 | tf_op jit(solution)/shard_map/ppermute | solution.py:657
  368.9 71.8 %collective-permute-start.37 = (bf16[4,50,16,128]{3,2,1,0:T(8,128)(2,1)}, bf16[4,50,16,128]{3,2,1,0:T(8,128)(2,1)S(1)}, u32[]{:S(2)}, u32[]{:S(2)}) collective-permute-start(bf16[4,50,16,128]{3,2,1,0:T(8,128)(2,1)} %get-tuple-element.73.refs_10_), channel_id=1, source_target_pairs={{0,1},{1,0},{2,3},{3,2},{4,5},{5,4},{6,7},{7,6},{8,9},{9,8},{10,11... | collective-permute-start | bytes 2457608 | tf_op jit(solution)/shard_map/ppermute | solution.py:657
  392.2 49.0 %collective-permute-start.35 = (bf16[6,50,16,128]{3,2,1,0:T(8,128)(2,1)}, bf16[6,50,16,128]{3,2,1,0:T(8,128)(2,1)S(1)}, u32[]{:S(2)}, u32[]{:S(2)}) collective-permute-start(bf16[6,50,16,128]{3,2,1,0:T(8,128)(2,1)} %get-tuple-element.78.refs_10_), channel_id=1, source_target_pairs={{1,2},{2,1},{5,6},{6,5},{9,10},{10,9},{13,14},{14,13},{17,18},{18,... | collective-permute-start | bytes 3686408 | tf_op jit(solution)/shard_map/ppermute | solution.py:657
  393.3 45.8 %collective-permute-start.36 = (bf16[4,50,16,128]{3,2,1,0:T(8,128)(2,1)}, bf16[4,50,16,128]{3,2,1,0:T(8,128)(2,1)S(1)}, u32[]{:S(2)}, u32[]{:S(2)}) collective-permute-start(bf16[4,50,16,128]{3,2,1,0:T(8,128)(2,1)} %get-tuple-element.85), channel_id=1, source_target_pairs={{0,1},{1,0},{2,3},{3,2},{4,5},{5,4},{6,7},{7,6},{8,9},{9,8},{10,11... | collective-permute-start | bytes 2457608 | tf_op jit(solution)/shard_map/ppermute | solution.py:657
  428.8 53.6 %collective-permute-start.38 = (bf16[8,64,320]{2,1,0:T(8,128)(2,1)}, bf16[8,64,320]{2,1,0:T(8,128)(2,1)S(1)}, u32[]{:S(2)}, u32[]{:S(2)}) collective-permute-start(bf16[8,64,320]{2,1,0:T(8,128)(2,1)} %get-tuple-element.86), channel_id=1, source_target_pairs={{0,8},{8,0},{16,24},{24,16},{1,9},{9,1},{17,25},{25,17},{2,10},{10... | collective-permute-start | bytes 983048 | tf_op jit(solution)/shard_map/ppermute | solution.py:689
  435.9 46.6 %collective-permute-start.39 = (bf16[8,64,320]{2,1,0:T(8,128)(2,1)}, bf16[8,64,320]{2,1,0:T(8,128)(2,1)S(1)}, u32[]{:S(2)}, u32[]{:S(2)}) collective-permute-start(bf16[8,64,320]{2,1,0:T(8,128)(2,1)} %get-tuple-element.87), channel_id=1, source_target_pairs={{0,16},{8,24},{16,0},{24,8},{1,17},{9,25},{17,1},{25,9},{2,18},{10... | collective-permute-start | bytes 983048 | tf_op jit(solution)/shard_map/ppermute | solution.py:689
  439.1 43.4 %collective-permute-start.40 = (bf16[8,64,320]{2,1,0:T(8,128)(2,1)}, bf16[8,64,320]{2,1,0:T(8,128)(2,1)S(1)}, u32[]{:S(2)}, u32[]{:S(2)}) collective-permute-start(bf16[8,64,320]{2,1,0:T(8,128)(2,1)} %get-tuple-element.88), channel_id=1, source_target_pairs={{0,24},{8,16},{16,8},{24,0},{1,25},{9,17},{17,9},{25,1},{2,26},{10... | collective-permute-start | bytes 983048 | tf_op jit(solution)/shard_map/ppermute | solution.py:689
  443.8 43.7 %collective-permute-start.42 = (bf16[4,50,16,128]{3,2,1,0:T(8,128)(2,1)}, bf16[4,50,16,128]{3,2,1,0:T(8,128)(2,1)S(1)}, u32[]{:S(2)}, u32[]{:S(2)}) collective-permute-start(bf16[4,50,16,128]{3,2,1,0:T(8,128)(2,1)} %pass_on.11.refs_10_), channel_id=1, source_target_pairs={{0,1},{1,0},{2,3},{3,2},{4,5},{5,4},{6,7},{7,6},{8,9},{9,8},{10,11... | collective-permute-start | bytes 2457608 | tf_op jit(solution)/shard_map/ppermute | solution.py:657
  (82 other events, 1034.9 us)

commit v10 on v8

--- a/solution.py
+++ b/solution.py
@@ -728,7 +728,7 @@
         if r <= chunks:
             fresh = r < chunks
             base = 3 * groups if fresh else 0
-            most = {0: 3, 1: 2}.get(r, 1) * groups if fresh else 0
+            most = {0: 1, 1: 3}.get(r, 1) * groups if fresh else 0
             at, size = take(most)
             length = max(base + size, 4 * groups) if fresh else 2 * groups
             given = dict(
@@ -754,7 +754,6 @@
             if r == 0:
                 late = mark[1]
                 outer = [lower(0, late), lower(2, late)]
-                extra = list(outer)
         t = r - 4
         if 0 <= t < chunks:
             if near_low is None:
@@ -808,7 +807,7 @@
             if r == 3:
                 near_table = make_table(flat_left(near_left), [done], windows, slab)
                 extra.append(near_table)
-            if (r - 5,) in halves:
+            if (r - 5,) in halves and r < chunks + 2:
                 extra.append(add_contr((r - 5,), [done]))
     t = chunks - 1
     blocks = [(own[t], 2 * groups), (sent[t], 2 * groups), (straight[t], 2 * groups), (turned[t + 1], 2 * groups)]
@@ -817,8 +816,11 @@
         (middle_low, near_low), sides, group, groups, slab, roles,
     )
     send_roles(t)
-    late = tuple(t for t in range(chunks) if (t,) not in halves)
-    done = [(t,) for t in range(chunks) if (t,) in halves]
+    late = tuple(c for c in range(chunks) if (c,) not in halves)
+    done = [(c,) for c in range(chunks) if (c,) in halves]
+    for ts in done:
+        if ts not in reduced:
+            add_contr(ts, [shares[t][0]])
     projected = project(done) if done else 0.0
     add_roles(late, [])
     add_contr(late, [])

time: 588 us -> 596 us (1.014)
  waiting for transfers between devices: 103 us -> 110 us
    ppermute x22, waiting for transfers between devices: 45.9 us -> 19.3 us  [on_device(): move = lambda value, perm: lax.ppermute(value, 'horiz', perm)]
    ppermute x12, waiting for transfers between devices: 9.91 us -> 33.9 us  [exchange(): piece = lax.ppermute(piece, 'role', [(j, j ^ s) for j in range(roles)])]
    ppermute x6, waiting for transfers between devices: 6.37 us -> 17.1 us  [project(): got = lax.ppermute(give, 'horiz', [(z, z ^ s) for z in range(sides)])]
    unnamed x79 -> x83, local copies, waits for them, and re-layouts: 20.9 us -> 20.5 us
  transfers between devices with their start and end apart: 65 -> 65, of which waited for: 20 -> 23; matrix products, arithmetic and copies ran while one was open for 14% -> 14% of each run, Pallas kernels for 40% -> 39%
where the time goes in v10:
time: 596 us; the launch traced here: 585 us
  Pallas kernels  246 us (41%)
  starting transfers between devices  121 us (20%)
  waiting for transfers between devices  110 us (18%)
  local copies, waits for them, and re-layouts  86.3 us (14%)
  other arithmetic  11.8 us (2%)
    pallas_call x6, Pallas kernels, even_product(): pl.pallas_call(functools.partial(even_kernel, sides, group, groups, slab,...  112 us
    ppermute x22, starting transfers between devices, on_device(): move = lambda value, perm: lax.ppermute(value, 'horiz', perm)  78 us
    pallas_call x5, Pallas kernels, odd_product(): pl.pallas_call(functools.partial(odd_kernel, sides, group, groups, slab,...  42.2 us
    ppermute x12, waiting for transfers between devices, exchange(): piece = lax.ppermute(piece, 'role', [(j, j ^ s) for j in range(roles)])  33.9 us
    pallas_call x6, Pallas kernels, pack(): pl.pallas_call(functools.partial(pack_kernel, group, len(pieces), given),...  26.8 us
    ppermute x15, waiting for transfers between devices, send_roles(): lax.ppermute(shares[t][s], 'role', [(j, j ^ s) for j in range(roles)])  22 us
    reshape x2, local copies, waits for them, and re-layouts, lower(): return low.reshape(depth, slab, downs * full)  21.1 us
    unnamed x83, local copies, waits for them, and re-layouts  20.5 us
  transfers between devices with their start and end apart: 65, of which 23 were waited for; matrix products, arithmetic and copies ran while one was open for 14% of the time, Pallas kernels for 39%

profile of v10, /device:TPU:0, one launch (start us, length us, event | category | flops | bytes accessed | tf_op | source)
XLA Modules:
  0.0 585.3 jit_solution(13772836517178841809)
XLA Ops:
  9.8 8.6 %dynamic-slice_multiply_fusion = bf16[1,40,80,2,320]{4,3,2,1,0:T(2,128)(2,1)} fusion(bf16[3,160,80,2,320]{4,3,2,1,0:T(2,128)(2,1)} %param.5, s32[]{:T(128)S(6)} %select_n.95), kind=kLoop, calls=%fused_computation | loop fusion | flops 2048000 | bytes 8192004 | tf_op jit(solution)/shard_map/mul | solution.py:668
  18.4 10.5 %mul.103.low_ref.refs_0_ = bf16[40,80,640]{2,1,0:T(8,128)(2,1)} reshape(bf16[1,40,80,2,320]{4,3,2,1,0:T(2,128)(2,1)} %dynamic-slice_multiply_fusion) | data formatting | bytes 8192000 | tf_op jit(solution)/shard_map/mul | solution.py:668
  51.1 12.2 %collective-permute-done.7.refs_2_ = bf16[1,3,40,16,80]{4,3,2,1,0:T(8,128)(2,1)S(1)} collective-permute-done((bf16[1,3,40,16,80]{4,3,2,1,0:T(8,128)(2,1)S(1)}, bf16[1,3,40,16,80]{4,3,2,1,0:T(8,128)(2,1)S(1)}, u32[]{:S(2)}, u32[]{:S(2)}) %collective-permute-start.7) | collective-permute-done | bytes 307232 | tf_op jit(solution)/shard_map/ppermute | solution.py:641
  63.3 9.8 %collective-permute-done.8.refs_3_ = bf16[1,3,40,16,80]{4,3,2,1,0:T(8,128)(2,1)S(1)} collective-permute-done((bf16[1,3,40,16,80]{4,3,2,1,0:T(8,128)(2,1)S(1)}, bf16[1,3,40,16,80]{4,3,2,1,0:T(8,128)(2,1)S(1)}, u32[]{:S(2)}, u32[]{:S(2)}) %collective-permute-start.8) | collective-permute-done | bytes 307232 | tf_op jit(solution)/shard_map/ppermute | solution.py:641
  95.6 9.6 %constant_dynamic-slice_fusion.16 = (bf16[1,40,80,2,320]{4,3,2,1,0:T(2,128)(2,1)}, bf16[1,40,80,2,320]{4,3,2,1,0:T(2,128)(2,1)}) fusion(bf16[3,160,80,2,320]{4,3,2,1,0:T(2,128)(2,1)} %param.5, s32[]{:T(128)S(6)} %select_n.99), kind=kLoop, calls=%fused_computation.56 | loop fusion | bytes 16384004 | tf_op jit(solution)/shard_map/dynamic_slice | solution.py:647
  105.3 10.5 %reshape.89.refs_0_ = bf16[40,80,640]{2,1,0:T(8,128)(2,1)} reshape(bf16[1,40,80,2,320]{4,3,2,1,0:T(2,128)(2,1)} %get-tuple-element.104) | data formatting | bytes 8192000 | tf_op jit(solution)/shard_map/reshape | solution.py:650
  115.8 10.5 %reshape.90.refs_1_ = bf16[40,80,640]{2,1,0:T(8,128)(2,1)} reshape(bf16[1,40,80,2,320]{4,3,2,1,0:T(2,128)(2,1)} %get-tuple-element.103) | data formatting | bytes 8192000 | tf_op jit(solution)/shard_map/reshape | solution.py:650
  181.5 10.1 %collective-permute-done.20.refs_3_ = bf16[2,3,40,16,80]{4,3,2,1,0:T(8,128)(2,1)S(1)} collective-permute-done((bf16[2,3,40,16,80]{4,3,2,1,0:T(8,128)(2,1)}, bf16[2,3,40,16,80]{4,3,2,1,0:T(8,128)(2,1)S(1)}, u32[]{:S(2)}, u32[]{:S(2)}) %collective-permute-start.20) | collective-permute-done | bytes 614432 | tf_op jit(solution)/shard_map/ppermute | solution.py:641
  222.9 21.2 %even_product.7.refs_0_.refs_7_.refs_5_.refs_4_ = f32[2,512,640]{2,1,0:T(8,128)} custom-call(s32[3]{0:T(128)} %pad_add_fusion.spot_ref, bf16[6,50,16,128]{3,2,1,0:T(8,128)(2,1)} %get-tuple-element.58.refs_0_.refs_4_, bf16[12,50,16,128]{3,2,1,0:T(8,128)(2,1)} %copy-done, bf16[6,50,16,128]{3,2,1,0:T(8,128)(2,1)} %collective-permute-done.14.refs_4_.refs_2_, ...), custom_call_target="tpu_custom_call" | custom-call | flops 11072962560 | bytes 20971520 | tf_op jit(solution)/shard_map/even_product/pallas_call | solution.py:506
  271.7 8.4 %odd_product.5 = (bf16[8,64,320]{2,1,0:T(8,128)(2,1)}, bf16[8,64,320]{2,1,0:T(8,128)(2,1)}, bf16[8,64,320]{2,1,0:T(8,128)(2,1)}, bf16[8,64,320]{2,1,0:T(8,128)(2,1)}) custom-call(s32[3]{0:T(128)} %pad_add_fusion.spot_ref, bf16[6,50,16,128]{3,2,1,0:T(8,128)(2,1)} %get-tuple-element.54.refs_0_.refs_4_, bf16[8,50,16,128]{3,2,1,0:T(8,128)(2,1)} %copy-done.1, ...), custom_call_target="tpu_custom_call" | custom-call | flops 8724152320 | bytes 20971520 | tf_op jit(solution)/shard_map/odd_product/pallas_call | solution.py:591
  285.2 21.1 %even_product.8.refs_3_.refs_5_.refs_4_ = f32[2,512,640]{2,1,0:T(8,128)} custom-call(s32[3]{0:T(128)} %pad_add_fusion.spot_ref, bf16[6,50,16,128]{3,2,1,0:T(8,128)(2,1)} %get-tuple-element.63.refs_0_.refs_4_, bf16[8,50,16,128]{3,2,1,0:T(8,128)(2,1)} %copy-done.2, bf16[6,50,16,128]{3,2,1,0:T(8,128)(2,1)} %collective-permute-done.21.refs_4_.refs_2_, ...), custom_call_target="tpu_custom_call" | custom-call | flops 11072962560 | bytes 20971520 | tf_op jit(solution)/shard_map/even_product/pallas_call | solution.py:506
  307.7 17.2 %collective-permute-start.33 = (bf16[4,50,16,128]{3,2,1,0:T(8,128)(2,1)}, bf16[4,50,16,128]{3,2,1,0:T(8,128)(2,1)}, u32[]{:S(2)}, u32[]{:S(2)}) collective-permute-start(bf16[4,50,16,128]{3,2,1,0:T(8,128)(2,1)} %get-tuple-element.79), channel_id=1, source_target_pairs={{0,1},{1,0},{2,3},{3,2},{4,5},{5,4},{6,7},{7,6},{8,9},{9,8},{10,11... | collective-permute-start | bytes 2457608 | tf_op jit(solution)/shard_map/ppermute | solution.py:655
  326.5 8.4 %odd_product.6 = (bf16[8,64,320]{2,1,0:T(8,128)(2,1)}, bf16[8,64,320]{2,1,0:T(8,128)(2,1)}, bf16[8,64,320]{2,1,0:T(8,128)(2,1)}, bf16[8,64,320]{2,1,0:T(8,128)(2,1)}) custom-call(s32[3]{0:T(128)} %pad_add_fusion.spot_ref, bf16[6,50,16,128]{3,2,1,0:T(8,128)(2,1)} %get-tuple-element.58.refs_0_.refs_4_, bf16[12,50,16,128]{3,2,1,0:T(8,128)(2,1)} %copy-done, ...), custom_call_target="tpu_custom_call" | custom-call | flops 8724152320 | bytes 20971520 | tf_op jit(solution)/shard_map/odd_product/pallas_call | solution.py:591
  334.9 14.9 %collective-permute-start.40 = (bf16[4,50,16,128]{3,2,1,0:T(8,128)(2,1)}, bf16[4,50,16,128]{3,2,1,0:T(8,128)(2,1)S(1)}, u32[]{:S(2)}, u32[]{:S(2)}) collective-permute-start(bf16[4,50,16,128]{3,2,1,0:T(8,128)(2,1)} %get-tuple-element.75.refs_10_), channel_id=1, source_target_pairs={{0,1},{1,0},{2,3},{3,2},{4,5},{5,4},{6,7},{7,6},{8,9},{9,8},{10,11... | collective-permute-start | bytes 2457608 | tf_op jit(solution)/shard_map/ppermute | solution.py:655
  362.0 21.2 %even_product.9.refs_0_.refs_5_.refs_10_.refs_4_ = f32[2,512,640]{2,1,0:T(8,128)} custom-call(s32[3]{0:T(128)} %pad_add_fusion.spot_ref, bf16[6,50,16,128]{3,2,1,0:T(8,128)(2,1)} %get-tuple-element.67.refs_0_.refs_4_, bf16[8,50,16,128]{3,2,1,0:T(8,128)(2,1)} %copy-done.3, bf16[6,50,16,128]{3,2,1,0:T(8,128)(2,1)} %collective-permute-done.24.refs_4_.refs_2_, ...), custom_call_target="tpu_custom_call" | custom-call | flops 11072962560 | bytes 20971520 | tf_op jit(solution)/shard_map/even_product/pallas_call | solution.py:506
  386.7 8.4 %odd_product.7 = (bf16[8,64,320]{2,1,0:T(8,128)(2,1)}, bf16[8,64,320]{2,1,0:T(8,128)(2,1)}, bf16[8,64,320]{2,1,0:T(8,128)(2,1)}, bf16[8,64,320]{2,1,0:T(8,128)(2,1)}) custom-call(s32[3]{0:T(128)} %pad_add_fusion.spot_ref, bf16[6,50,16,128]{3,2,1,0:T(8,128)(2,1)} %get-tuple-element.63.refs_0_.refs_4_, bf16[8,50,16,128]{3,2,1,0:T(8,128)(2,1)} %copy-done.2, ...), custom_call_target="tpu_custom_call" | custom-call | flops 8724152320 | bytes 20971520 | tf_op jit(solution)/shard_map/odd_product/pallas_call | solution.py:591
  410.8 7.8 %collective-permute-start.45 = (bf16[4,50,16,128]{3,2,1,0:T(8,128)(2,1)}, bf16[4,50,16,128]{3,2,1,0:T(8,128)(2,1)S(1)}, u32[]{:S(2)}, u32[]{:S(2)}) collective-permute-start(bf16[4,50,16,128]{3,2,1,0:T(8,128)(2,1)} %pass_on.11.refs_10_), channel_id=1, source_target_pairs={{0,1},{1,0},{2,3},{3,2},{4,5},{5,4},{6,7},{7,6},{8,9},{9,8},{10,11... | collective-permute-start | bytes 2457608 | tf_op jit(solution)/shard_map/ppermute | solution.py:655
  418.6 21.3 %even_product.10.refs_0_.refs_5_.refs_10_.refs_4_ = f32[2,512,640]{2,1,0:T(8,128)} custom-call(s32[3]{0:T(128)} %pad_add_fusion.spot_ref, bf16[6,50,16,128]{3,2,1,0:T(8,128)(2,1)} %get-tuple-element.74.refs_0_.refs_4_, bf16[8,50,16,128]{3,2,1,0:T(8,128)(2,1)} %copy-done.4, bf16[6,50,16,128]{3,2,1,0:T(8,128)(2,1)} %collective-permute-done.29.refs_0_.refs_2_, ...), custom_call_target="tpu_custom_call" | custom-call | flops 11072962560 | bytes 20971520 | tf_op jit(solution)/shard_map/even_product/pallas_call | solution.py:506
  441.8 8.4 %odd_product.8 = (bf16[8,64,320]{2,1,0:T(8,128)(2,1)}, bf16[8,64,320]{2,1,0:T(8,128)(2,1)}, bf16[8,64,320]{2,1,0:T(8,128)(2,1)}, bf16[8,64,320]{2,1,0:T(8,128)(2,1)}) custom-call(s32[3]{0:T(128)} %pad_add_fusion.spot_ref, bf16[6,50,16,128]{3,2,1,0:T(8,128)(2,1)} %get-tuple-element.67.refs_0_.refs_4_, bf16[8,50,16,128]{3,2,1,0:T(8,128)(2,1)} %copy-done.3, ...), custom_call_target="tpu_custom_call" | custom-call | flops 8724152320 | bytes 20971520 | tf_op jit(solution)/shard_map/odd_product/pallas_call | solution.py:591
  456.4 21.7 %even_product.11.refs_5_.refs_10_ = f32[2,512,640]{2,1,0:T(8,128)} custom-call(s32[3]{0:T(128)} %pad_add_fusion.spot_ref, bf16[6,50,16,128]{3,2,1,0:T(8,128)(2,1)} %get-tuple-element.74.refs_0_.refs_4_, bf16[8,50,16,128]{3,2,1,0:T(8,128)(2,1)} %copy-done.4, bf16[4,50,16,128]{3,2,1,0:T(8,128)(2,1)} %copy-done.16, bf16[4,50,16,128]{3,2,1,0:T(8,128)(2,1)} %copy-done.36, ...), custom_call_target="tpu_custom_call" | custom-call | flops 11072962560 | bytes 20971520 | tf_op jit(solution)/shard_map/even_product/pallas_call | solution.py:506
  478.2 8.7 %odd_product.9 = (bf16[8,64,320]{2,1,0:T(8,128)(2,1)}, bf16[8,64,320]{2,1,0:T(8,128)(2,1)}, bf16[8,64,320]{2,1,0:T(8,128)(2,1)}, bf16[8,64,320]{2,1,0:T(8,128)(2,1)}) custom-call(s32[3]{0:T(128)} %pad_add_fusion.spot_ref, bf16[6,50,16,128]{3,2,1,0:T(8,128)(2,1)} %get-tuple-element.74.refs_0_.refs_4_, bf16[8,50,16,128]{3,2,1,0:T(8,128)(2,1)} %copy-done.4, ...), custom_call_target="tpu_custom_call" | custom-call | flops 8724152320 | bytes 20971520 | tf_op jit(solution)/shard_map/odd_product/pallas_call | solution.py:591
  490.5 9.6 %collective-permute-start.46 = (bf16[3,8,1,8,320]{4,3,2,1,0:T(8,128)(2,1)S(1)}, bf16[3,8,1,8,320]{4,3,2,1,0:T(8,128)(2,1)S(1)}, u32[]{:S(2)}, u32[]{:S(2)}) collective-permute-start(bf16[3,8,1,8,320]{4,3,2,1,0:T(8,128)(2,1)S(1)} %get-tuple-element.121), channel_id=1, source_target_pairs={{0,1},{1,0},{2,3},{3,2},{4,5},{5,4},{6,7},{7,6},{8,9},{9,8},{10,11... | collective-permute-start | bytes 368648 | tf_op jit(solution)/shard_map/ppermute | solution.py:719
  505.7 8.4 %collective-permute-done.47 = bf16[3,8,1,8,320]{4,3,2,1,0:T(8,128)(2,1)S(1)} collective-permute-done((bf16[3,8,1,8,320]{4,3,2,1,0:T(8,128)(2,1)S(1)}, bf16[3,8,1,8,320]{4,3,2,1,0:T(8,128)(2,1)S(1)}, u32[]{:S(2)}, u32[]{:S(2)}) %collective-permute-start.47) | collective-permute-done | bytes 122912 | tf_op jit(solution)/shard_map/ppermute | solution.py:719
  521.4 10.3 %collective-permute-done.53.refs_6_ = bf16[8,64,320]{2,1,0:T(8,128)(2,1)} collective-permute-done((bf16[8,64,320]{2,1,0:T(8,128)(2,1)}, bf16[8,64,320]{2,1,0:T(8,128)(2,1)}, u32[]{:S(2)}, u32[]{:S(2)}) %collective-permute-start.53) | collective-permute-done | bytes 327712 | tf_op jit(solution)/shard_map/ppermute | solution.py:689
  (260 shorter events, 280.7 us)
Async XLA Ops:
  85.1 63.5 %collective-permute-start.10 = (bf16[12,50,16,128]{3,2,1,0:T(8,128)(2,1)}, bf16[12,50,16,128]{3,2,1,0:T(8,128)(2,1)S(1)}, u32[]{:S(2)}, u32[]{:S(2)}) collective-permute-start(bf16[12,50,16,128]{3,2,1,0:T(8,128)(2,1)} %get-tuple-element.57.refs_3_), channel_id=1, source_target_pairs={{0,1},{1,0},{2,3},{3,2},{4,5},{5,4},{6,7},{7,6},{8,9},{9,8},{10,11... | collective-permute-start | bytes 7372808 | tf_op jit(solution)/shard_map/ppermute | solution.py:655
  85.4 63.1 %collective-permute-start.14 = (bf16[6,50,16,128]{3,2,1,0:T(8,128)(2,1)}, bf16[6,50,16,128]{3,2,1,0:T(8,128)(2,1)}, u32[]{:S(2)}, u32[]{:S(2)}) collective-permute-start(bf16[6,50,16,128]{3,2,1,0:T(8,128)(2,1)} %get-tuple-element.58.refs_0_.refs_4_), channel_id=1, source_target_pairs={{1,2},{2,1},{5,6},{6,5},{9,10},{10,9},{13,14},{14,13},{17,18},{18,... | collective-permute-start | bytes 3686408 | tf_op jit(solution)/shard_map/ppermute | solution.py:655
  89.0 57.8 %collective-permute-start.12 = (bf16[1,3,40,16,80]{4,3,2,1,0:T(8,128)(2,1)}, bf16[1,3,40,16,80]{4,3,2,1,0:T(8,128)(2,1)}, u32[]{:S(2)}, u32[]{:S(2)}) collective-permute-start(bf16[1,3,40,16,80]{4,3,2,1,0:T(8,128)(2,1)} %get-tuple-element.111), channel_id=1, source_target_pairs={{0,16},{8,24},{16,0},{24,8},{1,17},{9,25},{17,1},{25,9},{2,18},{10... | collective-permute-start | bytes 921608 | tf_op jit(solution)/shard_map/ppermute | solution.py:641
  90.5 56.6 %collective-permute-start.13 = (bf16[1,3,40,16,80]{4,3,2,1,0:T(8,128)(2,1)}, bf16[1,3,40,16,80]{4,3,2,1,0:T(8,128)(2,1)}, u32[]{:S(2)}, u32[]{:S(2)}) collective-permute-start(bf16[1,3,40,16,80]{4,3,2,1,0:T(8,128)(2,1)} %get-tuple-element.110), channel_id=1, source_target_pairs={{0,24},{8,16},{16,8},{24,0},{1,25},{9,17},{17,9},{25,1},{2,26},{10... | collective-permute-start | bytes 921608 | tf_op jit(solution)/shard_map/ppermute | solution.py:641
  93.9 70.3 %collective-permute-start.9 = (bf16[6,50,16,128]{3,2,1,0:T(8,128)(2,1)}, bf16[6,50,16,128]{3,2,1,0:T(8,128)(2,1)}, u32[]{:S(2)}, u32[]{:S(2)}) collective-permute-start(bf16[6,50,16,128]{3,2,1,0:T(8,128)(2,1)} %pass_on.6.refs_0_), channel_id=1, source_target_pairs={{1,2},{2,1},{5,6},{6,5},{9,10},{10,9},{13,14},{14,13},{17,18},{18,... | collective-permute-start | bytes 3686408 | tf_op jit(solution)/shard_map/ppermute | solution.py:655
  167.8 45.6 %collective-permute-start.15 = (bf16[6,50,16,128]{3,2,1,0:T(8,128)(2,1)}, bf16[6,50,16,128]{3,2,1,0:T(8,128)(2,1)}, u32[]{:S(2)}, u32[]{:S(2)}) collective-permute-start(bf16[6,50,16,128]{3,2,1,0:T(8,128)(2,1)} %get-tuple-element.60.refs_10_), channel_id=1, source_target_pairs={{1,2},{2,1},{5,6},{6,5},{9,10},{10,9},{13,14},{14,13},{17,18},{18,... | collective-permute-start | bytes 3686408 | tf_op jit(solution)/shard_map/ppermute | solution.py:655
  202.1 46.6 %collective-permute-start.22 = (bf16[8,50,16,128]{3,2,1,0:T(8,128)(2,1)}, bf16[8,50,16,128]{3,2,1,0:T(8,128)(2,1)S(1)}, u32[]{:S(2)}, u32[]{:S(2)}) collective-permute-start(bf16[8,50,16,128]{3,2,1,0:T(8,128)(2,1)} %get-tuple-element.64.refs_3_), channel_id=1, source_target_pairs={{0,1},{1,0},{2,3},{3,2},{4,5},{5,4},{6,7},{7,6},{8,9},{9,8},{10,11... | collective-permute-start | bytes 4915208 | tf_op jit(solution)/shard_map/ppermute | solution.py:655
  217.9 48.2 %collective-permute-start.23 = (bf16[4,50,16,128]{3,2,1,0:T(8,128)(2,1)}, bf16[4,50,16,128]{3,2,1,0:T(8,128)(2,1)S(1)}, u32[]{:S(2)}, u32[]{:S(2)}) collective-permute-start(bf16[4,50,16,128]{3,2,1,0:T(8,128)(2,1)} %get-tuple-element.66), channel_id=1, source_target_pairs={{0,1},{1,0},{2,3},{3,2},{4,5},{5,4},{6,7},{7,6},{8,9},{9,8},{10,11... | collective-permute-start | bytes 2457608 | tf_op jit(solution)/shard_map/ppermute | solution.py:655
  221.1 59.6 %collective-permute-start.28 = (bf16[6,50,16,128]{3,2,1,0:T(8,128)(2,1)}, bf16[6,50,16,128]{3,2,1,0:T(8,128)(2,1)}, u32[]{:S(2)}, u32[]{:S(2)}) collective-permute-start(bf16[6,50,16,128]{3,2,1,0:T(8,128)(2,1)} %get-tuple-element.65.refs_10_), channel_id=1, source_target_pairs={{1,2},{2,1},{5,6},{6,5},{9,10},{10,9},{13,14},{14,13},{17,18},{18,... | collective-permute-start | bytes 3686408 | tf_op jit(solution)/shard_map/ppermute | solution.py:655
  254.8 52.9 %collective-permute-start.30 = (bf16[8,50,16,128]{3,2,1,0:T(8,128)(2,1)}, bf16[8,50,16,128]{3,2,1,0:T(8,128)(2,1)S(1)}, u32[]{:S(2)}, u32[]{:S(2)}) collective-permute-start(bf16[8,50,16,128]{3,2,1,0:T(8,128)(2,1)} %get-tuple-element.68.refs_6_.refs_10_), channel_id=1, source_target_pairs={{0,1},{1,0},{2,3},{3,2},{4,5},{5,4},{6,7},{7,6},{8,9},{9,8},{10,11... | collective-permute-start | bytes 4915208 | tf_op jit(solution)/shard_map/ppermute | solution.py:655
  256.8 49.5 %collective-permute-start.29 = (bf16[6,50,16,128]{3,2,1,0:T(8,128)(2,1)}, bf16[6,50,16,128]{3,2,1,0:T(8,128)(2,1)}, u32[]{:S(2)}, u32[]{:S(2)}) collective-permute-start(bf16[6,50,16,128]{3,2,1,0:T(8,128)(2,1)} %get-tuple-element.74.refs_0_.refs_4_), channel_id=1, source_target_pairs={{1,2},{2,1},{5,6},{6,5},{9,10},{10,9},{13,14},{14,13},{17,18},{18,... | collective-permute-start | bytes 3686408 | tf_op jit(solution)/shard_map/ppermute | solution.py:655
  280.1 54.8 %collective-permute-start.25 = (bf16[8,64,320]{2,1,0:T(8,128)(2,1)}, bf16[8,64,320]{2,1,0:T(8,128)(2,1)S(1)}, u32[]{:S(2)}, u32[]{:S(2)}) collective-permute-start(bf16[8,64,320]{2,1,0:T(8,128)(2,1)} %get-tuple-element.70), channel_id=1, source_target_pairs={{0,8},{8,0},{16,24},{24,16},{1,9},{9,1},{17,25},{25,17},{2,10},{10... | collective-permute-start | bytes 983048 | tf_op jit(solution)/shard_map/ppermute | solution.py:689
  280.2 69.6 %collective-permute-start.26 = (bf16[8,64,320]{2,1,0:T(8,128)(2,1)}, bf16[8,64,320]{2,1,0:T(8,128)(2,1)}, u32[]{:S(2)}, u32[]{:S(2)}) collective-permute-start(bf16[8,64,320]{2,1,0:T(8,128)(2,1)} %get-tuple-element.71), channel_id=1, source_target_pairs={{0,16},{8,24},{16,0},{24,8},{1,17},{9,25},{17,1},{25,9},{2,18},{10... | collective-permute-start | bytes 983048 | tf_op jit(solution)/shard_map/ppermute | solution.py:689
  284.0 69.9 %collective-permute-start.32 = (bf16[6,50,16,128]{3,2,1,0:T(8,128)(2,1)}, bf16[6,50,16,128]{3,2,1,0:T(8,128)(2,1)S(1)}, u32[]{:S(2)}, u32[]{:S(2)}) collective-permute-start(bf16[6,50,16,128]{3,2,1,0:T(8,128)(2,1)} %get-tuple-element.73.refs_10_), channel_id=1, source_target_pairs={{1,2},{2,1},{5,6},{6,5},{9,10},{10,9},{13,14},{14,13},{17,18},{18,... | collective-permute-start | bytes 3686408 | tf_op jit(solution)/shard_map/ppermute | solution.py:655
  306.3 43.5 %collective-permute-start.27 = (bf16[8,64,320]{2,1,0:T(8,128)(2,1)}, bf16[8,64,320]{2,1,0:T(8,128)(2,1)}, u32[]{:S(2)}, u32[]{:S(2)}) collective-permute-start(bf16[8,64,320]{2,1,0:T(8,128)(2,1)} %get-tuple-element.72), channel_id=1, source_target_pairs={{0,24},{8,16},{16,8},{24,0},{1,25},{9,17},{17,9},{25,1},{2,26},{10... | collective-permute-start | bytes 983048 | tf_op jit(solution)/shard_map/ppermute | solution.py:689
  307.7 46.2 %collective-permute-start.33 = (bf16[4,50,16,128]{3,2,1,0:T(8,128)(2,1)}, bf16[4,50,16,128]{3,2,1,0:T(8,128)(2,1)}, u32[]{:S(2)}, u32[]{:S(2)}) collective-permute-start(bf16[4,50,16,128]{3,2,1,0:T(8,128)(2,1)} %get-tuple-element.79), channel_id=1, source_target_pairs={{0,1},{1,0},{2,3},{3,2},{4,5},{5,4},{6,7},{7,6},{8,9},{9,8},{10,11... | collective-permute-start | bytes 2457608 | tf_op jit(solution)/shard_map/ppermute | solution.py:655
  334.9 72.7 %collective-permute-start.40 = (bf16[4,50,16,128]{3,2,1,0:T(8,128)(2,1)}, bf16[4,50,16,128]{3,2,1,0:T(8,128)(2,1)S(1)}, u32[]{:S(2)}, u32[]{:S(2)}) collective-permute-start(bf16[4,50,16,128]{3,2,1,0:T(8,128)(2,1)} %get-tuple-element.75.refs_10_), channel_id=1, source_target_pairs={{0,1},{1,0},{2,3},{3,2},{4,5},{5,4},{6,7},{7,6},{8,9},{9,8},{10,11... | collective-permute-start | bytes 2457608 | tf_op jit(solution)/shard_map/ppermute | solution.py:655
  358.3 49.9 %collective-permute-start.38 = (bf16[6,50,16,128]{3,2,1,0:T(8,128)(2,1)}, bf16[6,50,16,128]{3,2,1,0:T(8,128)(2,1)S(1)}, u32[]{:S(2)}, u32[]{:S(2)}) collective-permute-start(bf16[6,50,16,128]{3,2,1,0:T(8,128)(2,1)} %get-tuple-element.80.refs_10_), channel_id=1, source_target_pairs={{1,2},{2,1},{5,6},{6,5},{9,10},{10,9},{13,14},{14,13},{17,18},{18,... | collective-permute-start | bytes 3686408 | tf_op jit(solution)/shard_map/ppermute | solution.py:655
  359.2 46.9 %collective-permute-start.39 = (bf16[4,50,16,128]{3,2,1,0:T(8,128)(2,1)}, bf16[4,50,16,128]{3,2,1,0:T(8,128)(2,1)S(1)}, u32[]{:S(2)}, u32[]{:S(2)}) collective-permute-start(bf16[4,50,16,128]{3,2,1,0:T(8,128)(2,1)} %get-tuple-element.87), channel_id=1, source_target_pairs={{0,1},{1,0},{2,3},{3,2},{4,5},{5,4},{6,7},{7,6},{8,9},{9,8},{10,11... | collective-permute-start | bytes 2457608 | tf_op jit(solution)/shard_map/ppermute | solution.py:655
  396.9 53.5 %collective-permute-start.41 = (bf16[8,64,320]{2,1,0:T(8,128)(2,1)}, bf16[8,64,320]{2,1,0:T(8,128)(2,1)S(1)}, u32[]{:S(2)}, u32[]{:S(2)}) collective-permute-start(bf16[8,64,320]{2,1,0:T(8,128)(2,1)} %get-tuple-element.88), channel_id=1, source_target_pairs={{0,8},{8,0},{16,24},{24,16},{1,9},{9,1},{17,25},{25,17},{2,10},{10... | collective-permute-start | bytes 983048 | tf_op jit(solution)/shard_map/ppermute | solution.py:689
  402.5 48.0 %collective-permute-start.42 = (bf16[8,64,320]{2,1,0:T(8,128)(2,1)}, bf16[8,64,320]{2,1,0:T(8,128)(2,1)S(1)}, u32[]{:S(2)}, u32[]{:S(2)}) collective-permute-start(bf16[8,64,320]{2,1,0:T(8,128)(2,1)} %get-tuple-element.89), channel_id=1, source_target_pairs={{0,16},{8,24},{16,0},{24,8},{1,17},{9,25},{17,1},{25,9},{2,18},{10... | collective-permute-start | bytes 983048 | tf_op jit(solution)/shard_map/ppermute | solution.py:689
  406.1 44.4 %collective-permute-start.43 = (bf16[8,64,320]{2,1,0:T(8,128)(2,1)}, bf16[8,64,320]{2,1,0:T(8,128)(2,1)S(1)}, u32[]{:S(2)}, u32[]{:S(2)}) collective-permute-start(bf16[8,64,320]{2,1,0:T(8,128)(2,1)} %get-tuple-element.90), channel_id=1, source_target_pairs={{0,24},{8,16},{16,8},{24,0},{1,25},{9,17},{17,9},{25,1},{2,26},{10... | collective-permute-start | bytes 983048 | tf_op jit(solution)/shard_map/ppermute | solution.py:689
  410.8 44.6 %collective-permute-start.45 = (bf16[4,50,16,128]{3,2,1,0:T(8,128)(2,1)}, bf16[4,50,16,128]{3,2,1,0:T(8,128)(2,1)S(1)}, u32[]{:S(2)}, u32[]{:S(2)}) collective-permute-start(bf16[4,50,16,128]{3,2,1,0:T(8,128)(2,1)} %pass_on.11.refs_10_), channel_id=1, source_target_pairs={{0,1},{1,0},{2,3},{3,2},{4,5},{5,4},{6,7},{7,6},{8,9},{9,8},{10,11... | collective-permute-start | bytes 2457608 | tf_op jit(solution)/shard_map/ppermute | solution.py:655
  450.1 53.0 %collective-permute-start.49 = (bf16[8,64,320]{2,1,0:T(8,128)(2,1)}, bf16[8,64,320]{2,1,0:T(8,128)(2,1)S(1)}, u32[]{:S(2)}, u32[]{:S(2)}) collective-permute-start(bf16[8,64,320]{2,1,0:T(8,128)(2,1)} %get-tuple-element.95), channel_id=1, source_target_pairs={{0,8},{8,0},{16,24},{24,16},{1,9},{9,1},{17,25},{25,17},{2,10},{10... | collective-permute-start | bytes 983048 | tf_op jit(solution)/shard_map/ppermute | solution.py:689
  (80 other events, 1072.6 us)

commit v11 on v8

--- a/solution.py
+++ b/solution.py
@@ -728,7 +728,7 @@
         if r <= chunks:
             fresh = r < chunks
             base = 3 * groups if fresh else 0
-            most = {0: 3, 1: 2}.get(r, 1) * groups if fresh else 0
+            most = {0: 1, 1: 3}.get(r, 1) * groups if fresh else 0
             at, size = take(most)
             length = max(base + size, 4 * groups) if fresh else 2 * groups
             given = dict(
@@ -754,7 +754,7 @@
             if r == 0:
                 late = mark[1]
                 outer = [lower(0, late), lower(2, late)]
-                extra = list(outer)
+                extra = outer[:1]
         t = r - 4
         if 0 <= t < chunks:
             if near_low is None:

time: 588 us -> 579 us (0.985)
  waiting for transfers between devices: 103 us -> 94 us
    ppermute x22, waiting for transfers between devices: 45.9 us -> 35.1 us  [on_device(): move = lambda value, perm: lax.ppermute(value, 'horiz', perm)]
  transfers between devices with their start and end apart: 65 -> 65, of which waited for: 20 -> 20; matrix products, arithmetic and copies ran while one was open for 14% -> 15% of each run, Pallas kernels for 40% -> 40%
where the time goes in v11:
time: 579 us; the launch traced here: 570 us
  Pallas kernels  246 us (42%)
  starting transfers between devices  120 us (21%)
  waiting for transfers between devices  94 us (16%)
  local copies, waits for them, and re-layouts  86.6 us (15%)
  other arithmetic  12.8 us (2%)
    pallas_call x6, Pallas kernels, even_product(): pl.pallas_call(functools.partial(even_kernel, sides, group, groups, slab,...  112 us
    ppermute x22, starting transfers between devices, on_device(): move = lambda value, perm: lax.ppermute(value, 'horiz', perm)  72 us
    pallas_call x5, Pallas kernels, odd_product(): pl.pallas_call(functools.partial(odd_kernel, sides, group, groups, slab,...  42 us
    ppermute x22, waiting for transfers between devices, on_device(): move = lambda value, perm: lax.ppermute(value, 'horiz', perm)  35.1 us
    pallas_call x6, Pallas kernels, pack(): pl.pallas_call(functools.partial(pack_kernel, group, len(pieces), given),...  27.4 us
    ppermute x15, waiting for transfers between devices, send_roles(): lax.ppermute(shares[t][s], 'role', [(j, j ^ s) for j in range(roles)])  24.2 us
    reshape x2, local copies, waits for them, and re-layouts, lower(): return low.reshape(depth, slab, downs * full)  21.1 us
    unnamed x79, local copies, waits for them, and re-layouts  20.6 us
  transfers between devices with their start and end apart: 65, of which 20 were waited for; matrix products, arithmetic and copies ran while one was open for 15% of the time, Pallas kernels for 40%

profile of v11, /device:TPU:0, one launch (start us, length us, event | category | flops | bytes accessed | tf_op | source)
XLA Modules:
  0.0 570.1 jit_solution(8744018643575742684)
XLA Ops:
  9.7 8.6 %dynamic-slice_multiply_fusion = bf16[1,40,80,2,320]{4,3,2,1,0:T(2,128)(2,1)} fusion(bf16[3,160,80,2,320]{4,3,2,1,0:T(2,128)(2,1)} %param.5, s32[]{:T(128)S(6)} %select_n.95), kind=kLoop, calls=%fused_computation | loop fusion | flops 2048000 | bytes 8192004 | tf_op jit(solution)/shard_map/mul | solution.py:668
  18.4 10.5 %mul.103.low_ref.refs_0_ = bf16[40,80,640]{2,1,0:T(8,128)(2,1)} reshape(bf16[1,40,80,2,320]{4,3,2,1,0:T(2,128)(2,1)} %dynamic-slice_multiply_fusion) | data formatting | bytes 8192000 | tf_op jit(solution)/shard_map/mul | solution.py:668
  51.4 9.7 %constant_dynamic-slice_fusion.16 = (bf16[1,40,80,2,320]{4,3,2,1,0:T(2,128)(2,1)}, bf16[1,40,80,2,320]{4,3,2,1,0:T(2,128)(2,1)}) fusion(bf16[3,160,80,2,320]{4,3,2,1,0:T(2,128)(2,1)} %param.5, s32[]{:T(128)S(6)} %select_n.99), kind=kLoop, calls=%fused_computation.56 | loop fusion | bytes 16384004 | tf_op jit(solution)/shard_map/dynamic_slice | solution.py:647
  61.1 10.5 %reshape.88.refs_7_.refs_0_ = bf16[40,80,640]{2,1,0:T(8,128)(2,1)} reshape(bf16[1,40,80,2,320]{4,3,2,1,0:T(2,128)(2,1)} %get-tuple-element.104) | data formatting | bytes 8192000 | tf_op jit(solution)/shard_map/reshape | solution.py:650
  95.4 10.5 %reshape.90.refs_1_ = bf16[40,80,640]{2,1,0:T(8,128)(2,1)} reshape(bf16[1,40,80,2,320]{4,3,2,1,0:T(2,128)(2,1)} %get-tuple-element.103) | data formatting | bytes 8192000 | tf_op jit(solution)/shard_map/reshape | solution.py:650
  128.2 11.6 %collective-permute-done.10.refs_6_.refs_0_.refs_1_.refs_5_ = bf16[12,50,16,128]{3,2,1,0:T(8,128)(2,1)S(1)} collective-permute-done((bf16[12,50,16,128]{3,2,1,0:T(8,128)(2,1)}, bf16[12,50,16,128]{3,2,1,0:T(8,128)(2,1)S(1)}, u32[]{:S(2)}, u32[]{:S(2)}) %collective-permute-start.10) | collective-permute-done | bytes 2457632 | tf_op jit(solution)/shard_map/ppermute | solution.py:655
  167.3 10.4 %collective-permute-done.20.refs_3_ = bf16[2,3,40,16,80]{4,3,2,1,0:T(8,128)(2,1)S(1)} collective-permute-done((bf16[2,3,40,16,80]{4,3,2,1,0:T(8,128)(2,1)}, bf16[2,3,40,16,80]{4,3,2,1,0:T(8,128)(2,1)S(1)}, u32[]{:S(2)}, u32[]{:S(2)}) %collective-permute-start.20) | collective-permute-done | bytes 614432 | tf_op jit(solution)/shard_map/ppermute | solution.py:641
  177.8 8.0 %collective-permute-done.17.refs_6_.refs_0_.refs_2_.refs_1_.refs_5_ = bf16[8,50,16,128]{3,2,1,0:T(8,128)(2,1)S(1)} collective-permute-done((bf16[8,50,16,128]{3,2,1,0:T(8,128)(2,1)}, bf16[8,50,16,128]{3,2,1,0:T(8,128)(2,1)S(1)}, u32[]{:S(2)}, u32[]{:S(2)}) %collective-permute-start.17) | collective-permute-done | bytes 1638432 | tf_op jit(solution)/shard_map/ppermute | solution.py:655
  212.8 21.2 %even_product.7.refs_0_.refs_7_.refs_5_.refs_4_ = f32[2,512,640]{2,1,0:T(8,128)} custom-call(s32[3]{0:T(128)} %pad_add_fusion.spot_ref, bf16[6,50,16,128]{3,2,1,0:T(8,128)(2,1)} %get-tuple-element.58.refs_0_.refs_4_, bf16[12,50,16,128]{3,2,1,0:T(8,128)(2,1)} %copy-done, bf16[6,50,16,128]{3,2,1,0:T(8,128)(2,1)} %collective-permute-done.14.refs_4_.refs_2_, ...), custom_call_target="tpu_custom_call" | custom-call | flops 11072962560 | bytes 20971520 | tf_op jit(solution)/shard_map/even_product/pallas_call | solution.py:506
  248.2 7.8 %collective-permute-done.23.refs_5_.refs_4_.refs_7_ = bf16[4,50,16,128]{3,2,1,0:T(8,128)(2,1)S(1)} collective-permute-done((bf16[4,50,16,128]{3,2,1,0:T(8,128)(2,1)}, bf16[4,50,16,128]{3,2,1,0:T(8,128)(2,1)S(1)}, u32[]{:S(2)}, u32[]{:S(2)}) %collective-permute-start.23) | collective-permute-done | bytes 819232 | tf_op jit(solution)/shard_map/ppermute | solution.py:655
  261.7 8.4 %odd_product.5 = (bf16[8,64,320]{2,1,0:T(8,128)(2,1)}, bf16[8,64,320]{2,1,0:T(8,128)(2,1)}, bf16[8,64,320]{2,1,0:T(8,128)(2,1)}, bf16[8,64,320]{2,1,0:T(8,128)(2,1)}) custom-call(s32[3]{0:T(128)} %pad_add_fusion.spot_ref, bf16[6,50,16,128]{3,2,1,0:T(8,128)(2,1)} %get-tuple-element.54.refs_0_.refs_4_, bf16[8,50,16,128]{3,2,1,0:T(8,128)(2,1)} %copy-done.1, ...), custom_call_target="tpu_custom_call" | custom-call | flops 8724152320 | bytes 20971520 | tf_op jit(solution)/shard_map/odd_product/pallas_call | solution.py:591
  276.1 21.1 %even_product.8.refs_3_.refs_5_.refs_4_ = f32[2,512,640]{2,1,0:T(8,128)} custom-call(s32[3]{0:T(128)} %pad_add_fusion.spot_ref, bf16[6,50,16,128]{3,2,1,0:T(8,128)(2,1)} %get-tuple-element.63.refs_0_.refs_4_, bf16[8,50,16,128]{3,2,1,0:T(8,128)(2,1)} %copy-done.2, bf16[6,50,16,128]{3,2,1,0:T(8,128)(2,1)} %collective-permute-done.21.refs_4_.refs_2_, ...), custom_call_target="tpu_custom_call" | custom-call | flops 11072962560 | bytes 20971520 | tf_op jit(solution)/shard_map/even_product/pallas_call | solution.py:506
  297.6 15.8 %collective-permute-start.33 = (bf16[4,50,16,128]{3,2,1,0:T(8,128)(2,1)}, bf16[4,50,16,128]{3,2,1,0:T(8,128)(2,1)S(1)}, u32[]{:S(2)}, u32[]{:S(2)}) collective-permute-start(bf16[4,50,16,128]{3,2,1,0:T(8,128)(2,1)} %get-tuple-element.79), channel_id=1, source_target_pairs={{0,1},{1,0},{2,3},{3,2},{4,5},{5,4},{6,7},{7,6},{8,9},{9,8},{10,11... | collective-permute-start | bytes 2457608 | tf_op jit(solution)/shard_map/ppermute | solution.py:655
  315.0 8.4 %odd_product.6 = (bf16[8,64,320]{2,1,0:T(8,128)(2,1)}, bf16[8,64,320]{2,1,0:T(8,128)(2,1)}, bf16[8,64,320]{2,1,0:T(8,128)(2,1)}, bf16[8,64,320]{2,1,0:T(8,128)(2,1)}) custom-call(s32[3]{0:T(128)} %pad_add_fusion.spot_ref, bf16[6,50,16,128]{3,2,1,0:T(8,128)(2,1)} %get-tuple-element.58.refs_0_.refs_4_, bf16[12,50,16,128]{3,2,1,0:T(8,128)(2,1)} %copy-done, ...), custom_call_target="tpu_custom_call" | custom-call | flops 8724152320 | bytes 20971520 | tf_op jit(solution)/shard_map/odd_product/pallas_call | solution.py:591
  323.4 14.8 %collective-permute-start.40 = (bf16[4,50,16,128]{3,2,1,0:T(8,128)(2,1)}, bf16[4,50,16,128]{3,2,1,0:T(8,128)(2,1)S(1)}, u32[]{:S(2)}, u32[]{:S(2)}) collective-permute-start(bf16[4,50,16,128]{3,2,1,0:T(8,128)(2,1)} %get-tuple-element.75.refs_10_), channel_id=1, source_target_pairs={{0,1},{1,0},{2,3},{3,2},{4,5},{5,4},{6,7},{7,6},{8,9},{9,8},{10,11... | collective-permute-start | bytes 2457608 | tf_op jit(solution)/shard_map/ppermute | solution.py:655
  351.7 21.1 %even_product.9.refs_0_.refs_5_.refs_10_.refs_4_ = f32[2,512,640]{2,1,0:T(8,128)} custom-call(s32[3]{0:T(128)} %pad_add_fusion.spot_ref, bf16[6,50,16,128]{3,2,1,0:T(8,128)(2,1)} %get-tuple-element.67.refs_0_.refs_4_, bf16[8,50,16,128]{3,2,1,0:T(8,128)(2,1)} %copy-done.3, bf16[6,50,16,128]{3,2,1,0:T(8,128)(2,1)} %collective-permute-done.24.refs_4_.refs_2_, ...), custom_call_target="tpu_custom_call" | custom-call | flops 11072962560 | bytes 20971520 | tf_op jit(solution)/shard_map/even_product/pallas_call | solution.py:506
  376.3 8.4 %odd_product.7 = (bf16[8,64,320]{2,1,0:T(8,128)(2,1)}, bf16[8,64,320]{2,1,0:T(8,128)(2,1)}, bf16[8,64,320]{2,1,0:T(8,128)(2,1)}, bf16[8,64,320]{2,1,0:T(8,128)(2,1)}) custom-call(s32[3]{0:T(128)} %pad_add_fusion.spot_ref, bf16[6,50,16,128]{3,2,1,0:T(8,128)(2,1)} %get-tuple-element.63.refs_0_.refs_4_, bf16[8,50,16,128]{3,2,1,0:T(8,128)(2,1)} %copy-done.2, ...), custom_call_target="tpu_custom_call" | custom-call | flops 8724152320 | bytes 20971520 | tf_op jit(solution)/shard_map/odd_product/pallas_call | solution.py:591
  399.3 7.9 %collective-permute-start.45 = (bf16[4,50,16,128]{3,2,1,0:T(8,128)(2,1)}, bf16[4,50,16,128]{3,2,1,0:T(8,128)(2,1)S(1)}, u32[]{:S(2)}, u32[]{:S(2)}) collective-permute-start(bf16[4,50,16,128]{3,2,1,0:T(8,128)(2,1)} %pass_on.11.refs_10_), channel_id=1, source_target_pairs={{0,1},{1,0},{2,3},{3,2},{4,5},{5,4},{6,7},{7,6},{8,9},{9,8},{10,11... | collective-permute-start | bytes 2457608 | tf_op jit(solution)/shard_map/ppermute | solution.py:655
  407.2 21.3 %even_product.10.refs_0_.refs_5_.refs_10_.refs_4_ = f32[2,512,640]{2,1,0:T(8,128)} custom-call(s32[3]{0:T(128)} %pad_add_fusion.spot_ref, bf16[6,50,16,128]{3,2,1,0:T(8,128)(2,1)} %get-tuple-element.74.refs_0_.refs_4_, bf16[8,50,16,128]{3,2,1,0:T(8,128)(2,1)} %copy-done.4, bf16[6,50,16,128]{3,2,1,0:T(8,128)(2,1)} %collective-permute-done.29.refs_0_.refs_2_, ...), custom_call_target="tpu_custom_call" | custom-call | flops 11072962560 | bytes 20971520 | tf_op jit(solution)/shard_map/even_product/pallas_call | solution.py:506
  431.0 8.4 %odd_product.8 = (bf16[8,64,320]{2,1,0:T(8,128)(2,1)}, bf16[8,64,320]{2,1,0:T(8,128)(2,1)}, bf16[8,64,320]{2,1,0:T(8,128)(2,1)}, bf16[8,64,320]{2,1,0:T(8,128)(2,1)}) custom-call(s32[3]{0:T(128)} %pad_add_fusion.spot_ref, bf16[6,50,16,128]{3,2,1,0:T(8,128)(2,1)} %get-tuple-element.67.refs_0_.refs_4_, bf16[8,50,16,128]{3,2,1,0:T(8,128)(2,1)} %copy-done.3, ...), custom_call_target="tpu_custom_call" | custom-call | flops 8724152320 | bytes 20971520 | tf_op jit(solution)/shard_map/odd_product/pallas_call | solution.py:591
  446.4 21.6 %even_product.11.refs_0_.refs_5_.refs_10_ = f32[2,512,640]{2,1,0:T(8,128)} custom-call(s32[3]{0:T(128)} %pad_add_fusion.spot_ref, bf16[6,50,16,128]{3,2,1,0:T(8,128)(2,1)} %get-tuple-element.74.refs_0_.refs_4_, bf16[8,50,16,128]{3,2,1,0:T(8,128)(2,1)} %copy-done.4, bf16[4,50,16,128]{3,2,1,0:T(8,128)(2,1)} %copy-done.16, bf16[4,50,16,128]{3,2,1,0:T(8,128)(2,1)} %copy-done.34, ...), custom_call_target="tpu_custom_call" | custom-call | flops 11072962560 | bytes 20971520 | tf_op jit(solution)/shard_map/even_product/pallas_call | solution.py:506
  476.2 8.5 %odd_product.9 = (bf16[8,64,320]{2,1,0:T(8,128)(2,1)}, bf16[8,64,320]{2,1,0:T(8,128)(2,1)}, bf16[8,64,320]{2,1,0:T(8,128)(2,1)}, bf16[8,64,320]{2,1,0:T(8,128)(2,1)}) custom-call(s32[3]{0:T(128)} %pad_add_fusion.spot_ref, bf16[6,50,16,128]{3,2,1,0:T(8,128)(2,1)} %get-tuple-element.74.refs_0_.refs_4_, bf16[8,50,16,128]{3,2,1,0:T(8,128)(2,1)} %copy-done.4, ...), custom_call_target="tpu_custom_call" | custom-call | flops 8724152320 | bytes 20971520 | tf_op jit(solution)/shard_map/odd_product/pallas_call | solution.py:591
  504.1 8.9 %collective-permute-done.54.refs_7_ = bf16[8,64,320]{2,1,0:T(8,128)(2,1)} collective-permute-done((bf16[8,64,320]{2,1,0:T(8,128)(2,1)}, bf16[8,64,320]{2,1,0:T(8,128)(2,1)}, u32[]{:S(2)}, u32[]{:S(2)}) %collective-permute-start.54) | collective-permute-done | bytes 327712 | tf_op jit(solution)/shard_map/ppermute | solution.py:689
  531.1 12.2 %collective-permute-start.56 = (bf16[2,8,1,8,320]{4,1,3,0,2:T(8,128)(2,1)S(1)}, bf16[2,8,1,8,320]{4,1,3,0,2:T(8,128)(2,1)S(1)}, u32[]{:S(2)}, u32[]{:S(2)}) collective-permute-start(bf16[2,8,1,8,320]{4,1,3,0,2:T(8,128)(2,1)S(1)} %copy.120), channel_id=1, source_target_pairs={{0,1},{1,0},{2,3},{3,2},{4,5},{5,4},{6,7},{7,6},{8,9},{9,8},{10,11... | collective-permute-start | bytes 245768 | tf_op jit(solution)/shard_map/ppermute | solution.py:719
  (256 shorter events, 268.7 us)
Async XLA Ops:
  85.1 54.7 %collective-permute-start.10 = (bf16[12,50,16,128]{3,2,1,0:T(8,128)(2,1)}, bf16[12,50,16,128]{3,2,1,0:T(8,128)(2,1)S(1)}, u32[]{:S(2)}, u32[]{:S(2)}) collective-permute-start(bf16[12,50,16,128]{3,2,1,0:T(8,128)(2,1)} %get-tuple-element.57.refs_3_), channel_id=1, source_target_pairs={{0,1},{1,0},{2,3},{3,2},{4,5},{5,4},{6,7},{7,6},{8,9},{9,8},{10,11... | collective-permute-start | bytes 7372808 | tf_op jit(solution)/shard_map/ppermute | solution.py:655
  85.5 42.8 %collective-permute-start.14 = (bf16[6,50,16,128]{3,2,1,0:T(8,128)(2,1)}, bf16[6,50,16,128]{3,2,1,0:T(8,128)(2,1)}, u32[]{:S(2)}, u32[]{:S(2)}) collective-permute-start(bf16[6,50,16,128]{3,2,1,0:T(8,128)(2,1)} %get-tuple-element.58.refs_0_.refs_4_), channel_id=1, source_target_pairs={{1,2},{2,1},{5,6},{6,5},{9,10},{10,9},{13,14},{14,13},{17,18},{18,... | collective-permute-start | bytes 3686408 | tf_op jit(solution)/shard_map/ppermute | solution.py:655
  90.3 63.3 %collective-permute-start.9 = (bf16[6,50,16,128]{3,2,1,0:T(8,128)(2,1)}, bf16[6,50,16,128]{3,2,1,0:T(8,128)(2,1)}, u32[]{:S(2)}, u32[]{:S(2)}) collective-permute-start(bf16[6,50,16,128]{3,2,1,0:T(8,128)(2,1)} %pass_on.6.refs_0_), channel_id=1, source_target_pairs={{1,2},{2,1},{5,6},{6,5},{9,10},{10,9},{13,14},{14,13},{17,18},{18,... | collective-permute-start | bytes 3686408 | tf_op jit(solution)/shard_map/ppermute | solution.py:655
  157.5 45.8 %collective-permute-start.15 = (bf16[6,50,16,128]{3,2,1,0:T(8,128)(2,1)}, bf16[6,50,16,128]{3,2,1,0:T(8,128)(2,1)}, u32[]{:S(2)}, u32[]{:S(2)}) collective-permute-start(bf16[6,50,16,128]{3,2,1,0:T(8,128)(2,1)} %get-tuple-element.60.refs_10_), channel_id=1, source_target_pairs={{1,2},{2,1},{5,6},{6,5},{9,10},{10,9},{13,14},{14,13},{17,18},{18,... | collective-permute-start | bytes 3686408 | tf_op jit(solution)/shard_map/ppermute | solution.py:655
  159.3 44.1 %collective-permute-start.16 = (bf16[4,50,16,128]{3,2,1,0:T(8,128)(2,1)}, bf16[4,50,16,128]{3,2,1,0:T(8,128)(2,1)S(1)}, u32[]{:S(2)}, u32[]{:S(2)}) collective-permute-start(bf16[4,50,16,128]{3,2,1,0:T(8,128)(2,1)} %get-tuple-element.61), channel_id=1, source_target_pairs={{0,1},{1,0},{2,3},{3,2},{4,5},{5,4},{6,7},{7,6},{8,9},{9,8},{10,11... | collective-permute-start | bytes 2457608 | tf_op jit(solution)/shard_map/ppermute | solution.py:655
  192.0 46.6 %collective-permute-start.22 = (bf16[8,50,16,128]{3,2,1,0:T(8,128)(2,1)}, bf16[8,50,16,128]{3,2,1,0:T(8,128)(2,1)S(1)}, u32[]{:S(2)}, u32[]{:S(2)}) collective-permute-start(bf16[8,50,16,128]{3,2,1,0:T(8,128)(2,1)} %get-tuple-element.64.refs_3_), channel_id=1, source_target_pairs={{0,1},{1,0},{2,3},{3,2},{4,5},{5,4},{6,7},{7,6},{8,9},{9,8},{10,11... | collective-permute-start | bytes 4915208 | tf_op jit(solution)/shard_map/ppermute | solution.py:655
  197.4 41.2 %collective-permute-start.24 = (bf16[6,50,16,128]{3,2,1,0:T(8,128)(2,1)}, bf16[6,50,16,128]{3,2,1,0:T(8,128)(2,1)}, u32[]{:S(2)}, u32[]{:S(2)}) collective-permute-start(bf16[6,50,16,128]{3,2,1,0:T(8,128)(2,1)} %get-tuple-element.67.refs_0_.refs_4_), channel_id=1, source_target_pairs={{1,2},{2,1},{5,6},{6,5},{9,10},{10,9},{13,14},{14,13},{17,18},{18,... | collective-permute-start | bytes 3686408 | tf_op jit(solution)/shard_map/ppermute | solution.py:655
  207.8 48.2 %collective-permute-start.23 = (bf16[4,50,16,128]{3,2,1,0:T(8,128)(2,1)}, bf16[4,50,16,128]{3,2,1,0:T(8,128)(2,1)S(1)}, u32[]{:S(2)}, u32[]{:S(2)}) collective-permute-start(bf16[4,50,16,128]{3,2,1,0:T(8,128)(2,1)} %get-tuple-element.66), channel_id=1, source_target_pairs={{0,1},{1,0},{2,3},{3,2},{4,5},{5,4},{6,7},{7,6},{8,9},{9,8},{10,11... | collective-permute-start | bytes 2457608 | tf_op jit(solution)/shard_map/ppermute | solution.py:655
  211.0 60.7 %collective-permute-start.28 = (bf16[6,50,16,128]{3,2,1,0:T(8,128)(2,1)}, bf16[6,50,16,128]{3,2,1,0:T(8,128)(2,1)}, u32[]{:S(2)}, u32[]{:S(2)}) collective-permute-start(bf16[6,50,16,128]{3,2,1,0:T(8,128)(2,1)} %get-tuple-element.65.refs_10_), channel_id=1, source_target_pairs={{1,2},{2,1},{5,6},{6,5},{9,10},{10,9},{13,14},{14,13},{17,18},{18,... | collective-permute-start | bytes 3686408 | tf_op jit(solution)/shard_map/ppermute | solution.py:655
  244.7 52.9 %collective-permute-start.30 = (bf16[8,50,16,128]{3,2,1,0:T(8,128)(2,1)}, bf16[8,50,16,128]{3,2,1,0:T(8,128)(2,1)S(1)}, u32[]{:S(2)}, u32[]{:S(2)}) collective-permute-start(bf16[8,50,16,128]{3,2,1,0:T(8,128)(2,1)} %get-tuple-element.68.refs_6_.refs_10_), channel_id=1, source_target_pairs={{0,1},{1,0},{2,3},{3,2},{4,5},{5,4},{6,7},{7,6},{8,9},{9,8},{10,11... | collective-permute-start | bytes 4915208 | tf_op jit(solution)/shard_map/ppermute | solution.py:655
  246.5 50.7 %collective-permute-start.29 = (bf16[6,50,16,128]{3,2,1,0:T(8,128)(2,1)}, bf16[6,50,16,128]{3,2,1,0:T(8,128)(2,1)}, u32[]{:S(2)}, u32[]{:S(2)}) collective-permute-start(bf16[6,50,16,128]{3,2,1,0:T(8,128)(2,1)} %get-tuple-element.74.refs_0_.refs_4_), channel_id=1, source_target_pairs={{1,2},{2,1},{5,6},{6,5},{9,10},{10,9},{13,14},{14,13},{17,18},{18,... | collective-permute-start | bytes 3686408 | tf_op jit(solution)/shard_map/ppermute | solution.py:655
  270.0 53.4 %collective-permute-start.25 = (bf16[8,64,320]{2,1,0:T(8,128)(2,1)}, bf16[8,64,320]{2,1,0:T(8,128)(2,1)S(1)}, u32[]{:S(2)}, u32[]{:S(2)}) collective-permute-start(bf16[8,64,320]{2,1,0:T(8,128)(2,1)} %get-tuple-element.70), channel_id=1, source_target_pairs={{0,8},{8,0},{16,24},{24,16},{1,9},{9,1},{17,25},{25,17},{2,10},{10... | collective-permute-start | bytes 983048 | tf_op jit(solution)/shard_map/ppermute | solution.py:689
  270.1 68.2 %collective-permute-start.26 = (bf16[8,64,320]{2,1,0:T(8,128)(2,1)}, bf16[8,64,320]{2,1,0:T(8,128)(2,1)}, u32[]{:S(2)}, u32[]{:S(2)}) collective-permute-start(bf16[8,64,320]{2,1,0:T(8,128)(2,1)} %get-tuple-element.71), channel_id=1, source_target_pairs={{0,16},{8,24},{16,0},{24,8},{1,17},{9,25},{17,1},{25,9},{2,18},{10... | collective-permute-start | bytes 983048 | tf_op jit(solution)/shard_map/ppermute | solution.py:689
  274.9 67.5 %collective-permute-start.32 = (bf16[6,50,16,128]{3,2,1,0:T(8,128)(2,1)}, bf16[6,50,16,128]{3,2,1,0:T(8,128)(2,1)S(1)}, u32[]{:S(2)}, u32[]{:S(2)}) collective-permute-start(bf16[6,50,16,128]{3,2,1,0:T(8,128)(2,1)} %get-tuple-element.73.refs_10_), channel_id=1, source_target_pairs={{1,2},{2,1},{5,6},{6,5},{9,10},{10,9},{13,14},{14,13},{17,18},{18,... | collective-permute-start | bytes 3686408 | tf_op jit(solution)/shard_map/ppermute | solution.py:655
  297.2 41.1 %collective-permute-start.27 = (bf16[8,64,320]{2,1,0:T(8,128)(2,1)}, bf16[8,64,320]{2,1,0:T(8,128)(2,1)}, u32[]{:S(2)}, u32[]{:S(2)}) collective-permute-start(bf16[8,64,320]{2,1,0:T(8,128)(2,1)} %get-tuple-element.72), channel_id=1, source_target_pairs={{0,24},{8,16},{16,8},{24,0},{1,25},{9,17},{17,9},{25,1},{2,26},{10... | collective-permute-start | bytes 983048 | tf_op jit(solution)/shard_map/ppermute | solution.py:689
  297.6 44.8 %collective-permute-start.33 = (bf16[4,50,16,128]{3,2,1,0:T(8,128)(2,1)}, bf16[4,50,16,128]{3,2,1,0:T(8,128)(2,1)S(1)}, u32[]{:S(2)}, u32[]{:S(2)}) collective-permute-start(bf16[4,50,16,128]{3,2,1,0:T(8,128)(2,1)} %get-tuple-element.79), channel_id=1, source_target_pairs={{0,1},{1,0},{2,3},{3,2},{4,5},{5,4},{6,7},{7,6},{8,9},{9,8},{10,11... | collective-permute-start | bytes 2457608 | tf_op jit(solution)/shard_map/ppermute | solution.py:655
  323.4 72.7 %collective-permute-start.40 = (bf16[4,50,16,128]{3,2,1,0:T(8,128)(2,1)}, bf16[4,50,16,128]{3,2,1,0:T(8,128)(2,1)S(1)}, u32[]{:S(2)}, u32[]{:S(2)}) collective-permute-start(bf16[4,50,16,128]{3,2,1,0:T(8,128)(2,1)} %get-tuple-element.75.refs_10_), channel_id=1, source_target_pairs={{0,1},{1,0},{2,3},{3,2},{4,5},{5,4},{6,7},{7,6},{8,9},{9,8},{10,11... | collective-permute-start | bytes 2457608 | tf_op jit(solution)/shard_map/ppermute | solution.py:655
  347.1 49.5 %collective-permute-start.38 = (bf16[6,50,16,128]{3,2,1,0:T(8,128)(2,1)}, bf16[6,50,16,128]{3,2,1,0:T(8,128)(2,1)S(1)}, u32[]{:S(2)}, u32[]{:S(2)}) collective-permute-start(bf16[6,50,16,128]{3,2,1,0:T(8,128)(2,1)} %get-tuple-element.80.refs_10_), channel_id=1, source_target_pairs={{1,2},{2,1},{5,6},{6,5},{9,10},{10,9},{13,14},{14,13},{17,18},{18,... | collective-permute-start | bytes 3686408 | tf_op jit(solution)/shard_map/ppermute | solution.py:655
  348.0 46.9 %collective-permute-start.39 = (bf16[4,50,16,128]{3,2,1,0:T(8,128)(2,1)}, bf16[4,50,16,128]{3,2,1,0:T(8,128)(2,1)S(1)}, u32[]{:S(2)}, u32[]{:S(2)}) collective-permute-start(bf16[4,50,16,128]{3,2,1,0:T(8,128)(2,1)} %get-tuple-element.87), channel_id=1, source_target_pairs={{0,1},{1,0},{2,3},{3,2},{4,5},{5,4},{6,7},{7,6},{8,9},{9,8},{10,11... | collective-permute-start | bytes 2457608 | tf_op jit(solution)/shard_map/ppermute | solution.py:655
  385.9 53.4 %collective-permute-start.41 = (bf16[8,64,320]{2,1,0:T(8,128)(2,1)}, bf16[8,64,320]{2,1,0:T(8,128)(2,1)S(1)}, u32[]{:S(2)}, u32[]{:S(2)}) collective-permute-start(bf16[8,64,320]{2,1,0:T(8,128)(2,1)} %get-tuple-element.88), channel_id=1, source_target_pairs={{0,8},{8,0},{16,24},{24,16},{1,9},{9,1},{17,25},{25,17},{2,10},{10... | collective-permute-start | bytes 983048 | tf_op jit(solution)/shard_map/ppermute | solution.py:689
  391.3 48.0 %collective-permute-start.42 = (bf16[8,64,320]{2,1,0:T(8,128)(2,1)}, bf16[8,64,320]{2,1,0:T(8,128)(2,1)S(1)}, u32[]{:S(2)}, u32[]{:S(2)}) collective-permute-start(bf16[8,64,320]{2,1,0:T(8,128)(2,1)} %get-tuple-element.89), channel_id=1, source_target_pairs={{0,16},{8,24},{16,0},{24,8},{1,17},{9,25},{17,1},{25,9},{2,18},{10... | collective-permute-start | bytes 983048 | tf_op jit(solution)/shard_map/ppermute | solution.py:689
  394.9 44.4 %collective-permute-start.43 = (bf16[8,64,320]{2,1,0:T(8,128)(2,1)}, bf16[8,64,320]{2,1,0:T(8,128)(2,1)}, u32[]{:S(2)}, u32[]{:S(2)}) collective-permute-start(bf16[8,64,320]{2,1,0:T(8,128)(2,1)} %get-tuple-element.90), channel_id=1, source_target_pairs={{0,24},{8,16},{16,8},{24,0},{1,25},{9,17},{17,9},{25,1},{2,26},{10... | collective-permute-start | bytes 983048 | tf_op jit(solution)/shard_map/ppermute | solution.py:689
  399.3 46.3 %collective-permute-start.45 = (bf16[4,50,16,128]{3,2,1,0:T(8,128)(2,1)}, bf16[4,50,16,128]{3,2,1,0:T(8,128)(2,1)S(1)}, u32[]{:S(2)}, u32[]{:S(2)}) collective-permute-start(bf16[4,50,16,128]{3,2,1,0:T(8,128)(2,1)} %pass_on.11.refs_10_), channel_id=1, source_target_pairs={{0,1},{1,0},{2,3},{3,2},{4,5},{5,4},{6,7},{7,6},{8,9},{9,8},{10,11... | collective-permute-start | bytes 2457608 | tf_op jit(solution)/shard_map/ppermute | solution.py:655
  444.3 50.3 %collective-permute-start.50 = (bf16[8,64,320]{2,1,0:T(8,128)(2,1)}, bf16[8,64,320]{2,1,0:T(8,128)(2,1)S(1)}, u32[]{:S(2)}, u32[]{:S(2)}) collective-permute-start(bf16[8,64,320]{2,1,0:T(8,128)(2,1)} %get-tuple-element.95), channel_id=1, source_target_pairs={{0,16},{8,24},{16,0},{24,8},{1,17},{9,25},{17,1},{25,9},{2,18},{10... | collective-permute-start | bytes 983048 | tf_op jit(solution)/shard_map/ppermute | solution.py:689
  (78 other events, 1059.5 us)
